TPU v7x, 256 devices: a whole 4x4x8 slice. The times are simulated.
256 devices in a mesh: fsdp: 32 (over z, y_hi, core), ctx: 8 (over y_lo, x).
Axes of the slice: x: 4, y: 4 (y_hi: 2, y_lo: 2; y = y_hi * 2 + y_lo), z: 8, core: 2. Of those that a mesh axis runs over, the one named last changes fastest.
Arguments:
- inputs: bfloat16 [32, 1024, 2560], P('fsdp', 'ctx'), may hold values from -6 to 6
- queries: bfloat16 [32, 1024, 4096], P('fsdp', 'ctx')
- keys: bfloat16 [32, 1024, 512], P('fsdp', 'ctx')
- values: bfloat16 [32, 1024, 512], P('fsdp', 'ctx'), may hold values from -6 to 6
- output_cotangent: bfloat16 [32, 1024, 4096], P('fsdp', 'ctx'), may hold values from -6 to 6
- key_value_weight: bfloat16 [2560, 1024], P('fsdp'), may hold values from -0.1875 to 0.1875
- doc_ids: int32 [32, 32], P('fsdp'), may hold values from 0 to 7, never falling along the last dimension, each value on 1 to 16 neighbouring positions
- block_order: int32 [32], replicated, may hold values from 0 to 31, each once
Outputs:
- input_grad: bfloat16 [32, 1024, 2560], P('fsdp', 'ctx')
- query_grad: bfloat16 [32, 1024, 4096], P('fsdp', 'ctx')
- kv_grad: bfloat16 [32, 1024, 1024], P('fsdp', 'ctx')
- weight_grad: float32 [2560, 1024], P(('fsdp', 'ctx'))
Inputs may be any that keep to these rules, and one draw needn't show every extreme that they name: `doc_ids`: each slab's document numbers are 0 to 7 in sequence order, never falling; every document covers 1 to 16 blocks and one covers exactly 16. `block_order`: each sequence block is held by exactly one stored block.
All inputs are finite; a program needn't handle non-finite values.
Results may differ from a plain program's by a relative error of at most 0.015.
Values may be sent and summed in bfloat16 or wider, within the bound.
No kernel may reach another device: no remote copies, remote signals or barrier semaphores. Data moves between devices by JAX's collectives and lax.ppermute only.
A program may use at most 128 MiB of HBM per device.

v0:
```python
import functools
import math

import jax
import jax.numpy as jnp
from jax import lax
from jax.experimental import pallas as pl
from jax.experimental.pallas import tpu as pltpu
from jax.sharding import PartitionSpec as P

HQ = 32
KEY_VALUE_HEADS = 4
HEAD_WIDTH = 128
BLK = 32
QUERY_PER_KEY = 8

CTX = 8
FSDP = 32
ROWS = 128
SLAB = 1024
FEATURES = 2560
FEAT_TILE = FEATURES // CTX
Q_COLS = 512
PACK_COLS = 2 * Q_COLS + 2 * HEAD_WIDTH
HALF = 512
SCALE = 1.0 / math.sqrt(HEAD_WIDTH)
LOG2E = math.log2(math.e)
LOWEST = -1e30
NN = (((1,), (0,)), ((), ()))
NT = (((1,), (1,)), ((), ()))
VMEM = pl.BlockSpec(memory_space=pltpu.VMEM)
SMEM = pl.BlockSpec(memory_space=pltpu.SMEM)
VMEM_LIMIT = 48 * 1024 * 1024


def dot(a, b, dims):
    return lax.dot_general(a, b, dims, preferred_element_type=jnp.float32)


def shape(dims, kind=jnp.bfloat16):
    return jax.ShapeDtypeStruct(dims, kind)


def params():
    return pltpu.CompilerParams(vmem_limit_bytes=VMEM_LIMIT)


def cost(flops, moved):
    return pl.CostEstimate(flops=flops, bytes_accessed=moved, transcendentals=0)


def pack_kernel(q_ref, d_ref, k_ref, v_ref, out_ref):
    for dest in range(CTX):
        cols = slice(dest * Q_COLS, (dest + 1) * Q_COLS)
        head = slice((dest // 2) * HEAD_WIDTH, (dest // 2 + 1) * HEAD_WIDTH)
        out_ref[dest, :, 0:Q_COLS] = q_ref[:, cols]
        out_ref[dest, :, Q_COLS : 2 * Q_COLS] = d_ref[:, cols]
        out_ref[dest, :, 2 * Q_COLS : 2 * Q_COLS + HEAD_WIDTH] = k_ref[:, head]
        out_ref[dest, :, 2 * Q_COLS + HEAD_WIDTH :] = v_ref[:, head]


def turn_kernel(x_ref, out_ref, turned):
    turned[FEATURES:, :] = jnp.zeros((16, ROWS), jnp.float32)
    for j in range(FEATURES // 128):
        block = x_ref[:, j * 128 : (j + 1) * 128].T
        turned[j * 128 : (j + 1) * 128, :] = block.astype(jnp.float32)
    for dest in range(CTX):
        for shard in range(FSDP):
            at = shard * 80 + dest * 10
            window = turned[at : at + 16, :]
            out_ref[dest, shard * 16 : (shard + 1) * 16, :] = window.astype(jnp.bfloat16)


def attention_kernel(c_ref, docs_ref, order_ref, *refs):
    in_ref, dq_ref, keep_ref, send_ref = refs[:4]
    q_s, d_s, k_s, v_s, kt_s, dq_s, dkv_s, place, begin = refs[4:]
    c = c_ref[0]

    first = lax.fori_loop(
        0, 17, lambda i, a: jnp.where(docs_ref[i] == docs_ref[i + 15], i, a), jnp.int32(0)
    )

    def place_block(st, carry):
        b = order_ref[st]
        inside = (b >= first) & (b < first + 16)
        place[st] = jnp.where(inside, b - first, jnp.where(b < first, b + 16, b))
        return carry

    lax.fori_loop(0, 32, place_block, 0)

    def begin_block(t, carry):
        last_doc, last_begin = carry
        doc = docs_ref[jnp.where(t < first, t, t + 16)]
        now = jnp.where(doc == last_doc, last_begin, t)
        begin[t] = jnp.int32(0)
        begin[t + 16] = now * BLK
        return doc, now

    lax.fori_loop(0, 16, begin_block, (jnp.int32(-1), jnp.int32(0)))

    for st in range(32):
        rows = pl.ds(pl.multiple_of(place[st] * BLK, BLK), BLK)
        src, block = st // 4, slice((st % 4) * BLK, (st % 4 + 1) * BLK)
        q_s[rows, :] = in_ref[src, block, 0:Q_COLS]
        d_s[rows, :] = in_ref[src, block, Q_COLS : 2 * Q_COLS]
        k_s[rows, :] = in_ref[src, block, 2 * Q_COLS : 2 * Q_COLS + HEAD_WIDTH]
        v_s[rows, :] = in_ref[src, block, 2 * Q_COLS + HEAD_WIDTH :]
    for j in range(SLAB // 128):
        kt_s[:, j * 128 : (j + 1) * 128] = k_s[j * 128 : (j + 1) * 128, :].T
    dkv_s[...] = jnp.zeros_like(dkv_s)

    def half(hf, carry):
        base = pl.multiple_of(hf * HALF, HALF)
        for i in range(HALF // 128):
            n = (i + 1) * 128
            rows = pl.ds(pl.multiple_of(base + i * 128, 128), 128)
            keys = pl.ds(base, n)
            key_n = k_s[keys, :]
            value_n = v_s[keys, :]
            lane = lax.broadcasted_iota(jnp.int32, (n, 128), 1)
            row = lax.broadcasted_iota(jnp.int32, (n, 128), 0)
            low = jnp.zeros((n, 128), jnp.int32)
            for kk in range(4):
                low = jnp.where(lane // BLK == kk, begin[hf * 16 + i * 4 + kk], low)
            seen = (row >= low) & (row <= lane + i * 128)
            bias = jnp.where(seen, 0.0, LOWEST)
            bias = jnp.concatenate([bias, bias], axis=1)
            for g in range(2):
                cols = [slice((2 * g + e) * 128, (2 * g + e + 1) * 128) for e in range(2)]
                qs = jnp.concatenate([q_s[rows, e] for e in cols], axis=0)
                ds = jnp.concatenate([d_s[rows, e] for e in cols], axis=0)
                scores = dot(key_n, qs, NT) * (SCALE * LOG2E) + bias
                top = jnp.max(scores, axis=0, keepdims=True)
                probs = jnp.exp2(scores - top)
                total = jnp.sum(probs, axis=0, keepdims=True)
                probs = probs * (1.0 / total)
                products = dot(value_n, ds, NT)
                delta = jnp.sum(probs * products, axis=0, keepdims=True)
                score_grad = (probs * (products - delta)).astype(jnp.bfloat16)
                probs_low = probs.astype(jnp.bfloat16)
                dkv_s[keys, 0:128] += dot(score_grad, qs, NN)
                dkv_s[keys, 128:256] += dot(probs_low, ds, NN)
                dqt = dot(kt_s[:, keys], score_grad, NN) * SCALE
                for e in range(2):
                    dq_s[rows, cols[e]] = dqt[:, e * 128 : (e + 1) * 128].T.astype(jnp.bfloat16)
        return carry

    lax.fori_loop(0, 2, half, 0)

    odd = lax.rem(c, 2)
    own = pl.ds(pl.multiple_of(odd * 128, 128), 128)
    other = pl.ds(pl.multiple_of((1 - odd) * 128, 128), 128)
    own_scale = jnp.where(odd == 0, SCALE, 1.0)
    other_scale = jnp.where(odd == 0, 1.0, SCALE)
    for st in range(32):
        rows = pl.ds(pl.multiple_of(place[st] * BLK, BLK), BLK)
        block = slice(st * BLK, (st + 1) * BLK)
        keep_ref[block, :] = dkv_s[rows, own] * own_scale
        send_ref[block, :] = (dkv_s[rows, other] * other_scale).astype(jnp.bfloat16)
        dq_ref[st // 4, (st % 4) * BLK : (st % 4 + 1) * BLK, :] = dq_s[rows, :]


def pair_kernel(keep_ref, taken_ref, out_ref):
    total = (keep_ref[...] + taken_ref[...].astype(jnp.float32)).astype(jnp.bfloat16)
    for dest in range(CTX):
        out_ref[dest] = total


def weight_kernel(pieces_ref, x_ref, kv_ref, out_ref, x_s):
    for src in range(CTX):
        block = src // 2 + KEY_VALUE_HEADS * (src % 2)
        kv_ref[:, block * 128 : (block + 1) * 128] = pieces_ref[src]
        x_s[:, src * 128 : (src + 1) * 128] = x_ref[src]
    for j in range(4):
        cols = slice(j * 256, (j + 1) * 256)
        tile = dot(x_s[...], kv_ref[:, cols], NN).astype(jnp.bfloat16)
        for k in range(FSDP):
            out_ref[k, :, cols] = tile[k * 16 : (k + 1) * 16, :]


def input_kernel(c_ref, kv_ref, w_ref, kv_rows_ref, out_ref):
    c = c_ref[0]
    for j in range(4):
        rows = slice(j * 256, (j + 1) * 256)
        tile = dot(w_ref[...], kv_ref[rows, :], NT).astype(jnp.bfloat16)
        out_ref[2 * j] = tile[:, 0:128]
        out_ref[2 * j + 1] = tile[:, 128:256]
    kv_rows_ref[...] = kv_ref[pl.ds(pl.multiple_of(c * ROWS, ROWS), ROWS), :]


def out_kernel(ig_ref, dq_ref, input_ref, query_ref):
    for src in range(CTX):
        query_ref[:, src * Q_COLS : (src + 1) * Q_COLS] = dq_ref[src]
    for j in range(FEATURES // 128):
        input_ref[:, j * 128 : (j + 1) * 128] = ig_ref[j * 128 : (j + 1) * 128, :].T


def sum_kernel(parts_ref, out_ref):
    total = parts_ref[0].astype(jnp.float32)
    for k in range(1, FSDP):
        total = total + parts_ref[k].astype(jnp.float32)
    out_ref[...] = total[0:10, :]


def exchange(value, axis):
    return lax.all_to_all(value, axis, 0, 0, tiled=True)


def body(inputs, queries, keys, values, output_cotangent, key_value_weight, doc_ids, block_order):
    c = lax.axis_index("ctx").astype(jnp.int32)
    c_at = c.reshape(1)

    packed = pl.pallas_call(
        pack_kernel,
        in_specs=[VMEM] * 4,
        out_specs=VMEM,
        out_shape=shape((CTX, ROWS, PACK_COLS)),
        compiler_params=params(),
        cost_estimate=cost(0, 5_000_000),
    )(queries[0], output_cotangent[0], keys[0], values[0])
    got = exchange(packed, "ctx")

    own_rows = lax.dynamic_slice_in_dim(key_value_weight, c * 10, 10, 0)
    perm = [(f1 * CTX + c1, ((f1 * CTX + c1) % FSDP) * CTX + (f1 * CTX + c1) // FSDP)
            for f1 in range(FSDP) for c1 in range(CTX)]
    own_rows = lax.ppermute(own_rows, ("fsdp", "ctx"), perm)
    weight_tile = exchange(jnp.broadcast_to(own_rows[None], (FSDP, 10, 1024)), "fsdp")
    weight_tile = weight_tile.reshape(FEAT_TILE, 1024)

    turned = pl.pallas_call(
        turn_kernel,
        in_specs=[VMEM],
        out_specs=VMEM,
        out_shape=shape((CTX, FSDP * 16, ROWS)),
        scratch_shapes=[pltpu.VMEM((FEATURES + 16, ROWS), jnp.float32)],
        compiler_params=params(),
        cost_estimate=cost(0, 1_300_000),
    )(inputs[0])
    got_x = exchange(turned, "ctx")

    dq_parts, keep, send = pl.pallas_call(
        attention_kernel,
        in_specs=[SMEM] * 3 + [VMEM],
        out_specs=[VMEM] * 3,
        out_shape=[
            shape((CTX, ROWS, Q_COLS)),
            shape((SLAB, HEAD_WIDTH), jnp.float32),
            shape((SLAB, HEAD_WIDTH)),
        ],
        scratch_shapes=[
            pltpu.VMEM((SLAB, Q_COLS), jnp.bfloat16),
            pltpu.VMEM((SLAB, Q_COLS), jnp.bfloat16),
            pltpu.VMEM((SLAB, HEAD_WIDTH), jnp.bfloat16),
            pltpu.VMEM((SLAB, HEAD_WIDTH), jnp.bfloat16),
            pltpu.VMEM((HEAD_WIDTH, SLAB), jnp.bfloat16),
            pltpu.VMEM((SLAB, Q_COLS), jnp.bfloat16),
            pltpu.VMEM((SLAB, 2 * HEAD_WIDTH), jnp.float32),
            pltpu.SMEM((32,), jnp.int32),
            pltpu.SMEM((32,), jnp.int32),
        ],
        compiler_params=params(),
        cost_estimate=cost(2_000_000_000, 5_000_000),
    )(c_at, doc_ids[0], block_order, got)

    taken = lax.ppermute(send, "ctx", [(i, i ^ 1) for i in range(CTX)])
    own_cols = pl.pallas_call(
        pair_kernel,
        in_specs=[VMEM] * 2,
        out_specs=VMEM,
        out_shape=shape((CTX, SLAB, HEAD_WIDTH)),
        compiler_params=params(),
        cost_estimate=cost(0, 3_000_000),
    )(keep, taken)
    pieces = exchange(own_cols, "ctx")

    kv_all, wg_parts = pl.pallas_call(
        weight_kernel,
        in_specs=[VMEM] * 2,
        out_specs=[VMEM] * 2,
        out_shape=[shape((SLAB, 1024)), shape((FSDP, 16, 1024))],
        scratch_shapes=[pltpu.VMEM((FSDP * 16, SLAB), jnp.bfloat16)],
        compiler_params=params(),
        cost_estimate=cost(1_100_000_000, 5_000_000),
    )(pieces, got_x)
    wg_got = exchange(wg_parts, "fsdp")

    kv_rows, ig_parts = pl.pallas_call(
        input_kernel,
        in_specs=[SMEM] + [VMEM] * 2,
        out_specs=[VMEM] * 2,
        out_shape=[shape((ROWS, 1024)), shape((CTX, FEAT_TILE, ROWS))],
        compiler_params=params(),
        cost_estimate=cost(700_000_000, 4_000_000),
    )(c_at, kv_all, weight_tile)
    ig_got = exchange(ig_parts, "ctx").reshape(FEATURES, ROWS)
    dq_got = exchange(dq_parts, "ctx")

    input_grad, query_grad = pl.pallas_call(
        out_kernel,
        in_specs=[VMEM] * 2,
        out_specs=[VMEM] * 2,
        out_shape=[shape((ROWS, FEATURES)), shape((ROWS, HQ * HEAD_WIDTH))],
        compiler_params=params(),
        cost_estimate=cost(0, 3_300_000),
    )(ig_got, dq_got)
    weight_grad = pl.pallas_call(
        sum_kernel,
        in_specs=[VMEM],
        out_specs=VMEM,
        out_shape=shape((10, 1024), jnp.float32),
        compiler_params=params(),
        cost_estimate=cost(0, 1_000_000),
    )(wg_got)
    return (input_grad[None], query_grad[None], kv_rows[None], weight_grad)


def solution(mesh):
    placed = (
        P("fsdp", "ctx", None),
        P("fsdp", "ctx", None),
        P("fsdp", "ctx", None),
        P("fsdp", "ctx", None),
        P("fsdp", "ctx", None),
        P("fsdp", None),
        P("fsdp", None),
        P(),
    )
    return jax.shard_map(
        body,
        mesh=mesh,
        in_specs=placed,
        out_specs=(
            P("fsdp", "ctx", None),
            P("fsdp", "ctx", None),
            P("fsdp", "ctx", None),
            P(("fsdp", "ctx"), None),
        ),
        check_vma=False,
    )
```

profile of v0, /device:TPU:8, one launch (start us, length us, event | category | flops | bytes accessed | tf_op | source)
XLA Modules:
  0.0 207.7 jit_solution(142658490950173176)
XLA Ops:
  0.7 1.2 copy-done.6
  1.9 1.3 shard_map.114
  3.2 5.8 %all-to-all-start.2 = ((bf16[8,512,128]{2,1,0:T(8,128)(2,1)}), bf16[8,512,128]{2,1,0:T(8,128)(2,1)S(1)}, u32[]{:S(2)}, u32[]{:S(2)}) async-start(bf16[8,512,128]{2,1,0:T(8,128)(2,1)} %shard_map.114), calls=%async_computation.2 | async-start | bytes 2097152 | tf_op jit(solution)/shard_map/all_to_all | solution.py:206
  9.9 1.7 shard_map.111
  11.5 11.6 %all-to-all-done.2.x_ref = bf16[8,512,128]{2,1,0:T(8,128)(2,1)S(1)} async-done(((bf16[8,512,128]{2,1,0:T(8,128)(2,1)}), bf16[8,512,128]{2,1,0:T(8,128)(2,1)S(1)}, u32[]{:S(2)}, u32[]{:S(2)}) %all-to-all-start.2) | async-done | bytes 1048608 | tf_op jit(solution)/shard_map/all_to_all | solution.py:206
  24.2 5.0 %all-to-all-start = ((bf16[8,128,1280]{2,1,0:T(8,128)(2,1)}), bf16[8,128,1280]{2,1,0:T(8,128)(2,1)S(1)}, u32[]{:S(2)}, u32[]{:S(2)}) async-start(bf16[8,128,1280]{2,1,0:T(8,128)(2,1)} %shard_map.111), calls=%async_computation | async-start | bytes 5242880 | tf_op jit(solution)/shard_map/all_to_all | solution.py:206
  29.2 3.4 %collective-permute-start.1 = (bf16[10,1024]{1,0:T(8,128)(2,1)S(1)}, bf16[10,1024]{1,0:T(8,128)(2,1)S(1)}, u32[]{:S(2)}, u32[]{:S(2)}) collective-permute-start(bf16[10,1024]{1,0:T(8,128)(2,1)S(1)} %constant_dynamic-slice_fusion), channel_id=1, source_target_pairs={{0,0},{1,8},{2,16},{3,24},{4,32},{5,40},{6,48},{7,56},{8,64},{9,72... | collective-permute-start | bytes 61448 | tf_op jit(solution)/shard_map/ppermute | solution.py:226
  32.6 7.4 %collective-permute-done.1 = bf16[10,1024]{1,0:T(8,128)(2,1)S(1)} collective-permute-done((bf16[10,1024]{1,0:T(8,128)(2,1)S(1)}, bf16[10,1024]{1,0:T(8,128)(2,1)S(1)}, u32[]{:S(2)}, u32[]{:S(2)}) %collective-permute-start.1) | collective-permute-done | bytes 20512 | tf_op jit(solution)/shard_map/ppermute | solution.py:226
  40.1 21.0 %all-to-all-done.refs_0_ = bf16[8,128,1280]{2,1,0:T(8,128)(2,1)S(1)} async-done(((bf16[8,128,1280]{2,1,0:T(8,128)(2,1)}), bf16[8,128,1280]{2,1,0:T(8,128)(2,1)S(1)}, u32[]{:S(2)}, u32[]{:S(2)}) %all-to-all-start) | async-done | bytes 2621472 | tf_op jit(solution)/shard_map/all_to_all | solution.py:206
  61.1 1.1 broadcast_in_dim.15
  62.2 16.1 %all-to-all-start.3 = ((bf16[32,10,1024]{2,1,0:T(8,128)(2,1)}), bf16[32,10,1024]{2,1,0:T(8,128)(2,1)}, u32[]{:S(2)}, u32[]{:S(2)}) async-start(bf16[32,10,1024]{2,1,0:T(8,128)(2,1)} %broadcast_in_dim.15), calls=%async_computation.3 | async-start | bytes 2097152 | tf_op jit(solution)/shard_map/all_to_all | solution.py:206
  78.4 9.8 %shard_map.112 = (bf16[8,128,512]{2,1,0:T(8,128)(2,1)}, f32[1024,128]{1,0:T(8,128)S(1)}, bf16[1024,128]{1,0:T(8,128)(2,1)S(1)}) custom-call(s32[1]{0:T(128)} %bitcast.c_ref, s32[32]{0:T(128)S(1)} %bitcast.17, s32[32]{0:T(128)S(1)} %copy-done.11, bf16[8,128,1280]{2,1,0:T(8,128)(2,1)S(1)} %all-to-all-done.refs_0_), custom_call_target="tpu_custom_call" | custom-call | flops 2000000000 | bytes 5000000 | tf_op jit(solution)/shard_map/pallas_call | solution.py:241
  88.1 8.4 %collective-permute-done.taken_ref = bf16[1024,128]{1,0:T(8,128)(2,1)S(1)} collective-permute-done((bf16[1024,128]{1,0:T(8,128)(2,1)S(1)}, bf16[1024,128]{1,0:T(8,128)(2,1)S(1)}, u32[]{:S(2)}, u32[]{:S(2)}) %collective-permute-start) | collective-permute-done | bytes 262176 | tf_op jit(solution)/shard_map/ppermute | solution.py:265
  96.7 10.7 %all-to-all-done.3 = bf16[32,10,1024]{2,1,0:T(8,128)(2,1)} async-done(((bf16[32,10,1024]{2,1,0:T(8,128)(2,1)}), bf16[32,10,1024]{2,1,0:T(8,128)(2,1)}, u32[]{:S(2)}, u32[]{:S(2)}) %all-to-all-start.3) | async-done | bytes 655392 | tf_op jit(solution)/shard_map/all_to_all | solution.py:206
  107.4 30.4 %all_to_all.35.pieces_ref = bf16[8,1024,128]{2,1,0:T(8,128)(2,1)} all-to-all(bf16[8,1024,128]{2,1,0:T(8,128)(2,1)S(1)} %shard_map.113), channel_id=1, replica_groups=mesh['fsdp'=32,'ctx'=8] {'ctx'}, dimensions={0} | all-to-all | bytes 4194304 | tf_op jit(solution)/shard_map/all_to_all | solution.py:206
  137.9 5.1 %all-to-all-start.5 = ((bf16[8,128,512]{2,1,0:T(8,128)(2,1)}), bf16[8,128,512]{2,1,0:T(8,128)(2,1)S(1)}, u32[]{:S(2)}, u32[]{:S(2)}) async-start(bf16[8,128,512]{2,1,0:T(8,128)(2,1)} %get-tuple-element.17), calls=%async_computation.5 | async-start | bytes 2097152 | tf_op jit(solution)/shard_map/all_to_all | solution.py:206
  143.0 1.4 reshape.19.w_ref
  144.3 3.0 %shard_map.115 = (bf16[1024,1024]{1,0:T(8,128)(2,1)S(1)}, bf16[32,16,1024]{2,1,0:T(8,128)(2,1)S(1)}) custom-call(bf16[8,1024,128]{2,1,0:T(8,128)(2,1)} %all_to_all.35.pieces_ref, bf16[8,512,128]{2,1,0:T(8,128)(2,1)S(1)} %copy-done.4), custom_call_target="tpu_custom_call" | custom-call | flops 1100000000 | bytes 5000000 | tf_op jit(solution)/shard_map/pallas_call | solution.py:276
  148.4 1.5 shard_map.116
  150.7 5.2 %all-to-all-done.5.dq_ref = bf16[8,128,512]{2,1,0:T(8,128)(2,1)S(1)} async-done(((bf16[8,128,512]{2,1,0:T(8,128)(2,1)}), bf16[8,128,512]{2,1,0:T(8,128)(2,1)S(1)}, u32[]{:S(2)}, u32[]{:S(2)}) %all-to-all-start.5) | async-done | bytes 1048608 | tf_op jit(solution)/shard_map/all_to_all | solution.py:206
  156.0 15.1 %all_to_all.36 = bf16[8,320,128]{2,1,0:T(8,128)(2,1)S(1)} all-to-all(bf16[8,320,128]{2,1,0:T(8,128)(2,1)} %copy-done.7), channel_id=1, replica_groups=mesh['fsdp'=32,'ctx'=8] {'ctx'}, dimensions={0} | all-to-all | bytes 1310720 | tf_op jit(solution)/shard_map/all_to_all | solution.py:206
  171.0 6.8 %all-to-all-start.6 = ((bf16[32,16,1024]{2,1,0:T(8,128)(2,1)}), bf16[32,16,1024]{2,1,0:T(8,128)(2,1)S(1)}, u32[]{:S(2)}, u32[]{:S(2)}) async-start(bf16[32,16,1024]{2,1,0:T(8,128)(2,1)} %copy-done.5), calls=%async_computation.6 | async-start | bytes 2097152 | tf_op jit(solution)/shard_map/all_to_all | solution.py:206
  177.8 1.4 shard_map.117
  179.2 27.7 %all-to-all-done.6.parts_ref = bf16[32,16,1024]{2,1,0:T(8,128)(2,1)S(1)} async-done(((bf16[32,16,1024]{2,1,0:T(8,128)(2,1)}), bf16[32,16,1024]{2,1,0:T(8,128)(2,1)S(1)}, u32[]{:S(2)}, u32[]{:S(2)}) %all-to-all-start.6) | async-done | bytes 1048608 | tf_op jit(solution)/shard_map/all_to_all | solution.py:206
  (27 shorter events, 4.7 us)
Async XLA Ops:
  0.6 28.6 %copy-start = (bf16[80,1024]{1,0:T(8,128)(2,1)S(1)}, bf16[80,1024]{1,0:T(8,128)(2,1)}, u32[]{:S(2)}) copy-start(bf16[80,1024]{1,0:T(8,128)(2,1)} %param.13) | copy-start | bytes 491524
  0.6 8.3 %copy-start.1 = (bf16[1,128,4096]{2,1,0:T(8,128)(2,1)S(1)}, bf16[1,128,4096]{2,1,0:T(8,128)(2,1)}, u32[]{:S(2)}) copy-start(bf16[1,128,4096]{2,1,0:T(8,128)(2,1)} %param.9) | copy-start | bytes 3145732
  0.7 8.3 %copy-start.2 = (bf16[1,128,4096]{2,1,0:T(8,128)(2,1)S(1)}, bf16[1,128,4096]{2,1,0:T(8,128)(2,1)}, u32[]{:S(2)}) copy-start(bf16[1,128,4096]{2,1,0:T(8,128)(2,1)} %param.12) | copy-start | bytes 3145732
  0.7 1.2 copy-start.6
  1.9 7.0 %copy-start.8 = (bf16[1,128,512]{2,1,0:T(8,128)(2,1)S(1)}, bf16[1,128,512]{2,1,0:T(8,128)(2,1)}, u32[]{:S(2)}) copy-start(bf16[1,128,512]{2,1,0:T(8,128)(2,1)} %param.10) | copy-start | bytes 393220
  3.2 20.0 %all-to-all-start.2 = ((bf16[8,512,128]{2,1,0:T(8,128)(2,1)}), bf16[8,512,128]{2,1,0:T(8,128)(2,1)S(1)}, u32[]{:S(2)}, u32[]{:S(2)}) async-start(bf16[8,512,128]{2,1,0:T(8,128)(2,1)} %shard_map.114), calls=%async_computation.2 | async-start | bytes 2097152 | tf_op jit(solution)/shard_map/all_to_all | solution.py:206
  9.0 0.9 copy-start.9
  23.2 1.0 copy-start.3
  24.2 36.9 %all-to-all-start = ((bf16[8,128,1280]{2,1,0:T(8,128)(2,1)}), bf16[8,128,1280]{2,1,0:T(8,128)(2,1)S(1)}, u32[]{:S(2)}, u32[]{:S(2)}) async-start(bf16[8,128,1280]{2,1,0:T(8,128)(2,1)} %shard_map.111), calls=%async_computation | async-start | bytes 5242880 | tf_op jit(solution)/shard_map/all_to_all | solution.py:206
  29.2 49.1 %copy-start.10 = (s32[1,32]{1,0:T(1,128)S(1)}, s32[1,32]{1,0:T(1,128)}, u32[]{:S(2)}) copy-start(s32[1,32]{1,0:T(1,128)} %param.14) | copy-start | bytes 388
  29.2 49.1 %copy-start.11 = (s32[32]{0:T(128)S(1)}, s32[32]{0:T(128)}, u32[]{:S(2)}) copy-start(s32[32]{0:T(128)} %order_ref.1) | copy-start | bytes 388
  29.2 10.8 %collective-permute-start.1 = (bf16[10,1024]{1,0:T(8,128)(2,1)S(1)}, bf16[10,1024]{1,0:T(8,128)(2,1)S(1)}, u32[]{:S(2)}, u32[]{:S(2)}) collective-permute-start(bf16[10,1024]{1,0:T(8,128)(2,1)S(1)} %constant_dynamic-slice_fusion), channel_id=1, source_target_pairs={{0,0},{1,8},{2,16},{3,24},{4,32},{5,40},{6,48},{7,56},{8,64},{9,72... | collective-permute-start | bytes 61448 | tf_op jit(solution)/shard_map/ppermute | solution.py:226
  62.2 45.2 %all-to-all-start.3 = ((bf16[32,10,1024]{2,1,0:T(8,128)(2,1)}), bf16[32,10,1024]{2,1,0:T(8,128)(2,1)}, u32[]{:S(2)}, u32[]{:S(2)}) async-start(bf16[32,10,1024]{2,1,0:T(8,128)(2,1)} %broadcast_in_dim.15), calls=%async_computation.3 | async-start | bytes 2097152 | tf_op jit(solution)/shard_map/all_to_all | solution.py:206
  88.1 8.4 %collective-permute-start = (bf16[1024,128]{1,0:T(8,128)(2,1)S(1)}, bf16[1024,128]{1,0:T(8,128)(2,1)S(1)}, u32[]{:S(2)}, u32[]{:S(2)}) collective-permute-start(bf16[1024,128]{1,0:T(8,128)(2,1)S(1)} %get-tuple-element.14), channel_id=1, source_target_pairs={{0,1},{1,0},{2,3},{3,2},{4,5},{5,4},{6,7},{7,6},{8,9},{9,8},{10,11... | collective-permute-start | bytes 786440 | tf_op jit(solution)/shard_map/ppermute | solution.py:265
  137.9 6.5 %copy-start.4 = (bf16[8,512,128]{2,1,0:T(8,128)(2,1)S(1)}, bf16[8,512,128]{2,1,0:T(8,128)(2,1)}, u32[]{:S(2)}) copy-start(bf16[8,512,128]{2,1,0:T(8,128)(2,1)} %copy-done.3) | copy-start | bytes 3145732
  137.9 18.1 %all-to-all-start.5 = ((bf16[8,128,512]{2,1,0:T(8,128)(2,1)}), bf16[8,128,512]{2,1,0:T(8,128)(2,1)S(1)}, u32[]{:S(2)}, u32[]{:S(2)}) async-start(bf16[8,128,512]{2,1,0:T(8,128)(2,1)} %get-tuple-element.17), calls=%async_computation.5 | async-start | bytes 2097152 | tf_op jit(solution)/shard_map/all_to_all | solution.py:206
  147.4 1.0 copy-start.5
  149.9 0.8 copy-start.7
  171.0 35.9 %all-to-all-start.6 = ((bf16[32,16,1024]{2,1,0:T(8,128)(2,1)}), bf16[32,16,1024]{2,1,0:T(8,128)(2,1)S(1)}, u32[]{:S(2)}, u32[]{:S(2)}) async-start(bf16[32,16,1024]{2,1,0:T(8,128)(2,1)} %copy-done.5), calls=%async_computation.6 | async-start | bytes 2097152 | tf_op jit(solution)/shard_map/all_to_all | solution.py:206
where the time goes:
time: 210 us; the launch traced here: 208 us
  waiting for transfers between devices  92.1 us (44%)
  blocking collectives  45.5 us (22%)
  starting transfers between devices  42.2 us (20%)
  Pallas kernels  19.6 us (9%)
  local copies, waits for them, and re-layouts  7.47 us (4%)
    all_to_all x5, waiting for transfers between devices, exchange(): return lax.all_to_all(value, axis, 0, 0, tiled=True)  76.3 us
    all_to_all x2, blocking collectives, exchange(): return lax.all_to_all(value, axis, 0, 0, tiled=True)  45.5 us
    all_to_all x5, starting transfers between devices, exchange(): return lax.all_to_all(value, axis, 0, 0, tiled=True)  38.8 us
    pallas_call x1, Pallas kernels, body(): pl.pallas_call(attention_kernel, in_specs=[SMEM] * 3 + [VMEM], out_specs=...  9.79 us
    ppermute x1, waiting for transfers between devices, body(): taken = lax.ppermute(send, 'ctx', [(i, i ^ 1) for i in range(CTX)])  8.41 us
    ppermute x1, waiting for transfers between devices, body(): own_rows = lax.ppermute(own_rows, ('fsdp', 'ctx'), perm)  7.44 us
    unnamed x24, local copies, waits for them, and re-layouts  5.01 us
  transfers between devices with their start and end apart: 7, of which 7 were waited for; matrix products, arithmetic and copies ran while one was open for 1% of the time, Pallas kernels for 8%

commit v1 on v0

--- a/solution.py
+++ b/solution.py
@@ -19,7 +19,7 @@
 ROWS = 128
 SLAB = 1024
 FEATURES = 2560
-FEAT_TILE = FEATURES // CTX
+FEAT_TILE = FEATURES // 4
 Q_COLS = 512
 PACK_COLS = 2 * Q_COLS + 2 * HEAD_WIDTH
 HALF = 512
@@ -49,26 +49,35 @@
     return pl.CostEstimate(flops=flops, bytes_accessed=moved, transcendentals=0)
 
 
+def q_block(device):
+    return (device % 4) * 2 + device // 4
+
+
 def pack_kernel(q_ref, d_ref, k_ref, v_ref, out_ref):
     for dest in range(CTX):
-        cols = slice(dest * Q_COLS, (dest + 1) * Q_COLS)
-        head = slice((dest // 2) * HEAD_WIDTH, (dest // 2 + 1) * HEAD_WIDTH)
+        at = q_block(dest)
+        cols = slice(at * Q_COLS, (at + 1) * Q_COLS)
+        head = slice((dest % 4) * HEAD_WIDTH, (dest % 4 + 1) * HEAD_WIDTH)
         out_ref[dest, :, 0:Q_COLS] = q_ref[:, cols]
         out_ref[dest, :, Q_COLS : 2 * Q_COLS] = d_ref[:, cols]
         out_ref[dest, :, 2 * Q_COLS : 2 * Q_COLS + HEAD_WIDTH] = k_ref[:, head]
         out_ref[dest, :, 2 * Q_COLS + HEAD_WIDTH :] = v_ref[:, head]
 
 
-def turn_kernel(x_ref, out_ref, turned):
-    turned[FEATURES:, :] = jnp.zeros((16, ROWS), jnp.float32)
+def turn_kernel(x_ref, out_ref, turned, tile):
     for j in range(FEATURES // 128):
         block = x_ref[:, j * 128 : (j + 1) * 128].T
         turned[j * 128 : (j + 1) * 128, :] = block.astype(jnp.float32)
-    for dest in range(CTX):
-        for shard in range(FSDP):
-            at = shard * 80 + dest * 10
-            window = turned[at : at + 16, :]
-            out_ref[dest, shard * 16 : (shard + 1) * 16, :] = window.astype(jnp.bfloat16)
+    for x in range(4):
+        for low in range(4):
+            for y in range(2):
+                for z in range(8):
+                    source = (z * 4 + low) * 80 + y * 40 + x * 10
+                    at = (low * 2 + y) * 80 + z * 10
+                    tile[at : at + 10, :] = turned[source : source + 10, :]
+        piece = tile[...].astype(jnp.bfloat16)
+        out_ref[x] = piece
+        out_ref[x + 4] = piece
 
 
 def attention_kernel(c_ref, docs_ref, order_ref, *refs):
@@ -147,7 +156,7 @@
 
     lax.fori_loop(0, 2, half, 0)
 
-    odd = lax.rem(c, 2)
+    odd = c // 4
     own = pl.ds(pl.multiple_of(odd * 128, 128), 128)
     other = pl.ds(pl.multiple_of((1 - odd) * 128, 128), 128)
     own_scale = jnp.where(odd == 0, SCALE, 1.0)
@@ -162,44 +171,63 @@
 
 def pair_kernel(keep_ref, taken_ref, out_ref):
     total = (keep_ref[...] + taken_ref[...].astype(jnp.float32)).astype(jnp.bfloat16)
-    for dest in range(CTX):
+    for dest in range(4):
         out_ref[dest] = total
 
 
 def weight_kernel(pieces_ref, x_ref, kv_ref, out_ref, x_s):
+    for src in range(4):
+        kv_ref[:, src * 128 : (src + 1) * 128] = pieces_ref[src]
     for src in range(CTX):
-        block = src // 2 + KEY_VALUE_HEADS * (src % 2)
-        kv_ref[:, block * 128 : (block + 1) * 128] = pieces_ref[src]
         x_s[:, src * 128 : (src + 1) * 128] = x_ref[src]
-    for j in range(4):
+    for j in range(2):
         cols = slice(j * 256, (j + 1) * 256)
         tile = dot(x_s[...], kv_ref[:, cols], NN).astype(jnp.bfloat16)
-        for k in range(FSDP):
-            out_ref[k, :, cols] = tile[k * 16 : (k + 1) * 16, :]
-
-
-def input_kernel(c_ref, kv_ref, w_ref, kv_rows_ref, out_ref):
-    c = c_ref[0]
+        for k in range(8):
+            out_ref[k, :, cols] = tile[k * 80 : (k + 1) * 80, :]
+
+
+def input_kernel(kv_ref, w_ref, own_ref, out_ref):
     for j in range(4):
         rows = slice(j * 256, (j + 1) * 256)
         tile = dot(w_ref[...], kv_ref[rows, :], NT).astype(jnp.bfloat16)
-        out_ref[2 * j] = tile[:, 0:128]
-        out_ref[2 * j + 1] = tile[:, 128:256]
-    kv_rows_ref[...] = kv_ref[pl.ds(pl.multiple_of(c * ROWS, ROWS), ROWS), :]
-
-
-def out_kernel(ig_ref, dq_ref, input_ref, query_ref):
+        out_ref[2 * j, 0:FEAT_TILE, :] = tile[:, 0:128]
+        out_ref[2 * j + 1, 0:FEAT_TILE, :] = tile[:, 128:256]
+    for dest in range(CTX):
+        out_ref[dest, FEAT_TILE:, :] = own_ref[0, dest * ROWS : (dest + 1) * ROWS, :]
+
+
+def input_out_kernel(parts_ref, input_ref, kv_rows_ref):
+    for x in range(4):
+        for j in range(FEAT_TILE // 128):
+            rows = slice(j * 128, (j + 1) * 128)
+            total = parts_ref[x, rows, :].astype(jnp.float32) + parts_ref[x + 4, rows, :].astype(jnp.float32)
+            at = x * FEAT_TILE + j * 128
+            input_ref[:, at : at + 128] = total.T.astype(jnp.bfloat16)
     for src in range(CTX):
-        query_ref[:, src * Q_COLS : (src + 1) * Q_COLS] = dq_ref[src]
-    for j in range(FEATURES // 128):
-        input_ref[:, j * 128 : (j + 1) * 128] = ig_ref[j * 128 : (j + 1) * 128, :].T
-
-
-def sum_kernel(parts_ref, out_ref):
+        kv_rows_ref[:, src * 128 : (src + 1) * 128] = parts_ref[src, FEAT_TILE:, :]
+
+
+def query_out_kernel(dq_ref, query_ref):
+    for src in range(CTX):
+        at = q_block(src)
+        query_ref[:, at * Q_COLS : (at + 1) * Q_COLS] = dq_ref[src]
+
+
+def first_sum_kernel(parts_ref, out_ref):
+    for y in range(2):
+        total = parts_ref[y].astype(jnp.float32)
+        for low in range(1, 4):
+            total = total + parts_ref[low * 2 + y].astype(jnp.float32)
+        for z in range(8):
+            out_ref[z, :, y * 512 : (y + 1) * 512] = total[z * 10 : (z + 1) * 10, :].astype(jnp.bfloat16)
+
+
+def second_sum_kernel(parts_ref, out_ref):
     total = parts_ref[0].astype(jnp.float32)
-    for k in range(1, FSDP):
+    for k in range(1, 8):
         total = total + parts_ref[k].astype(jnp.float32)
-    out_ref[...] = total[0:10, :]
+    out_ref[...] = total
 
 
 def exchange(value, axis):
@@ -207,7 +235,7 @@
 
 
 def body(inputs, queries, keys, values, output_cotangent, key_value_weight, doc_ids, block_order):
-    c = lax.axis_index("ctx").astype(jnp.int32)
+    c = lax.axis_index(("y", "x")).astype(jnp.int32)
     c_at = c.reshape(1)
 
     packed = pl.pallas_call(
@@ -218,25 +246,35 @@
         compiler_params=params(),
         cost_estimate=cost(0, 5_000_000),
     )(queries[0], output_cotangent[0], keys[0], values[0])
-    got = exchange(packed, "ctx")
-
-    own_rows = lax.dynamic_slice_in_dim(key_value_weight, c * 10, 10, 0)
-    perm = [(f1 * CTX + c1, ((f1 * CTX + c1) % FSDP) * CTX + (f1 * CTX + c1) // FSDP)
-            for f1 in range(FSDP) for c1 in range(CTX)]
-    own_rows = lax.ppermute(own_rows, ("fsdp", "ctx"), perm)
-    weight_tile = exchange(jnp.broadcast_to(own_rows[None], (FSDP, 10, 1024)), "fsdp")
-    weight_tile = weight_tile.reshape(FEAT_TILE, 1024)
+    got = exchange(packed, ("y", "x"))
 
     turned = pl.pallas_call(
         turn_kernel,
         in_specs=[VMEM],
         out_specs=VMEM,
-        out_shape=shape((CTX, FSDP * 16, ROWS)),
-        scratch_shapes=[pltpu.VMEM((FEATURES + 16, ROWS), jnp.float32)],
+        out_shape=shape((CTX, FEAT_TILE, ROWS)),
+        scratch_shapes=[
+            pltpu.VMEM((FEATURES, ROWS), jnp.float32),
+            pltpu.VMEM((FEAT_TILE, ROWS), jnp.float32),
+        ],
         compiler_params=params(),
         cost_estimate=cost(0, 1_300_000),
     )(inputs[0])
-    got_x = exchange(turned, "ctx")
+    own_rows = lax.dynamic_slice(
+        key_value_weight, (lax.rem(c, 4) * 20, (c // 4) * 512), (20, 512)
+    )
+    perm = []
+    for f1 in range(FSDP):
+        for c1 in range(CTX):
+            y1, x1 = c1 // 4, c1 % 4
+            perm.append((f1 * CTX + c1, ((f1 % 8) * 4 + x1) * CTX + y1 * 4 + f1 // 8))
+    own_rows = lax.ppermute(own_rows, ("z", "yh", "core", "y", "x"), perm)
+    weight_tile = exchange(
+        jnp.broadcast_to(own_rows[None], (FSDP, 20, 512)), ("z", "yh", "core")
+    ).reshape(FEAT_TILE, 512)
+
+    got, turned, weight_tile = lax.optimization_barrier((got, turned, weight_tile))
+    got_x = exchange(turned, ("y", "x"))
 
     dq_parts, keep, send = pl.pallas_call(
         attention_kernel,
@@ -262,78 +300,84 @@
         cost_estimate=cost(2_000_000_000, 5_000_000),
     )(c_at, doc_ids[0], block_order, got)
 
-    taken = lax.ppermute(send, "ctx", [(i, i ^ 1) for i in range(CTX)])
+    taken = lax.ppermute(send, "y", [(0, 1), (1, 0)])
     own_cols = pl.pallas_call(
         pair_kernel,
         in_specs=[VMEM] * 2,
         out_specs=VMEM,
-        out_shape=shape((CTX, SLAB, HEAD_WIDTH)),
+        out_shape=shape((4, SLAB, HEAD_WIDTH)),
         compiler_params=params(),
         cost_estimate=cost(0, 3_000_000),
     )(keep, taken)
-    pieces = exchange(own_cols, "ctx")
-
-    kv_all, wg_parts = pl.pallas_call(
+    pieces = exchange(own_cols, "x")
+    dq_got = exchange(dq_parts, ("y", "x"))
+
+    kv_half, wg_parts = pl.pallas_call(
         weight_kernel,
         in_specs=[VMEM] * 2,
         out_specs=[VMEM] * 2,
-        out_shape=[shape((SLAB, 1024)), shape((FSDP, 16, 1024))],
-        scratch_shapes=[pltpu.VMEM((FSDP * 16, SLAB), jnp.bfloat16)],
-        compiler_params=params(),
-        cost_estimate=cost(1_100_000_000, 5_000_000),
+        out_shape=[shape((SLAB, 512)), shape((8, 80, 512))],
+        scratch_shapes=[pltpu.VMEM((FEAT_TILE, SLAB), jnp.bfloat16)],
+        compiler_params=params(),
+        cost_estimate=cost(700_000_000, 5_000_000),
     )(pieces, got_x)
-    wg_got = exchange(wg_parts, "fsdp")
-
-    kv_rows, ig_parts = pl.pallas_call(
+    wg_got = exchange(wg_parts, ("yh", "core", "y"))
+
+    ig_parts = pl.pallas_call(
         input_kernel,
-        in_specs=[SMEM] + [VMEM] * 2,
-        out_specs=[VMEM] * 2,
-        out_shape=[shape((ROWS, 1024)), shape((CTX, FEAT_TILE, ROWS))],
+        in_specs=[VMEM] * 3,
+        out_specs=VMEM,
+        out_shape=shape((CTX, FEAT_TILE + ROWS, ROWS)),
         compiler_params=params(),
         cost_estimate=cost(700_000_000, 4_000_000),
-    )(c_at, kv_all, weight_tile)
-    ig_got = exchange(ig_parts, "ctx").reshape(FEATURES, ROWS)
-    dq_got = exchange(dq_parts, "ctx")
-
-    input_grad, query_grad = pl.pallas_call(
-        out_kernel,
-        in_specs=[VMEM] * 2,
-        out_specs=[VMEM] * 2,
-        out_shape=[shape((ROWS, FEATURES)), shape((ROWS, HQ * HEAD_WIDTH))],
-        compiler_params=params(),
-        cost_estimate=cost(0, 3_300_000),
-    )(ig_got, dq_got)
-    weight_grad = pl.pallas_call(
-        sum_kernel,
-        in_specs=[VMEM],
-        out_specs=VMEM,
-        out_shape=shape((10, 1024), jnp.float32),
+    )(kv_half, weight_tile, own_cols)
+    ig_got = exchange(ig_parts, ("y", "x"))
+
+    wg_second = pl.pallas_call(
+        first_sum_kernel,
+        in_specs=[VMEM],
+        out_specs=VMEM,
+        out_shape=shape((8, 10, 1024)),
         compiler_params=params(),
         cost_estimate=cost(0, 1_000_000),
     )(wg_got)
+    wg_last = exchange(wg_second, "z")
+
+    query_grad = pl.pallas_call(
+        query_out_kernel,
+        in_specs=[VMEM],
+        out_specs=VMEM,
+        out_shape=shape((ROWS, HQ * HEAD_WIDTH)),
+        compiler_params=params(),
+        cost_estimate=cost(0, 2_000_000),
+    )(dq_got)
+    input_grad, kv_rows = pl.pallas_call(
+        input_out_kernel,
+        in_specs=[VMEM],
+        out_specs=[VMEM] * 2,
+        out_shape=[shape((ROWS, FEATURES)), shape((ROWS, 1024))],
+        compiler_params=params(),
+        cost_estimate=cost(0, 2_000_000),
+    )(ig_got)
+    weight_grad = pl.pallas_call(
+        second_sum_kernel,
+        in_specs=[VMEM],
+        out_specs=VMEM,
+        out_shape=shape((10, 1024), jnp.float32),
+        compiler_params=params(),
+        cost_estimate=cost(0, 200_000),
+    )(wg_last)
     return (input_grad[None], query_grad[None], kv_rows[None], weight_grad)
 
 
 def solution(mesh):
-    placed = (
-        P("fsdp", "ctx", None),
-        P("fsdp", "ctx", None),
-        P("fsdp", "ctx", None),
-        P("fsdp", "ctx", None),
-        P("fsdp", "ctx", None),
-        P("fsdp", None),
-        P("fsdp", None),
-        P(),
-    )
+    axes = ("z", "yh", "core", "y", "x")
+    named = jax.sharding.Mesh(mesh.devices.reshape(8, 2, 2, 2, 4), axes)
+    fsdp, ctx = axes[:3], axes[3:]
     return jax.shard_map(
         body,
-        mesh=mesh,
-        in_specs=placed,
-        out_specs=(
-            P("fsdp", "ctx", None),
-            P("fsdp", "ctx", None),
-            P("fsdp", "ctx", None),
-            P(("fsdp", "ctx"), None),
-        ),
+        mesh=named,
+        in_specs=(P(fsdp, ctx, None),) * 5 + (P(fsdp, None), P(fsdp, None), P()),
+        out_specs=(P(fsdp, ctx, None),) * 3 + (P(axes, None),),
         check_vma=False,
     )

time: 210 us -> 227 us (1.081)
  blocking collectives: 45.5 us -> 55.5 us
  starting transfers between devices: 42.2 us -> 48 us
  waiting for transfers between devices: 92.1 us -> 94.8 us
    all_to_all x5, waiting for transfers between devices: 76.3 us -> 88.4 us  [exchange(): return lax.all_to_all(value, axis, 0, 0, tiled=True)]
    all_to_all x2 -> x3, blocking collectives: 45.5 us -> 55.5 us  [exchange(): return lax.all_to_all(value, axis, 0, 0, tiled=True)]
    ppermute x2, waiting for transfers between devices: 15.8 us -> 6.37 us  [the longest x1 6.37 us: body(): taken = lax.ppermute(send, 'y', [(0, 1), (1, 0)])]
    all_to_all x5, starting transfers between devices: 38.8 us -> 45.8 us  [exchange(): return lax.all_to_all(value, axis, 0, 0, tiled=True)]
    pallas_call x3 -> x5, Pallas kernels: 3.72 us -> 5.76 us  [the longest x1 2.04 us: body(): pl.pallas_call(input_kernel, in_specs=[VMEM] * 3, out_specs=VMEM, out_sha...]
    unnamed x24 -> x22, local copies, waits for them, and re-layouts: 5.01 us -> 3.31 us
  transfers between devices with their start and end apart: 7 -> 7, of which waited for: 7 -> 6; matrix products, arithmetic and copies ran while one was open for 1% -> 0% of each run, Pallas kernels for 8% -> 3%
where the time goes in v1:
time: 227 us; the launch traced here: 224 us
  waiting for transfers between devices  94.8 us (42%)
  blocking collectives  55.5 us (24%)
  starting transfers between devices  48 us (21%)
  Pallas kernels  19 us (8%)
  local copies, waits for them, and re-layouts  6.2 us (3%)
    all_to_all x5, waiting for transfers between devices, exchange(): return lax.all_to_all(value, axis, 0, 0, tiled=True)  88.4 us
    all_to_all x3, blocking collectives, exchange(): return lax.all_to_all(value, axis, 0, 0, tiled=True)  55.5 us
    all_to_all x5, starting transfers between devices, exchange(): return lax.all_to_all(value, axis, 0, 0, tiled=True)  45.8 us
    pallas_call x1, Pallas kernels, body(): pl.pallas_call(attention_kernel, in_specs=[SMEM] * 3 + [VMEM], out_specs=...  10 us
    ppermute x1, waiting for transfers between devices, body(): taken = lax.ppermute(send, 'y', [(0, 1), (1, 0)])  6.37 us
  transfers between devices with their start and end apart: 7, of which 6 were waited for; matrix products, arithmetic and copies ran while one was open for 0% of the time, Pallas kernels for 3%

profile of v1, /device:TPU:8, one launch (start us, length us, event | category | flops | bytes accessed | tf_op | source)
XLA Modules:
  0.0 224.3 jit_solution(10272368732218134979)
XLA Ops:
  0.7 1.0 dynamic_slice.3
  3.3 23.4 %all-to-all-start.1 = ((bf16[32,20,512]{2,1,0:T(8,128)(2,1)}), bf16[32,20,512]{2,1,0:T(8,128)(2,1)S(1)}, u32[]{:S(2)}, u32[]{:S(2)}) async-start(bf16[32,20,512]{2,1,0:T(8,128)(2,1)} %broadcast_in_dim.15), calls=%async_computation.1 | async-start | bytes 1572864 | tf_op jit(solution)/shard_map/all_to_all | solution.py:234
  26.8 1.8 shard_map.111
  28.6 21.6 %all-to-all-done.1 = bf16[32,20,512]{2,1,0:T(8,128)(2,1)S(1)} async-done(((bf16[32,20,512]{2,1,0:T(8,128)(2,1)}), bf16[32,20,512]{2,1,0:T(8,128)(2,1)S(1)}, u32[]{:S(2)}, u32[]{:S(2)}) %all-to-all-start.1) | async-done | bytes 655392 | tf_op jit(solution)/shard_map/all_to_all | solution.py:234
  50.2 5.6 %all-to-all-start = ((bf16[8,128,1280]{2,1,0:T(8,128)(2,1)}), bf16[8,128,1280]{2,1,0:T(8,128)(2,1)}, u32[]{:S(2)}, u32[]{:S(2)}) async-start(bf16[8,128,1280]{2,1,0:T(8,128)(2,1)} %shard_map.111), calls=%async_computation | async-start | bytes 5242880 | tf_op jit(solution)/shard_map/all_to_all | solution.py:234
  56.3 1.0 reshape.16.w_ref
  57.3 29.6 %all-to-all-done.refs_0_ = bf16[8,128,1280]{2,1,0:T(8,128)(2,1)} async-done(((bf16[8,128,1280]{2,1,0:T(8,128)(2,1)}), bf16[8,128,1280]{2,1,0:T(8,128)(2,1)}, u32[]{:S(2)}, u32[]{:S(2)}) %all-to-all-start) | async-done | bytes 2621472 | tf_op jit(solution)/shard_map/all_to_all | solution.py:234
  86.9 10.0 %shard_map.113 = (bf16[8,128,512]{2,1,0:T(8,128)(2,1)S(1)}, f32[1024,128]{1,0:T(8,128)S(1)}, bf16[1024,128]{1,0:T(8,128)(2,1)S(1)}) custom-call(s32[1]{0:T(128)} %bitcast.c_ref, s32[32]{0:T(128)S(1)} %bitcast.15, s32[32]{0:T(128)S(1)} %copy-done.10, bf16[8,128,1280]{2,1,0:T(8,128)(2,1)} %all-to-all-done.refs_0_), custom_call_target="tpu_custom_call" | custom-call | flops 2000000000 | bytes 5000000 | tf_op jit(solution)/shard_map/pallas_call | solution.py:279
  96.9 1.6 collective-permute-start.1
  98.5 6.4 %collective-permute-done.1.taken_ref = bf16[1024,128]{1,0:T(8,128)(2,1)S(1)} collective-permute-done((bf16[1024,128]{1,0:T(8,128)(2,1)S(1)}, bf16[1024,128]{1,0:T(8,128)(2,1)S(1)}, u32[]{:S(2)}, u32[]{:S(2)}) %collective-permute-start.1) | collective-permute-done | bytes 262176 | tf_op jit(solution)/shard_map/ppermute | solution.py:303
  105.0 19.7 %all_to_all.40.pieces_ref = bf16[4,1024,128]{2,1,0:T(8,128)(2,1)S(1)} all-to-all(bf16[4,1024,128]{2,1,0:T(8,128)(2,1)S(1)} %shard_map.114.own_ref), channel_id=1, replica_groups=mesh['z'=8,'yh'=2,'core'=2,'y'=2,'x'=4] {'x'}, dimensions={0} | all-to-all | bytes 2097152 | tf_op jit(solution)/shard_map/all_to_all | solution.py:234
  124.6 17.2 %all_to_all.41.x_ref = bf16[8,640,128]{2,1,0:T(8,128)(2,1)S(1)} all-to-all(bf16[8,640,128]{2,1,0:T(8,128)(2,1)S(1)} %shard_map.112), channel_id=1, replica_groups=mesh['z'=8,'yh'=2,'core'=2,'y'=2,'x'=4] {'y','x'}, dimensions={0} | all-to-all | bytes 2621440 | tf_op jit(solution)/shard_map/all_to_all | solution.py:234
  143.8 18.6 %all_to_all.42.parts_ref = bf16[8,80,512]{2,1,0:T(8,128)(2,1)S(1)} all-to-all(bf16[8,80,512]{2,1,0:T(8,128)(2,1)S(1)} %get-tuple-element.23), channel_id=1, replica_groups=mesh['z'=8,'yh'=2,'core'=2,'y'=2,'x'=4] {'yh','core','y'}, dimensions={0} | all-to-all | bytes 1310720 | tf_op jit(solution)/shard_map/all_to_all | solution.py:234
  162.4 4.9 %all-to-all-start.5 = ((bf16[8,128,512]{2,1,0:T(8,128)(2,1)}), bf16[8,128,512]{2,1,0:T(8,128)(2,1)S(1)}, u32[]{:S(2)}, u32[]{:S(2)}) async-start(bf16[8,128,512]{2,1,0:T(8,128)(2,1)} %copy-done.3), calls=%async_computation.5 | async-start | bytes 2097152 | tf_op jit(solution)/shard_map/all_to_all | solution.py:234
  168.1 13.3 %all-to-all-done.5.dq_ref = bf16[8,128,512]{2,1,0:T(8,128)(2,1)S(1)} async-done(((bf16[8,128,512]{2,1,0:T(8,128)(2,1)}), bf16[8,128,512]{2,1,0:T(8,128)(2,1)S(1)}, u32[]{:S(2)}, u32[]{:S(2)}) %all-to-all-start.5) | async-done | bytes 1048608 | tf_op jit(solution)/shard_map/all_to_all | solution.py:234
  181.5 6.8 %all-to-all-start.7 = ((bf16[8,10,1024]{2,1,0:T(8,128)(2,1)}), bf16[8,10,1024]{2,1,0:T(8,128)(2,1)S(1)}, u32[]{:S(2)}, u32[]{:S(2)}) async-start(bf16[8,10,1024]{2,1,0:T(8,128)(2,1)} %shard_map.119), calls=%async_computation.7 | async-start | bytes 524288 | tf_op jit(solution)/shard_map/all_to_all | solution.py:234
  188.3 1.1 copy-done
  189.4 1.2 copy-done.5
  190.6 2.0 shard_map.116
  192.6 7.3 %all-to-all-done.7.parts_ref = bf16[8,10,1024]{2,1,0:T(8,128)(2,1)S(1)} async-done(((bf16[8,10,1024]{2,1,0:T(8,128)(2,1)}), bf16[8,10,1024]{2,1,0:T(8,128)(2,1)S(1)}, u32[]{:S(2)}, u32[]{:S(2)}) %all-to-all-start.7) | async-done | bytes 163872 | tf_op jit(solution)/shard_map/all_to_all | solution.py:234
  200.0 5.0 %all-to-all-start.4 = ((bf16[8,768,128]{2,1,0:T(8,128)(2,1)}), bf16[8,768,128]{2,1,0:T(8,128)(2,1)S(1)}, u32[]{:S(2)}, u32[]{:S(2)}) async-start(bf16[8,768,128]{2,1,0:T(8,128)(2,1)} %shard_map.116), calls=%async_computation.4 | async-start | bytes 3145728 | tf_op jit(solution)/shard_map/all_to_all | solution.py:234
  205.0 1.0 shard_map.118
  206.7 16.5 %all-to-all-done.4.parts_ref = bf16[8,768,128]{2,1,0:T(8,128)(2,1)S(1)} async-done(((bf16[8,768,128]{2,1,0:T(8,128)(2,1)}), bf16[8,768,128]{2,1,0:T(8,128)(2,1)S(1)}, u32[]{:S(2)}, u32[]{:S(2)}) %all-to-all-start.4) | async-done | bytes 1572896 | tf_op jit(solution)/shard_map/all_to_all | solution.py:234
  223.1 1.2 shard_map.117
  (28 shorter events, 5.5 us)
Async XLA Ops:
  0.6 26.1 %copy-start.1 = (bf16[1,128,4096]{2,1,0:T(8,128)(2,1)S(1)}, bf16[1,128,4096]{2,1,0:T(8,128)(2,1)}, u32[]{:S(2)}) copy-start(bf16[1,128,4096]{2,1,0:T(8,128)(2,1)} %param.9) | copy-start | bytes 3145732
  0.6 26.1 %copy-start.2 = (bf16[1,128,4096]{2,1,0:T(8,128)(2,1)S(1)}, bf16[1,128,4096]{2,1,0:T(8,128)(2,1)}, u32[]{:S(2)}) copy-start(bf16[1,128,4096]{2,1,0:T(8,128)(2,1)} %param.12) | copy-start | bytes 3145732
  0.7 26.1 %copy-start.7 = (bf16[1,128,512]{2,1,0:T(8,128)(2,1)S(1)}, bf16[1,128,512]{2,1,0:T(8,128)(2,1)}, u32[]{:S(2)}) copy-start(bf16[1,128,512]{2,1,0:T(8,128)(2,1)} %param.10) | copy-start | bytes 393220
  0.7 26.1 %copy-start.8 = (bf16[1,128,512]{2,1,0:T(8,128)(2,1)S(1)}, bf16[1,128,512]{2,1,0:T(8,128)(2,1)}, u32[]{:S(2)}) copy-start(bf16[1,128,512]{2,1,0:T(8,128)(2,1)} %param.11) | copy-start | bytes 393220
  1.7 0.7 collective-permute-start
  3.3 46.9 %all-to-all-start.1 = ((bf16[32,20,512]{2,1,0:T(8,128)(2,1)}), bf16[32,20,512]{2,1,0:T(8,128)(2,1)S(1)}, u32[]{:S(2)}, u32[]{:S(2)}) async-start(bf16[32,20,512]{2,1,0:T(8,128)(2,1)} %broadcast_in_dim.15), calls=%async_computation.1 | async-start | bytes 1572864 | tf_op jit(solution)/shard_map/all_to_all | solution.py:234
  28.6 27.3 %copy-start.6 = (bf16[1,128,2560]{2,1,0:T(8,128)(2,1)S(1)}, bf16[1,128,2560]{2,1,0:T(8,128)(2,1)}, u32[]{:S(2)}) copy-start(bf16[1,128,2560]{2,1,0:T(8,128)(2,1)} %param.8) | copy-start | bytes 1966084
  50.2 36.7 %all-to-all-start = ((bf16[8,128,1280]{2,1,0:T(8,128)(2,1)}), bf16[8,128,1280]{2,1,0:T(8,128)(2,1)}, u32[]{:S(2)}, u32[]{:S(2)}) async-start(bf16[8,128,1280]{2,1,0:T(8,128)(2,1)} %shard_map.111), calls=%async_computation | async-start | bytes 5242880 | tf_op jit(solution)/shard_map/all_to_all | solution.py:234
  55.9 31.0 %copy-start.9 = (s32[1,32]{1,0:T(1,128)S(1)}, s32[1,32]{1,0:T(1,128)}, u32[]{:S(2)}) copy-start(s32[1,32]{1,0:T(1,128)} %param.14) | copy-start | bytes 388
  55.9 31.0 %copy-start.10 = (s32[32]{0:T(128)S(1)}, s32[32]{0:T(128)}, u32[]{:S(2)}) copy-start(s32[32]{0:T(128)} %order_ref.1) | copy-start | bytes 388
  96.9 8.0 %copy-start.3 = (bf16[8,128,512]{2,1,0:T(8,128)(2,1)}, bf16[8,128,512]{2,1,0:T(8,128)(2,1)S(1)}, u32[]{:S(2)}) copy-start(bf16[8,128,512]{2,1,0:T(8,128)(2,1)S(1)} %get-tuple-element.21) | copy-start | bytes 3145732
  96.9 8.0 %collective-permute-start.1 = (bf16[1024,128]{1,0:T(8,128)(2,1)S(1)}, bf16[1024,128]{1,0:T(8,128)(2,1)S(1)}, u32[]{:S(2)}, u32[]{:S(2)}) collective-permute-start(bf16[1024,128]{1,0:T(8,128)(2,1)S(1)} %get-tuple-element.16), channel_id=1, source_target_pairs={{0,4},{4,0},{1,5},{5,1},{2,6},{6,2},{3,7},{7,3},{8,12},{12,8},{9,1... | collective-permute-start | bytes 786440 | tf_op jit(solution)/shard_map/ppermute | solution.py:303
  142.8 1.0 copy-start.4
  162.4 19.1 %all-to-all-start.5 = ((bf16[8,128,512]{2,1,0:T(8,128)(2,1)}), bf16[8,128,512]{2,1,0:T(8,128)(2,1)S(1)}, u32[]{:S(2)}, u32[]{:S(2)}) async-start(bf16[8,128,512]{2,1,0:T(8,128)(2,1)} %copy-done.3), calls=%async_computation.5 | async-start | bytes 2097152 | tf_op jit(solution)/shard_map/all_to_all | solution.py:234
  181.5 18.5 %all-to-all-start.7 = ((bf16[8,10,1024]{2,1,0:T(8,128)(2,1)}), bf16[8,10,1024]{2,1,0:T(8,128)(2,1)S(1)}, u32[]{:S(2)}, u32[]{:S(2)}) async-start(bf16[8,10,1024]{2,1,0:T(8,128)(2,1)} %shard_map.119), calls=%async_computation.7 | async-start | bytes 524288 | tf_op jit(solution)/shard_map/all_to_all | solution.py:234
  188.3 1.1 copy-start
  189.4 1.2 copy-start.5
  200.0 23.2 %all-to-all-start.4 = ((bf16[8,768,128]{2,1,0:T(8,128)(2,1)}), bf16[8,768,128]{2,1,0:T(8,128)(2,1)S(1)}, u32[]{:S(2)}, u32[]{:S(2)}) async-start(bf16[8,768,128]{2,1,0:T(8,128)(2,1)} %shard_map.116), calls=%async_computation.4 | async-start | bytes 3145728 | tf_op jit(solution)/shard_map/all_to_all | solution.py:234

commit v2 on v1

--- a/solution.py
+++ b/solution.py
@@ -64,6 +64,11 @@
         out_ref[dest, :, 2 * Q_COLS + HEAD_WIDTH :] = v_ref[:, head]
 
 
+def tile_row(z, low, y):
+    row = (low % 2) * 320 + (low // 2) * 160
+    return row + (z % 2) * 80 + (z // 2 % 2) * 40 + (z // 4) * 20 + y * 10
+
+
 def turn_kernel(x_ref, out_ref, turned, tile):
     for j in range(FEATURES // 128):
         block = x_ref[:, j * 128 : (j + 1) * 128].T
@@ -73,7 +78,7 @@
             for y in range(2):
                 for z in range(8):
                     source = (z * 4 + low) * 80 + y * 40 + x * 10
-                    at = (low * 2 + y) * 80 + z * 10
+                    at = tile_row(z, low, y)
                     tile[at : at + 10, :] = turned[source : source + 10, :]
         piece = tile[...].astype(jnp.bfloat16)
         out_ref[x] = piece
@@ -166,7 +171,9 @@
         block = slice(st * BLK, (st + 1) * BLK)
         keep_ref[block, :] = dkv_s[rows, own] * own_scale
         send_ref[block, :] = (dkv_s[rows, other] * other_scale).astype(jnp.bfloat16)
-        dq_ref[st // 4, (st % 4) * BLK : (st % 4 + 1) * BLK, :] = dq_s[rows, :]
+        for g in range(4):
+            at = g * 128 + (st % 4) * BLK
+            dq_ref[st // 4, at : at + BLK, :] = dq_s[rows, g * 128 : (g + 1) * 128]
 
 
 def pair_kernel(keep_ref, taken_ref, out_ref):
@@ -175,29 +182,52 @@
         out_ref[dest] = total
 
 
-def weight_kernel(pieces_ref, x_ref, kv_ref, out_ref, x_s):
+def weight_kernel(core_ref, pieces_ref, x_ref, kv_ref, send_ref, keep_ref, x_s):
     for src in range(4):
         kv_ref[:, src * 128 : (src + 1) * 128] = pieces_ref[src]
     for src in range(CTX):
         x_s[:, src * 128 : (src + 1) * 128] = x_ref[src]
+    core, part = core_ref[0], FEAT_TILE // 2
+    other = pl.ds(pl.multiple_of((1 - core) * part, part), part)
+    own = pl.ds(pl.multiple_of(core * part, part), part)
     for j in range(2):
         cols = slice(j * 256, (j + 1) * 256)
-        tile = dot(x_s[...], kv_ref[:, cols], NN).astype(jnp.bfloat16)
-        for k in range(8):
-            out_ref[k, :, cols] = tile[k * 80 : (k + 1) * 80, :]
-
-
-def input_kernel(kv_ref, w_ref, own_ref, out_ref):
+        send_ref[:, cols] = dot(x_s[other, :], kv_ref[:, cols], NN).astype(jnp.bfloat16)
+        keep_ref[:, cols] = dot(x_s[own, :], kv_ref[:, cols], NN)
+
+
+def halve_kernel(bit_ref, keep_ref, got_ref, send_ref, kept_ref):
+    part = kept_ref.shape[0]
+    total = keep_ref[...] + got_ref[...].astype(jnp.float32)
+    low, high, upper = total[:part, :], total[part:, :], bit_ref[0] == 1
+    send_ref[...] = jnp.where(upper, low, high).astype(send_ref.dtype)
+    kept_ref[...] = jnp.where(upper, high, low)
+
+
+def join_kernel(y_ref, own_ref, got_ref, out_ref):
+    upper = y_ref[0] == 1
+    out_ref[:, 0:512] = jnp.where(upper, got_ref[...], own_ref[...])
+    out_ref[:, 512:1024] = jnp.where(upper, own_ref[...], got_ref[...])
+
+
+def input_kernel(f_ref, kv_ref, w_ref, own_ref, dq_ref, out_ref, w_s):
+    for at in range(FSDP):
+        mask = sum(((at >> i) & 1) << bit for i, bit in enumerate(GATHER_BITS))
+        source = f_ref[0] ^ mask
+        rows = pl.ds(pl.multiple_of((source // 4) * 80, 80), 80)
+        cols = pl.ds(pl.multiple_of(lax.rem(source, 4) * 128, 128), 128)
+        w_s[rows, cols] = w_ref[at]
     for j in range(4):
         rows = slice(j * 256, (j + 1) * 256)
-        tile = dot(w_ref[...], kv_ref[rows, :], NT).astype(jnp.bfloat16)
+        tile = dot(w_s[...], kv_ref[rows, :], NT).astype(jnp.bfloat16)
         out_ref[2 * j, 0:FEAT_TILE, :] = tile[:, 0:128]
         out_ref[2 * j + 1, 0:FEAT_TILE, :] = tile[:, 128:256]
     for dest in range(CTX):
-        out_ref[dest, FEAT_TILE:, :] = own_ref[0, dest * ROWS : (dest + 1) * ROWS, :]
-
-
-def input_out_kernel(parts_ref, input_ref, kv_rows_ref):
+        out_ref[dest, FEAT_TILE : FEAT_TILE + ROWS, :] = own_ref[0, dest * ROWS : (dest + 1) * ROWS, :]
+        out_ref[dest, FEAT_TILE + ROWS :, :] = dq_ref[dest]
+
+
+def out_kernel(parts_ref, input_ref, query_ref, kv_rows_ref):
     for x in range(4):
         for j in range(FEAT_TILE // 128):
             rows = slice(j * 128, (j + 1) * 128)
@@ -205,29 +235,20 @@
             at = x * FEAT_TILE + j * 128
             input_ref[:, at : at + 128] = total.T.astype(jnp.bfloat16)
     for src in range(CTX):
-        kv_rows_ref[:, src * 128 : (src + 1) * 128] = parts_ref[src, FEAT_TILE:, :]
-
-
-def query_out_kernel(dq_ref, query_ref):
-    for src in range(CTX):
-        at = q_block(src)
-        query_ref[:, at * Q_COLS : (at + 1) * Q_COLS] = dq_ref[src]
-
-
-def first_sum_kernel(parts_ref, out_ref):
-    for y in range(2):
-        total = parts_ref[y].astype(jnp.float32)
-        for low in range(1, 4):
-            total = total + parts_ref[low * 2 + y].astype(jnp.float32)
-        for z in range(8):
-            out_ref[z, :, y * 512 : (y + 1) * 512] = total[z * 10 : (z + 1) * 10, :].astype(jnp.bfloat16)
-
-
-def second_sum_kernel(parts_ref, out_ref):
-    total = parts_ref[0].astype(jnp.float32)
-    for k in range(1, 8):
-        total = total + parts_ref[k].astype(jnp.float32)
-    out_ref[...] = total
+        kv_rows_ref[:, src * 128 : (src + 1) * 128] = parts_ref[src, FEAT_TILE : FEAT_TILE + ROWS, :]
+        for g in range(4):
+            at = q_block(src) * Q_COLS + g * 128
+            rows = slice(FEAT_TILE + ROWS + g * 128, FEAT_TILE + ROWS + (g + 1) * 128)
+            query_ref[:, at : at + 128] = parts_ref[src, rows, :]
+
+
+GATHER_BITS = (4, 3, 2, 1, 0)
+BIT_AXES = (("core", 1), ("yh", 1), ("z", 1), ("z", 2), ("z", 4))
+
+
+def swap(value, bit):
+    axis, mask = BIT_AXES[bit]
+    return lax.ppermute(value, axis, [(i, i ^ mask) for i in range(8 if axis == "z" else 2)])
 
 
 def exchange(value, axis):
@@ -260,20 +281,18 @@
         compiler_params=params(),
         cost_estimate=cost(0, 1_300_000),
     )(inputs[0])
-    own_rows = lax.dynamic_slice(
-        key_value_weight, (lax.rem(c, 4) * 20, (c // 4) * 512), (20, 512)
-    )
+    f = lax.axis_index(("z", "yh", "core")).astype(jnp.int32)
+    tile = lax.dynamic_slice(key_value_weight, (0, c * 128), (80, 128))
     perm = []
     for f1 in range(FSDP):
         for c1 in range(CTX):
             y1, x1 = c1 // 4, c1 % 4
             perm.append((f1 * CTX + c1, ((f1 % 8) * 4 + x1) * CTX + y1 * 4 + f1 // 8))
-    own_rows = lax.ppermute(own_rows, ("z", "yh", "core", "y", "x"), perm)
-    weight_tile = exchange(
-        jnp.broadcast_to(own_rows[None], (FSDP, 20, 512)), ("z", "yh", "core")
-    ).reshape(FEAT_TILE, 512)
-
-    got, turned, weight_tile = lax.optimization_barrier((got, turned, weight_tile))
+    tile = lax.ppermute(tile, ("z", "yh", "core", "y", "x"), perm)[None]
+    for bit in GATHER_BITS:
+        tile = jnp.concatenate([tile, swap(tile, bit)], axis=0)
+
+    got, turned, weight_tile = lax.optimization_barrier((got, turned, tile))
     got_x = exchange(turned, ("y", "x"))
 
     dq_parts, keep, send = pl.pallas_call(
@@ -281,7 +300,7 @@
         in_specs=[SMEM] * 3 + [VMEM],
         out_specs=[VMEM] * 3,
         out_shape=[
-            shape((CTX, ROWS, Q_COLS)),
+            shape((CTX, Q_COLS, ROWS)),
             shape((SLAB, HEAD_WIDTH), jnp.float32),
             shape((SLAB, HEAD_WIDTH)),
         ],
@@ -297,10 +316,11 @@
             pltpu.SMEM((32,), jnp.int32),
         ],
         compiler_params=params(),
-        cost_estimate=cost(2_000_000_000, 5_000_000),
+        cost_estimate=cost(10_000_000_000, 5_000_000),
     )(c_at, doc_ids[0], block_order, got)
 
     taken = lax.ppermute(send, "y", [(0, 1), (1, 0)])
+    taken, got_x = lax.optimization_barrier((taken, got_x))
     own_cols = pl.pallas_call(
         pair_kernel,
         in_specs=[VMEM] * 2,
@@ -310,63 +330,63 @@
         cost_estimate=cost(0, 3_000_000),
     )(keep, taken)
     pieces = exchange(own_cols, "x")
-    dq_got = exchange(dq_parts, ("y", "x"))
-
-    kv_half, wg_parts = pl.pallas_call(
+
+    core, y = lax.rem(f, 2), c // 4
+    kv_half, wg_send, wg_keep = pl.pallas_call(
         weight_kernel,
-        in_specs=[VMEM] * 2,
-        out_specs=[VMEM] * 2,
-        out_shape=[shape((SLAB, 512)), shape((8, 80, 512))],
+        in_specs=[SMEM] + [VMEM] * 2,
+        out_specs=[VMEM] * 3,
+        out_shape=[shape((SLAB, 512)), shape((320, 512)), shape((320, 512), jnp.float32)],
         scratch_shapes=[pltpu.VMEM((FEAT_TILE, SLAB), jnp.bfloat16)],
         compiler_params=params(),
         cost_estimate=cost(700_000_000, 5_000_000),
-    )(pieces, got_x)
-    wg_got = exchange(wg_parts, ("yh", "core", "y"))
-
-    ig_parts = pl.pallas_call(
+    )(core.reshape(1), pieces, got_x)
+
+    wg_got = swap(wg_send, 0)
+    parts = pl.pallas_call(
         input_kernel,
-        in_specs=[VMEM] * 3,
+        in_specs=[SMEM] + [VMEM] * 4,
         out_specs=VMEM,
-        out_shape=shape((CTX, FEAT_TILE + ROWS, ROWS)),
+        out_shape=shape((CTX, FEAT_TILE + ROWS + Q_COLS, ROWS)),
+        scratch_shapes=[pltpu.VMEM((FEAT_TILE, 512), jnp.bfloat16)],
         compiler_params=params(),
         cost_estimate=cost(700_000_000, 4_000_000),
-    )(kv_half, weight_tile, own_cols)
-    ig_got = exchange(ig_parts, ("y", "x"))
-
-    wg_second = pl.pallas_call(
-        first_sum_kernel,
-        in_specs=[VMEM],
-        out_specs=VMEM,
-        out_shape=shape((8, 10, 1024)),
-        compiler_params=params(),
-        cost_estimate=cost(0, 1_000_000),
-    )(wg_got)
-    wg_last = exchange(wg_second, "z")
-
-    query_grad = pl.pallas_call(
-        query_out_kernel,
-        in_specs=[VMEM],
-        out_specs=VMEM,
-        out_shape=shape((ROWS, HQ * HEAD_WIDTH)),
-        compiler_params=params(),
-        cost_estimate=cost(0, 2_000_000),
-    )(dq_got)
-    input_grad, kv_rows = pl.pallas_call(
-        input_out_kernel,
-        in_specs=[VMEM],
-        out_specs=[VMEM] * 2,
-        out_shape=[shape((ROWS, FEATURES)), shape((ROWS, 1024))],
-        compiler_params=params(),
-        cost_estimate=cost(0, 2_000_000),
-    )(ig_got)
+    )(f.reshape(1), kv_half, weight_tile, own_cols, dq_parts)
+    parts_got = exchange(parts, ("y", "x"))
+
+    def halve(bit, keep, got, kind):
+        rows = keep.shape[0] // 2
+        return pl.pallas_call(
+            halve_kernel,
+            in_specs=[SMEM] + [VMEM] * 2,
+            out_specs=[VMEM] * 2,
+            out_shape=[shape((rows, 512), kind), shape((rows, 512), jnp.float32)],
+            compiler_params=params(),
+            cost_estimate=cost(0, rows * 512 * 16),
+        )(bit.reshape(1), keep, got)
+
+    for bit, kind in ((1, jnp.bfloat16), (2, jnp.bfloat16), (3, jnp.float32), (4, jnp.float32)):
+        wg_send, wg_keep = halve((f >> bit) & 1, wg_keep, wg_got, kind)
+        wg_got = swap(wg_send, bit)
+    wg_send, wg_keep = halve(y, wg_keep, wg_got, jnp.float32)
+    wg_got = lax.ppermute(wg_send, "y", [(0, 1), (1, 0)])
     weight_grad = pl.pallas_call(
-        second_sum_kernel,
-        in_specs=[VMEM],
+        join_kernel,
+        in_specs=[SMEM] + [VMEM] * 2,
         out_specs=VMEM,
         out_shape=shape((10, 1024), jnp.float32),
         compiler_params=params(),
-        cost_estimate=cost(0, 200_000),
-    )(wg_last)
+        cost_estimate=cost(0, 100_000),
+    )(y.reshape(1), wg_keep, wg_got)
+
+    input_grad, query_grad, kv_rows = pl.pallas_call(
+        out_kernel,
+        in_specs=[VMEM],
+        out_specs=[VMEM] * 3,
+        out_shape=[shape((ROWS, FEATURES)), shape((ROWS, HQ * HEAD_WIDTH)), shape((ROWS, 1024))],
+        compiler_params=params(),
+        cost_estimate=cost(0, 5_000_000),
+    )(parts_got)
     return (input_grad[None], query_grad[None], kv_rows[None], weight_grad)
 
 

time: 227 us -> 198 us (0.87)
  blocking collectives: 55.5 us -> 0 us
  starting transfers between devices: 48 us -> 73.9 us
  waiting for transfers between devices: 94.8 us -> 86.6 us
  local copies, waits for them, and re-layouts: 6.2 us -> 11.7 us
  Pallas kernels: 19 us -> 23.7 us
    all_to_all x5 -> x4, waiting for transfers between devices: 88.4 us -> 15 us  [exchange(): return lax.all_to_all(value, axis, 0, 0, tiled=True)]
    ppermute x1 -> x12, waiting for transfers between devices: 0.01 us -> 59.8 us  [the longest x10 57.2 us: swap(): lax.ppermute(value, axis, [(i, i ^ mask) for i in range(8 if axis == 'z'...]
    all_to_all x3 -> x0, blocking collectives: 55.5 us -> none  [exchange(): return lax.all_to_all(value, axis, 0, 0, tiled=True)]
    ppermute x1 -> x12, starting transfers between devices: 0.65 us -> 54.3 us  [the longest x10 52.3 us: swap(): lax.ppermute(value, axis, [(i, i ^ mask) for i in range(8 if axis == 'z'...]
    all_to_all x5 -> x4, starting transfers between devices: 45.8 us -> 19.5 us  [exchange(): return lax.all_to_all(value, axis, 0, 0, tiled=True)]
    unnamed x22 -> x38, local copies, waits for them, and re-layouts: 3.31 us -> 11.6 us
    ppermute x1, waiting for transfers between devices: 6.37 us -> 11.8 us  [body(): taken = lax.ppermute(send, 'y', [(0, 1), (1, 0)])]
    pallas_call x6 -> x9, Pallas kernels: 6.72 us -> 10.5 us  [the longest x1 3.75 us: body(): pl.pallas_call(input_kernel, in_specs=[SMEM] + [VMEM] * 4, out_specs=VMEM...]
  transfers between devices with their start and end apart: 7 -> 17, of which waited for: 6 -> 12; matrix products, arithmetic and copies ran while one was open for 0% -> 0% of each run, Pallas kernels for 3% -> 7%
where the time goes in v2:
time: 198 us; the launch traced here: 197 us
  waiting for transfers between devices  86.6 us (44%)
  starting transfers between devices  73.9 us (37%)
  Pallas kernels  23.7 us (12%)
  local copies, waits for them, and re-layouts  11.7 us (6%)
    ppermute x10, waiting for transfers between devices, swap(): lax.ppermute(value, axis, [(i, i ^ mask) for i in range(8 if axis == 'z'...  57.2 us
    ppermute x10, starting transfers between devices, swap(): lax.ppermute(value, axis, [(i, i ^ mask) for i in range(8 if axis == 'z'...  52.3 us
    all_to_all x4, starting transfers between devices, exchange(): return lax.all_to_all(value, axis, 0, 0, tiled=True)  19.5 us
    all_to_all x4, waiting for transfers between devices, exchange(): return lax.all_to_all(value, axis, 0, 0, tiled=True)  15 us
    ppermute x1, waiting for transfers between devices, body(): taken = lax.ppermute(send, 'y', [(0, 1), (1, 0)])  11.8 us
    unnamed x38, local copies, waits for them, and re-layouts  11.6 us
    pallas_call x1, Pallas kernels, body(): pl.pallas_call(attention_kernel, in_specs=[SMEM] * 3 + [VMEM], out_specs=...  8.94 us
  transfers between devices with their start and end apart: 17, of which 12 were waited for; matrix products, arithmetic and copies ran while one was open for 0% of the time, Pallas kernels for 7%

profile of v2, /device:TPU:8, one launch (start us, length us, event | category | flops | bytes accessed | tf_op | source)
XLA Modules:
  0.0 196.8 jit_solution(4566514808683784272)
XLA Ops:
  6.7 5.8 %all-to-all-start = ((bf16[8,128,1280]{2,1,0:T(8,128)(2,1)}), bf16[8,128,1280]{2,1,0:T(8,128)(2,1)S(1)}, u32[]{:S(2)}, u32[]{:S(2)}) async-start(bf16[8,128,1280]{2,1,0:T(8,128)(2,1)} %shard_map.111), calls=%async_computation | async-start | bytes 5242880 | tf_op jit(solution)/shard_map/all_to_all | solution.py:255
  13.1 15.2 %collective-permute-start.1 = (bf16[1,80,128]{2,1,0:T(8,128)(2,1)S(1)}, bf16[1,80,128]{2,1,0:T(8,128)(2,1)S(1)}, u32[]{:S(2)}, u32[]{:S(2)}) collective-permute-start(bf16[1,80,128]{2,1,0:T(8,128)(2,1)S(1)} %bitcast.26), channel_id=1, source_target_pairs={{0,128},{32,160},{64,192},{96,224},{128,0},{160,32},{192,64},{224,... | collective-permute-start | bytes 61448 | tf_op jit(solution)/shard_map/ppermute | solution.py:251
  28.3 1.8 collective-permute-done.1
  30.1 4.1 %collective-permute-start.2 = (bf16[2,80,128]{2,1,0:T(8,128)(2,1)S(1)}, bf16[2,80,128]{2,1,0:T(8,128)(2,1)S(1)}, u32[]{:S(2)}, u32[]{:S(2)}) collective-permute-start(bf16[2,80,128]{2,1,0:T(8,128)(2,1)S(1)} %pad_maximum_fusion.2), channel_id=1, source_target_pairs={{0,64},{32,96},{64,0},{96,32},{128,192},{160,224},{192,128},{224,1... | collective-permute-start | bytes 122888 | tf_op jit(solution)/shard_map/ppermute | solution.py:251
  34.2 2.4 %collective-permute-done.2 = bf16[2,80,128]{2,1,0:T(8,128)(2,1)S(1)} collective-permute-done((bf16[2,80,128]{2,1,0:T(8,128)(2,1)S(1)}, bf16[2,80,128]{2,1,0:T(8,128)(2,1)S(1)}, u32[]{:S(2)}, u32[]{:S(2)}) %collective-permute-start.2) | collective-permute-done | bytes 40992 | tf_op jit(solution)/shard_map/ppermute | solution.py:251
  36.9 4.3 %collective-permute-done.3 = bf16[4,80,128]{2,1,0:T(8,128)(2,1)S(1)} collective-permute-done((bf16[4,80,128]{2,1,0:T(8,128)(2,1)S(1)}, bf16[4,80,128]{2,1,0:T(8,128)(2,1)S(1)}, u32[]{:S(2)}, u32[]{:S(2)}) %collective-permute-start.3) | collective-permute-done | bytes 81952 | tf_op jit(solution)/shard_map/ppermute | solution.py:251
  41.2 27.4 %collective-permute-start.4 = (bf16[8,80,128]{2,1,0:T(8,128)(2,1)S(1)}, bf16[8,80,128]{2,1,0:T(8,128)(2,1)S(1)}, u32[]{:S(2)}, u32[]{:S(2)}) collective-permute-start(bf16[8,80,128]{2,1,0:T(8,128)(2,1)S(1)} %pad_maximum_fusion), channel_id=1, source_target_pairs={{0,16},{16,0},{1,17},{17,1},{2,18},{18,2},{3,19},{19,3},{4,20},{20... | collective-permute-start | bytes 491528 | tf_op jit(solution)/shard_map/ppermute | solution.py:251
  68.7 3.2 %collective-permute-done.4 = bf16[8,80,128]{2,1,0:T(8,128)(2,1)S(1)} collective-permute-done((bf16[8,80,128]{2,1,0:T(8,128)(2,1)S(1)}, bf16[8,80,128]{2,1,0:T(8,128)(2,1)S(1)}, u32[]{:S(2)}, u32[]{:S(2)}) %collective-permute-start.4) | collective-permute-done | bytes 163872 | tf_op jit(solution)/shard_map/ppermute | solution.py:251
  74.8 4.6 %all-to-all-start.1 = ((bf16[8,640,128]{2,1,0:T(8,128)(2,1)}), bf16[8,640,128]{2,1,0:T(8,128)(2,1)}, u32[]{:S(2)}, u32[]{:S(2)}) async-start(bf16[8,640,128]{2,1,0:T(8,128)(2,1)} %shard_map.112), calls=%async_computation.1 | async-start | bytes 2621440 | tf_op jit(solution)/shard_map/all_to_all | solution.py:255
  79.4 8.9 %shard_map.113 = (bf16[8,512,128]{2,1,0:T(8,128)(2,1)S(1)}, f32[1024,128]{1,0:T(8,128)S(1)}, bf16[1024,128]{1,0:T(8,128)(2,1)S(1)}) custom-call(s32[1]{0:T(128)} %bitcast.2.c_ref, s32[32]{0:T(128)S(1)} %bitcast.25, s32[32]{0:T(128)S(1)} %copy-done.16, bf16[8,128,1280]{2,1,0:T(8,128)(2,1)S(1)} %all-to-all-done.refs_0_), custom_call_target="tpu_custom_call" | custom-call | flops 10000000000 | bytes 5000000 | tf_op jit(solution)/shard_map/pallas_call | solution.py:298
  90.3 11.8 %collective-permute-done.6.taken_ref = bf16[1024,128]{1,0:T(8,128)(2,1)S(1)} collective-permute-done((bf16[1024,128]{1,0:T(8,128)(2,1)S(1)}, bf16[1024,128]{1,0:T(8,128)(2,1)S(1)}, u32[]{:S(2)}, u32[]{:S(2)}) %collective-permute-start.6) | collective-permute-done | bytes 262176 | tf_op jit(solution)/shard_map/ppermute | solution.py:322
  104.2 3.6 %all-to-all-start.2 = ((bf16[4,1024,128]{2,1,0:T(8,128)(2,1)}), bf16[4,1024,128]{2,1,0:T(8,128)(2,1)S(1)}, u32[]{:S(2)}, u32[]{:S(2)}) async-start(bf16[4,1024,128]{2,1,0:T(8,128)(2,1)} %shard_map.114.own_ref), calls=%async_computation.2 | async-start | bytes 2097152 | tf_op jit(solution)/shard_map/all_to_all | solution.py:255
  107.9 15.0 %all-to-all-done.2.pieces_ref = bf16[4,1024,128]{2,1,0:T(8,128)(2,1)S(1)} async-done(((bf16[4,1024,128]{2,1,0:T(8,128)(2,1)}), bf16[4,1024,128]{2,1,0:T(8,128)(2,1)S(1)}, u32[]{:S(2)}, u32[]{:S(2)}) %all-to-all-start.2) | async-done | bytes 1048608 | tf_op jit(solution)/shard_map/all_to_all | solution.py:255
  122.8 2.5 %shard_map.115 = (bf16[1024,512]{1,0:T(8,128)(2,1)S(1)}, bf16[320,512]{1,0:T(8,128)(2,1)S(1)}, f32[320,512]{1,0:T(8,128)S(1)}) custom-call(s32[1]{0:T(128)} %bitcast.1.core_ref, bf16[4,1024,128]{2,1,0:T(8,128)(2,1)S(1)} %all-to-all-done.2.pieces_ref, bf16[8,640,128]{2,1,0:T(8,128)(2,1)} %all-to-all-done.1.x_ref), custom_call_target="tpu_custom_call" | custom-call | flops 700000000 | bytes 5000000 | tf_op jit(solution)/shard_map/pallas_call | solution.py:335
  127.0 3.7 %shard_map.116 = bf16[8,1280,128]{2,1,0:T(8,128)(2,1)} custom-call(s32[1]{0:T(128)} %bitcast.f_ref, bf16[1024,512]{1,0:T(8,128)(2,1)S(1)} %get-tuple-element.34.kv_ref, bf16[32,80,128]{2,1,0:T(8,128)(2,1)S(1)} %constant_dynamic-update-slice_fusion.5.w_ref, bf16[4,1024,128]{2,1,0:T(8,128)(2,1)} %shard_map.114.own_ref, bf16[8,512,128]{2,1,0:T(8,128)(2,1)S(1)} %copy-done.4), custom_call_target="tpu_custom_call" | custom-call | flops 700000000 | bytes 4000000 | tf_op jit(solution)/shard_map/pallas_call | solution.py:346
  130.7 5.5 %all-to-all-start.3 = ((bf16[8,1280,128]{2,1,0:T(8,128)(2,1)}), bf16[8,1280,128]{2,1,0:T(8,128)(2,1)S(1)}, u32[]{:S(2)}, u32[]{:S(2)}) async-start(bf16[8,1280,128]{2,1,0:T(8,128)(2,1)} %shard_map.116), calls=%async_computation.3 | async-start | bytes 5242880 | tf_op jit(solution)/shard_map/all_to_all | solution.py:255
  136.2 2.0 %collective-permute-done.7.got_ref = bf16[320,512]{1,0:T(8,128)(2,1)} collective-permute-done((bf16[320,512]{1,0:T(8,128)(2,1)}, bf16[320,512]{1,0:T(8,128)(2,1)}, u32[]{:S(2)}, u32[]{:S(2)}) %collective-permute-start.7) | collective-permute-done | bytes 327712 | tf_op jit(solution)/shard_map/ppermute | solution.py:251
  140.6 2.9 %collective-permute-start.8 = (bf16[160,512]{1,0:T(8,128)(2,1)}, bf16[160,512]{1,0:T(8,128)(2,1)S(1)}, u32[]{:S(2)}, u32[]{:S(2)}) collective-permute-start(bf16[160,512]{1,0:T(8,128)(2,1)} %get-tuple-element.43), channel_id=1, source_target_pairs={{0,16},{16,0},{1,17},{17,1},{2,18},{18,2},{3,19},{19,3},{4,20},{20... | collective-permute-start | bytes 491528 | tf_op jit(solution)/shard_map/ppermute | solution.py:251
  143.5 27.2 %collective-permute-done.8.got_ref = bf16[160,512]{1,0:T(8,128)(2,1)S(1)} collective-permute-done((bf16[160,512]{1,0:T(8,128)(2,1)}, bf16[160,512]{1,0:T(8,128)(2,1)S(1)}, u32[]{:S(2)}, u32[]{:S(2)}) %collective-permute-start.8) | collective-permute-done | bytes 163872 | tf_op jit(solution)/shard_map/ppermute | solution.py:251
  172.1 4.4 %collective-permute-done.9.got_ref = bf16[80,512]{1,0:T(8,128)(2,1)S(1)} collective-permute-done((bf16[80,512]{1,0:T(8,128)(2,1)S(1)}, bf16[80,512]{1,0:T(8,128)(2,1)S(1)}, u32[]{:S(2)}, u32[]{:S(2)}) %collective-permute-start.9) | collective-permute-done | bytes 81952 | tf_op jit(solution)/shard_map/ppermute | solution.py:251
  176.6 5.6 %collective-permute-done.10.got_ref = f32[40,512]{1,0:T(8,128)S(1)} collective-permute-done((f32[40,512]{1,0:T(8,128)S(1)}, f32[40,512]{1,0:T(8,128)S(1)}, u32[]{:S(2)}, u32[]{:S(2)}) %collective-permute-start.10) | collective-permute-done | bytes 81952 | tf_op jit(solution)/shard_map/ppermute | solution.py:251
  182.3 1.8 collective-permute-start.11
  184.1 6.3 %collective-permute-done.11.got_ref = f32[20,512]{1,0:T(8,128)S(1)} collective-permute-done((f32[20,512]{1,0:T(8,128)S(1)}, f32[20,512]{1,0:T(8,128)S(1)}, u32[]{:S(2)}, u32[]{:S(2)}) %collective-permute-start.11) | collective-permute-done | bytes 40992 | tf_op jit(solution)/shard_map/ppermute | solution.py:251
  191.8 2.6 %collective-permute-done.12.got_ref = f32[10,512]{1,0:T(8,128)S(1)} collective-permute-done((f32[10,512]{1,0:T(8,128)S(1)}, f32[10,512]{1,0:T(8,128)S(1)}, u32[]{:S(2)}, u32[]{:S(2)}) %collective-permute-start.12) | collective-permute-done | bytes 20512 | tf_op jit(solution)/shard_map/ppermute | solution.py:372
  (67 shorter events, 23.1 us)
Async XLA Ops:
  0.6 11.8 %copy-start = (bf16[80,1024]{1,0:T(8,128)(2,1)S(1)}, bf16[80,1024]{1,0:T(8,128)(2,1)}, u32[]{:S(2)}) copy-start(bf16[80,1024]{1,0:T(8,128)(2,1)} %param.13) | copy-start | bytes 491524
  0.6 1.3 copy-start.1
  1.9 1.2 copy-start.2
  6.7 68.1 %all-to-all-start = ((bf16[8,128,1280]{2,1,0:T(8,128)(2,1)}), bf16[8,128,1280]{2,1,0:T(8,128)(2,1)S(1)}, u32[]{:S(2)}, u32[]{:S(2)}) async-start(bf16[8,128,1280]{2,1,0:T(8,128)(2,1)} %shard_map.111), calls=%async_computation | async-start | bytes 5242880 | tf_op jit(solution)/shard_map/all_to_all | solution.py:255
  12.5 0.7 collective-permute-start
  13.1 17.0 %collective-permute-start.1 = (bf16[1,80,128]{2,1,0:T(8,128)(2,1)S(1)}, bf16[1,80,128]{2,1,0:T(8,128)(2,1)S(1)}, u32[]{:S(2)}, u32[]{:S(2)}) collective-permute-start(bf16[1,80,128]{2,1,0:T(8,128)(2,1)S(1)} %bitcast.26), channel_id=1, source_target_pairs={{0,128},{32,160},{64,192},{96,224},{128,0},{160,32},{192,64},{224,... | collective-permute-start | bytes 61448 | tf_op jit(solution)/shard_map/ppermute | solution.py:251
  30.1 6.5 %collective-permute-start.2 = (bf16[2,80,128]{2,1,0:T(8,128)(2,1)S(1)}, bf16[2,80,128]{2,1,0:T(8,128)(2,1)S(1)}, u32[]{:S(2)}, u32[]{:S(2)}) collective-permute-start(bf16[2,80,128]{2,1,0:T(8,128)(2,1)S(1)} %pad_maximum_fusion.2), channel_id=1, source_target_pairs={{0,64},{32,96},{64,0},{96,32},{128,192},{160,224},{192,128},{224,1... | collective-permute-start | bytes 122888 | tf_op jit(solution)/shard_map/ppermute | solution.py:251
  36.6 4.5 %collective-permute-start.3 = (bf16[4,80,128]{2,1,0:T(8,128)(2,1)S(1)}, bf16[4,80,128]{2,1,0:T(8,128)(2,1)S(1)}, u32[]{:S(2)}, u32[]{:S(2)}) collective-permute-start(bf16[4,80,128]{2,1,0:T(8,128)(2,1)S(1)} %pad_maximum_fusion.1), channel_id=1, source_target_pairs={{0,32},{32,0},{64,96},{96,64},{128,160},{160,128},{192,224},{224,1... | collective-permute-start | bytes 245768 | tf_op jit(solution)/shard_map/ppermute | solution.py:251
  41.2 30.7 %collective-permute-start.4 = (bf16[8,80,128]{2,1,0:T(8,128)(2,1)S(1)}, bf16[8,80,128]{2,1,0:T(8,128)(2,1)S(1)}, u32[]{:S(2)}, u32[]{:S(2)}) collective-permute-start(bf16[8,80,128]{2,1,0:T(8,128)(2,1)S(1)} %pad_maximum_fusion), channel_id=1, source_target_pairs={{0,16},{16,0},{1,17},{17,1},{2,18},{18,2},{3,19},{19,3},{4,20},{20... | collective-permute-start | bytes 491528 | tf_op jit(solution)/shard_map/ppermute | solution.py:251
  72.0 2.7 %collective-permute-start.5 = (bf16[16,80,128]{2,1,0:T(8,128)(2,1)S(1)}, bf16[16,80,128]{2,1,0:T(8,128)(2,1)S(1)}, u32[]{:S(2)}, u32[]{:S(2)}) collective-permute-start(bf16[16,80,128]{2,1,0:T(8,128)(2,1)S(1)} %get-tuple-element.52), channel_id=1, source_target_pairs={{0,8},{8,0},{1,9},{9,1},{2,10},{10,2},{3,11},{11,3},{4,12},{12,4},... | collective-permute-start | bytes 983048 | tf_op jit(solution)/shard_map/ppermute | solution.py:251
  73.2 6.3 %copy-start.15 = (s32[1,32]{1,0:T(1,128)S(1)}, s32[1,32]{1,0:T(1,128)}, u32[]{:S(2)}) copy-start(s32[1,32]{1,0:T(1,128)} %param.14) | copy-start | bytes 388
  73.2 6.3 %copy-start.16 = (s32[32]{0:T(128)S(1)}, s32[32]{0:T(128)}, u32[]{:S(2)}) copy-start(s32[32]{0:T(128)} %order_ref.1) | copy-start | bytes 388
  74.8 27.3 %all-to-all-start.1 = ((bf16[8,640,128]{2,1,0:T(8,128)(2,1)}), bf16[8,640,128]{2,1,0:T(8,128)(2,1)}, u32[]{:S(2)}, u32[]{:S(2)}) async-start(bf16[8,640,128]{2,1,0:T(8,128)(2,1)} %shard_map.112), calls=%async_computation.1 | async-start | bytes 2621440 | tf_op jit(solution)/shard_map/all_to_all | solution.py:255
  90.2 11.9 %collective-permute-start.6 = (bf16[1024,128]{1,0:T(8,128)(2,1)S(1)}, bf16[1024,128]{1,0:T(8,128)(2,1)S(1)}, u32[]{:S(2)}, u32[]{:S(2)}) collective-permute-start(bf16[1024,128]{1,0:T(8,128)(2,1)S(1)} %get-tuple-element.30), channel_id=1, source_target_pairs={{0,4},{4,0},{1,5},{5,1},{2,6},{6,2},{3,7},{7,3},{8,12},{12,8},{9,1... | collective-permute-start | bytes 786440 | tf_op jit(solution)/shard_map/ppermute | solution.py:322
  104.2 22.7 %copy-start.4 = (bf16[8,512,128]{2,1,0:T(8,128)(2,1)S(1)}, bf16[8,512,128]{2,1,0:T(8,128)(2,1)}, u32[]{:S(2)}) copy-start(bf16[8,512,128]{2,1,0:T(8,128)(2,1)} %copy-done.3) | copy-start | bytes 3145732
  104.2 18.6 %all-to-all-start.2 = ((bf16[4,1024,128]{2,1,0:T(8,128)(2,1)}), bf16[4,1024,128]{2,1,0:T(8,128)(2,1)S(1)}, u32[]{:S(2)}, u32[]{:S(2)}) async-start(bf16[4,1024,128]{2,1,0:T(8,128)(2,1)} %shard_map.114.own_ref), calls=%async_computation.2 | async-start | bytes 2097152 | tf_op jit(solution)/shard_map/all_to_all | solution.py:255
  130.7 7.5 %copy-start.6 = (f32[320,512]{1,0:T(8,128)S(1)}, f32[320,512]{1,0:T(8,128)}, u32[]{:S(2)}) copy-start(f32[320,512]{1,0:T(8,128)} %copy-done.5) | copy-start | bytes 1966084
  130.7 64.3 %all-to-all-start.3 = ((bf16[8,1280,128]{2,1,0:T(8,128)(2,1)}), bf16[8,1280,128]{2,1,0:T(8,128)(2,1)S(1)}, u32[]{:S(2)}, u32[]{:S(2)}) async-start(bf16[8,1280,128]{2,1,0:T(8,128)(2,1)} %shard_map.116), calls=%async_computation.3 | async-start | bytes 5242880 | tf_op jit(solution)/shard_map/all_to_all | solution.py:255
  136.2 2.0 %collective-permute-start.7 = (bf16[320,512]{1,0:T(8,128)(2,1)}, bf16[320,512]{1,0:T(8,128)(2,1)}, u32[]{:S(2)}, u32[]{:S(2)}) collective-permute-start(bf16[320,512]{1,0:T(8,128)(2,1)} %copy-done.14), channel_id=1, source_target_pairs={{0,8},{8,0},{1,9},{9,1},{2,10},{10,2},{3,11},{11,3},{4,12},{12,4},... | collective-permute-start | bytes 983048 | tf_op jit(solution)/shard_map/ppermute | solution.py:251
  140.6 30.2 %collective-permute-start.8 = (bf16[160,512]{1,0:T(8,128)(2,1)}, bf16[160,512]{1,0:T(8,128)(2,1)S(1)}, u32[]{:S(2)}, u32[]{:S(2)}) collective-permute-start(bf16[160,512]{1,0:T(8,128)(2,1)} %get-tuple-element.43), channel_id=1, source_target_pairs={{0,16},{16,0},{1,17},{17,1},{2,18},{18,2},{3,19},{19,3},{4,20},{20... | collective-permute-start | bytes 491528 | tf_op jit(solution)/shard_map/ppermute | solution.py:251
  171.8 4.7 %collective-permute-start.9 = (bf16[80,512]{1,0:T(8,128)(2,1)S(1)}, bf16[80,512]{1,0:T(8,128)(2,1)S(1)}, u32[]{:S(2)}, u32[]{:S(2)}) collective-permute-start(bf16[80,512]{1,0:T(8,128)(2,1)S(1)} %get-tuple-element.45), channel_id=1, source_target_pairs={{0,32},{32,0},{64,96},{96,64},{128,160},{160,128},{192,224},{224,1... | collective-permute-start | bytes 245768 | tf_op jit(solution)/shard_map/ppermute | solution.py:251
  176.5 5.7 %collective-permute-start.10 = (f32[40,512]{1,0:T(8,128)S(1)}, f32[40,512]{1,0:T(8,128)S(1)}, u32[]{:S(2)}, u32[]{:S(2)}) collective-permute-start(f32[40,512]{1,0:T(8,128)S(1)} %get-tuple-element.47), channel_id=1, source_target_pairs={{0,64},{32,96},{64,0},{96,32},{128,192},{160,224},{192,128},{224,1... | collective-permute-start | bytes 245768 | tf_op jit(solution)/shard_map/ppermute | solution.py:251
  182.3 8.1 %collective-permute-start.11 = (f32[20,512]{1,0:T(8,128)S(1)}, f32[20,512]{1,0:T(8,128)S(1)}, u32[]{:S(2)}, u32[]{:S(2)}) collective-permute-start(f32[20,512]{1,0:T(8,128)S(1)} %get-tuple-element.49), channel_id=1, source_target_pairs={{0,128},{32,160},{64,192},{96,224},{128,0},{160,32},{192,64},{224,... | collective-permute-start | bytes 122888 | tf_op jit(solution)/shard_map/ppermute | solution.py:251
  190.4 4.0 %collective-permute-start.12 = (f32[10,512]{1,0:T(8,128)S(1)}, f32[10,512]{1,0:T(8,128)S(1)}, u32[]{:S(2)}, u32[]{:S(2)}) collective-permute-start(f32[10,512]{1,0:T(8,128)S(1)} %get-tuple-element.51), channel_id=1, source_target_pairs={{0,4},{4,0},{1,5},{5,1},{2,6},{6,2},{3,7},{7,3},{8,12},{12,8},{9,1... | collective-permute-start | bytes 61448 | tf_op jit(solution)/shard_map/ppermute | solution.py:372
  (10 other events, 9.0 us)

commit v3 on v2

v3 whole, which is shorter than its diff:
```python
import functools
import math

import jax
import jax.numpy as jnp
from jax import lax
from jax.experimental import pallas as pl
from jax.experimental.pallas import tpu as pltpu
from jax.sharding import PartitionSpec as P

HQ = 32
KEY_VALUE_HEADS = 4
HEAD_WIDTH = 128
BLK = 32
QUERY_PER_KEY = 8

CTX = 8
FSDP = 32
ROWS = 128
SLAB = 1024
FEATURES = 2560
FEAT_TILE = FEATURES // 4
Q_COLS = 512
PACK_COLS = 2 * Q_COLS + 2 * HEAD_WIDTH
HALF = 512
SCALE = 1.0 / math.sqrt(HEAD_WIDTH)
LOG2E = math.log2(math.e)
LOWEST = -1e30
NN = (((1,), (0,)), ((), ()))
NT = (((1,), (1,)), ((), ()))
VMEM = pl.BlockSpec(memory_space=pltpu.VMEM)
HBM = pl.BlockSpec(memory_space=pltpu.HBM)
SMEM = pl.BlockSpec(memory_space=pltpu.SMEM)


def dot(a, b, dims):
    return lax.dot_general(a, b, dims, preferred_element_type=jnp.float32)


def shape(dims, kind=jnp.bfloat16):
    return jax.ShapeDtypeStruct(dims, kind)


def params(mib):
    return pltpu.CompilerParams(vmem_limit_bytes=mib * 1024 * 1024)


def cost(flops, moved):
    return pl.CostEstimate(flops=flops, bytes_accessed=moved, transcendentals=0)


def q_block(device):
    return (device % 4) * 2 + device // 4


def pack_kernel(q_ref, d_ref, k_ref, v_ref, out_ref, sems):
    copies = []
    for dest in range(CTX):
        at = q_block(dest) * Q_COLS
        head = (dest % 4) * HEAD_WIDTH
        place = 0
        for ref, first, width in (
            (q_ref, at, Q_COLS),
            (d_ref, at, Q_COLS),
            (k_ref, head, HEAD_WIDTH),
            (v_ref, head, HEAD_WIDTH),
        ):
            copy = pltpu.make_async_copy(
                ref.at[:, first : first + width],
                out_ref.at[dest, :, place : place + width],
                sems.at[len(copies)],
            )
            copy.start()
            copies.append(copy)
            place += width
    for copy in copies:
        copy.wait()


def tile_row(z, low, y):
    row = (low % 2) * 320 + (z % 2) * 160 + (z // 2 % 2) * 80 + (z // 4) * 40
    return row + (low // 2) * 20 + y * 10


def turn_kernel(x_ref, out_ref, turned, tile):
    for j in range(FEATURES // 128):
        block = x_ref[:, j * 128 : (j + 1) * 128].T
        turned[j * 128 : (j + 1) * 128, :] = block.astype(jnp.float32)
    for x in range(4):
        for low in range(4):
            for y in range(2):
                for z in range(8):
                    source = (z * 4 + low) * 80 + y * 40 + x * 10
                    at = tile_row(z, low, y)
                    tile[at : at + 10, :] = turned[source : source + 10, :]
        out_ref[x] = tile[...].astype(jnp.bfloat16)


def attention_kernel(c_ref, docs_ref, order_ref, *refs):
    in_ref, dq_ref, keep_ref, send_ref = refs[:4]
    q_s, d_s, k_s, v_s, kt_s, dq_s, dkv_s, place, begin = refs[4:]
    c = c_ref[0]

    first = lax.fori_loop(
        0, 17, lambda i, a: jnp.where(docs_ref[i] == docs_ref[i + 15], i, a), jnp.int32(0)
    )

    def place_block(st, carry):
        b = order_ref[st]
        inside = (b >= first) & (b < first + 16)
        place[st] = jnp.where(inside, b - first, jnp.where(b < first, b + 16, b))
        return carry

    lax.fori_loop(0, 32, place_block, 0)

    def begin_block(t, carry):
        last_doc, last_begin = carry
        doc = docs_ref[jnp.where(t < first, t, t + 16)]
        now = jnp.where(doc == last_doc, last_begin, t)
        begin[t] = jnp.int32(0)
        begin[t + 16] = now * BLK
        return doc, now

    lax.fori_loop(0, 16, begin_block, (jnp.int32(-1), jnp.int32(0)))

    for st in range(32):
        rows = pl.ds(pl.multiple_of(place[st] * BLK, BLK), BLK)
        src, block = st // 4, slice((st % 4) * BLK, (st % 4 + 1) * BLK)
        q_s[rows, :] = in_ref[src, block, 0:Q_COLS]
        d_s[rows, :] = in_ref[src, block, Q_COLS : 2 * Q_COLS]
        k_s[rows, :] = in_ref[src, block, 2 * Q_COLS : 2 * Q_COLS + HEAD_WIDTH]
        v_s[rows, :] = in_ref[src, block, 2 * Q_COLS + HEAD_WIDTH :]
    for j in range(SLAB // 128):
        kt_s[:, j * 128 : (j + 1) * 128] = k_s[j * 128 : (j + 1) * 128, :].T
    dkv_s[...] = jnp.zeros_like(dkv_s)

    def half(hf, carry):
        base = pl.multiple_of(hf * HALF, HALF)
        for i in range(HALF // 128):
            n = (i + 1) * 128
            rows = pl.ds(pl.multiple_of(base + i * 128, 128), 128)
            keys = pl.ds(base, n)
            key_n = k_s[keys, :]
            value_n = v_s[keys, :]
            lane = lax.broadcasted_iota(jnp.int32, (n, 128), 1)
            row = lax.broadcasted_iota(jnp.int32, (n, 128), 0)
            low = jnp.zeros((n, 128), jnp.int32)
            for kk in range(4):
                low = jnp.where(lane // BLK == kk, begin[hf * 16 + i * 4 + kk], low)
            seen = (row >= low) & (row <= lane + i * 128)
            bias = jnp.where(seen, 0.0, LOWEST)
            bias = jnp.concatenate([bias, bias], axis=1)
            for g in range(2):
                cols = [slice((2 * g + e) * 128, (2 * g + e + 1) * 128) for e in range(2)]
                qs = jnp.concatenate([q_s[rows, e] for e in cols], axis=0)
                ds = jnp.concatenate([d_s[rows, e] for e in cols], axis=0)
                scores = dot(key_n, qs, NT) * (SCALE * LOG2E) + bias
                top = jnp.max(scores, axis=0, keepdims=True)
                probs = jnp.exp2(scores - top)
                total = jnp.sum(probs, axis=0, keepdims=True)
                probs = probs * (1.0 / total)
                products = dot(value_n, ds, NT)
                delta = jnp.sum(probs * products, axis=0, keepdims=True)
                score_grad = (probs * (products - delta)).astype(jnp.bfloat16)
                probs_low = probs.astype(jnp.bfloat16)
                dkv_s[keys, 0:128] += dot(score_grad, qs, NN)
                dkv_s[keys, 128:256] += dot(probs_low, ds, NN)
                dqt = dot(kt_s[:, keys], score_grad, NN) * SCALE
                for e in range(2):
                    dq_s[rows, cols[e]] = dqt[:, e * 128 : (e + 1) * 128].T.astype(jnp.bfloat16)
        return carry

    lax.fori_loop(0, 2, half, 0)

    y = c // 4
    for t in range(16):
        block = slice(t * BLK, (t + 1) * BLK)
        for half_y, ref in ((y, keep_ref), (1 - y, send_ref)):
            rows = pl.ds(pl.multiple_of(place[half_y * 16 + t] * BLK, BLK), BLK)
            ref[block, 0:128] = (dkv_s[rows, 0:128] * SCALE).astype(ref.dtype)
            ref[block, 128:256] = dkv_s[rows, 128:256].astype(ref.dtype)
    for st in range(32):
        rows = pl.ds(pl.multiple_of(place[st] * BLK, BLK), BLK)
        dq_ref[st // 4, (st % 4) * BLK : (st % 4 + 1) * BLK, :] = dq_s[rows, :]


def pair_kernel(keep_ref, taken_ref, out_ref):
    total = (keep_ref[...] + taken_ref[...].astype(jnp.float32)).astype(jnp.bfloat16)
    for dest in range(4):
        out_ref[dest] = total


def weight_kernel(at_ref, pieces_ref, x_ref, kv_ref, kv_rows_ref, send_ref, keep_ref, x_s):
    core, x = at_ref[0], at_ref[1]
    for src in range(4):
        kv_ref[:, src * 128 : (src + 1) * 128] = pieces_ref[src, :, 0:128]
        kv_ref[:, 512 + src * 128 : 512 + (src + 1) * 128] = pieces_ref[src, :, 128:256]
        x_s[:, src * 128 : (src + 1) * 128] = x_ref[src]
    part = FEAT_TILE // 2
    other = pl.ds(pl.multiple_of((1 - core) * part, part), part)
    own = pl.ds(pl.multiple_of(core * part, part), part)
    for j in range(4):
        cols = slice(j * 256, (j + 1) * 256)
        send_ref[:, cols] = dot(x_s[other, :], kv_ref[:, cols], NN).astype(jnp.bfloat16)
        keep_ref[:, cols] = dot(x_s[own, :], kv_ref[:, cols], NN)
    kv_rows_ref[...] = kv_ref[pl.ds(pl.multiple_of(x * ROWS, ROWS), ROWS), :]


def halve_kernel(bit_ref, keep_ref, got_ref, send_ref, kept_ref):
    part = kept_ref.shape[0]
    total = keep_ref[...] + got_ref[...].astype(jnp.float32)
    low, high, upper = total[:part, :], total[part:, :], bit_ref[0] == 1
    send_ref[...] = jnp.where(upper, low, high).astype(send_ref.dtype)
    kept_ref[...] = jnp.where(upper, high, low)


def input_kernel(f_ref, kv_ref, w_ref, out_ref, w_s):
    for at in range(FSDP):
        mask = sum(((at >> i) & 1) << bit for i, bit in enumerate(GATHER_BITS))
        source = f_ref[0] ^ mask
        rows = pl.ds(pl.multiple_of((source // 4) * 80, 80), 80)
        cols = pl.ds(pl.multiple_of(lax.rem(source, 4) * 256, 256), 256)
        w_s[rows, cols] = w_ref[at]
    for j in range(2):
        rows = slice(j * 256, (j + 1) * 256)
        tile = dot(w_s[...], kv_ref[rows, :], NT).astype(jnp.bfloat16)
        out_ref[2 * j] = tile[:, 0:128]
        out_ref[2 * j + 1] = tile[:, 128:256]


def input_out_kernel(parts_ref, out_ref):
    for x in range(4):
        for j in range(FEAT_TILE // 128):
            at = x * FEAT_TILE + j * 128
            out_ref[:, at : at + 128] = parts_ref[x, j * 128 : (j + 1) * 128, :].T


def query_out_kernel(dq_ref, out_ref):
    for src in range(CTX):
        at = q_block(src) * Q_COLS
        out_ref[:, at : at + Q_COLS] = dq_ref[src]


GATHER_BITS = (1, 4, 3, 2, 0)
BIT_AXES = (("core", 1), ("yh", 1), ("z", 1), ("z", 2), ("z", 4))


def swap(value, bit):
    axis, mask = BIT_AXES[bit]
    return lax.ppermute(value, axis, [(i, i ^ mask) for i in range(8 if axis == "z" else 2)])


def exchange(value, axis):
    return lax.all_to_all(value, axis, 0, 0, tiled=True)


def body(inputs, queries, keys, values, output_cotangent, key_value_weight, doc_ids, block_order):
    f = lax.axis_index(("z", "yh", "core")).astype(jnp.int32)
    y, x = lax.axis_index("y").astype(jnp.int32), lax.axis_index("x").astype(jnp.int32)
    c_at = (y * 4 + x).reshape(1)

    tile = lax.dynamic_slice(key_value_weight, (0, x * 256), (80, 256))
    perm = []
    for f1 in range(FSDP):
        for c1 in range(CTX):
            y1, x1 = c1 // 4, c1 % 4
            perm.append((f1 * CTX + c1, ((f1 % 8) * 4 + x1) * CTX + y1 * 4 + f1 // 8))
    tile = lax.ppermute(tile, ("z", "yh", "core", "y", "x"), perm)[None]

    def widen(tile, bit):
        return jnp.concatenate([tile, swap(tile, bit)], axis=0)

    tile = widen(tile, GATHER_BITS[0])

    packed = pl.pallas_call(
        pack_kernel,
        in_specs=[HBM] * 4,
        out_specs=HBM,
        out_shape=shape((CTX, ROWS, PACK_COLS)),
        scratch_shapes=[pltpu.SemaphoreType.DMA((4 * CTX,))],
        cost_estimate=cost(0, 5_000_000),
    )(queries[0], output_cotangent[0], keys[0], values[0])
    packed, tile = lax.optimization_barrier((packed, tile))
    got = exchange(packed, ("y", "x"))
    tile = widen(widen(tile, GATHER_BITS[1]), GATHER_BITS[2])

    turned = pl.pallas_call(
        turn_kernel,
        in_specs=[VMEM],
        out_specs=VMEM,
        out_shape=shape((4, FEAT_TILE, ROWS)),
        scratch_shapes=[
            pltpu.VMEM((FEATURES, ROWS), jnp.float32),
            pltpu.VMEM((FEAT_TILE, ROWS), jnp.float32),
        ],
        compiler_params=params(8),
        cost_estimate=cost(0, 1_300_000),
    )(inputs[0])

    got, turned, tile = lax.optimization_barrier((got, turned, tile))
    got_x = exchange(turned, "x")
    weight_tile = widen(widen(tile, GATHER_BITS[3]), GATHER_BITS[4])

    dq_parts, keep, send = pl.pallas_call(
        attention_kernel,
        in_specs=[SMEM] * 3 + [VMEM],
        out_specs=[VMEM] * 3,
        out_shape=[
            shape((CTX, ROWS, Q_COLS)),
            shape((SLAB // 2, 2 * HEAD_WIDTH), jnp.float32),
            shape((SLAB // 2, 2 * HEAD_WIDTH)),
        ],
        scratch_shapes=[
            pltpu.VMEM((SLAB, Q_COLS), jnp.bfloat16),
            pltpu.VMEM((SLAB, Q_COLS), jnp.bfloat16),
            pltpu.VMEM((SLAB, HEAD_WIDTH), jnp.bfloat16),
            pltpu.VMEM((SLAB, HEAD_WIDTH), jnp.bfloat16),
            pltpu.VMEM((HEAD_WIDTH, SLAB), jnp.bfloat16),
            pltpu.VMEM((SLAB, Q_COLS), jnp.bfloat16),
            pltpu.VMEM((SLAB, 2 * HEAD_WIDTH), jnp.float32),
            pltpu.SMEM((32,), jnp.int32),
            pltpu.SMEM((32,), jnp.int32),
        ],
        compiler_params=params(24),
        cost_estimate=cost(10_000_000_000, 5_000_000),
    )(c_at, doc_ids[0], block_order, got)

    taken = lax.ppermute(send, "y", [(0, 1), (1, 0)])
    taken, got_x, weight_tile = lax.optimization_barrier((taken, got_x, weight_tile))
    own_cols = pl.pallas_call(
        pair_kernel,
        in_specs=[VMEM] * 2,
        out_specs=VMEM,
        out_shape=shape((4, SLAB // 2, 2 * HEAD_WIDTH)),
        compiler_params=params(6),
        cost_estimate=cost(0, 2_000_000),
    )(keep, taken)
    pieces = exchange(own_cols, "x")
    pieces, dq_parts = lax.optimization_barrier((pieces, dq_parts))
    dq_got = exchange(dq_parts, ("y", "x"))

    kv_half, kv_rows, wg_send, wg_keep = pl.pallas_call(
        weight_kernel,
        in_specs=[SMEM] + [VMEM] * 2,
        out_specs=[VMEM] * 4,
        out_shape=[
            shape((SLAB // 2, 1024)),
            shape((ROWS, 1024)),
            shape((FEAT_TILE // 2, 1024)),
            shape((FEAT_TILE // 2, 1024), jnp.float32),
        ],
        scratch_shapes=[pltpu.VMEM((FEAT_TILE, SLAB // 2), jnp.bfloat16)],
        compiler_params=params(12),
        cost_estimate=cost(700_000_000, 6_000_000),
    )(jnp.stack([lax.rem(f, 2), x]), pieces, got_x)

    wg_got = swap(wg_send, 0)
    parts = pl.pallas_call(
        input_kernel,
        in_specs=[SMEM] + [VMEM] * 2,
        out_specs=VMEM,
        out_shape=shape((4, FEAT_TILE, ROWS)),
        scratch_shapes=[pltpu.VMEM((FEAT_TILE, 1024), jnp.bfloat16)],
        compiler_params=params(12),
        cost_estimate=cost(700_000_000, 4_000_000),
    )(f.reshape(1), kv_half, weight_tile)
    ig_got = exchange(parts, "x")

    def halve(bit, keep, got, kind):
        rows = keep.shape[0] // 2
        return pl.pallas_call(
            halve_kernel,
            in_specs=[SMEM] + [VMEM] * 2,
            out_specs=[VMEM] * 2,
            out_shape=[shape((rows, 1024), kind), shape((rows, 1024), jnp.float32)],
            compiler_params=params(6),
            cost_estimate=cost(0, rows * 1024 * 16),
        )(bit.reshape(1), keep, got)

    for bit, kind in ((2, jnp.bfloat16), (3, jnp.bfloat16), (4, jnp.bfloat16), (1, jnp.float32)):
        wg_send, wg_keep = halve((f >> bit) & 1, wg_keep, wg_got, kind)
        wg_got = swap(wg_send, bit)
    wg_send, wg_keep = halve(y, wg_keep, wg_got, jnp.float32)
    weight_grad = wg_keep + lax.ppermute(wg_send, "y", [(0, 1), (1, 0)])

    query_grad = pl.pallas_call(
        query_out_kernel,
        in_specs=[VMEM],
        out_specs=VMEM,
        out_shape=shape((ROWS, HQ * HEAD_WIDTH)),
        compiler_params=params(6),
        cost_estimate=cost(0, 2_000_000),
    )(dq_got)
    input_grad = pl.pallas_call(
        input_out_kernel,
        in_specs=[VMEM],
        out_specs=VMEM,
        out_shape=shape((ROWS, FEATURES)),
        compiler_params=params(6),
        cost_estimate=cost(0, 1_300_000),
    )(ig_got)
    return (input_grad[None], query_grad[None], kv_rows[None], weight_grad)


def solution(mesh):
    axes = ("z", "yh", "core", "y", "x")
    named = jax.sharding.Mesh(mesh.devices.reshape(8, 2, 2, 2, 4), axes)
    fsdp, ctx = axes[:3], axes[3:]
    return jax.shard_map(
        body,
        mesh=named,
        in_specs=(P(fsdp, ctx, None),) * 5 + (P(fsdp, None), P(fsdp, None), P()),
        out_specs=(P(fsdp, ctx, None),) * 3 + (P(axes, None),),
        check_vma=False,
    )
```

time: 198 us -> 253 us (1.28)
  Pallas kernels: 23.7 us -> 99.7 us
  waiting for transfers between devices: 86.6 us -> 71.4 us
  starting transfers between devices: 73.9 us -> 68.2 us
  local copies, waits for them, and re-layouts: 11.7 us -> 7.42 us
  other arithmetic: 0.03 us -> 3.82 us
    pallas_call x4, Pallas kernels: 7.87 us -> 84.8 us  [the longest x1 80.8 us: body(): pl.pallas_call(pack_kernel, in_specs=[HBM] * 4, out_specs=HBM, out_shape=...]
    ppermute x10, waiting for transfers between devices: 57.2 us -> 26.8 us  [swap(): lax.ppermute(value, axis, [(i, i ^ mask) for i in range(8 if axis == 'z'...]
    all_to_all x4 -> x5, waiting for transfers between devices: 15 us -> 36.4 us  [exchange(): return lax.all_to_all(value, axis, 0, 0, tiled=True)]
    ppermute x10, starting transfers between devices: 52.3 us -> 33.2 us  [swap(): lax.ppermute(value, axis, [(i, i ^ mask) for i in range(8 if axis == 'z'...]
    all_to_all x4 -> x5, starting transfers between devices: 19.5 us -> 32.7 us  [exchange(): return lax.all_to_all(value, axis, 0, 0, tiled=True)]
    ppermute x1, waiting for transfers between devices: 11.8 us -> 5.99 us  [body(): taken = lax.ppermute(send, 'y', [(0, 1), (1, 0)])]
    unnamed x38 -> x26, local copies, waits for them, and re-layouts: 11.6 us -> 7.41 us
    concatenate x3 -> x5, other arithmetic: 0.03 us -> 3.11 us  [widen(): return jnp.concatenate([tile, swap(tile, bit)], axis=0)]
  transfers between devices with their start and end apart: 17 -> 18, of which waited for: 12 -> 12; matrix products, arithmetic and copies ran while one was open for 0% -> 1% of each run, Pallas kernels for 7% -> 38%
where the time goes in v3:
time: 253 us; the launch traced here: 251 us
  Pallas kernels  99.7 us (39%)
  waiting for transfers between devices  71.4 us (28%)
  starting transfers between devices  68.2 us (27%)
  local copies, waits for them, and re-layouts  7.42 us (3%)
  other arithmetic  3.82 us (2%)
    pallas_call x1, Pallas kernels, body(): pl.pallas_call(pack_kernel, in_specs=[HBM] * 4, out_specs=HBM, out_shape=...  80.8 us
    all_to_all x5, waiting for transfers between devices, exchange(): return lax.all_to_all(value, axis, 0, 0, tiled=True)  36.4 us
    ppermute x10, starting transfers between devices, swap(): lax.ppermute(value, axis, [(i, i ^ mask) for i in range(8 if axis == 'z'...  33.2 us
    all_to_all x5, starting transfers between devices, exchange(): return lax.all_to_all(value, axis, 0, 0, tiled=True)  32.7 us
    ppermute x10, waiting for transfers between devices, swap(): lax.ppermute(value, axis, [(i, i ^ mask) for i in range(8 if axis == 'z'...  26.8 us
    pallas_call x1, Pallas kernels, body(): pl.pallas_call(attention_kernel, in_specs=[SMEM] * 3 + [VMEM], out_specs=...  8.84 us
    unnamed x26, local copies, waits for them, and re-layouts  7.41 us
    ppermute x1, waiting for transfers between devices, body(): taken = lax.ppermute(send, 'y', [(0, 1), (1, 0)])  5.99 us
  transfers between devices with their start and end apart: 18, of which 12 were waited for; matrix products, arithmetic and copies ran while one was open for 1% of the time, Pallas kernels for 38%

profile of v3, /device:TPU:8, one launch (start us, length us, event | category | flops | bytes accessed | tf_op | source)
XLA Modules:
  0.0 251.3 jit_solution(593894059425849329)
XLA Ops:
  2.2 11.4 %collective-permute-start.1 = (bf16[1,80,256]{2,1,0:T(8,128)(2,1)S(1)}, bf16[1,80,256]{2,1,0:T(8,128)(2,1)S(1)}, u32[]{:S(2)}, u32[]{:S(2)}) collective-permute-start(bf16[1,80,256]{2,1,0:T(8,128)(2,1)S(1)} %bitcast.27), channel_id=1, source_target_pairs={{0,16},{16,0},{1,17},{17,1},{2,18},{18,2},{3,19},{19,3},{4,20},{20... | collective-permute-start | bytes 122888 | tf_op jit(solution)/shard_map/ppermute | solution.py:250
  13.6 80.8 %shard_map.111 = bf16[8,128,1280]{2,1,0:T(8,128)(2,1)} custom-call(bf16[128,4096]{1,0:T(8,128)(2,1)} %bitcast.21, bf16[128,4096]{1,0:T(8,128)(2,1)} %bitcast.22, bf16[128,512]{1,0:T(8,128)(2,1)} %bitcast.25, bf16[128,512]{1,0:T(8,128)(2,1)} %bitcast.26), custom_call_target="tpu_custom_call" | custom-call | bytes 5000000 | tf_op jit(solution)/shard_map/pallas_call | solution.py:275
  94.5 8.5 %all-to-all-start = ((bf16[8,128,1280]{2,1,0:T(8,128)(2,1)}), bf16[8,128,1280]{2,1,0:T(8,128)(2,1)S(1)}, u32[]{:S(2)}, u32[]{:S(2)}) async-start(bf16[8,128,1280]{2,1,0:T(8,128)(2,1)} %shard_map.111), calls=%async_computation | async-start | bytes 5242880 | tf_op jit(solution)/shard_map/all_to_all | solution.py:254
  103.0 7.7 %collective-permute-start.2 = (bf16[2,80,256]{2,1,0:T(8,128)(2,1)S(1)}, bf16[2,80,256]{2,1,0:T(8,128)(2,1)S(1)}, u32[]{:S(2)}, u32[]{:S(2)}) collective-permute-start(bf16[2,80,256]{2,1,0:T(8,128)(2,1)S(1)} %pad_maximum_fusion.4), channel_id=1, source_target_pairs={{0,128},{32,160},{64,192},{96,224},{128,0},{160,32},{192,64},{224,... | collective-permute-start | bytes 245768 | tf_op jit(solution)/shard_map/ppermute | solution.py:250
  110.6 2.8 %collective-permute-done.2 = bf16[2,80,256]{2,1,0:T(8,128)(2,1)S(1)} collective-permute-done((bf16[2,80,256]{2,1,0:T(8,128)(2,1)S(1)}, bf16[2,80,256]{2,1,0:T(8,128)(2,1)S(1)}, u32[]{:S(2)}, u32[]{:S(2)}) %collective-permute-start.2) | collective-permute-done | bytes 81952 | tf_op jit(solution)/shard_map/ppermute | solution.py:250
  115.6 5.9 %collective-permute-done.3 = bf16[4,80,256]{2,1,0:T(8,128)(2,1)S(1)} collective-permute-done((bf16[4,80,256]{2,1,0:T(8,128)(2,1)S(1)}, bf16[4,80,256]{2,1,0:T(8,128)(2,1)S(1)}, u32[]{:S(2)}, u32[]{:S(2)}) %collective-permute-start.3) | collective-permute-done | bytes 163872 | tf_op jit(solution)/shard_map/ppermute | solution.py:250
  122.3 11.8 %all-to-all-done.refs_0_ = bf16[8,128,1280]{2,1,0:T(8,128)(2,1)S(1)} async-done(((bf16[8,128,1280]{2,1,0:T(8,128)(2,1)}), bf16[8,128,1280]{2,1,0:T(8,128)(2,1)S(1)}, u32[]{:S(2)}, u32[]{:S(2)}) %all-to-all-start) | async-done | bytes 2621472 | tf_op jit(solution)/shard_map/all_to_all | solution.py:254
  134.5 8.7 %all-to-all-start.1 = ((bf16[4,640,128]{2,1,0:T(8,128)(2,1)}), bf16[4,640,128]{2,1,0:T(8,128)(2,1)S(1)}, u32[]{:S(2)}, u32[]{:S(2)}) async-start(bf16[4,640,128]{2,1,0:T(8,128)(2,1)} %shard_map.112), calls=%async_computation.1 | async-start | bytes 1310720 | tf_op jit(solution)/shard_map/all_to_all | solution.py:254
  144.9 8.8 %shard_map.113 = (bf16[8,128,512]{2,1,0:T(8,128)(2,1)S(1)}, f32[512,256]{1,0:T(8,128)S(1)}, bf16[512,256]{1,0:T(8,128)(2,1)S(1)}) custom-call(s32[1]{0:T(128)} %bitcast.3.c_ref, s32[32]{0:T(128)S(1)} %bitcast.20, s32[32]{0:T(128)S(1)} %copy-done.12, bf16[8,128,1280]{2,1,0:T(8,128)(2,1)S(1)} %all-to-all-done.refs_0_), custom_call_target="tpu_custom_call" | custom-call | flops 10000000000 | bytes 5000000 | tf_op jit(solution)/shard_map/pallas_call | solution.py:304
  156.6 6.0 %collective-permute-done.4.taken_ref = bf16[512,256]{1,0:T(8,128)(2,1)S(1)} collective-permute-done((bf16[512,256]{1,0:T(8,128)(2,1)S(1)}, bf16[512,256]{1,0:T(8,128)(2,1)S(1)}, u32[]{:S(2)}, u32[]{:S(2)}) %collective-permute-start.4) | collective-permute-done | bytes 262176 | tf_op jit(solution)/shard_map/ppermute | solution.py:328
  164.9 7.9 %all-to-all-start.2 = ((bf16[4,512,256]{2,1,0:T(8,128)(2,1)}), bf16[4,512,256]{2,1,0:T(8,128)(2,1)S(1)}, u32[]{:S(2)}, u32[]{:S(2)}) async-start(bf16[4,512,256]{2,1,0:T(8,128)(2,1)} %shard_map.114), calls=%async_computation.2 | async-start | bytes 2097152 | tf_op jit(solution)/shard_map/all_to_all | solution.py:254
  172.9 14.9 %all-to-all-done.2.pieces_ref = bf16[4,512,256]{2,1,0:T(8,128)(2,1)S(1)} async-done(((bf16[4,512,256]{2,1,0:T(8,128)(2,1)}), bf16[4,512,256]{2,1,0:T(8,128)(2,1)S(1)}, u32[]{:S(2)}, u32[]{:S(2)}) %all-to-all-start.2) | async-done | bytes 1048608 | tf_op jit(solution)/shard_map/all_to_all | solution.py:254
  191.1 2.4 shard_map.115
  195.3 3.5 %all-to-all-start.3 = ((bf16[4,640,128]{2,1,0:T(8,128)(2,1)}), bf16[4,640,128]{2,1,0:T(8,128)(2,1)S(1)}, u32[]{:S(2)}, u32[]{:S(2)}) async-start(bf16[4,640,128]{2,1,0:T(8,128)(2,1)} %shard_map.116), calls=%async_computation.3 | async-start | bytes 1310720 | tf_op jit(solution)/shard_map/all_to_all | solution.py:254
  198.9 9.7 %all-to-all-done.3.parts_ref = bf16[4,640,128]{2,1,0:T(8,128)(2,1)S(1)} async-done(((bf16[4,640,128]{2,1,0:T(8,128)(2,1)}), bf16[4,640,128]{2,1,0:T(8,128)(2,1)S(1)}, u32[]{:S(2)}, u32[]{:S(2)}) %all-to-all-start.3) | async-done | bytes 655392 | tf_op jit(solution)/shard_map/all_to_all | solution.py:254
  208.6 4.0 %all-to-all-start.4 = ((bf16[8,128,512]{2,1,0:T(8,128)(2,1)}), bf16[8,128,512]{2,1,0:T(8,128)(2,1)S(1)}, u32[]{:S(2)}, u32[]{:S(2)}) async-start(bf16[8,128,512]{2,1,0:T(8,128)(2,1)} %copy-done.1), calls=%async_computation.4 | async-start | bytes 2097152 | tf_op jit(solution)/shard_map/all_to_all | solution.py:254
  215.0 6.8 %collective-permute-done.8.got_ref = bf16[160,1024]{1,0:T(8,128)(2,1)S(1)} collective-permute-done((bf16[160,1024]{1,0:T(8,128)(2,1)S(1)}, bf16[160,1024]{1,0:T(8,128)(2,1)S(1)}, u32[]{:S(2)}, u32[]{:S(2)}) %collective-permute-start.8) | collective-permute-done | bytes 327712 | tf_op jit(solution)/shard_map/ppermute | solution.py:250
  223.0 4.4 %collective-permute-start.9 = (bf16[80,1024]{1,0:T(8,128)(2,1)S(1)}, bf16[80,1024]{1,0:T(8,128)(2,1)S(1)}, u32[]{:S(2)}, u32[]{:S(2)}) collective-permute-start(bf16[80,1024]{1,0:T(8,128)(2,1)S(1)} %get-tuple-element.51), channel_id=1, source_target_pairs={{0,64},{32,96},{64,0},{96,32},{128,192},{160,224},{192,128},{224,1... | collective-permute-start | bytes 491528 | tf_op jit(solution)/shard_map/ppermute | solution.py:250
  227.4 4.0 %collective-permute-done.9.got_ref = bf16[80,1024]{1,0:T(8,128)(2,1)S(1)} collective-permute-done((bf16[80,1024]{1,0:T(8,128)(2,1)S(1)}, bf16[80,1024]{1,0:T(8,128)(2,1)S(1)}, u32[]{:S(2)}, u32[]{:S(2)}) %collective-permute-start.9) | collective-permute-done | bytes 163872 | tf_op jit(solution)/shard_map/ppermute | solution.py:250
  231.5 5.0 %collective-permute-start.10 = (bf16[40,1024]{1,0:T(8,128)(2,1)S(1)}, bf16[40,1024]{1,0:T(8,128)(2,1)S(1)}, u32[]{:S(2)}, u32[]{:S(2)}) collective-permute-start(bf16[40,1024]{1,0:T(8,128)(2,1)S(1)} %get-tuple-element.53), channel_id=1, source_target_pairs={{0,128},{32,160},{64,192},{96,224},{128,0},{160,32},{192,64},{224,... | collective-permute-start | bytes 245768 | tf_op jit(solution)/shard_map/ppermute | solution.py:250
  236.5 3.5 %collective-permute-done.10.got_ref = bf16[40,1024]{1,0:T(8,128)(2,1)S(1)} collective-permute-done((bf16[40,1024]{1,0:T(8,128)(2,1)S(1)}, bf16[40,1024]{1,0:T(8,128)(2,1)S(1)}, u32[]{:S(2)}, u32[]{:S(2)}) %collective-permute-start.10) | collective-permute-done | bytes 81952 | tf_op jit(solution)/shard_map/ppermute | solution.py:250
  240.1 2.8 %collective-permute-start.11 = (f32[20,1024]{1,0:T(8,128)S(1)}, f32[20,1024]{1,0:T(8,128)S(1)}, u32[]{:S(2)}, u32[]{:S(2)}) collective-permute-start(f32[20,1024]{1,0:T(8,128)S(1)} %get-tuple-element.55), channel_id=1, source_target_pairs={{0,16},{16,0},{1,17},{17,1},{2,18},{18,2},{3,19},{19,3},{4,20},{20... | collective-permute-start | bytes 245768 | tf_op jit(solution)/shard_map/ppermute | solution.py:250
  242.9 3.4 %collective-permute-done.11.got_ref = f32[20,1024]{1,0:T(8,128)S(1)} collective-permute-done((f32[20,1024]{1,0:T(8,128)S(1)}, f32[20,1024]{1,0:T(8,128)S(1)}, u32[]{:S(2)}, u32[]{:S(2)}) %collective-permute-start.11) | collective-permute-done | bytes 81952 | tf_op jit(solution)/shard_map/ppermute | solution.py:250
  248.5 2.1 collective-permute-done.12
  (59 shorter events, 23.5 us)
Async XLA Ops:
  1.6 0.7 collective-permute-start
  2.2 92.2 %collective-permute-start.1 = (bf16[1,80,256]{2,1,0:T(8,128)(2,1)S(1)}, bf16[1,80,256]{2,1,0:T(8,128)(2,1)S(1)}, u32[]{:S(2)}, u32[]{:S(2)}) collective-permute-start(bf16[1,80,256]{2,1,0:T(8,128)(2,1)S(1)} %bitcast.27), channel_id=1, source_target_pairs={{0,16},{16,0},{1,17},{17,1},{2,18},{18,2},{3,19},{19,3},{4,20},{20... | collective-permute-start | bytes 122888 | tf_op jit(solution)/shard_map/ppermute | solution.py:250
  94.5 19.9 %copy-start.4 = (bf16[1,128,2560]{2,1,0:T(8,128)(2,1)S(1)}, bf16[1,128,2560]{2,1,0:T(8,128)(2,1)}, u32[]{:S(2)}) copy-start(bf16[1,128,2560]{2,1,0:T(8,128)(2,1)} %param.8) | copy-start | bytes 1966084
  94.5 39.6 %all-to-all-start = ((bf16[8,128,1280]{2,1,0:T(8,128)(2,1)}), bf16[8,128,1280]{2,1,0:T(8,128)(2,1)S(1)}, u32[]{:S(2)}, u32[]{:S(2)}) async-start(bf16[8,128,1280]{2,1,0:T(8,128)(2,1)} %shard_map.111), calls=%async_computation | async-start | bytes 5242880 | tf_op jit(solution)/shard_map/all_to_all | solution.py:254
  103.0 10.5 %collective-permute-start.2 = (bf16[2,80,256]{2,1,0:T(8,128)(2,1)S(1)}, bf16[2,80,256]{2,1,0:T(8,128)(2,1)S(1)}, u32[]{:S(2)}, u32[]{:S(2)}) collective-permute-start(bf16[2,80,256]{2,1,0:T(8,128)(2,1)S(1)} %pad_maximum_fusion.4), channel_id=1, source_target_pairs={{0,128},{32,160},{64,192},{96,224},{128,0},{160,32},{192,64},{224,... | collective-permute-start | bytes 245768 | tf_op jit(solution)/shard_map/ppermute | solution.py:250
  113.5 8.1 %collective-permute-start.3 = (bf16[4,80,256]{2,1,0:T(8,128)(2,1)S(1)}, bf16[4,80,256]{2,1,0:T(8,128)(2,1)S(1)}, u32[]{:S(2)}, u32[]{:S(2)}) collective-permute-start(bf16[4,80,256]{2,1,0:T(8,128)(2,1)S(1)} %pad_maximum_fusion.3), channel_id=1, source_target_pairs={{0,64},{32,96},{64,0},{96,32},{128,192},{160,224},{192,128},{224,1... | collective-permute-start | bytes 491528 | tf_op jit(solution)/shard_map/ppermute | solution.py:250
  134.1 9.6 %collective-permute-start.5 = (bf16[8,80,256]{2,1,0:T(8,128)(2,1)}, bf16[8,80,256]{2,1,0:T(8,128)(2,1)}, u32[]{:S(2)}, u32[]{:S(2)}) collective-permute-start(bf16[8,80,256]{2,1,0:T(8,128)(2,1)} %pad_maximum_fusion.2), channel_id=1, source_target_pairs={{0,32},{32,0},{64,96},{96,64},{128,160},{160,128},{192,224},{224,1... | collective-permute-start | bytes 983048 | tf_op jit(solution)/shard_map/ppermute | solution.py:250
  134.5 10.4 %copy-start.11 = (s32[1,32]{1,0:T(1,128)S(1)}, s32[1,32]{1,0:T(1,128)}, u32[]{:S(2)}) copy-start(s32[1,32]{1,0:T(1,128)} %param.14) | copy-start | bytes 388
  134.5 10.5 %copy-start.12 = (s32[32]{0:T(128)S(1)}, s32[32]{0:T(128)}, u32[]{:S(2)}) copy-start(s32[32]{0:T(128)} %order_ref.1) | copy-start | bytes 388
  134.5 28.1 %all-to-all-start.1 = ((bf16[4,640,128]{2,1,0:T(8,128)(2,1)}), bf16[4,640,128]{2,1,0:T(8,128)(2,1)S(1)}, u32[]{:S(2)}, u32[]{:S(2)}) async-start(bf16[4,640,128]{2,1,0:T(8,128)(2,1)} %shard_map.112), calls=%async_computation.1 | async-start | bytes 1310720 | tf_op jit(solution)/shard_map/all_to_all | solution.py:254
  144.8 10.5 %collective-permute-start.6 = (bf16[16,80,256]{2,1,0:T(8,128)(2,1)S(1)}, bf16[16,80,256]{2,1,0:T(8,128)(2,1)S(1)}, u32[]{:S(2)}, u32[]{:S(2)}) collective-permute-start(bf16[16,80,256]{2,1,0:T(8,128)(2,1)S(1)} %pad_maximum_fusion.1), channel_id=1, source_target_pairs={{0,8},{8,0},{1,9},{9,1},{2,10},{10,2},{3,11},{11,3},{4,12},{12,4},... | collective-permute-start | bytes 1966088 | tf_op jit(solution)/shard_map/ppermute | solution.py:250
  153.8 2.8 %copy-start.1 = (bf16[8,128,512]{2,1,0:T(8,128)(2,1)}, bf16[8,128,512]{2,1,0:T(8,128)(2,1)S(1)}, u32[]{:S(2)}) copy-start(bf16[8,128,512]{2,1,0:T(8,128)(2,1)S(1)} %get-tuple-element.44) | copy-start | bytes 3145732
  153.8 2.8 %copy-start.9 = (f32[512,256]{1,0:T(8,128)}, f32[512,256]{1,0:T(8,128)S(1)}, u32[]{:S(2)}) copy-start(f32[512,256]{1,0:T(8,128)S(1)} %get-tuple-element.34.keep_ref) | copy-start | bytes 1572868
  153.8 8.8 %collective-permute-start.4 = (bf16[512,256]{1,0:T(8,128)(2,1)S(1)}, bf16[512,256]{1,0:T(8,128)(2,1)S(1)}, u32[]{:S(2)}, u32[]{:S(2)}) collective-permute-start(bf16[512,256]{1,0:T(8,128)(2,1)S(1)} %get-tuple-element.35), channel_id=1, source_target_pairs={{0,4},{4,0},{1,5},{5,1},{2,6},{6,2},{3,7},{7,3},{8,12},{12,8},{9,1... | collective-permute-start | bytes 786440 | tf_op jit(solution)/shard_map/ppermute | solution.py:328
  162.6 2.3 copy-start.5
  164.9 22.9 %all-to-all-start.2 = ((bf16[4,512,256]{2,1,0:T(8,128)(2,1)}), bf16[4,512,256]{2,1,0:T(8,128)(2,1)S(1)}, u32[]{:S(2)}, u32[]{:S(2)}) async-start(bf16[4,512,256]{2,1,0:T(8,128)(2,1)} %shard_map.114), calls=%async_computation.2 | async-start | bytes 2097152 | tf_op jit(solution)/shard_map/all_to_all | solution.py:254
  195.3 13.3 %all-to-all-start.3 = ((bf16[4,640,128]{2,1,0:T(8,128)(2,1)}), bf16[4,640,128]{2,1,0:T(8,128)(2,1)S(1)}, u32[]{:S(2)}, u32[]{:S(2)}) async-start(bf16[4,640,128]{2,1,0:T(8,128)(2,1)} %shard_map.116), calls=%async_computation.3 | async-start | bytes 1310720 | tf_op jit(solution)/shard_map/all_to_all | solution.py:254
  198.8 13.8 %collective-permute-start.7 = (bf16[320,1024]{1,0:T(8,128)(2,1)}, bf16[320,1024]{1,0:T(8,128)(2,1)}, u32[]{:S(2)}, u32[]{:S(2)}) collective-permute-start(bf16[320,1024]{1,0:T(8,128)(2,1)} %get-tuple-element.47), channel_id=1, source_target_pairs={{0,8},{8,0},{1,9},{9,1},{2,10},{10,2},{3,11},{11,3},{4,12},{12,4},... | collective-permute-start | bytes 1966088 | tf_op jit(solution)/shard_map/ppermute | solution.py:250
  208.6 38.9 %all-to-all-start.4 = ((bf16[8,128,512]{2,1,0:T(8,128)(2,1)}), bf16[8,128,512]{2,1,0:T(8,128)(2,1)S(1)}, u32[]{:S(2)}, u32[]{:S(2)}) async-start(bf16[8,128,512]{2,1,0:T(8,128)(2,1)} %copy-done.1), calls=%async_computation.4 | async-start | bytes 2097152 | tf_op jit(solution)/shard_map/all_to_all | solution.py:254
  214.7 7.1 %collective-permute-start.8 = (bf16[160,1024]{1,0:T(8,128)(2,1)S(1)}, bf16[160,1024]{1,0:T(8,128)(2,1)S(1)}, u32[]{:S(2)}, u32[]{:S(2)}) collective-permute-start(bf16[160,1024]{1,0:T(8,128)(2,1)S(1)} %get-tuple-element.49), channel_id=1, source_target_pairs={{0,32},{32,0},{64,96},{96,64},{128,160},{160,128},{192,224},{224,1... | collective-permute-start | bytes 983048 | tf_op jit(solution)/shard_map/ppermute | solution.py:250
  223.0 8.5 %collective-permute-start.9 = (bf16[80,1024]{1,0:T(8,128)(2,1)S(1)}, bf16[80,1024]{1,0:T(8,128)(2,1)S(1)}, u32[]{:S(2)}, u32[]{:S(2)}) collective-permute-start(bf16[80,1024]{1,0:T(8,128)(2,1)S(1)} %get-tuple-element.51), channel_id=1, source_target_pairs={{0,64},{32,96},{64,0},{96,32},{128,192},{160,224},{192,128},{224,1... | collective-permute-start | bytes 491528 | tf_op jit(solution)/shard_map/ppermute | solution.py:250
  231.5 8.5 %collective-permute-start.10 = (bf16[40,1024]{1,0:T(8,128)(2,1)S(1)}, bf16[40,1024]{1,0:T(8,128)(2,1)S(1)}, u32[]{:S(2)}, u32[]{:S(2)}) collective-permute-start(bf16[40,1024]{1,0:T(8,128)(2,1)S(1)} %get-tuple-element.53), channel_id=1, source_target_pairs={{0,128},{32,160},{64,192},{96,224},{128,0},{160,32},{192,64},{224,... | collective-permute-start | bytes 245768 | tf_op jit(solution)/shard_map/ppermute | solution.py:250
  240.1 6.2 %collective-permute-start.11 = (f32[20,1024]{1,0:T(8,128)S(1)}, f32[20,1024]{1,0:T(8,128)S(1)}, u32[]{:S(2)}, u32[]{:S(2)}) collective-permute-start(f32[20,1024]{1,0:T(8,128)S(1)} %get-tuple-element.55), channel_id=1, source_target_pairs={{0,16},{16,0},{1,17},{17,1},{2,18},{18,2},{3,19},{19,3},{4,20},{20... | collective-permute-start | bytes 245768 | tf_op jit(solution)/shard_map/ppermute | solution.py:250
  246.3 4.4 %collective-permute-start.12 = (f32[10,1024]{1,0:T(8,128)S(1)}, f32[10,1024]{1,0:T(8,128)S(1)}, u32[]{:S(2)}, u32[]{:S(2)}) collective-permute-start(f32[10,1024]{1,0:T(8,128)S(1)} %get-tuple-element.57), channel_id=1, source_target_pairs={{0,4},{4,0},{1,5},{5,1},{2,6},{6,2},{3,7},{7,3},{8,12},{12,8},{9,1... | collective-permute-start | bytes 122888 | tf_op jit(solution)/shard_map/ppermute | solution.py:384
  (7 other events, 7.4 us)

commit v4 on v3

--- a/solution.py
+++ b/solution.py
@@ -82,9 +82,10 @@
     return row + (low // 2) * 20 + y * 10
 
 
-def turn_kernel(x_ref, out_ref, turned, tile):
+def turn_kernel(x_ref, in_ref, *refs):
+    outs, turned, tile = refs[:4], refs[4], refs[5]
     for j in range(FEATURES // 128):
-        block = x_ref[:, j * 128 : (j + 1) * 128].T
+        block = in_ref[:, j * 128 : (j + 1) * 128].T
         turned[j * 128 : (j + 1) * 128, :] = block.astype(jnp.float32)
     for x in range(4):
         for low in range(4):
@@ -92,8 +93,9 @@
                 for z in range(8):
                     source = (z * 4 + low) * 80 + y * 40 + x * 10
                     at = tile_row(z, low, y)
-                    tile[at : at + 10, :] = turned[source : source + 10, :]
-        out_ref[x] = tile[...].astype(jnp.bfloat16)
+                    tile[x, at : at + 10, :] = turned[source : source + 10, :]
+    for s in range(4):
+        outs[s][...] = tile[lax.rem(x_ref[0] + s, 4)].astype(jnp.bfloat16)
 
 
 def attention_kernel(c_ref, docs_ref, order_ref, *refs):
@@ -185,17 +187,18 @@
 
 
 def pair_kernel(keep_ref, taken_ref, out_ref):
-    total = (keep_ref[...] + taken_ref[...].astype(jnp.float32)).astype(jnp.bfloat16)
-    for dest in range(4):
-        out_ref[dest] = total
-
-
-def weight_kernel(at_ref, pieces_ref, x_ref, kv_ref, kv_rows_ref, send_ref, keep_ref, x_s):
+    out_ref[...] = (keep_ref[...] + taken_ref[...].astype(jnp.float32)).astype(jnp.bfloat16)
+
+
+def weight_kernel(at_ref, *refs):
+    pieces, ins = refs[:4], refs[4:8]
+    kv_ref, kv_rows_ref, send_ref, keep_ref, x_s = refs[8:]
     core, x = at_ref[0], at_ref[1]
-    for src in range(4):
-        kv_ref[:, src * 128 : (src + 1) * 128] = pieces_ref[src, :, 0:128]
-        kv_ref[:, 512 + src * 128 : 512 + (src + 1) * 128] = pieces_ref[src, :, 128:256]
-        x_s[:, src * 128 : (src + 1) * 128] = x_ref[src]
+    for s in range(4):
+        at = pl.multiple_of(lax.rem(x + 4 - s, 4) * 128, 128)
+        kv_ref[:, pl.ds(at, 128)] = pieces[s][:, 0:128]
+        kv_ref[:, pl.ds(pl.multiple_of(512 + at, 128), 128)] = pieces[s][:, 128:256]
+        x_s[:, pl.ds(at, 128)] = ins[s][...]
     part = FEAT_TILE // 2
     other = pl.ds(pl.multiple_of((1 - core) * part, part), part)
     own = pl.ds(pl.multiple_of(core * part, part), part)
@@ -214,13 +217,13 @@
     kept_ref[...] = jnp.where(upper, high, low)
 
 
-def input_kernel(f_ref, kv_ref, w_ref, out_ref, w_s):
+def input_kernel(f_ref, kv_ref, w_ref, far_ref, out_ref, w_s):
     for at in range(FSDP):
         mask = sum(((at >> i) & 1) << bit for i, bit in enumerate(GATHER_BITS))
         source = f_ref[0] ^ mask
         rows = pl.ds(pl.multiple_of((source // 4) * 80, 80), 80)
         cols = pl.ds(pl.multiple_of(lax.rem(source, 4) * 256, 256), 256)
-        w_s[rows, cols] = w_ref[at]
+        w_s[rows, cols] = w_ref[at] if at < FSDP // 2 else far_ref[at - FSDP // 2]
     for j in range(2):
         rows = slice(j * 256, (j + 1) * 256)
         tile = dot(w_s[...], kv_ref[rows, :], NT).astype(jnp.bfloat16)
@@ -241,13 +244,17 @@
         out_ref[:, at : at + Q_COLS] = dq_ref[src]
 
 
-GATHER_BITS = (1, 4, 3, 2, 0)
+GATHER_BITS = (4, 3, 2, 0, 1)
 BIT_AXES = (("core", 1), ("yh", 1), ("z", 1), ("z", 2), ("z", 4))
 
 
 def swap(value, bit):
     axis, mask = BIT_AXES[bit]
     return lax.ppermute(value, axis, [(i, i ^ mask) for i in range(8 if axis == "z" else 2)])
+
+
+def to_shift(value, s):
+    return lax.ppermute(value, "x", [(i, (i + s) % 4) for i in range(4)]) if s else value
 
 
 def exchange(value, axis):
@@ -270,36 +277,35 @@
     def widen(tile, bit):
         return jnp.concatenate([tile, swap(tile, bit)], axis=0)
 
-    tile = widen(tile, GATHER_BITS[0])
-
     packed = pl.pallas_call(
         pack_kernel,
         in_specs=[HBM] * 4,
-        out_specs=HBM,
+        out_specs=VMEM,
         out_shape=shape((CTX, ROWS, PACK_COLS)),
         scratch_shapes=[pltpu.SemaphoreType.DMA((4 * CTX,))],
+        compiler_params=params(6),
         cost_estimate=cost(0, 5_000_000),
     )(queries[0], output_cotangent[0], keys[0], values[0])
     packed, tile = lax.optimization_barrier((packed, tile))
     got = exchange(packed, ("y", "x"))
-    tile = widen(widen(tile, GATHER_BITS[1]), GATHER_BITS[2])
+    for bit in GATHER_BITS[:4]:
+        tile = widen(tile, bit)
 
     turned = pl.pallas_call(
         turn_kernel,
-        in_specs=[VMEM],
-        out_specs=VMEM,
-        out_shape=shape((4, FEAT_TILE, ROWS)),
+        in_specs=[SMEM, VMEM],
+        out_specs=[VMEM] * 4,
+        out_shape=[shape((FEAT_TILE, ROWS))] * 4,
         scratch_shapes=[
             pltpu.VMEM((FEATURES, ROWS), jnp.float32),
-            pltpu.VMEM((FEAT_TILE, ROWS), jnp.float32),
+            pltpu.VMEM((4, FEAT_TILE, ROWS), jnp.float32),
         ],
         compiler_params=params(8),
         cost_estimate=cost(0, 1_300_000),
-    )(inputs[0])
+    )(x.reshape(1), inputs[0])
 
     got, turned, tile = lax.optimization_barrier((got, turned, tile))
-    got_x = exchange(turned, "x")
-    weight_tile = widen(widen(tile, GATHER_BITS[3]), GATHER_BITS[4])
+    got_x = [to_shift(turned[s], s) for s in range(4)]
 
     dq_parts, keep, send = pl.pallas_call(
         attention_kernel,
@@ -326,22 +332,22 @@
     )(c_at, doc_ids[0], block_order, got)
 
     taken = lax.ppermute(send, "y", [(0, 1), (1, 0)])
-    taken, got_x, weight_tile = lax.optimization_barrier((taken, got_x, weight_tile))
+    taken, got_x, tile = lax.optimization_barrier((taken, got_x, tile))
+    far_tile = swap(tile, GATHER_BITS[4])
     own_cols = pl.pallas_call(
         pair_kernel,
         in_specs=[VMEM] * 2,
         out_specs=VMEM,
-        out_shape=shape((4, SLAB // 2, 2 * HEAD_WIDTH)),
+        out_shape=shape((SLAB // 2, 2 * HEAD_WIDTH)),
         compiler_params=params(6),
         cost_estimate=cost(0, 2_000_000),
     )(keep, taken)
-    pieces = exchange(own_cols, "x")
-    pieces, dq_parts = lax.optimization_barrier((pieces, dq_parts))
-    dq_got = exchange(dq_parts, ("y", "x"))
+    pieces = [to_shift(own_cols, s) for s in range(4)]
+    pieces, far_tile = lax.optimization_barrier((pieces, far_tile))
 
     kv_half, kv_rows, wg_send, wg_keep = pl.pallas_call(
         weight_kernel,
-        in_specs=[SMEM] + [VMEM] * 2,
+        in_specs=[SMEM] + [VMEM] * 8,
         out_specs=[VMEM] * 4,
         out_shape=[
             shape((SLAB // 2, 1024)),
@@ -352,19 +358,20 @@
         scratch_shapes=[pltpu.VMEM((FEAT_TILE, SLAB // 2), jnp.bfloat16)],
         compiler_params=params(12),
         cost_estimate=cost(700_000_000, 6_000_000),
-    )(jnp.stack([lax.rem(f, 2), x]), pieces, got_x)
+    )(jnp.stack([lax.rem(f, 2), x]), *pieces, *got_x)
 
     wg_got = swap(wg_send, 0)
     parts = pl.pallas_call(
         input_kernel,
-        in_specs=[SMEM] + [VMEM] * 2,
+        in_specs=[SMEM] + [VMEM] * 3,
         out_specs=VMEM,
         out_shape=shape((4, FEAT_TILE, ROWS)),
         scratch_shapes=[pltpu.VMEM((FEAT_TILE, 1024), jnp.bfloat16)],
         compiler_params=params(12),
         cost_estimate=cost(700_000_000, 4_000_000),
-    )(f.reshape(1), kv_half, weight_tile)
-    ig_got = exchange(parts, "x")
+    )(f.reshape(1), kv_half, tile, far_tile)
+    parts, dq_parts = lax.optimization_barrier((parts, dq_parts))
+    dq_got = exchange(dq_parts, ("y", "x"))
 
     def halve(bit, keep, got, kind):
         rows = keep.shape[0] // 2
@@ -380,6 +387,9 @@
     for bit, kind in ((2, jnp.bfloat16), (3, jnp.bfloat16), (4, jnp.bfloat16), (1, jnp.float32)):
         wg_send, wg_keep = halve((f >> bit) & 1, wg_keep, wg_got, kind)
         wg_got = swap(wg_send, bit)
+        if bit == 3:
+            wg_got, parts = lax.optimization_barrier((wg_got, parts))
+            ig_got = exchange(parts, "x")
     wg_send, wg_keep = halve(y, wg_keep, wg_got, jnp.float32)
     weight_grad = wg_keep + lax.ppermute(wg_send, "y", [(0, 1), (1, 0)])
 

time: 253 us -> 165 us (0.65)
  Pallas kernels: 99.7 us -> 19.7 us
  local copies, waits for them, and re-layouts: 7.42 us -> 20.3 us
  waiting for transfers between devices: 71.4 us -> 58.9 us
  starting transfers between devices: 68.2 us -> 60.8 us
    pallas_call x4, Pallas kernels: 86.3 us -> 7.23 us  [the longest x1 2.53 us: body(): pl.pallas_call(weight_kernel, in_specs=[SMEM] + [VMEM] * 8, out_specs=[VM...]
    all_to_all x5 -> x3, waiting for transfers between devices: 36.4 us -> 3.38 us  [exchange(): return lax.all_to_all(value, axis, 0, 0, tiled=True)]
    ppermute x0 -> x6, waiting for transfers between devices: none -> 16.5 us  [to_shift(): lax.ppermute(value, 'x', [(i, (i + s) % 4) for i in range(4)])]
    unnamed x26 -> x62, local copies, waits for them, and re-layouts: 7.41 us -> 20.3 us
    all_to_all x5 -> x3, starting transfers between devices: 32.7 us -> 20.9 us  [exchange(): return lax.all_to_all(value, axis, 0, 0, tiled=True)]
    ppermute x0 -> x6, starting transfers between devices: none -> 11.1 us  [to_shift(): lax.ppermute(value, 'x', [(i, (i + s) % 4) for i in range(4)])]
    ppermute x10, waiting for transfers between devices: 26.8 us -> 36 us  [swap(): lax.ppermute(value, axis, [(i, i ^ mask) for i in range(8 if axis == 'z'...]
    ppermute x10, starting transfers between devices: 33.2 us -> 26.4 us  [swap(): lax.ppermute(value, axis, [(i, i ^ mask) for i in range(8 if axis == 'z'...]
  transfers between devices with their start and end apart: 18 -> 22, of which waited for: 12 -> 12; matrix products, arithmetic and copies ran while one was open for 1% -> 3% of each run, Pallas kernels for 38% -> 4%
where the time goes in v4:
time: 165 us; the launch traced here: 164 us
  starting transfers between devices  60.8 us (37%)
  waiting for transfers between devices  58.9 us (36%)
  local copies, waits for them, and re-layouts  20.3 us (12%)
  Pallas kernels  19.7 us (12%)
  other arithmetic  3.16 us (2%)
    ppermute x10, waiting for transfers between devices, swap(): lax.ppermute(value, axis, [(i, i ^ mask) for i in range(8 if axis == 'z'...  36 us
    ppermute x10, starting transfers between devices, swap(): lax.ppermute(value, axis, [(i, i ^ mask) for i in range(8 if axis == 'z'...  26.4 us
    all_to_all x3, starting transfers between devices, exchange(): return lax.all_to_all(value, axis, 0, 0, tiled=True)  20.9 us
    unnamed x62, local copies, waits for them, and re-layouts  20.3 us
    ppermute x6, waiting for transfers between devices, to_shift(): lax.ppermute(value, 'x', [(i, (i + s) % 4) for i in range(4)])  16.5 us
    ppermute x6, starting transfers between devices, to_shift(): lax.ppermute(value, 'x', [(i, (i + s) % 4) for i in range(4)])  11.1 us
    pallas_call x1, Pallas kernels, body(): pl.pallas_call(attention_kernel, in_specs=[SMEM] * 3 + [VMEM], out_specs=...  8.84 us
    all_to_all x3, waiting for transfers between devices, exchange(): return lax.all_to_all(value, axis, 0, 0, tiled=True)  3.38 us
  transfers between devices with their start and end apart: 22, of which 12 were waited for; matrix products, arithmetic and copies ran while one was open for 3% of the time, Pallas kernels for 4%

profile of v4, /device:TPU:8, one launch (start us, length us, event | category | flops | bytes accessed | tf_op | source)
XLA Modules:
  0.0 163.7 jit_solution(1209568081258877925)
XLA Ops:
  6.5 2.2 %shard_map.111 = bf16[8,128,1280]{2,1,0:T(8,128)(2,1)} custom-call(bf16[128,4096]{1,0:T(8,128)(2,1)S(1)} %bitcast.19, bf16[128,4096]{1,0:T(8,128)(2,1)S(1)} %bitcast.20, bf16[128,512]{1,0:T(8,128)(2,1)S(1)} %bitcast.22, bf16[128,512]{1,0:T(8,128)(2,1)S(1)} %bitcast.23), custom_call_target="tpu_custom_call" | custom-call | bytes 5000000 | tf_op jit(solution)/shard_map/pallas_call | solution.py:280
  8.7 10.9 %all-to-all-start = ((bf16[8,128,1280]{2,1,0:T(8,128)(2,1)}), bf16[8,128,1280]{2,1,0:T(8,128)(2,1)S(1)}, u32[]{:S(2)}, u32[]{:S(2)}) async-start(bf16[8,128,1280]{2,1,0:T(8,128)(2,1)} %shard_map.111), calls=%async_computation | async-start | bytes 5242880 | tf_op jit(solution)/shard_map/all_to_all | solution.py:261
  19.7 4.8 %collective-permute-start.1 = (bf16[1,80,256]{2,1,0:T(8,128)(2,1)S(1)}, bf16[1,80,256]{2,1,0:T(8,128)(2,1)S(1)}, u32[]{:S(2)}, u32[]{:S(2)}) collective-permute-start(bf16[1,80,256]{2,1,0:T(8,128)(2,1)S(1)} %bitcast.26), channel_id=1, source_target_pairs={{0,128},{32,160},{64,192},{96,224},{128,0},{160,32},{192,64},{224,... | collective-permute-start | bytes 122888 | tf_op jit(solution)/shard_map/ppermute | solution.py:253
  24.4 3.2 %collective-permute-done.1 = bf16[1,80,256]{2,1,0:T(8,128)(2,1)S(1)} collective-permute-done((bf16[1,80,256]{2,1,0:T(8,128)(2,1)S(1)}, bf16[1,80,256]{2,1,0:T(8,128)(2,1)S(1)}, u32[]{:S(2)}, u32[]{:S(2)}) %collective-permute-start.1) | collective-permute-done | bytes 40992 | tf_op jit(solution)/shard_map/ppermute | solution.py:253
  27.6 5.3 %collective-permute-start.2 = (bf16[2,80,256]{2,1,0:T(8,128)(2,1)S(1)}, bf16[2,80,256]{2,1,0:T(8,128)(2,1)S(1)}, u32[]{:S(2)}, u32[]{:S(2)}) collective-permute-start(bf16[2,80,256]{2,1,0:T(8,128)(2,1)S(1)} %pad_maximum_fusion.2), channel_id=1, source_target_pairs={{0,64},{32,96},{64,0},{96,32},{128,192},{160,224},{192,128},{224,1... | collective-permute-start | bytes 245768 | tf_op jit(solution)/shard_map/ppermute | solution.py:253
  32.9 3.3 %collective-permute-done.2 = bf16[2,80,256]{2,1,0:T(8,128)(2,1)S(1)} collective-permute-done((bf16[2,80,256]{2,1,0:T(8,128)(2,1)S(1)}, bf16[2,80,256]{2,1,0:T(8,128)(2,1)S(1)}, u32[]{:S(2)}, u32[]{:S(2)}) %collective-permute-start.2) | collective-permute-done | bytes 81952 | tf_op jit(solution)/shard_map/ppermute | solution.py:253
  37.7 2.9 %collective-permute-start.3 = (bf16[4,80,256]{2,1,0:T(8,128)(2,1)}, bf16[4,80,256]{2,1,0:T(8,128)(2,1)}, u32[]{:S(2)}, u32[]{:S(2)}) collective-permute-start(bf16[4,80,256]{2,1,0:T(8,128)(2,1)} %pad_maximum_fusion.1), channel_id=1, source_target_pairs={{0,32},{32,0},{64,96},{96,64},{128,160},{160,128},{192,224},{224,1... | collective-permute-start | bytes 491528 | tf_op jit(solution)/shard_map/ppermute | solution.py:253
  47.5 3.4 %all-to-all-done.refs_0_ = bf16[8,128,1280]{2,1,0:T(8,128)(2,1)S(1)} async-done(((bf16[8,128,1280]{2,1,0:T(8,128)(2,1)}), bf16[8,128,1280]{2,1,0:T(8,128)(2,1)S(1)}, u32[]{:S(2)}, u32[]{:S(2)}) %all-to-all-start) | async-done | bytes 2621472 | tf_op jit(solution)/shard_map/all_to_all | solution.py:261
  50.9 8.8 %shard_map.113 = (bf16[8,128,512]{2,1,0:T(8,128)(2,1)S(1)}, f32[512,256]{1,0:T(8,128)S(1)}, bf16[512,256]{1,0:T(8,128)(2,1)S(1)}) custom-call(s32[1]{0:T(128)} %bitcast.4.c_ref, s32[32]{0:T(128)S(1)} %bitcast.24, s32[32]{0:T(128)S(1)} %copy-done.26, bf16[8,128,1280]{2,1,0:T(8,128)(2,1)S(1)} %all-to-all-done.refs_0_), custom_call_target="tpu_custom_call" | custom-call | flops 10000000000 | bytes 5000000 | tf_op jit(solution)/shard_map/pallas_call | solution.py:310
  62.2 4.1 %collective-permute-start.6 = (bf16[640,128]{1,0:T(8,128)(2,1)S(1)}, bf16[640,128]{1,0:T(8,128)(2,1)S(1)}, u32[]{:S(2)}, u32[]{:S(2)}) collective-permute-start(bf16[640,128]{1,0:T(8,128)(2,1)S(1)} %copy-done.24), channel_id=1, source_target_pairs={{0,1},{1,2},{2,3},{3,0},{4,5},{5,6},{6,7},{7,4},{8,9},{9,10},{10,1... | collective-permute-start | bytes 491528 | tf_op jit(solution)/shard_map/ppermute | solution.py:257
  66.3 4.5 %collective-permute-start.7 = (bf16[640,128]{1,0:T(8,128)(2,1)S(1)}, bf16[640,128]{1,0:T(8,128)(2,1)S(1)}, u32[]{:S(2)}, u32[]{:S(2)}) collective-permute-start(bf16[640,128]{1,0:T(8,128)(2,1)S(1)} %copy-done.22), channel_id=1, source_target_pairs={{0,2},{1,3},{2,0},{3,1},{4,6},{5,7},{6,4},{7,5},{8,10},{9,11},{10,... | collective-permute-start | bytes 491528 | tf_op jit(solution)/shard_map/ppermute | solution.py:257
  70.9 3.6 %collective-permute-done.6.refs_5_ = bf16[640,128]{1,0:T(8,128)(2,1)S(1)} collective-permute-done((bf16[640,128]{1,0:T(8,128)(2,1)S(1)}, bf16[640,128]{1,0:T(8,128)(2,1)S(1)}, u32[]{:S(2)}, u32[]{:S(2)}) %collective-permute-start.6) | collective-permute-done | bytes 163872 | tf_op jit(solution)/shard_map/ppermute | solution.py:257
  78.2 6.2 %collective-permute-start.12 = (bf16[16,80,256]{2,1,0:T(8,128)(2,1)S(1)}, bf16[16,80,256]{2,1,0:T(8,128)(2,1)S(1)}, u32[]{:S(2)}, u32[]{:S(2)}) collective-permute-start(bf16[16,80,256]{2,1,0:T(8,128)(2,1)S(1)} %constant_dynamic-update-slice_fusion.w_ref), channel_id=1, source_target_pairs={{0,16},{16,0},{1,17},{17,1},{2,18},{18,2},{3,19},{19,3},{4,20},{20... | collective-permute-start | bytes 1966088 | tf_op jit(solution)/shard_map/ppermute | solution.py:253
  86.9 8.2 %collective-permute-done.10.refs_2_ = bf16[512,256]{1,0:T(8,128)(2,1)S(1)} collective-permute-done((bf16[512,256]{1,0:T(8,128)(2,1)S(1)}, bf16[512,256]{1,0:T(8,128)(2,1)S(1)}, u32[]{:S(2)}, u32[]{:S(2)}) %collective-permute-start.10) | collective-permute-done | bytes 262176 | tf_op jit(solution)/shard_map/ppermute | solution.py:257
  95.2 2.9 %collective-permute-done.11.refs_3_ = bf16[512,256]{1,0:T(8,128)(2,1)S(1)} collective-permute-done((bf16[512,256]{1,0:T(8,128)(2,1)S(1)}, bf16[512,256]{1,0:T(8,128)(2,1)S(1)}, u32[]{:S(2)}, u32[]{:S(2)}) %collective-permute-start.11) | collective-permute-done | bytes 262176 | tf_op jit(solution)/shard_map/ppermute | solution.py:257
  105.1 2.5 %shard_map.115 = (bf16[512,1024]{1,0:T(8,128)(2,1)S(1)}, bf16[128,1024]{1,0:T(8,128)(2,1)}, bf16[320,1024]{1,0:T(8,128)(2,1)}, f32[320,1024]{1,0:T(8,128)S(1)}) custom-call(s32[2]{0:T(128)S(1)} %pad_add_fusion.at_ref, bf16[512,256]{1,0:T(8,128)(2,1)S(1)} %shard_map.114.refs_0_, bf16[512,256]{1,0:T(8,128)(2,1)S(1)} %copy-done.10, ...), custom_call_target="tpu_custom_call" | custom-call | flops 700000000 | bytes 6000000 | tf_op jit(solution)/shard_map/pallas_call | solution.py:348
  109.5 5.8 %all-to-all-start.2 = ((bf16[8,128,512]{2,1,0:T(8,128)(2,1)}), bf16[8,128,512]{2,1,0:T(8,128)(2,1)S(1)}, u32[]{:S(2)}, u32[]{:S(2)}) async-start(bf16[8,128,512]{2,1,0:T(8,128)(2,1)} %copy-done.3), calls=%async_computation.2 | async-start | bytes 2097152 | tf_op jit(solution)/shard_map/all_to_all | solution.py:261
  116.6 3.7 %collective-permute-start.14 = (bf16[160,1024]{1,0:T(8,128)(2,1)S(1)}, bf16[160,1024]{1,0:T(8,128)(2,1)S(1)}, u32[]{:S(2)}, u32[]{:S(2)}) collective-permute-start(bf16[160,1024]{1,0:T(8,128)(2,1)S(1)} %get-tuple-element.75), channel_id=1, source_target_pairs={{0,32},{32,0},{64,96},{96,64},{128,160},{160,128},{192,224},{224,1... | collective-permute-start | bytes 983048 | tf_op jit(solution)/shard_map/ppermute | solution.py:253
  120.3 7.8 %collective-permute-done.14.got_ref = bf16[160,1024]{1,0:T(8,128)(2,1)S(1)} collective-permute-done((bf16[160,1024]{1,0:T(8,128)(2,1)S(1)}, bf16[160,1024]{1,0:T(8,128)(2,1)S(1)}, u32[]{:S(2)}, u32[]{:S(2)}) %collective-permute-start.14) | collective-permute-done | bytes 327712 | tf_op jit(solution)/shard_map/ppermute | solution.py:253
  129.3 8.9 %collective-permute-done.15.got_ref = bf16[80,1024]{1,0:T(8,128)(2,1)S(1)} collective-permute-done((bf16[80,1024]{1,0:T(8,128)(2,1)S(1)}, bf16[80,1024]{1,0:T(8,128)(2,1)S(1)}, u32[]{:S(2)}, u32[]{:S(2)}) %collective-permute-start.15) | collective-permute-done | bytes 163872 | tf_op jit(solution)/shard_map/ppermute | solution.py:253
  138.2 4.2 %all-to-all-start.1 = ((bf16[4,640,128]{2,1,0:T(8,128)(2,1)}), bf16[4,640,128]{2,1,0:T(8,128)(2,1)S(1)}, u32[]{:S(2)}, u32[]{:S(2)}) async-start(bf16[4,640,128]{2,1,0:T(8,128)(2,1)} %shard_map.118), calls=%async_computation.1 | async-start | bytes 1310720 | tf_op jit(solution)/shard_map/all_to_all | solution.py:261
  142.9 8.0 %collective-permute-done.16.got_ref = bf16[40,1024]{1,0:T(8,128)(2,1)S(1)} collective-permute-done((bf16[40,1024]{1,0:T(8,128)(2,1)S(1)}, bf16[40,1024]{1,0:T(8,128)(2,1)S(1)}, u32[]{:S(2)}, u32[]{:S(2)}) %collective-permute-start.16) | collective-permute-done | bytes 81952 | tf_op jit(solution)/shard_map/ppermute | solution.py:253
  152.9 4.7 %collective-permute-done.17.got_ref = f32[20,1024]{1,0:T(8,128)S(1)} collective-permute-done((f32[20,1024]{1,0:T(8,128)S(1)}, f32[20,1024]{1,0:T(8,128)S(1)}, u32[]{:S(2)}, u32[]{:S(2)}) %collective-permute-start.17) | collective-permute-done | bytes 81952 | tf_op jit(solution)/shard_map/ppermute | solution.py:253
  158.9 3.1 %collective-permute-done.18 = f32[10,1024]{1,0:T(8,128)S(1)} collective-permute-done((f32[10,1024]{1,0:T(8,128)S(1)}, f32[10,1024]{1,0:T(8,128)S(1)}, u32[]{:S(2)}, u32[]{:S(2)}) %collective-permute-start.18) | collective-permute-done | bytes 40992 | tf_op jit(solution)/shard_map/ppermute | solution.py:394
  (102 shorter events, 39.6 us)
Async XLA Ops:
  1.6 7.1 %collective-permute-start = (bf16[80,256]{1,0:T(8,128)(2,1)S(1)}, bf16[80,256]{1,0:T(8,128)(2,1)S(1)}, u32[]{:S(2)}, u32[]{:S(2)}) collective-permute-start(bf16[80,256]{1,0:T(8,128)(2,1)S(1)} %constant_dynamic-slice_fusion), channel_id=1, source_target_pairs={{0,0},{1,8},{2,16},{3,24},{4,4},{5,12},{6,20},{7,28},{8,32},{9,40}... | collective-permute-start | bytes 122888 | tf_op jit(solution)/shard_map/ppermute | solution.py:275
  8.7 31.9 %copy-start.4 = (bf16[1,128,2560]{2,1,0:T(8,128)(2,1)S(1)}, bf16[1,128,2560]{2,1,0:T(8,128)(2,1)}, u32[]{:S(2)}) copy-start(bf16[1,128,2560]{2,1,0:T(8,128)(2,1)} %param.8) | copy-start | bytes 1966084
  8.7 42.1 %all-to-all-start = ((bf16[8,128,1280]{2,1,0:T(8,128)(2,1)}), bf16[8,128,1280]{2,1,0:T(8,128)(2,1)S(1)}, u32[]{:S(2)}, u32[]{:S(2)}) async-start(bf16[8,128,1280]{2,1,0:T(8,128)(2,1)} %shard_map.111), calls=%async_computation | async-start | bytes 5242880 | tf_op jit(solution)/shard_map/all_to_all | solution.py:261
  19.7 31.2 %copy-start.26 = (s32[32]{0:T(128)S(1)}, s32[32]{0:T(128)}, u32[]{:S(2)}) copy-start(s32[32]{0:T(128)} %order_ref.1) | copy-start | bytes 388
  19.7 7.9 %collective-permute-start.1 = (bf16[1,80,256]{2,1,0:T(8,128)(2,1)S(1)}, bf16[1,80,256]{2,1,0:T(8,128)(2,1)S(1)}, u32[]{:S(2)}, u32[]{:S(2)}) collective-permute-start(bf16[1,80,256]{2,1,0:T(8,128)(2,1)S(1)} %bitcast.26), channel_id=1, source_target_pairs={{0,128},{32,160},{64,192},{96,224},{128,0},{160,32},{192,64},{224,... | collective-permute-start | bytes 122888 | tf_op jit(solution)/shard_map/ppermute | solution.py:253
  27.6 8.6 %collective-permute-start.2 = (bf16[2,80,256]{2,1,0:T(8,128)(2,1)S(1)}, bf16[2,80,256]{2,1,0:T(8,128)(2,1)S(1)}, u32[]{:S(2)}, u32[]{:S(2)}) collective-permute-start(bf16[2,80,256]{2,1,0:T(8,128)(2,1)S(1)} %pad_maximum_fusion.2), channel_id=1, source_target_pairs={{0,64},{32,96},{64,0},{96,32},{128,192},{160,224},{192,128},{224,1... | collective-permute-start | bytes 245768 | tf_op jit(solution)/shard_map/ppermute | solution.py:253
  37.7 7.0 %collective-permute-start.3 = (bf16[4,80,256]{2,1,0:T(8,128)(2,1)}, bf16[4,80,256]{2,1,0:T(8,128)(2,1)}, u32[]{:S(2)}, u32[]{:S(2)}) collective-permute-start(bf16[4,80,256]{2,1,0:T(8,128)(2,1)} %pad_maximum_fusion.1), channel_id=1, source_target_pairs={{0,32},{32,0},{64,96},{96,64},{128,160},{160,128},{192,224},{224,1... | collective-permute-start | bytes 491528 | tf_op jit(solution)/shard_map/ppermute | solution.py:253
  45.6 1.8 %collective-permute-start.4 = (bf16[8,80,256]{2,1,0:T(8,128)(2,1)S(1)}, bf16[8,80,256]{2,1,0:T(8,128)(2,1)S(1)}, u32[]{:S(2)}, u32[]{:S(2)}) collective-permute-start(bf16[8,80,256]{2,1,0:T(8,128)(2,1)S(1)} %pad_maximum_fusion), channel_id=1, source_target_pairs={{0,8},{8,0},{1,9},{9,1},{2,10},{10,2},{3,11},{11,3},{4,12},{12,4},... | collective-permute-start | bytes 983048 | tf_op jit(solution)/shard_map/ppermute | solution.py:253
  60.7 17.5 %collective-permute-start.5 = (bf16[512,256]{1,0:T(8,128)(2,1)S(1)}, bf16[512,256]{1,0:T(8,128)(2,1)S(1)}, u32[]{:S(2)}, u32[]{:S(2)}) collective-permute-start(bf16[512,256]{1,0:T(8,128)(2,1)S(1)} %get-tuple-element.56), channel_id=1, source_target_pairs={{0,4},{4,0},{1,5},{5,1},{2,6},{6,2},{3,7},{7,3},{8,12},{12,8},{9,1... | collective-permute-start | bytes 786440 | tf_op jit(solution)/shard_map/ppermute | solution.py:334
  62.2 12.3 %collective-permute-start.6 = (bf16[640,128]{1,0:T(8,128)(2,1)S(1)}, bf16[640,128]{1,0:T(8,128)(2,1)S(1)}, u32[]{:S(2)}, u32[]{:S(2)}) collective-permute-start(bf16[640,128]{1,0:T(8,128)(2,1)S(1)} %copy-done.24), channel_id=1, source_target_pairs={{0,1},{1,2},{2,3},{3,0},{4,5},{5,6},{6,7},{7,4},{8,9},{9,10},{10,1... | collective-permute-start | bytes 491528 | tf_op jit(solution)/shard_map/ppermute | solution.py:257
  66.3 10.6 %collective-permute-start.7 = (bf16[640,128]{1,0:T(8,128)(2,1)S(1)}, bf16[640,128]{1,0:T(8,128)(2,1)S(1)}, u32[]{:S(2)}, u32[]{:S(2)}) collective-permute-start(bf16[640,128]{1,0:T(8,128)(2,1)S(1)} %copy-done.22), channel_id=1, source_target_pairs={{0,2},{1,3},{2,0},{3,1},{4,6},{5,7},{6,4},{7,5},{8,10},{9,11},{10,... | collective-permute-start | bytes 491528 | tf_op jit(solution)/shard_map/ppermute | solution.py:257
  70.9 6.7 %collective-permute-start.8 = (bf16[640,128]{1,0:T(8,128)(2,1)S(1)}, bf16[640,128]{1,0:T(8,128)(2,1)S(1)}, u32[]{:S(2)}, u32[]{:S(2)}) collective-permute-start(bf16[640,128]{1,0:T(8,128)(2,1)S(1)} %copy-done.20), channel_id=1, source_target_pairs={{0,3},{1,0},{2,1},{3,2},{4,7},{5,4},{6,5},{7,6},{8,11},{9,8},{10,9... | collective-permute-start | bytes 491528 | tf_op jit(solution)/shard_map/ppermute | solution.py:257
  78.2 21.3 %collective-permute-start.12 = (bf16[16,80,256]{2,1,0:T(8,128)(2,1)S(1)}, bf16[16,80,256]{2,1,0:T(8,128)(2,1)S(1)}, u32[]{:S(2)}, u32[]{:S(2)}) collective-permute-start(bf16[16,80,256]{2,1,0:T(8,128)(2,1)S(1)} %constant_dynamic-update-slice_fusion.w_ref), channel_id=1, source_target_pairs={{0,16},{16,0},{1,17},{17,1},{2,18},{18,2},{3,19},{19,3},{4,20},{20... | collective-permute-start | bytes 1966088 | tf_op jit(solution)/shard_map/ppermute | solution.py:253
  84.4 10.7 %collective-permute-start.10 = (bf16[512,256]{1,0:T(8,128)(2,1)S(1)}, bf16[512,256]{1,0:T(8,128)(2,1)S(1)}, u32[]{:S(2)}, u32[]{:S(2)}) collective-permute-start(bf16[512,256]{1,0:T(8,128)(2,1)S(1)} %shard_map.114.refs_0_), channel_id=1, source_target_pairs={{0,2},{1,3},{2,0},{3,1},{4,6},{5,7},{6,4},{7,5},{8,10},{9,11},{10,... | collective-permute-start | bytes 786440 | tf_op jit(solution)/shard_map/ppermute | solution.py:257
  84.5 13.6 %collective-permute-start.11 = (bf16[512,256]{1,0:T(8,128)(2,1)S(1)}, bf16[512,256]{1,0:T(8,128)(2,1)S(1)}, u32[]{:S(2)}, u32[]{:S(2)}) collective-permute-start(bf16[512,256]{1,0:T(8,128)(2,1)S(1)} %shard_map.114.refs_0_), channel_id=1, source_target_pairs={{0,3},{1,0},{2,1},{3,2},{4,7},{5,4},{6,5},{7,6},{8,11},{9,8},{10,9... | collective-permute-start | bytes 786440 | tf_op jit(solution)/shard_map/ppermute | solution.py:257
  86.3 12.5 %collective-permute-start.9 = (bf16[512,256]{1,0:T(8,128)(2,1)S(1)}, bf16[512,256]{1,0:T(8,128)(2,1)S(1)}, u32[]{:S(2)}, u32[]{:S(2)}) collective-permute-start(bf16[512,256]{1,0:T(8,128)(2,1)S(1)} %shard_map.114.refs_0_), channel_id=1, source_target_pairs={{0,1},{1,2},{2,3},{3,0},{4,5},{5,6},{6,7},{7,4},{8,9},{9,10},{10,1... | collective-permute-start | bytes 786440 | tf_op jit(solution)/shard_map/ppermute | solution.py:257
  107.6 7.7 %collective-permute-start.13 = (bf16[320,1024]{1,0:T(8,128)(2,1)}, bf16[320,1024]{1,0:T(8,128)(2,1)}, u32[]{:S(2)}, u32[]{:S(2)}) collective-permute-start(bf16[320,1024]{1,0:T(8,128)(2,1)} %get-tuple-element.73), channel_id=1, source_target_pairs={{0,8},{8,0},{1,9},{9,1},{2,10},{10,2},{3,11},{11,3},{4,12},{12,4},... | collective-permute-start | bytes 1966088 | tf_op jit(solution)/shard_map/ppermute | solution.py:253
  109.5 28.7 %all-to-all-start.2 = ((bf16[8,128,512]{2,1,0:T(8,128)(2,1)}), bf16[8,128,512]{2,1,0:T(8,128)(2,1)S(1)}, u32[]{:S(2)}, u32[]{:S(2)}) async-start(bf16[8,128,512]{2,1,0:T(8,128)(2,1)} %copy-done.3), calls=%async_computation.2 | async-start | bytes 2097152 | tf_op jit(solution)/shard_map/all_to_all | solution.py:261
  116.6 11.6 %collective-permute-start.14 = (bf16[160,1024]{1,0:T(8,128)(2,1)S(1)}, bf16[160,1024]{1,0:T(8,128)(2,1)S(1)}, u32[]{:S(2)}, u32[]{:S(2)}) collective-permute-start(bf16[160,1024]{1,0:T(8,128)(2,1)S(1)} %get-tuple-element.75), channel_id=1, source_target_pairs={{0,32},{32,0},{64,96},{96,64},{128,160},{160,128},{192,224},{224,1... | collective-permute-start | bytes 983048 | tf_op jit(solution)/shard_map/ppermute | solution.py:253
  128.2 10.0 %collective-permute-start.15 = (bf16[80,1024]{1,0:T(8,128)(2,1)S(1)}, bf16[80,1024]{1,0:T(8,128)(2,1)S(1)}, u32[]{:S(2)}, u32[]{:S(2)}) collective-permute-start(bf16[80,1024]{1,0:T(8,128)(2,1)S(1)} %get-tuple-element.76), channel_id=1, source_target_pairs={{0,64},{32,96},{64,0},{96,32},{128,192},{160,224},{192,128},{224,1... | collective-permute-start | bytes 491528 | tf_op jit(solution)/shard_map/ppermute | solution.py:253
  138.2 24.4 %all-to-all-start.1 = ((bf16[4,640,128]{2,1,0:T(8,128)(2,1)}), bf16[4,640,128]{2,1,0:T(8,128)(2,1)S(1)}, u32[]{:S(2)}, u32[]{:S(2)}) async-start(bf16[4,640,128]{2,1,0:T(8,128)(2,1)} %shard_map.118), calls=%async_computation.1 | async-start | bytes 1310720 | tf_op jit(solution)/shard_map/all_to_all | solution.py:261
  142.5 8.4 %collective-permute-start.16 = (bf16[40,1024]{1,0:T(8,128)(2,1)S(1)}, bf16[40,1024]{1,0:T(8,128)(2,1)S(1)}, u32[]{:S(2)}, u32[]{:S(2)}) collective-permute-start(bf16[40,1024]{1,0:T(8,128)(2,1)S(1)} %get-tuple-element.87), channel_id=1, source_target_pairs={{0,128},{32,160},{64,192},{96,224},{128,0},{160,32},{192,64},{224,... | collective-permute-start | bytes 245768 | tf_op jit(solution)/shard_map/ppermute | solution.py:253
  151.0 6.6 %collective-permute-start.17 = (f32[20,1024]{1,0:T(8,128)S(1)}, f32[20,1024]{1,0:T(8,128)S(1)}, u32[]{:S(2)}, u32[]{:S(2)}) collective-permute-start(f32[20,1024]{1,0:T(8,128)S(1)} %get-tuple-element.89), channel_id=1, source_target_pairs={{0,16},{16,0},{1,17},{17,1},{2,18},{18,2},{3,19},{19,3},{4,20},{20... | collective-permute-start | bytes 245768 | tf_op jit(solution)/shard_map/ppermute | solution.py:253
  157.6 4.4 %collective-permute-start.18 = (f32[10,1024]{1,0:T(8,128)S(1)}, f32[10,1024]{1,0:T(8,128)S(1)}, u32[]{:S(2)}, u32[]{:S(2)}) collective-permute-start(f32[10,1024]{1,0:T(8,128)S(1)} %get-tuple-element.91), channel_id=1, source_target_pairs={{0,4},{4,0},{1,5},{5,1},{2,6},{6,2},{3,7},{7,3},{8,12},{12,8},{9,1... | collective-permute-start | bytes 122888 | tf_op jit(solution)/shard_map/ppermute | solution.py:394
  (27 other events, 123.2 us)

commit v5 on v4

--- a/solution.py
+++ b/solution.py
@@ -78,11 +78,11 @@
 
 
 def tile_row(z, low, y):
-    row = (low % 2) * 320 + (z % 2) * 160 + (z // 2 % 2) * 80 + (z // 4) * 40
-    return row + (low // 2) * 20 + y * 10
-
-
-def turn_kernel(x_ref, in_ref, *refs):
+    row = (low % 2) * 320 + y * 160 + (low // 2) * 80
+    return row + (z % 2) * 40 + (z // 2 % 2) * 20 + (z // 4) * 10
+
+
+def turn_kernel(in_ref, *refs):
     outs, turned, tile = refs[:4], refs[4], refs[5]
     for j in range(FEATURES // 128):
         block = in_ref[:, j * 128 : (j + 1) * 128].T
@@ -95,13 +95,12 @@
                     at = tile_row(z, low, y)
                     tile[x, at : at + 10, :] = turned[source : source + 10, :]
     for s in range(4):
-        outs[s][...] = tile[lax.rem(x_ref[0] + s, 4)].astype(jnp.bfloat16)
-
-
-def attention_kernel(c_ref, docs_ref, order_ref, *refs):
+        outs[s][...] = tile[lax.rem(lax.axis_index("x") + s, 4)].astype(jnp.bfloat16)
+
+
+def attention_kernel(docs_ref, order_ref, *refs):
     in_ref, dq_ref, keep_ref, send_ref = refs[:4]
     q_s, d_s, k_s, v_s, kt_s, dq_s, dkv_s, place, begin = refs[4:]
-    c = c_ref[0]
 
     first = lax.fori_loop(
         0, 17, lambda i, a: jnp.where(docs_ref[i] == docs_ref[i + 15], i, a), jnp.int32(0)
@@ -174,7 +173,7 @@
 
     lax.fori_loop(0, 2, half, 0)
 
-    y = c // 4
+    y = lax.axis_index("y")
     for t in range(16):
         block = slice(t * BLK, (t + 1) * BLK)
         for half_y, ref in ((y, keep_ref), (1 - y, send_ref)):
@@ -190,10 +189,10 @@
     out_ref[...] = (keep_ref[...] + taken_ref[...].astype(jnp.float32)).astype(jnp.bfloat16)
 
 
-def weight_kernel(at_ref, *refs):
+def weight_kernel(*refs):
     pieces, ins = refs[:4], refs[4:8]
     kv_ref, kv_rows_ref, send_ref, keep_ref, x_s = refs[8:]
-    core, x = at_ref[0], at_ref[1]
+    core, x = lax.axis_index("core"), lax.axis_index("x")
     for s in range(4):
         at = pl.multiple_of(lax.rem(x + 4 - s, 4) * 128, 128)
         kv_ref[:, pl.ds(at, 128)] = pieces[s][:, 0:128]
@@ -209,18 +208,35 @@
     kv_rows_ref[...] = kv_ref[pl.ds(pl.multiple_of(x * ROWS, ROWS), ROWS), :]
 
 
-def halve_kernel(bit_ref, keep_ref, got_ref, send_ref, kept_ref):
+def halve_kernel(axis, mask, keep_ref, got_ref, send_ref, kept_ref):
     part = kept_ref.shape[0]
     total = keep_ref[...] + got_ref[...].astype(jnp.float32)
-    low, high, upper = total[:part, :], total[part:, :], bit_ref[0] == 1
+    low, high = total[:part, :], total[part:, :]
+    upper = (lax.axis_index(axis) & mask) != 0
     send_ref[...] = jnp.where(upper, low, high).astype(send_ref.dtype)
     kept_ref[...] = jnp.where(upper, high, low)
 
 
-def input_kernel(f_ref, kv_ref, w_ref, far_ref, out_ref, w_s):
+def add_kernel(keep_ref, got_ref, out_ref):
+    out_ref[...] = keep_ref[...] + got_ref[...].astype(jnp.float32)
+
+
+def slice_kernel(w_ref, out_ref):
+    at = pl.multiple_of(lax.axis_index("x") * 256, 256)
+    out_ref[0] = w_ref[:, pl.ds(at, 256)]
+
+
+def join_kernel(near_ref, far_ref, out_ref):
+    n = near_ref.shape[0]
+    out_ref[0:n] = near_ref[...]
+    out_ref[n:] = far_ref[...]
+
+
+def input_kernel(kv_ref, w_ref, far_ref, out_ref, w_s):
+    f = lax.axis_index("z") * 4 + lax.axis_index("yh") * 2 + lax.axis_index("core")
     for at in range(FSDP):
         mask = sum(((at >> i) & 1) << bit for i, bit in enumerate(GATHER_BITS))
-        source = f_ref[0] ^ mask
+        source = f ^ mask
         rows = pl.ds(pl.multiple_of((source // 4) * 80, 80), 80)
         cols = pl.ds(pl.multiple_of(lax.rem(source, 4) * 256, 256), 256)
         w_s[rows, cols] = w_ref[at] if at < FSDP // 2 else far_ref[at - FSDP // 2]
@@ -244,7 +260,7 @@
         out_ref[:, at : at + Q_COLS] = dq_ref[src]
 
 
-GATHER_BITS = (4, 3, 2, 0, 1)
+GATHER_BITS = (4, 3, 2, 1, 0)
 BIT_AXES = (("core", 1), ("yh", 1), ("z", 1), ("z", 2), ("z", 4))
 
 
@@ -262,20 +278,31 @@
 
 
 def body(inputs, queries, keys, values, output_cotangent, key_value_weight, doc_ids, block_order):
-    f = lax.axis_index(("z", "yh", "core")).astype(jnp.int32)
-    y, x = lax.axis_index("y").astype(jnp.int32), lax.axis_index("x").astype(jnp.int32)
-    c_at = (y * 4 + x).reshape(1)
-
-    tile = lax.dynamic_slice(key_value_weight, (0, x * 256), (80, 256))
+    tile = pl.pallas_call(
+        slice_kernel,
+        in_specs=[VMEM],
+        out_specs=VMEM,
+        out_shape=shape((1, 80, 256)),
+        compiler_params=params(2),
+        cost_estimate=cost(0, 200_000),
+    )(key_value_weight)
     perm = []
     for f1 in range(FSDP):
         for c1 in range(CTX):
             y1, x1 = c1 // 4, c1 % 4
             perm.append((f1 * CTX + c1, ((f1 % 8) * 4 + x1) * CTX + y1 * 4 + f1 // 8))
-    tile = lax.ppermute(tile, ("z", "yh", "core", "y", "x"), perm)[None]
+    tile = lax.ppermute(tile, ("z", "yh", "core", "y", "x"), perm)
 
     def widen(tile, bit):
-        return jnp.concatenate([tile, swap(tile, bit)], axis=0)
+        n = 2 * tile.shape[0]
+        return pl.pallas_call(
+            join_kernel,
+            in_specs=[VMEM] * 2,
+            out_specs=VMEM,
+            out_shape=shape((n, 80, 256)),
+            compiler_params=params(3),
+            cost_estimate=cost(0, n * 80_000),
+        )(tile, swap(tile, bit))
 
     packed = pl.pallas_call(
         pack_kernel,
@@ -283,17 +310,17 @@
         out_specs=VMEM,
         out_shape=shape((CTX, ROWS, PACK_COLS)),
         scratch_shapes=[pltpu.SemaphoreType.DMA((4 * CTX,))],
-        compiler_params=params(6),
+        compiler_params=params(56),
         cost_estimate=cost(0, 5_000_000),
     )(queries[0], output_cotangent[0], keys[0], values[0])
     packed, tile = lax.optimization_barrier((packed, tile))
     got = exchange(packed, ("y", "x"))
-    for bit in GATHER_BITS[:4]:
+    for bit in GATHER_BITS[:3]:
         tile = widen(tile, bit)
 
     turned = pl.pallas_call(
         turn_kernel,
-        in_specs=[SMEM, VMEM],
+        in_specs=[VMEM],
         out_specs=[VMEM] * 4,
         out_shape=[shape((FEAT_TILE, ROWS))] * 4,
         scratch_shapes=[
@@ -302,14 +329,15 @@
         ],
         compiler_params=params(8),
         cost_estimate=cost(0, 1_300_000),
-    )(x.reshape(1), inputs[0])
-
-    got, turned, tile = lax.optimization_barrier((got, turned, tile))
+    )(inputs[0])
+
     got_x = [to_shift(turned[s], s) for s in range(4)]
+    got, got_x, tile = lax.optimization_barrier((got, got_x, tile))
+    tile = widen(tile, GATHER_BITS[3])
 
     dq_parts, keep, send = pl.pallas_call(
         attention_kernel,
-        in_specs=[SMEM] * 3 + [VMEM],
+        in_specs=[SMEM] * 2 + [VMEM],
         out_specs=[VMEM] * 3,
         out_shape=[
             shape((CTX, ROWS, Q_COLS)),
@@ -329,10 +357,10 @@
         ],
         compiler_params=params(24),
         cost_estimate=cost(10_000_000_000, 5_000_000),
-    )(c_at, doc_ids[0], block_order, got)
-
+    )(doc_ids[0], block_order, got)
+
+    send, tile = lax.optimization_barrier((send, tile))
     taken = lax.ppermute(send, "y", [(0, 1), (1, 0)])
-    taken, got_x, tile = lax.optimization_barrier((taken, got_x, tile))
     far_tile = swap(tile, GATHER_BITS[4])
     own_cols = pl.pallas_call(
         pair_kernel,
@@ -347,7 +375,7 @@
 
     kv_half, kv_rows, wg_send, wg_keep = pl.pallas_call(
         weight_kernel,
-        in_specs=[SMEM] + [VMEM] * 8,
+        in_specs=[VMEM] * 8,
         out_specs=[VMEM] * 4,
         out_shape=[
             shape((SLAB // 2, 1024)),
@@ -358,40 +386,47 @@
         scratch_shapes=[pltpu.VMEM((FEAT_TILE, SLAB // 2), jnp.bfloat16)],
         compiler_params=params(12),
         cost_estimate=cost(700_000_000, 6_000_000),
-    )(jnp.stack([lax.rem(f, 2), x]), *pieces, *got_x)
+    )(*pieces, *got_x)
 
     wg_got = swap(wg_send, 0)
     parts = pl.pallas_call(
         input_kernel,
-        in_specs=[SMEM] + [VMEM] * 3,
+        in_specs=[VMEM] * 3,
         out_specs=VMEM,
         out_shape=shape((4, FEAT_TILE, ROWS)),
         scratch_shapes=[pltpu.VMEM((FEAT_TILE, 1024), jnp.bfloat16)],
         compiler_params=params(12),
         cost_estimate=cost(700_000_000, 4_000_000),
-    )(f.reshape(1), kv_half, tile, far_tile)
-    parts, dq_parts = lax.optimization_barrier((parts, dq_parts))
-    dq_got = exchange(dq_parts, ("y", "x"))
-
-    def halve(bit, keep, got, kind):
+    )(kv_half, tile, far_tile)
+    ig_got = exchange(parts, "x")
+
+    def halve(axis, mask, keep, got):
         rows = keep.shape[0] // 2
         return pl.pallas_call(
-            halve_kernel,
-            in_specs=[SMEM] + [VMEM] * 2,
+            functools.partial(halve_kernel, axis, mask),
+            in_specs=[VMEM] * 2,
             out_specs=[VMEM] * 2,
-            out_shape=[shape((rows, 1024), kind), shape((rows, 1024), jnp.float32)],
+            out_shape=[shape((rows, 1024)), shape((rows, 1024), jnp.float32)],
             compiler_params=params(6),
             cost_estimate=cost(0, rows * 1024 * 16),
-        )(bit.reshape(1), keep, got)
-
-    for bit, kind in ((2, jnp.bfloat16), (3, jnp.bfloat16), (4, jnp.bfloat16), (1, jnp.float32)):
-        wg_send, wg_keep = halve((f >> bit) & 1, wg_keep, wg_got, kind)
+        )(keep, got)
+
+    wg_send, wg_keep = halve("y", 1, wg_keep, wg_got)
+    wg_got = lax.ppermute(wg_send, "y", [(0, 1), (1, 0)])
+    for bit in (1, 2, 3, 4):
+        wg_send, wg_keep = halve(*BIT_AXES[bit], wg_keep, wg_got)
         wg_got = swap(wg_send, bit)
-        if bit == 3:
-            wg_got, parts = lax.optimization_barrier((wg_got, parts))
-            ig_got = exchange(parts, "x")
-    wg_send, wg_keep = halve(y, wg_keep, wg_got, jnp.float32)
-    weight_grad = wg_keep + lax.ppermute(wg_send, "y", [(0, 1), (1, 0)])
+        if bit == 1:
+            wg_got, dq_parts = lax.optimization_barrier((wg_got, dq_parts))
+            dq_got = exchange(dq_parts, ("y", "x"))
+    weight_grad = pl.pallas_call(
+        add_kernel,
+        in_specs=[VMEM] * 2,
+        out_specs=VMEM,
+        out_shape=shape((10, 1024), jnp.float32),
+        compiler_params=params(2),
+        cost_estimate=cost(0, 100_000),
+    )(wg_keep, wg_got)
 
     query_grad = pl.pallas_call(
         query_out_kernel,

time: 165 us -> 148 us (0.90)
  local copies, waits for them, and re-layouts: 20.3 us -> 1.6 us
  waiting for transfers between devices: 58.9 us -> 65.1 us
  other arithmetic: 3.16 us -> 0 us
  starting transfers between devices: 60.8 us -> 59.1 us
    unnamed x62 -> x12, local copies, waits for them, and re-layouts: 20.3 us -> 1.6 us
    ppermute x6, waiting for transfers between devices: 16.5 us -> 29.3 us  [to_shift(): lax.ppermute(value, 'x', [(i, (i + s) % 4) for i in range(4)])]
    ppermute x10, waiting for transfers between devices: 36 us -> 24.2 us  [swap(): lax.ppermute(value, axis, [(i, i ^ mask) for i in range(8 if axis == 'z'...]
    ppermute x1, waiting for transfers between devices: 0.01 us -> 7.47 us  [body(): taken = lax.ppermute(send, 'y', [(0, 1), (1, 0)])]
    ppermute x6, starting transfers between devices: 11.1 us -> 7.78 us  [to_shift(): lax.ppermute(value, 'x', [(i, (i + s) % 4) for i in range(4)])]
    all_to_all x3, waiting for transfers between devices: 3.38 us -> 0.85 us  [exchange(): return lax.all_to_all(value, axis, 0, 0, tiled=True)]
    concatenate x3 -> x0, other arithmetic: 2.45 us -> none  [widen(): return jnp.concatenate([tile, swap(tile, bit)], axis=0)]
    pallas_call x9 -> x15, Pallas kernels: 15.3 us -> 14.6 us  [the longest x1 9.79 us: body(): pl.pallas_call(attention_kernel, in_specs=[SMEM] * 2 + [VMEM], out_specs=...]
  transfers between devices with their start and end apart: 22 -> 22, of which waited for: 12 -> 16; matrix products, arithmetic and copies ran while one was open for 3% -> 0% of each run, Pallas kernels for 4% -> 12%
where the time goes in v5:
time: 148 us; the launch traced here: 147 us
  waiting for transfers between devices  65.1 us (44%)
  starting transfers between devices  59.1 us (40%)
  Pallas kernels  20.3 us (14%)
  local copies, waits for them, and re-layouts  1.6 us (1%)
    ppermute x6, waiting for transfers between devices, to_shift(): lax.ppermute(value, 'x', [(i, (i + s) % 4) for i in range(4)])  29.3 us
    ppermute x10, starting transfers between devices, swap(): lax.ppermute(value, axis, [(i, i ^ mask) for i in range(8 if axis == 'z'...  26.6 us
    ppermute x10, waiting for transfers between devices, swap(): lax.ppermute(value, axis, [(i, i ^ mask) for i in range(8 if axis == 'z'...  24.2 us
    all_to_all x3, starting transfers between devices, exchange(): return lax.all_to_all(value, axis, 0, 0, tiled=True)  21.5 us
    pallas_call x1, Pallas kernels, body(): pl.pallas_call(attention_kernel, in_specs=[SMEM] * 2 + [VMEM], out_specs=...  9.79 us
    ppermute x6, starting transfers between devices, to_shift(): lax.ppermute(value, 'x', [(i, (i + s) % 4) for i in range(4)])  7.78 us
    ppermute x1, waiting for transfers between devices, body(): taken = lax.ppermute(send, 'y', [(0, 1), (1, 0)])  7.47 us
    pallas_call x1, Pallas kernels, body(): pl.pallas_call(pack_kernel, in_specs=[HBM] * 4, out_specs=VMEM, out_shape...  3.58 us
  transfers between devices with their start and end apart: 22, of which 16 were waited for; matrix products, arithmetic and copies ran while one was open for 0% of the time, Pallas kernels for 12%

profile of v5, /device:TPU:8, one launch (start us, length us, event | category | flops | bytes accessed | tf_op | source)
XLA Modules:
  0.0 146.9 jit_solution(12636647213852323043)
XLA Ops:
  2.2 3.6 %shard_map.111 = bf16[8,128,1280]{2,1,0:T(8,128)(2,1)} custom-call(bf16[128,4096]{1,0:T(8,128)(2,1)} %bitcast.11, bf16[128,4096]{1,0:T(8,128)(2,1)} %bitcast.12, bf16[128,512]{1,0:T(8,128)(2,1)} %bitcast.15, bf16[128,512]{1,0:T(8,128)(2,1)} %bitcast.16), custom_call_target="tpu_custom_call" | custom-call | bytes 5000000 | tf_op jit(solution)/shard_map/pallas_call | solution.py:307
  5.8 13.7 %all-to-all-start = ((bf16[8,128,1280]{2,1,0:T(8,128)(2,1)}), bf16[8,128,1280]{2,1,0:T(8,128)(2,1)S(1)}, u32[]{:S(2)}, u32[]{:S(2)}) async-start(bf16[8,128,1280]{2,1,0:T(8,128)(2,1)} %shard_map.111), calls=%async_computation | async-start | bytes 5242880 | tf_op jit(solution)/shard_map/all_to_all | solution.py:277
  19.5 4.8 %collective-permute-start.4 = (bf16[1,80,256]{2,1,0:T(8,128)(2,1)S(1)}, bf16[1,80,256]{2,1,0:T(8,128)(2,1)S(1)}, u32[]{:S(2)}, u32[]{:S(2)}) collective-permute-start(bf16[1,80,256]{2,1,0:T(8,128)(2,1)S(1)} %collective-permute-done.near_ref), channel_id=1, source_target_pairs={{0,128},{32,160},{64,192},{96,224},{128,0},{160,32},{192,64},{224,... | collective-permute-start | bytes 122888 | tf_op jit(solution)/shard_map/ppermute | solution.py:269
  24.3 3.2 %collective-permute-done.4.far_ref = bf16[1,80,256]{2,1,0:T(8,128)(2,1)S(1)} collective-permute-done((bf16[1,80,256]{2,1,0:T(8,128)(2,1)S(1)}, bf16[1,80,256]{2,1,0:T(8,128)(2,1)S(1)}, u32[]{:S(2)}, u32[]{:S(2)}) %collective-permute-start.4) | collective-permute-done | bytes 40992 | tf_op jit(solution)/shard_map/ppermute | solution.py:269
  27.4 5.2 %collective-permute-start.5 = (bf16[2,80,256]{2,1,0:T(8,128)(2,1)S(1)}, bf16[2,80,256]{2,1,0:T(8,128)(2,1)S(1)}, u32[]{:S(2)}, u32[]{:S(2)}) collective-permute-start(bf16[2,80,256]{2,1,0:T(8,128)(2,1)S(1)} %shard_map.114.near_ref), channel_id=1, source_target_pairs={{0,64},{32,96},{64,0},{96,32},{128,192},{160,224},{192,128},{224,1... | collective-permute-start | bytes 245768 | tf_op jit(solution)/shard_map/ppermute | solution.py:269
  36.3 3.0 %collective-permute-start.2 = (bf16[640,128]{1,0:T(8,128)(2,1)S(1)}, bf16[640,128]{1,0:T(8,128)(2,1)S(1)}, u32[]{:S(2)}, u32[]{:S(2)}) collective-permute-start(bf16[640,128]{1,0:T(8,128)(2,1)S(1)} %get-tuple-element.45), channel_id=1, source_target_pairs={{0,2},{1,3},{2,0},{3,1},{4,6},{5,7},{6,4},{7,5},{8,10},{9,11},{10,... | collective-permute-start | bytes 491528 | tf_op jit(solution)/shard_map/ppermute | solution.py:273
  41.4 12.9 %collective-permute-done.1.refs_5_ = bf16[640,128]{1,0:T(8,128)(2,1)S(1)} collective-permute-done((bf16[640,128]{1,0:T(8,128)(2,1)S(1)}, bf16[640,128]{1,0:T(8,128)(2,1)S(1)}, u32[]{:S(2)}, u32[]{:S(2)}) %collective-permute-start.1) | collective-permute-done | bytes 163872 | tf_op jit(solution)/shard_map/ppermute | solution.py:273
  54.3 3.4 %collective-permute-done.2.refs_6_ = bf16[640,128]{1,0:T(8,128)(2,1)S(1)} collective-permute-done((bf16[640,128]{1,0:T(8,128)(2,1)S(1)}, bf16[640,128]{1,0:T(8,128)(2,1)S(1)}, u32[]{:S(2)}, u32[]{:S(2)}) %collective-permute-start.2) | collective-permute-done | bytes 163872 | tf_op jit(solution)/shard_map/ppermute | solution.py:273
  58.4 9.0 %collective-permute-start.7 = (bf16[8,80,256]{2,1,0:T(8,128)(2,1)S(1)}, bf16[8,80,256]{2,1,0:T(8,128)(2,1)S(1)}, u32[]{:S(2)}, u32[]{:S(2)}) collective-permute-start(bf16[8,80,256]{2,1,0:T(8,128)(2,1)S(1)} %shard_map.116.near_ref), channel_id=1, source_target_pairs={{0,16},{16,0},{1,17},{17,1},{2,18},{18,2},{3,19},{19,3},{4,20},{20... | collective-permute-start | bytes 983048 | tf_op jit(solution)/shard_map/ppermute | solution.py:269
  67.4 9.8 %shard_map.117 = (bf16[8,128,512]{2,1,0:T(8,128)(2,1)}, f32[512,256]{1,0:T(8,128)S(1)}, bf16[512,256]{1,0:T(8,128)(2,1)S(1)}) custom-call(s32[32]{0:T(128)S(1)} %bitcast.10, s32[32]{0:T(128)S(1)} %copy-done.5, bf16[8,128,1280]{2,1,0:T(8,128)(2,1)S(1)} %all-to-all-done.refs_0_), custom_call_target="tpu_custom_call" | custom-call | flops 10000000000 | bytes 5000000 | tf_op jit(solution)/shard_map/pallas_call | solution.py:338
  78.6 7.5 %collective-permute-done.8.taken_ref = bf16[512,256]{1,0:T(8,128)(2,1)S(1)} collective-permute-done((bf16[512,256]{1,0:T(8,128)(2,1)S(1)}, bf16[512,256]{1,0:T(8,128)(2,1)S(1)}, u32[]{:S(2)}, u32[]{:S(2)}) %collective-permute-start.8) | collective-permute-done | bytes 262176 | tf_op jit(solution)/shard_map/ppermute | solution.py:363
  88.2 7.2 %collective-permute-done.11.refs_3_ = bf16[512,256]{1,0:T(8,128)(2,1)S(1)} collective-permute-done((bf16[512,256]{1,0:T(8,128)(2,1)S(1)}, bf16[512,256]{1,0:T(8,128)(2,1)S(1)}, u32[]{:S(2)}, u32[]{:S(2)}) %collective-permute-start.11) | collective-permute-done | bytes 262176 | tf_op jit(solution)/shard_map/ppermute | solution.py:273
  97.3 4.0 %collective-permute-done.9.refs_1_ = bf16[512,256]{1,0:T(8,128)(2,1)S(1)} collective-permute-done((bf16[512,256]{1,0:T(8,128)(2,1)S(1)}, bf16[512,256]{1,0:T(8,128)(2,1)S(1)}, u32[]{:S(2)}, u32[]{:S(2)}) %collective-permute-start.9) | collective-permute-done | bytes 262176 | tf_op jit(solution)/shard_map/ppermute | solution.py:273
  102.6 2.1 %collective-permute-done.13.got_ref = bf16[320,1024]{1,0:T(8,128)(2,1)S(1)} collective-permute-done((bf16[320,1024]{1,0:T(8,128)(2,1)S(1)}, bf16[320,1024]{1,0:T(8,128)(2,1)S(1)}, u32[]{:S(2)}, u32[]{:S(2)}) %collective-permute-start.13) | collective-permute-done | bytes 655392 | tf_op jit(solution)/shard_map/ppermute | solution.py:269
  106.1 1.9 %shard_map.121 = bf16[4,640,128]{2,1,0:T(8,128)(2,1)} custom-call(bf16[512,1024]{1,0:T(8,128)(2,1)S(1)} %get-tuple-element.62.kv_ref, bf16[16,80,256]{2,1,0:T(8,128)(2,1)S(1)} %shard_map.118.w_ref, bf16[16,80,256]{2,1,0:T(8,128)(2,1)S(1)} %collective-permute-done.12.far_ref), custom_call_target="tpu_custom_call" | custom-call | flops 700000000 | bytes 4000000 | tf_op jit(solution)/shard_map/pallas_call | solution.py:392
  108.0 3.5 %all-to-all-start.1 = ((bf16[4,640,128]{2,1,0:T(8,128)(2,1)}), bf16[4,640,128]{2,1,0:T(8,128)(2,1)S(1)}, u32[]{:S(2)}, u32[]{:S(2)}) async-start(bf16[4,640,128]{2,1,0:T(8,128)(2,1)} %shard_map.121), calls=%async_computation.1 | async-start | bytes 1310720 | tf_op jit(solution)/shard_map/all_to_all | solution.py:277
  111.5 3.2 %collective-permute-done.14.got_ref = bf16[160,1024]{1,0:T(8,128)(2,1)S(1)} collective-permute-done((bf16[160,1024]{1,0:T(8,128)(2,1)S(1)}, bf16[160,1024]{1,0:T(8,128)(2,1)S(1)}, u32[]{:S(2)}, u32[]{:S(2)}) %collective-permute-start.14) | collective-permute-done | bytes 327712 | tf_op jit(solution)/shard_map/ppermute | solution.py:415
  115.1 6.6 %collective-permute-done.15.got_ref = bf16[80,1024]{1,0:T(8,128)(2,1)S(1)} collective-permute-done((bf16[80,1024]{1,0:T(8,128)(2,1)S(1)}, bf16[80,1024]{1,0:T(8,128)(2,1)S(1)}, u32[]{:S(2)}, u32[]{:S(2)}) %collective-permute-start.15) | collective-permute-done | bytes 163872 | tf_op jit(solution)/shard_map/ppermute | solution.py:269
  122.6 4.3 %all-to-all-start.2 = ((bf16[8,128,512]{2,1,0:T(8,128)(2,1)}), bf16[8,128,512]{2,1,0:T(8,128)(2,1)S(1)}, u32[]{:S(2)}, u32[]{:S(2)}) async-start(bf16[8,128,512]{2,1,0:T(8,128)(2,1)} %get-tuple-element.70), calls=%async_computation.2 | async-start | bytes 2097152 | tf_op jit(solution)/shard_map/all_to_all | solution.py:277
  127.0 2.7 %collective-permute-start.16 = (bf16[40,1024]{1,0:T(8,128)(2,1)S(1)}, bf16[40,1024]{1,0:T(8,128)(2,1)S(1)}, u32[]{:S(2)}, u32[]{:S(2)}) collective-permute-start(bf16[40,1024]{1,0:T(8,128)(2,1)S(1)} %get-tuple-element.75), channel_id=1, source_target_pairs={{0,32},{32,0},{64,96},{96,64},{128,160},{160,128},{192,224},{224,1... | collective-permute-start | bytes 245768 | tf_op jit(solution)/shard_map/ppermute | solution.py:269
  129.7 2.4 %collective-permute-done.16.got_ref = bf16[40,1024]{1,0:T(8,128)(2,1)S(1)} collective-permute-done((bf16[40,1024]{1,0:T(8,128)(2,1)S(1)}, bf16[40,1024]{1,0:T(8,128)(2,1)S(1)}, u32[]{:S(2)}, u32[]{:S(2)}) %collective-permute-start.16) | collective-permute-done | bytes 81952 | tf_op jit(solution)/shard_map/ppermute | solution.py:269
  133.6 3.7 %collective-permute-done.17.got_ref = bf16[20,1024]{1,0:T(8,128)(2,1)S(1)} collective-permute-done((bf16[20,1024]{1,0:T(8,128)(2,1)S(1)}, bf16[20,1024]{1,0:T(8,128)(2,1)S(1)}, u32[]{:S(2)}, u32[]{:S(2)}) %collective-permute-start.17) | collective-permute-done | bytes 40992 | tf_op jit(solution)/shard_map/ppermute | solution.py:269
  137.3 2.8 %collective-permute-start.18 = (bf16[10,1024]{1,0:T(8,128)(2,1)S(1)}, bf16[10,1024]{1,0:T(8,128)(2,1)S(1)}, u32[]{:S(2)}, u32[]{:S(2)}) collective-permute-start(bf16[10,1024]{1,0:T(8,128)(2,1)S(1)} %get-tuple-element.79), channel_id=1, source_target_pairs={{0,128},{32,160},{64,192},{96,224},{128,0},{160,32},{192,64},{224,... | collective-permute-start | bytes 61448 | tf_op jit(solution)/shard_map/ppermute | solution.py:269
  141.1 4.1 %collective-permute-done.18.got_ref = bf16[10,1024]{1,0:T(8,128)(2,1)S(1)} collective-permute-done((bf16[10,1024]{1,0:T(8,128)(2,1)S(1)}, bf16[10,1024]{1,0:T(8,128)(2,1)S(1)}, u32[]{:S(2)}, u32[]{:S(2)}) %collective-permute-start.18) | collective-permute-done | bytes 20512 | tf_op jit(solution)/shard_map/ppermute | solution.py:269
  (51 shorter events, 21.8 us)
Async XLA Ops:
  1.6 4.3 %collective-permute-start = (bf16[1,80,256]{2,1,0:T(8,128)(2,1)S(1)}, bf16[1,80,256]{2,1,0:T(8,128)(2,1)S(1)}, u32[]{:S(2)}, u32[]{:S(2)}) collective-permute-start(bf16[1,80,256]{2,1,0:T(8,128)(2,1)S(1)} %shard_map.112), channel_id=1, source_target_pairs={{0,0},{1,8},{2,16},{3,24},{4,4},{5,12},{6,20},{7,28},{8,32},{9,40}... | collective-permute-start | bytes 122888 | tf_op jit(solution)/shard_map/ppermute | solution.py:294
  5.8 61.5 %copy-start.4 = (s32[1,32]{1,0:T(1,128)S(1)}, s32[1,32]{1,0:T(1,128)}, u32[]{:S(2)}) copy-start(s32[1,32]{1,0:T(1,128)} %param.14) | copy-start | bytes 388
  5.8 61.5 %copy-start.5 = (s32[32]{0:T(128)S(1)}, s32[32]{0:T(128)}, u32[]{:S(2)}) copy-start(s32[32]{0:T(128)} %order_ref.1) | copy-start | bytes 388
  5.8 52.5 %all-to-all-start = ((bf16[8,128,1280]{2,1,0:T(8,128)(2,1)}), bf16[8,128,1280]{2,1,0:T(8,128)(2,1)S(1)}, u32[]{:S(2)}, u32[]{:S(2)}) async-start(bf16[8,128,1280]{2,1,0:T(8,128)(2,1)} %shard_map.111), calls=%async_computation | async-start | bytes 5242880 | tf_op jit(solution)/shard_map/all_to_all | solution.py:277
  19.5 7.9 %collective-permute-start.4 = (bf16[1,80,256]{2,1,0:T(8,128)(2,1)S(1)}, bf16[1,80,256]{2,1,0:T(8,128)(2,1)S(1)}, u32[]{:S(2)}, u32[]{:S(2)}) collective-permute-start(bf16[1,80,256]{2,1,0:T(8,128)(2,1)S(1)} %collective-permute-done.near_ref), channel_id=1, source_target_pairs={{0,128},{32,160},{64,192},{96,224},{128,0},{160,32},{192,64},{224,... | collective-permute-start | bytes 122888 | tf_op jit(solution)/shard_map/ppermute | solution.py:269
  27.4 8.5 %collective-permute-start.5 = (bf16[2,80,256]{2,1,0:T(8,128)(2,1)S(1)}, bf16[2,80,256]{2,1,0:T(8,128)(2,1)S(1)}, u32[]{:S(2)}, u32[]{:S(2)}) collective-permute-start(bf16[2,80,256]{2,1,0:T(8,128)(2,1)S(1)} %shard_map.114.near_ref), channel_id=1, source_target_pairs={{0,64},{32,96},{64,0},{96,32},{128,192},{160,224},{192,128},{224,1... | collective-permute-start | bytes 245768 | tf_op jit(solution)/shard_map/ppermute | solution.py:269
  33.2 21.1 %collective-permute-start.1 = (bf16[640,128]{1,0:T(8,128)(2,1)S(1)}, bf16[640,128]{1,0:T(8,128)(2,1)S(1)}, u32[]{:S(2)}, u32[]{:S(2)}) collective-permute-start(bf16[640,128]{1,0:T(8,128)(2,1)S(1)} %get-tuple-element.44), channel_id=1, source_target_pairs={{0,1},{1,2},{2,3},{3,0},{4,5},{5,6},{6,7},{7,4},{8,9},{9,10},{10,1... | collective-permute-start | bytes 491528 | tf_op jit(solution)/shard_map/ppermute | solution.py:273
  36.0 5.4 %collective-permute-start.6 = (bf16[4,80,256]{2,1,0:T(8,128)(2,1)S(1)}, bf16[4,80,256]{2,1,0:T(8,128)(2,1)S(1)}, u32[]{:S(2)}, u32[]{:S(2)}) collective-permute-start(bf16[4,80,256]{2,1,0:T(8,128)(2,1)S(1)} %shard_map.115.near_ref), channel_id=1, source_target_pairs={{0,32},{32,0},{64,96},{96,64},{128,160},{160,128},{192,224},{224,1... | collective-permute-start | bytes 491528 | tf_op jit(solution)/shard_map/ppermute | solution.py:269
  36.3 21.4 %collective-permute-start.2 = (bf16[640,128]{1,0:T(8,128)(2,1)S(1)}, bf16[640,128]{1,0:T(8,128)(2,1)S(1)}, u32[]{:S(2)}, u32[]{:S(2)}) collective-permute-start(bf16[640,128]{1,0:T(8,128)(2,1)S(1)} %get-tuple-element.45), channel_id=1, source_target_pairs={{0,2},{1,3},{2,0},{3,1},{4,6},{5,7},{6,4},{7,5},{8,10},{9,11},{10,... | collective-permute-start | bytes 491528 | tf_op jit(solution)/shard_map/ppermute | solution.py:273
  39.3 18.4 %collective-permute-start.3 = (bf16[640,128]{1,0:T(8,128)(2,1)S(1)}, bf16[640,128]{1,0:T(8,128)(2,1)S(1)}, u32[]{:S(2)}, u32[]{:S(2)}) collective-permute-start(bf16[640,128]{1,0:T(8,128)(2,1)S(1)} %get-tuple-element.46), channel_id=1, source_target_pairs={{0,3},{1,0},{2,1},{3,2},{4,7},{5,4},{6,5},{7,6},{8,11},{9,8},{10,9... | collective-permute-start | bytes 491528 | tf_op jit(solution)/shard_map/ppermute | solution.py:273
  58.4 18.8 %collective-permute-start.7 = (bf16[8,80,256]{2,1,0:T(8,128)(2,1)S(1)}, bf16[8,80,256]{2,1,0:T(8,128)(2,1)S(1)}, u32[]{:S(2)}, u32[]{:S(2)}) collective-permute-start(bf16[8,80,256]{2,1,0:T(8,128)(2,1)S(1)} %shard_map.116.near_ref), channel_id=1, source_target_pairs={{0,16},{16,0},{1,17},{17,1},{2,18},{18,2},{3,19},{19,3},{4,20},{20... | collective-permute-start | bytes 983048 | tf_op jit(solution)/shard_map/ppermute | solution.py:269
  77.2 24.0 %collective-permute-start.12 = (bf16[16,80,256]{2,1,0:T(8,128)(2,1)S(1)}, bf16[16,80,256]{2,1,0:T(8,128)(2,1)S(1)}, u32[]{:S(2)}, u32[]{:S(2)}) collective-permute-start(bf16[16,80,256]{2,1,0:T(8,128)(2,1)S(1)} %shard_map.118.w_ref), channel_id=1, source_target_pairs={{0,8},{8,0},{1,9},{9,1},{2,10},{10,2},{3,11},{11,3},{4,12},{12,4},... | collective-permute-start | bytes 1966088 | tf_op jit(solution)/shard_map/ppermute | solution.py:269
  77.3 8.7 %collective-permute-start.8 = (bf16[512,256]{1,0:T(8,128)(2,1)S(1)}, bf16[512,256]{1,0:T(8,128)(2,1)S(1)}, u32[]{:S(2)}, u32[]{:S(2)}) collective-permute-start(bf16[512,256]{1,0:T(8,128)(2,1)S(1)} %get-tuple-element.52), channel_id=1, source_target_pairs={{0,4},{4,0},{1,5},{5,1},{2,6},{6,2},{3,7},{7,3},{8,12},{12,8},{9,1... | collective-permute-start | bytes 786440 | tf_op jit(solution)/shard_map/ppermute | solution.py:363
  86.1 9.3 %collective-permute-start.11 = (bf16[512,256]{1,0:T(8,128)(2,1)S(1)}, bf16[512,256]{1,0:T(8,128)(2,1)S(1)}, u32[]{:S(2)}, u32[]{:S(2)}) collective-permute-start(bf16[512,256]{1,0:T(8,128)(2,1)S(1)} %shard_map.119.refs_0_), channel_id=1, source_target_pairs={{0,3},{1,0},{2,1},{3,2},{4,7},{5,4},{6,5},{7,6},{8,11},{9,8},{10,9... | collective-permute-start | bytes 786440 | tf_op jit(solution)/shard_map/ppermute | solution.py:273
  86.5 10.8 %collective-permute-start.10 = (bf16[512,256]{1,0:T(8,128)(2,1)S(1)}, bf16[512,256]{1,0:T(8,128)(2,1)S(1)}, u32[]{:S(2)}, u32[]{:S(2)}) collective-permute-start(bf16[512,256]{1,0:T(8,128)(2,1)S(1)} %shard_map.119.refs_0_), channel_id=1, source_target_pairs={{0,2},{1,3},{2,0},{3,1},{4,6},{5,7},{6,4},{7,5},{8,10},{9,11},{10,... | collective-permute-start | bytes 786440 | tf_op jit(solution)/shard_map/ppermute | solution.py:273
  87.8 13.5 %collective-permute-start.9 = (bf16[512,256]{1,0:T(8,128)(2,1)S(1)}, bf16[512,256]{1,0:T(8,128)(2,1)S(1)}, u32[]{:S(2)}, u32[]{:S(2)}) collective-permute-start(bf16[512,256]{1,0:T(8,128)(2,1)S(1)} %shard_map.119.refs_0_), channel_id=1, source_target_pairs={{0,1},{1,2},{2,3},{3,0},{4,5},{5,6},{6,7},{7,4},{8,9},{9,10},{10,1... | collective-permute-start | bytes 786440 | tf_op jit(solution)/shard_map/ppermute | solution.py:273
  102.6 2.1 %collective-permute-start.13 = (bf16[320,1024]{1,0:T(8,128)(2,1)S(1)}, bf16[320,1024]{1,0:T(8,128)(2,1)S(1)}, u32[]{:S(2)}, u32[]{:S(2)}) collective-permute-start(bf16[320,1024]{1,0:T(8,128)(2,1)S(1)} %get-tuple-element.65), channel_id=1, source_target_pairs={{0,8},{8,0},{1,9},{9,1},{2,10},{10,2},{3,11},{11,3},{4,12},{12,4},... | collective-permute-start | bytes 1966088 | tf_op jit(solution)/shard_map/ppermute | solution.py:269
  104.8 9.8 %collective-permute-start.14 = (bf16[160,1024]{1,0:T(8,128)(2,1)S(1)}, bf16[160,1024]{1,0:T(8,128)(2,1)S(1)}, u32[]{:S(2)}, u32[]{:S(2)}) collective-permute-start(bf16[160,1024]{1,0:T(8,128)(2,1)S(1)} %get-tuple-element.67), channel_id=1, source_target_pairs={{0,4},{4,0},{1,5},{5,1},{2,6},{6,2},{3,7},{7,3},{8,12},{12,8},{9,1... | collective-permute-start | bytes 983048 | tf_op jit(solution)/shard_map/ppermute | solution.py:415
  108.0 14.6 %all-to-all-start.1 = ((bf16[4,640,128]{2,1,0:T(8,128)(2,1)}), bf16[4,640,128]{2,1,0:T(8,128)(2,1)S(1)}, u32[]{:S(2)}, u32[]{:S(2)}) async-start(bf16[4,640,128]{2,1,0:T(8,128)(2,1)} %shard_map.121), calls=%async_computation.1 | async-start | bytes 1310720 | tf_op jit(solution)/shard_map/all_to_all | solution.py:277
  114.8 7.0 %collective-permute-start.15 = (bf16[80,1024]{1,0:T(8,128)(2,1)S(1)}, bf16[80,1024]{1,0:T(8,128)(2,1)S(1)}, u32[]{:S(2)}, u32[]{:S(2)}) collective-permute-start(bf16[80,1024]{1,0:T(8,128)(2,1)S(1)} %get-tuple-element.68), channel_id=1, source_target_pairs={{0,16},{16,0},{1,17},{17,1},{2,18},{18,2},{3,19},{19,3},{4,20},{20... | collective-permute-start | bytes 491528 | tf_op jit(solution)/shard_map/ppermute | solution.py:269
  122.6 23.2 %all-to-all-start.2 = ((bf16[8,128,512]{2,1,0:T(8,128)(2,1)}), bf16[8,128,512]{2,1,0:T(8,128)(2,1)S(1)}, u32[]{:S(2)}, u32[]{:S(2)}) async-start(bf16[8,128,512]{2,1,0:T(8,128)(2,1)} %get-tuple-element.70), calls=%async_computation.2 | async-start | bytes 2097152 | tf_op jit(solution)/shard_map/all_to_all | solution.py:277
  127.0 5.1 %collective-permute-start.16 = (bf16[40,1024]{1,0:T(8,128)(2,1)S(1)}, bf16[40,1024]{1,0:T(8,128)(2,1)S(1)}, u32[]{:S(2)}, u32[]{:S(2)}) collective-permute-start(bf16[40,1024]{1,0:T(8,128)(2,1)S(1)} %get-tuple-element.75), channel_id=1, source_target_pairs={{0,32},{32,0},{64,96},{96,64},{128,160},{160,128},{192,224},{224,1... | collective-permute-start | bytes 245768 | tf_op jit(solution)/shard_map/ppermute | solution.py:269
  132.2 5.1 %collective-permute-start.17 = (bf16[20,1024]{1,0:T(8,128)(2,1)S(1)}, bf16[20,1024]{1,0:T(8,128)(2,1)S(1)}, u32[]{:S(2)}, u32[]{:S(2)}) collective-permute-start(bf16[20,1024]{1,0:T(8,128)(2,1)S(1)} %get-tuple-element.77), channel_id=1, source_target_pairs={{0,64},{32,96},{64,0},{96,32},{128,192},{160,224},{192,128},{224,1... | collective-permute-start | bytes 122888 | tf_op jit(solution)/shard_map/ppermute | solution.py:269
  137.3 7.9 %collective-permute-start.18 = (bf16[10,1024]{1,0:T(8,128)(2,1)S(1)}, bf16[10,1024]{1,0:T(8,128)(2,1)S(1)}, u32[]{:S(2)}, u32[]{:S(2)}) collective-permute-start(bf16[10,1024]{1,0:T(8,128)(2,1)S(1)} %get-tuple-element.79), channel_id=1, source_target_pairs={{0,128},{32,160},{64,192},{96,224},{128,0},{160,32},{192,64},{224,... | collective-permute-start | bytes 61448 | tf_op jit(solution)/shard_map/ppermute | solution.py:269
  (4 other events, 62.3 us)

commit v6 on v5

--- a/solution.py
+++ b/solution.py
@@ -53,8 +53,8 @@
     return (device % 4) * 2 + device // 4
 
 
-def pack_kernel(q_ref, d_ref, k_ref, v_ref, out_ref, sems):
-    copies = []
+def pack_kernel(q_ref, d_ref, k_ref, v_ref, out_ref, packed, load_sems, store_sems):
+    loads, stores = [], []
     for dest in range(CTX):
         at = q_block(dest) * Q_COLS
         head = (dest % 4) * HEAD_WIDTH
@@ -65,16 +65,22 @@
             (k_ref, head, HEAD_WIDTH),
             (v_ref, head, HEAD_WIDTH),
         ):
-            copy = pltpu.make_async_copy(
+            load = pltpu.make_async_copy(
                 ref.at[:, first : first + width],
-                out_ref.at[dest, :, place : place + width],
-                sems.at[len(copies)],
+                packed.at[dest, :, place : place + width],
+                load_sems.at[len(loads)],
             )
-            copy.start()
-            copies.append(copy)
+            load.start()
+            loads.append(load)
             place += width
-    for copy in copies:
-        copy.wait()
+    for dest in range(CTX):
+        for load in loads[4 * dest : 4 * dest + 4]:
+            load.wait()
+        store = pltpu.make_async_copy(packed.at[dest], out_ref.at[dest], store_sems.at[dest])
+        store.start()
+        stores.append(store)
+    for store in stores:
+        store.wait()
 
 
 def tile_row(z, low, y):
@@ -99,8 +105,8 @@
 
 
 def attention_kernel(docs_ref, order_ref, *refs):
-    in_ref, dq_ref, keep_ref, send_ref = refs[:4]
-    q_s, d_s, k_s, v_s, kt_s, dq_s, dkv_s, place, begin = refs[4:]
+    in_ref, dq_ref, dq_far_ref, keep_ref, send_ref = refs[:5]
+    q_s, d_s, k_s, v_s, kt_s, dq_s, dkv_s, place, begin = refs[5:]
 
     first = lax.fori_loop(
         0, 17, lambda i, a: jnp.where(docs_ref[i] == docs_ref[i + 15], i, a), jnp.int32(0)
@@ -180,9 +186,12 @@
             rows = pl.ds(pl.multiple_of(place[half_y * 16 + t] * BLK, BLK), BLK)
             ref[block, 0:128] = (dkv_s[rows, 0:128] * SCALE).astype(ref.dtype)
             ref[block, 128:256] = dkv_s[rows, 128:256].astype(ref.dtype)
-    for st in range(32):
-        rows = pl.ds(pl.multiple_of(place[st] * BLK, BLK), BLK)
-        dq_ref[st // 4, (st % 4) * BLK : (st % 4 + 1) * BLK, :] = dq_s[rows, :]
+    for t in range(16):
+        for half_y, ref in ((y, dq_ref), (1 - y, dq_far_ref)):
+            rows = pl.ds(pl.multiple_of(place[half_y * 16 + t] * BLK, BLK), BLK)
+            for g in range(4):
+                at = g * 128 + (t % 4) * BLK
+                ref[t // 4, at : at + BLK, :] = dq_s[rows, g * 128 : (g + 1) * 128]
 
 
 def pair_kernel(keep_ref, taken_ref, out_ref):
@@ -221,9 +230,13 @@
     out_ref[...] = keep_ref[...] + got_ref[...].astype(jnp.float32)
 
 
-def slice_kernel(w_ref, out_ref):
-    at = pl.multiple_of(lax.axis_index("x") * 256, 256)
-    out_ref[0] = w_ref[:, pl.ds(at, 256)]
+def holds(z, x, step):
+    return z // 2 == x if step == 0 else z // 2 % 2 == x % 2
+
+
+def take_kernel(step, own_ref, got_ref, out_ref):
+    own = holds(lax.axis_index("z"), lax.axis_index("x"), step)
+    out_ref[...] = jnp.where(own, own_ref[...], got_ref[...])
 
 
 def join_kernel(near_ref, far_ref, out_ref):
@@ -232,35 +245,42 @@
     out_ref[n:] = far_ref[...]
 
 
-def input_kernel(kv_ref, w_ref, far_ref, out_ref, w_s):
-    f = lax.axis_index("z") * 4 + lax.axis_index("yh") * 2 + lax.axis_index("core")
-    for at in range(FSDP):
-        mask = sum(((at >> i) & 1) << bit for i, bit in enumerate(GATHER_BITS))
-        source = f ^ mask
-        rows = pl.ds(pl.multiple_of((source // 4) * 80, 80), 80)
-        cols = pl.ds(pl.multiple_of(lax.rem(source, 4) * 256, 256), 256)
-        w_s[rows, cols] = w_ref[at] if at < FSDP // 2 else far_ref[at - FSDP // 2]
+def input_kernel(kv_ref, w_ref, far_ref, dq_ref, dq_got_ref, *refs):
+    outs, w_s, tile = refs[:4], refs[4], refs[5]
+    z, yh, core = lax.axis_index("z"), lax.axis_index("yh"), lax.axis_index("core")
+    x, y = lax.axis_index("x"), lax.axis_index("y")
+    for at in range(8):
+        shard = ((z & 1) ^ (at & 1)) * 4 + (yh ^ (at // 2 % 2)) * 2 + (core ^ (at // 4))
+        rows = pl.ds(pl.multiple_of(shard * 80, 80), 80)
+        w_s[rows, :] = w_ref[at] if at < 4 else far_ref[at - 4]
     for j in range(2):
         rows = slice(j * 256, (j + 1) * 256)
-        tile = dot(w_s[...], kv_ref[rows, :], NT).astype(jnp.bfloat16)
-        out_ref[2 * j] = tile[:, 0:128]
-        out_ref[2 * j + 1] = tile[:, 128:256]
-
-
-def input_out_kernel(parts_ref, out_ref):
-    for x in range(4):
+        block = dot(w_s[...], kv_ref[rows, :], NT).astype(jnp.bfloat16)
+        tile[2 * j] = block[:, 0:128]
+        tile[2 * j + 1] = block[:, 128:256]
+    near = pl.multiple_of(FEAT_TILE + y * Q_COLS, 128)
+    far = pl.multiple_of(FEAT_TILE + (1 - y) * Q_COLS, 128)
+    for s in range(4):
+        dest = lax.rem(x + s, 4)
+        outs[s][0:FEAT_TILE, :] = tile[dest]
+        outs[s][pl.ds(near, Q_COLS), :] = dq_ref[dest]
+        outs[s][pl.ds(far, Q_COLS), :] = dq_got_ref[dest]
+
+
+def out_kernel(*refs):
+    parts, input_ref, query_ref = refs[:4], refs[4], refs[5]
+    x = lax.axis_index("x")
+    for s in range(4):
+        src = lax.rem(x + 4 - s, 4)
         for j in range(FEAT_TILE // 128):
-            at = x * FEAT_TILE + j * 128
-            out_ref[:, at : at + 128] = parts_ref[x, j * 128 : (j + 1) * 128, :].T
-
-
-def query_out_kernel(dq_ref, out_ref):
-    for src in range(CTX):
-        at = q_block(src) * Q_COLS
-        out_ref[:, at : at + Q_COLS] = dq_ref[src]
-
-
-GATHER_BITS = (4, 3, 2, 1, 0)
+            cols = pl.ds(pl.multiple_of(src * FEAT_TILE + j * 128, 128), 128)
+            input_ref[:, cols] = parts[s][j * 128 : (j + 1) * 128, :].T
+        for g in range(8):
+            cols = pl.ds(pl.multiple_of(src * 2 * Q_COLS + g * 128, 128), 128)
+            at = FEAT_TILE + g * 128
+            query_ref[:, cols] = parts[s][at : at + 128, :]
+
+
 BIT_AXES = (("core", 1), ("yh", 1), ("z", 1), ("z", 2), ("z", 4))
 
 
@@ -278,45 +298,47 @@
 
 
 def body(inputs, queries, keys, values, output_cotangent, key_value_weight, doc_ids, block_order):
-    tile = pl.pallas_call(
-        slice_kernel,
-        in_specs=[VMEM],
-        out_specs=VMEM,
-        out_shape=shape((1, 80, 256)),
-        compiler_params=params(2),
-        cost_estimate=cost(0, 200_000),
-    )(key_value_weight)
-    perm = []
-    for f1 in range(FSDP):
-        for c1 in range(CTX):
-            y1, x1 = c1 // 4, c1 % 4
-            perm.append((f1 * CTX + c1, ((f1 % 8) * 4 + x1) * CTX + y1 * 4 + f1 // 8))
-    tile = lax.ppermute(tile, ("z", "yh", "core", "y", "x"), perm)
-
-    def widen(tile, bit):
+    packed = pl.pallas_call(
+        pack_kernel,
+        in_specs=[HBM] * 4,
+        out_specs=HBM,
+        out_shape=shape((CTX, ROWS, PACK_COLS)),
+        scratch_shapes=[
+            pltpu.VMEM((CTX, ROWS, PACK_COLS), jnp.bfloat16),
+            pltpu.SemaphoreType.DMA((4 * CTX,)),
+            pltpu.SemaphoreType.DMA((CTX,)),
+        ],
+        compiler_params=params(56),
+        cost_estimate=cost(0, 5_000_000),
+    )(queries[0], output_cotangent[0], keys[0], values[0])
+    got = exchange(packed, ("y", "x"))
+
+    _, tile = lax.optimization_barrier((packed, key_value_weight))
+    for step in range(2):
+        mask = (4, 2)[step]
+        pairs = [(z * 4 + x, (z ^ mask) * 4 + x) for z in range(8) for x in range(4) if holds(z, x, step)]
+        tile = pl.pallas_call(
+            functools.partial(take_kernel, step),
+            in_specs=[VMEM] * 2,
+            out_specs=VMEM,
+            out_shape=shape((80, 1024)),
+            compiler_params=params(3),
+            cost_estimate=cost(0, 500_000),
+        )(tile, lax.ppermute(tile, ("z", "x"), pairs))
+
+    def widen(tile, tile_got):
         n = 2 * tile.shape[0]
         return pl.pallas_call(
             join_kernel,
             in_specs=[VMEM] * 2,
             out_specs=VMEM,
-            out_shape=shape((n, 80, 256)),
-            compiler_params=params(3),
-            cost_estimate=cost(0, n * 80_000),
-        )(tile, swap(tile, bit))
-
-    packed = pl.pallas_call(
-        pack_kernel,
-        in_specs=[HBM] * 4,
-        out_specs=VMEM,
-        out_shape=shape((CTX, ROWS, PACK_COLS)),
-        scratch_shapes=[pltpu.SemaphoreType.DMA((4 * CTX,))],
-        compiler_params=params(56),
-        cost_estimate=cost(0, 5_000_000),
-    )(queries[0], output_cotangent[0], keys[0], values[0])
-    packed, tile = lax.optimization_barrier((packed, tile))
-    got = exchange(packed, ("y", "x"))
-    for bit in GATHER_BITS[:3]:
-        tile = widen(tile, bit)
+            out_shape=shape((n, 80, 1024)),
+            compiler_params=params(4),
+            cost_estimate=cost(0, n * 330_000),
+        )(tile, tile_got)
+
+    tile = widen(tile[None], swap(tile[None], 2))
+    got, tile, inputs = lax.optimization_barrier((got, tile, inputs))
 
     turned = pl.pallas_call(
         turn_kernel,
@@ -330,17 +352,15 @@
         compiler_params=params(8),
         cost_estimate=cost(0, 1_300_000),
     )(inputs[0])
-
     got_x = [to_shift(turned[s], s) for s in range(4)]
-    got, got_x, tile = lax.optimization_barrier((got, got_x, tile))
-    tile = widen(tile, GATHER_BITS[3])
-
-    dq_parts, keep, send = pl.pallas_call(
+
+    dq_near, dq_far, keep, send = pl.pallas_call(
         attention_kernel,
         in_specs=[SMEM] * 2 + [VMEM],
-        out_specs=[VMEM] * 3,
+        out_specs=[VMEM] * 4,
         out_shape=[
-            shape((CTX, ROWS, Q_COLS)),
+            shape((4, Q_COLS, ROWS)),
+            shape((4, Q_COLS, ROWS)),
             shape((SLAB // 2, 2 * HEAD_WIDTH), jnp.float32),
             shape((SLAB // 2, 2 * HEAD_WIDTH)),
         ],
@@ -359,9 +379,11 @@
         cost_estimate=cost(10_000_000_000, 5_000_000),
     )(doc_ids[0], block_order, got)
 
-    send, tile = lax.optimization_barrier((send, tile))
+    send, got_x = lax.optimization_barrier((send, got_x))
     taken = lax.ppermute(send, "y", [(0, 1), (1, 0)])
-    far_tile = swap(tile, GATHER_BITS[4])
+    taken, tile, dq_far = lax.optimization_barrier((taken, tile, dq_far))
+    dq_got = lax.ppermute(dq_far, "y", [(0, 1), (1, 0)])
+    tile_got = swap(tile, 1)
     own_cols = pl.pallas_call(
         pair_kernel,
         in_specs=[VMEM] * 2,
@@ -371,7 +393,7 @@
         cost_estimate=cost(0, 2_000_000),
     )(keep, taken)
     pieces = [to_shift(own_cols, s) for s in range(4)]
-    pieces, far_tile = lax.optimization_barrier((pieces, far_tile))
+    pieces, dq_got, tile_got = lax.optimization_barrier((pieces, dq_got, tile_got))
 
     kv_half, kv_rows, wg_send, wg_keep = pl.pallas_call(
         weight_kernel,
@@ -389,16 +411,21 @@
     )(*pieces, *got_x)
 
     wg_got = swap(wg_send, 0)
+    tile = widen(tile, tile_got)
+    far_tile = swap(tile, 0)
     parts = pl.pallas_call(
         input_kernel,
-        in_specs=[VMEM] * 3,
-        out_specs=VMEM,
-        out_shape=shape((4, FEAT_TILE, ROWS)),
-        scratch_shapes=[pltpu.VMEM((FEAT_TILE, 1024), jnp.bfloat16)],
+        in_specs=[VMEM] * 5,
+        out_specs=[VMEM] * 4,
+        out_shape=[shape((FEAT_TILE + 2 * Q_COLS, ROWS))] * 4,
+        scratch_shapes=[
+            pltpu.VMEM((FEAT_TILE, 1024), jnp.bfloat16),
+            pltpu.VMEM((4, FEAT_TILE, ROWS), jnp.bfloat16),
+        ],
         compiler_params=params(12),
-        cost_estimate=cost(700_000_000, 4_000_000),
-    )(kv_half, tile, far_tile)
-    ig_got = exchange(parts, "x")
+        cost_estimate=cost(700_000_000, 6_000_000),
+    )(kv_half, tile, far_tile, dq_near, dq_got)
+    parts_got = [to_shift(parts[s], s) for s in range(4)]
 
     def halve(axis, mask, keep, got):
         rows = keep.shape[0] // 2
@@ -416,9 +443,6 @@
     for bit in (1, 2, 3, 4):
         wg_send, wg_keep = halve(*BIT_AXES[bit], wg_keep, wg_got)
         wg_got = swap(wg_send, bit)
-        if bit == 1:
-            wg_got, dq_parts = lax.optimization_barrier((wg_got, dq_parts))
-            dq_got = exchange(dq_parts, ("y", "x"))
     weight_grad = pl.pallas_call(
         add_kernel,
         in_specs=[VMEM] * 2,
@@ -428,22 +452,14 @@
         cost_estimate=cost(0, 100_000),
     )(wg_keep, wg_got)
 
-    query_grad = pl.pallas_call(
-        query_out_kernel,
-        in_specs=[VMEM],
-        out_specs=VMEM,
-        out_shape=shape((ROWS, HQ * HEAD_WIDTH)),
-        compiler_params=params(6),
-        cost_estimate=cost(0, 2_000_000),
-    )(dq_got)
-    input_grad = pl.pallas_call(
-        input_out_kernel,
-        in_specs=[VMEM],
-        out_specs=VMEM,
-        out_shape=shape((ROWS, FEATURES)),
-        compiler_params=params(6),
-        cost_estimate=cost(0, 1_300_000),
-    )(ig_got)
+    input_grad, query_grad = pl.pallas_call(
+        out_kernel,
+        in_specs=[VMEM] * 4,
+        out_specs=[VMEM] * 2,
+        out_shape=[shape((ROWS, FEATURES)), shape((ROWS, HQ * HEAD_WIDTH))],
+        compiler_params=params(8),
+        cost_estimate=cost(0, 3_300_000),
+    )(*parts_got)
     return (input_grad[None], query_grad[None], kv_rows[None], weight_grad)
 
 

time: 148 us -> 129 us (0.87)
  waiting for transfers between devices: 65.1 us -> 47.7 us
  Pallas kernels: 20.3 us -> 17.6 us
    ppermute x6 -> x9, waiting for transfers between devices: 29.3 us -> 6.46 us  [to_shift(): lax.ppermute(value, 'x', [(i, (i + s) % 4) for i in range(4)])]
    all_to_all x3 -> x1, starting transfers between devices: 21.5 us -> 5.9 us  [exchange(): return lax.all_to_all(value, axis, 0, 0, tiled=True)]
    ppermute x6 -> x9, starting transfers between devices: 7.78 us -> 19.2 us  [to_shift(): lax.ppermute(value, 'x', [(i, (i + s) % 4) for i in range(4)])]
    ppermute x1 -> x3, starting transfers between devices: 0.65 us -> 10.9 us  [the longest x2 10.4 us: body(): lax.ppermute(tile, ('z', 'x'), pairs)]
    ppermute x10 -> x8, starting transfers between devices: 26.6 us -> 20.6 us  [swap(): lax.ppermute(value, axis, [(i, i ^ mask) for i in range(8 if axis == 'z'...]
    ppermute x1 -> x3, waiting for transfers between devices: 0.01 us -> 5.73 us  [the longest x2 5.73 us: body(): lax.ppermute(tile, ('z', 'x'), pairs)]
    all_to_all x3 -> x1, waiting for transfers between devices: 0.85 us -> 6.2 us  [exchange(): return lax.all_to_all(value, axis, 0, 0, tiled=True)]
    ppermute x10 -> x8, waiting for transfers between devices: 24.2 us -> 21.1 us  [swap(): lax.ppermute(value, axis, [(i, i ^ mask) for i in range(8 if axis == 'z'...]
  transfers between devices with their start and end apart: 22 -> 23, of which waited for: 16 -> 14; matrix products, arithmetic and copies ran while one was open for 0% -> 0% of each run, Pallas kernels for 12% -> 10%
where the time goes in v6:
time: 129 us; the launch traced here: 127 us
  starting transfers between devices  59.4 us (46%)
  waiting for transfers between devices  47.7 us (37%)
  Pallas kernels  17.6 us (14%)
    ppermute x8, waiting for transfers between devices, swap(): lax.ppermute(value, axis, [(i, i ^ mask) for i in range(8 if axis == 'z'...  21.1 us
    ppermute x8, starting transfers between devices, swap(): lax.ppermute(value, axis, [(i, i ^ mask) for i in range(8 if axis == 'z'...  20.6 us
    ppermute x9, starting transfers between devices, to_shift(): lax.ppermute(value, 'x', [(i, (i + s) % 4) for i in range(4)])  19.2 us
    ppermute x2, starting transfers between devices, body(): lax.ppermute(tile, ('z', 'x'), pairs)  10.4 us
    pallas_call x1, Pallas kernels, body(): pl.pallas_call(attention_kernel, in_specs=[SMEM] * 2 + [VMEM], out_specs=...  8.97 us
    ppermute x9, waiting for transfers between devices, to_shift(): lax.ppermute(value, 'x', [(i, (i + s) % 4) for i in range(4)])  6.46 us
    ppermute x1, waiting for transfers between devices, body(): taken = lax.ppermute(send, 'y', [(0, 1), (1, 0)])  6.27 us
    all_to_all x1, waiting for transfers between devices, exchange(): return lax.all_to_all(value, axis, 0, 0, tiled=True)  6.2 us
  transfers between devices with their start and end apart: 23, of which 14 were waited for; matrix products, arithmetic and copies ran while one was open for 0% of the time, Pallas kernels for 10%

profile of v6, /device:TPU:8, one launch (start us, length us, event | category | flops | bytes accessed | tf_op | source)
XLA Modules:
  0.0 126.7 jit_solution(5945369584665883346)
XLA Ops:
  0.6 2.9 %shard_map.111 = bf16[8,128,1280]{2,1,0:T(8,128)(2,1)} custom-call(bf16[128,4096]{1,0:T(8,128)(2,1)} %bitcast.14, bf16[128,4096]{1,0:T(8,128)(2,1)} %bitcast.15, bf16[128,512]{1,0:T(8,128)(2,1)} %bitcast.16, bf16[128,512]{1,0:T(8,128)(2,1)} %bitcast.17), custom_call_target="tpu_custom_call" | custom-call | bytes 5000000 | tf_op jit(solution)/shard_map/pallas_call | solution.py:301
  3.6 5.9 %all-to-all-start = ((bf16[8,128,1280]{2,1,0:T(8,128)(2,1)}), bf16[8,128,1280]{2,1,0:T(8,128)(2,1)S(1)}, u32[]{:S(2)}, u32[]{:S(2)}) async-start(bf16[8,128,1280]{2,1,0:T(8,128)(2,1)} %shard_map.111), calls=%async_computation | async-start | bytes 5242880 | tf_op jit(solution)/shard_map/all_to_all | solution.py:297
  9.5 9.1 %collective-permute-start = (bf16[80,1024]{1,0:T(8,128)(2,1)S(1)}, bf16[80,1024]{1,0:T(8,128)(2,1)S(1)}, u32[]{:S(2)}, u32[]{:S(2)}) collective-permute-start(bf16[80,1024]{1,0:T(8,128)(2,1)S(1)} %copy-done.1), channel_id=1, source_target_pairs={{0,128},{32,160},{65,193},{97,225},{130,2},{162,34},{195,67},{227,... | collective-permute-start | bytes 491528 | tf_op jit(solution)/shard_map/ppermute | solution.py:327
  18.6 2.9 %collective-permute-done.got_ref = bf16[80,1024]{1,0:T(8,128)(2,1)S(1)} collective-permute-done((bf16[80,1024]{1,0:T(8,128)(2,1)S(1)}, bf16[80,1024]{1,0:T(8,128)(2,1)S(1)}, u32[]{:S(2)}, u32[]{:S(2)}) %collective-permute-start) | collective-permute-done | bytes 163872 | tf_op jit(solution)/shard_map/ppermute | solution.py:327
  22.8 2.9 %collective-permute-done.1.got_ref = bf16[80,1024]{1,0:T(8,128)(2,1)S(1)} collective-permute-done((bf16[80,1024]{1,0:T(8,128)(2,1)S(1)}, bf16[80,1024]{1,0:T(8,128)(2,1)S(1)}, u32[]{:S(2)}, u32[]{:S(2)}) %collective-permute-start.1) | collective-permute-done | bytes 163872 | tf_op jit(solution)/shard_map/ppermute | solution.py:327
  25.7 4.4 %collective-permute-start.2 = (bf16[1,80,1024]{2,1,0:T(8,128)(2,1)S(1)}, bf16[1,80,1024]{2,1,0:T(8,128)(2,1)S(1)}, u32[]{:S(2)}, u32[]{:S(2)}) collective-permute-start(bf16[1,80,1024]{2,1,0:T(8,128)(2,1)S(1)} %bitcast.11), channel_id=1, source_target_pairs={{0,32},{32,0},{64,96},{96,64},{128,160},{160,128},{192,224},{224,1... | collective-permute-start | bytes 491528 | tf_op jit(solution)/shard_map/ppermute | solution.py:289
  30.1 4.3 %collective-permute-done.2.far_ref = bf16[1,80,1024]{2,1,0:T(8,128)(2,1)S(1)} collective-permute-done((bf16[1,80,1024]{2,1,0:T(8,128)(2,1)S(1)}, bf16[1,80,1024]{2,1,0:T(8,128)(2,1)S(1)}, u32[]{:S(2)}, u32[]{:S(2)}) %collective-permute-start.2) | collective-permute-done | bytes 163872 | tf_op jit(solution)/shard_map/ppermute | solution.py:289
  34.4 6.2 %all-to-all-done.refs_0_ = bf16[8,128,1280]{2,1,0:T(8,128)(2,1)S(1)} async-done(((bf16[8,128,1280]{2,1,0:T(8,128)(2,1)}), bf16[8,128,1280]{2,1,0:T(8,128)(2,1)S(1)}, u32[]{:S(2)}, u32[]{:S(2)}) %all-to-all-start) | async-done | bytes 2621472 | tf_op jit(solution)/shard_map/all_to_all | solution.py:297
  42.2 4.7 %collective-permute-start.3 = (bf16[640,128]{1,0:T(8,128)(2,1)S(1)}, bf16[640,128]{1,0:T(8,128)(2,1)S(1)}, u32[]{:S(2)}, u32[]{:S(2)}) collective-permute-start(bf16[640,128]{1,0:T(8,128)(2,1)S(1)} %get-tuple-element.56), channel_id=1, source_target_pairs={{0,1},{1,2},{2,3},{3,0},{4,5},{5,6},{6,7},{7,4},{8,9},{9,10},{10,1... | collective-permute-start | bytes 491528 | tf_op jit(solution)/shard_map/ppermute | solution.py:293
  46.8 4.5 %collective-permute-start.4 = (bf16[640,128]{1,0:T(8,128)(2,1)S(1)}, bf16[640,128]{1,0:T(8,128)(2,1)S(1)}, u32[]{:S(2)}, u32[]{:S(2)}) collective-permute-start(bf16[640,128]{1,0:T(8,128)(2,1)S(1)} %get-tuple-element.57), channel_id=1, source_target_pairs={{0,2},{1,3},{2,0},{3,1},{4,6},{5,7},{6,4},{7,5},{8,10},{9,11},{10,... | collective-permute-start | bytes 491528 | tf_op jit(solution)/shard_map/ppermute | solution.py:293
  51.4 9.0 %shard_map.115 = (bf16[4,512,128]{2,1,0:T(8,128)(2,1)S(1)}, bf16[4,512,128]{2,1,0:T(8,128)(2,1)S(1)}, f32[512,256]{1,0:T(8,128)S(1)}, bf16[512,256]{1,0:T(8,128)(2,1)S(1)}) custom-call(s32[32]{0:T(128)S(1)} %bitcast.13, s32[32]{0:T(128)S(1)} %copy-done.3, bf16[8,128,1280]{2,1,0:T(8,128)(2,1)S(1)} %all-to-all-done.refs_0_), custom_call_target="tpu_custom_call" | custom-call | flops 10000000000 | bytes 5000000 | tf_op jit(solution)/shard_map/pallas_call | solution.py:357
  61.0 6.3 %collective-permute-done.6.taken_ref = bf16[512,256]{1,0:T(8,128)(2,1)S(1)} collective-permute-done((bf16[512,256]{1,0:T(8,128)(2,1)S(1)}, bf16[512,256]{1,0:T(8,128)(2,1)S(1)}, u32[]{:S(2)}, u32[]{:S(2)}) %collective-permute-start.6) | collective-permute-done | bytes 262176 | tf_op jit(solution)/shard_map/ppermute | solution.py:383
  67.9 2.3 %collective-permute-start.11 = (bf16[2,80,1024]{2,1,0:T(8,128)(2,1)S(1)}, bf16[2,80,1024]{2,1,0:T(8,128)(2,1)S(1)}, u32[]{:S(2)}, u32[]{:S(2)}) collective-permute-start(bf16[2,80,1024]{2,1,0:T(8,128)(2,1)S(1)} %shard_map.114.near_ref), channel_id=1, source_target_pairs={{0,16},{16,0},{1,17},{17,1},{2,18},{18,2},{3,19},{19,3},{4,20},{20... | collective-permute-start | bytes 983048 | tf_op jit(solution)/shard_map/ppermute | solution.py:289
  70.2 2.4 %collective-permute-start.7 = (bf16[512,256]{1,0:T(8,128)(2,1)S(1)}, bf16[512,256]{1,0:T(8,128)(2,1)S(1)}, u32[]{:S(2)}, u32[]{:S(2)}) collective-permute-start(bf16[512,256]{1,0:T(8,128)(2,1)S(1)} %shard_map.117.refs_0_), channel_id=1, source_target_pairs={{0,1},{1,2},{2,3},{3,0},{4,5},{5,6},{6,7},{7,4},{8,9},{9,10},{10,1... | collective-permute-start | bytes 786440 | tf_op jit(solution)/shard_map/ppermute | solution.py:293
  72.6 2.8 %collective-permute-start.9 = (bf16[512,256]{1,0:T(8,128)(2,1)S(1)}, bf16[512,256]{1,0:T(8,128)(2,1)S(1)}, u32[]{:S(2)}, u32[]{:S(2)}) collective-permute-start(bf16[512,256]{1,0:T(8,128)(2,1)S(1)} %shard_map.117.refs_0_), channel_id=1, source_target_pairs={{0,3},{1,0},{2,1},{3,2},{4,7},{5,4},{6,5},{7,6},{8,11},{9,8},{10,9... | collective-permute-start | bytes 786440 | tf_op jit(solution)/shard_map/ppermute | solution.py:293
  75.4 5.8 %collective-permute-done.7.refs_1_ = bf16[512,256]{1,0:T(8,128)(2,1)S(1)} collective-permute-done((bf16[512,256]{1,0:T(8,128)(2,1)S(1)}, bf16[512,256]{1,0:T(8,128)(2,1)S(1)}, u32[]{:S(2)}, u32[]{:S(2)}) %collective-permute-start.7) | collective-permute-done | bytes 262176 | tf_op jit(solution)/shard_map/ppermute | solution.py:293
  81.8 4.1 %collective-permute-done.11.far_ref = bf16[2,80,1024]{2,1,0:T(8,128)(2,1)S(1)} collective-permute-done((bf16[2,80,1024]{2,1,0:T(8,128)(2,1)S(1)}, bf16[2,80,1024]{2,1,0:T(8,128)(2,1)S(1)}, u32[]{:S(2)}, u32[]{:S(2)}) %collective-permute-start.11) | collective-permute-done | bytes 327712 | tf_op jit(solution)/shard_map/ppermute | solution.py:289
  89.5 2.2 %collective-permute-start.17 = (bf16[160,1024]{1,0:T(8,128)(2,1)S(1)}, bf16[160,1024]{1,0:T(8,128)(2,1)S(1)}, u32[]{:S(2)}, u32[]{:S(2)}) collective-permute-start(bf16[160,1024]{1,0:T(8,128)(2,1)S(1)} %get-tuple-element.87), channel_id=1, source_target_pairs={{0,4},{4,0},{1,5},{5,1},{2,6},{6,2},{3,7},{7,3},{8,12},{12,8},{9,1... | collective-permute-start | bytes 983048 | tf_op jit(solution)/shard_map/ppermute | solution.py:442
  92.9 2.1 %collective-permute-start.13 = (bf16[1664,128]{1,0:T(8,128)(2,1)S(1)}, bf16[1664,128]{1,0:T(8,128)(2,1)S(1)}, u32[]{:S(2)}, u32[]{:S(2)}) collective-permute-start(bf16[1664,128]{1,0:T(8,128)(2,1)S(1)} %get-tuple-element.78), channel_id=1, source_target_pairs={{0,1},{1,2},{2,3},{3,0},{4,5},{5,6},{6,7},{7,4},{8,9},{9,10},{10,1... | collective-permute-start | bytes 1277960 | tf_op jit(solution)/shard_map/ppermute | solution.py:293
  95.0 2.7 %collective-permute-start.15 = (bf16[1664,128]{1,0:T(8,128)(2,1)S(1)}, bf16[1664,128]{1,0:T(8,128)(2,1)S(1)}, u32[]{:S(2)}, u32[]{:S(2)}) collective-permute-start(bf16[1664,128]{1,0:T(8,128)(2,1)S(1)} %get-tuple-element.80), channel_id=1, source_target_pairs={{0,3},{1,0},{2,1},{3,2},{4,7},{5,4},{6,5},{7,6},{8,11},{9,8},{10,9... | collective-permute-start | bytes 1277960 | tf_op jit(solution)/shard_map/ppermute | solution.py:293
  100.8 6.3 %collective-permute-done.18.got_ref = bf16[80,1024]{1,0:T(8,128)(2,1)S(1)} collective-permute-done((bf16[80,1024]{1,0:T(8,128)(2,1)S(1)}, bf16[80,1024]{1,0:T(8,128)(2,1)S(1)}, u32[]{:S(2)}, u32[]{:S(2)}) %collective-permute-start.18) | collective-permute-done | bytes 163872 | tf_op jit(solution)/shard_map/ppermute | solution.py:289
  109.2 2.5 %collective-permute-done.19.got_ref = bf16[40,1024]{1,0:T(8,128)(2,1)S(1)} collective-permute-done((bf16[40,1024]{1,0:T(8,128)(2,1)S(1)}, bf16[40,1024]{1,0:T(8,128)(2,1)S(1)}, u32[]{:S(2)}, u32[]{:S(2)}) %collective-permute-start.19) | collective-permute-done | bytes 81952 | tf_op jit(solution)/shard_map/ppermute | solution.py:289
  111.7 3.4 %collective-permute-start.20 = (bf16[20,1024]{1,0:T(8,128)(2,1)S(1)}, bf16[20,1024]{1,0:T(8,128)(2,1)S(1)}, u32[]{:S(2)}, u32[]{:S(2)}) collective-permute-start(bf16[20,1024]{1,0:T(8,128)(2,1)S(1)} %get-tuple-element.93), channel_id=1, source_target_pairs={{0,64},{32,96},{64,0},{96,32},{128,192},{160,224},{192,128},{224,1... | collective-permute-start | bytes 122888 | tf_op jit(solution)/shard_map/ppermute | solution.py:289
  117.2 6.9 %collective-permute-start.21 = (bf16[10,1024]{1,0:T(8,128)(2,1)S(1)}, bf16[10,1024]{1,0:T(8,128)(2,1)S(1)}, u32[]{:S(2)}, u32[]{:S(2)}) collective-permute-start(bf16[10,1024]{1,0:T(8,128)(2,1)S(1)} %get-tuple-element.95), channel_id=1, source_target_pairs={{0,128},{32,160},{64,192},{96,224},{128,0},{160,32},{192,64},{224,... | collective-permute-start | bytes 61448 | tf_op jit(solution)/shard_map/ppermute | solution.py:289
  (47 shorter events, 19.4 us)
Async XLA Ops:
  3.6 47.8 %copy-start.2 = (s32[1,32]{1,0:T(1,128)S(1)}, s32[1,32]{1,0:T(1,128)}, u32[]{:S(2)}) copy-start(s32[1,32]{1,0:T(1,128)} %param.14) | copy-start | bytes 388
  3.6 37.0 %all-to-all-start = ((bf16[8,128,1280]{2,1,0:T(8,128)(2,1)}), bf16[8,128,1280]{2,1,0:T(8,128)(2,1)S(1)}, u32[]{:S(2)}, u32[]{:S(2)}) async-start(bf16[8,128,1280]{2,1,0:T(8,128)(2,1)} %shard_map.111), calls=%async_computation | async-start | bytes 5242880 | tf_op jit(solution)/shard_map/all_to_all | solution.py:297
  9.5 12.0 %collective-permute-start = (bf16[80,1024]{1,0:T(8,128)(2,1)S(1)}, bf16[80,1024]{1,0:T(8,128)(2,1)S(1)}, u32[]{:S(2)}, u32[]{:S(2)}) collective-permute-start(bf16[80,1024]{1,0:T(8,128)(2,1)S(1)} %copy-done.1), channel_id=1, source_target_pairs={{0,128},{32,160},{65,193},{97,225},{130,2},{162,34},{195,67},{227,... | collective-permute-start | bytes 491528 | tf_op jit(solution)/shard_map/ppermute | solution.py:327
  21.5 4.2 %collective-permute-start.1 = (bf16[80,1024]{1,0:T(8,128)(2,1)S(1)}, bf16[80,1024]{1,0:T(8,128)(2,1)S(1)}, u32[]{:S(2)}, u32[]{:S(2)}) collective-permute-start(bf16[80,1024]{1,0:T(8,128)(2,1)S(1)} %shard_map.112.own_ref), channel_id=1, source_target_pairs={{0,64},{2,66},{32,96},{34,98},{65,1},{67,3},{97,33},{99,35},{128,1... | collective-permute-start | bytes 491528 | tf_op jit(solution)/shard_map/ppermute | solution.py:327
  25.7 8.7 %collective-permute-start.2 = (bf16[1,80,1024]{2,1,0:T(8,128)(2,1)S(1)}, bf16[1,80,1024]{2,1,0:T(8,128)(2,1)S(1)}, u32[]{:S(2)}, u32[]{:S(2)}) collective-permute-start(bf16[1,80,1024]{2,1,0:T(8,128)(2,1)S(1)} %bitcast.11), channel_id=1, source_target_pairs={{0,32},{32,0},{64,96},{96,64},{128,160},{160,128},{192,224},{224,1... | collective-permute-start | bytes 491528 | tf_op jit(solution)/shard_map/ppermute | solution.py:289
  42.2 18.2 %collective-permute-start.3 = (bf16[640,128]{1,0:T(8,128)(2,1)S(1)}, bf16[640,128]{1,0:T(8,128)(2,1)S(1)}, u32[]{:S(2)}, u32[]{:S(2)}) collective-permute-start(bf16[640,128]{1,0:T(8,128)(2,1)S(1)} %get-tuple-element.56), channel_id=1, source_target_pairs={{0,1},{1,2},{2,3},{3,0},{4,5},{5,6},{6,7},{7,4},{8,9},{9,10},{10,1... | collective-permute-start | bytes 491528 | tf_op jit(solution)/shard_map/ppermute | solution.py:293
  46.8 13.5 %collective-permute-start.4 = (bf16[640,128]{1,0:T(8,128)(2,1)S(1)}, bf16[640,128]{1,0:T(8,128)(2,1)S(1)}, u32[]{:S(2)}, u32[]{:S(2)}) collective-permute-start(bf16[640,128]{1,0:T(8,128)(2,1)S(1)} %get-tuple-element.57), channel_id=1, source_target_pairs={{0,2},{1,3},{2,0},{3,1},{4,6},{5,7},{6,4},{7,5},{8,10},{9,11},{10,... | collective-permute-start | bytes 491528 | tf_op jit(solution)/shard_map/ppermute | solution.py:293
  51.4 9.0 %collective-permute-start.5 = (bf16[640,128]{1,0:T(8,128)(2,1)S(1)}, bf16[640,128]{1,0:T(8,128)(2,1)S(1)}, u32[]{:S(2)}, u32[]{:S(2)}) collective-permute-start(bf16[640,128]{1,0:T(8,128)(2,1)S(1)} %get-tuple-element.58), channel_id=1, source_target_pairs={{0,3},{1,0},{2,1},{3,2},{4,7},{5,4},{6,5},{7,6},{8,11},{9,8},{10,9... | collective-permute-start | bytes 491528 | tf_op jit(solution)/shard_map/ppermute | solution.py:293
  60.4 6.9 %collective-permute-start.6 = (bf16[512,256]{1,0:T(8,128)(2,1)S(1)}, bf16[512,256]{1,0:T(8,128)(2,1)S(1)}, u32[]{:S(2)}, u32[]{:S(2)}) collective-permute-start(bf16[512,256]{1,0:T(8,128)(2,1)S(1)} %get-tuple-element.59), channel_id=1, source_target_pairs={{0,4},{4,0},{1,5},{5,1},{2,6},{6,2},{3,7},{7,3},{8,12},{12,8},{9,1... | collective-permute-start | bytes 786440 | tf_op jit(solution)/shard_map/ppermute | solution.py:383
  67.3 18.6 %collective-permute-start.10 = (bf16[4,512,128]{2,1,0:T(8,128)(2,1)S(1)}, bf16[4,512,128]{2,1,0:T(8,128)(2,1)S(1)}, u32[]{:S(2)}, u32[]{:S(2)}) collective-permute-start(bf16[4,512,128]{2,1,0:T(8,128)(2,1)S(1)} %get-tuple-element.63), channel_id=1, source_target_pairs={{0,4},{4,0},{1,5},{5,1},{2,6},{6,2},{3,7},{7,3},{8,12},{12,8},{9,1... | collective-permute-start | bytes 1572872 | tf_op jit(solution)/shard_map/ppermute | solution.py:385
  67.9 18.1 %collective-permute-start.11 = (bf16[2,80,1024]{2,1,0:T(8,128)(2,1)S(1)}, bf16[2,80,1024]{2,1,0:T(8,128)(2,1)S(1)}, u32[]{:S(2)}, u32[]{:S(2)}) collective-permute-start(bf16[2,80,1024]{2,1,0:T(8,128)(2,1)S(1)} %shard_map.114.near_ref), channel_id=1, source_target_pairs={{0,16},{16,0},{1,17},{17,1},{2,18},{18,2},{3,19},{19,3},{4,20},{20... | collective-permute-start | bytes 983048 | tf_op jit(solution)/shard_map/ppermute | solution.py:289
  70.2 11.0 %collective-permute-start.7 = (bf16[512,256]{1,0:T(8,128)(2,1)S(1)}, bf16[512,256]{1,0:T(8,128)(2,1)S(1)}, u32[]{:S(2)}, u32[]{:S(2)}) collective-permute-start(bf16[512,256]{1,0:T(8,128)(2,1)S(1)} %shard_map.117.refs_0_), channel_id=1, source_target_pairs={{0,1},{1,2},{2,3},{3,0},{4,5},{5,6},{6,7},{7,4},{8,9},{9,10},{10,1... | collective-permute-start | bytes 786440 | tf_op jit(solution)/shard_map/ppermute | solution.py:293
  72.6 8.6 %collective-permute-start.8 = (bf16[512,256]{1,0:T(8,128)(2,1)S(1)}, bf16[512,256]{1,0:T(8,128)(2,1)S(1)}, u32[]{:S(2)}, u32[]{:S(2)}) collective-permute-start(bf16[512,256]{1,0:T(8,128)(2,1)S(1)} %shard_map.117.refs_0_), channel_id=1, source_target_pairs={{0,2},{1,3},{2,0},{3,1},{4,6},{5,7},{6,4},{7,5},{8,10},{9,11},{10,... | collective-permute-start | bytes 786440 | tf_op jit(solution)/shard_map/ppermute | solution.py:293
  72.6 9.2 %collective-permute-start.9 = (bf16[512,256]{1,0:T(8,128)(2,1)S(1)}, bf16[512,256]{1,0:T(8,128)(2,1)S(1)}, u32[]{:S(2)}, u32[]{:S(2)}) collective-permute-start(bf16[512,256]{1,0:T(8,128)(2,1)S(1)} %shard_map.117.refs_0_), channel_id=1, source_target_pairs={{0,3},{1,0},{2,1},{3,2},{4,7},{5,4},{6,5},{7,6},{8,11},{9,8},{10,9... | collective-permute-start | bytes 786440 | tf_op jit(solution)/shard_map/ppermute | solution.py:293
  87.3 2.1 %collective-permute-start.16 = (bf16[320,1024]{1,0:T(8,128)(2,1)S(1)}, bf16[320,1024]{1,0:T(8,128)(2,1)S(1)}, u32[]{:S(2)}, u32[]{:S(2)}) collective-permute-start(bf16[320,1024]{1,0:T(8,128)(2,1)S(1)} %get-tuple-element.85), channel_id=1, source_target_pairs={{0,8},{8,0},{1,9},{9,1},{2,10},{10,2},{3,11},{11,3},{4,12},{12,4},... | collective-permute-start | bytes 1966088 | tf_op jit(solution)/shard_map/ppermute | solution.py:289
  87.3 4.4 %collective-permute-start.12 = (bf16[4,80,1024]{2,1,0:T(8,128)(2,1)S(1)}, bf16[4,80,1024]{2,1,0:T(8,128)(2,1)S(1)}, u32[]{:S(2)}, u32[]{:S(2)}) collective-permute-start(bf16[4,80,1024]{2,1,0:T(8,128)(2,1)S(1)} %shard_map.119.w_ref), channel_id=1, source_target_pairs={{0,8},{8,0},{1,9},{9,1},{2,10},{10,2},{3,11},{11,3},{4,12},{12,4},... | collective-permute-start | bytes 1966088 | tf_op jit(solution)/shard_map/ppermute | solution.py:289
  89.5 10.2 %collective-permute-start.17 = (bf16[160,1024]{1,0:T(8,128)(2,1)S(1)}, bf16[160,1024]{1,0:T(8,128)(2,1)S(1)}, u32[]{:S(2)}, u32[]{:S(2)}) collective-permute-start(bf16[160,1024]{1,0:T(8,128)(2,1)S(1)} %get-tuple-element.87), channel_id=1, source_target_pairs={{0,4},{4,0},{1,5},{5,1},{2,6},{6,2},{3,7},{7,3},{8,12},{12,8},{9,1... | collective-permute-start | bytes 983048 | tf_op jit(solution)/shard_map/ppermute | solution.py:442
  92.9 31.3 %collective-permute-start.13 = (bf16[1664,128]{1,0:T(8,128)(2,1)S(1)}, bf16[1664,128]{1,0:T(8,128)(2,1)S(1)}, u32[]{:S(2)}, u32[]{:S(2)}) collective-permute-start(bf16[1664,128]{1,0:T(8,128)(2,1)S(1)} %get-tuple-element.78), channel_id=1, source_target_pairs={{0,1},{1,2},{2,3},{3,0},{4,5},{5,6},{6,7},{7,4},{8,9},{9,10},{10,1... | collective-permute-start | bytes 1277960 | tf_op jit(solution)/shard_map/ppermute | solution.py:293
  95.0 29.2 %collective-permute-start.14 = (bf16[1664,128]{1,0:T(8,128)(2,1)S(1)}, bf16[1664,128]{1,0:T(8,128)(2,1)S(1)}, u32[]{:S(2)}, u32[]{:S(2)}) collective-permute-start(bf16[1664,128]{1,0:T(8,128)(2,1)S(1)} %get-tuple-element.79), channel_id=1, source_target_pairs={{0,2},{1,3},{2,0},{3,1},{4,6},{5,7},{6,4},{7,5},{8,10},{9,11},{10,... | collective-permute-start | bytes 1277960 | tf_op jit(solution)/shard_map/ppermute | solution.py:293
  95.0 29.1 %collective-permute-start.15 = (bf16[1664,128]{1,0:T(8,128)(2,1)S(1)}, bf16[1664,128]{1,0:T(8,128)(2,1)S(1)}, u32[]{:S(2)}, u32[]{:S(2)}) collective-permute-start(bf16[1664,128]{1,0:T(8,128)(2,1)S(1)} %get-tuple-element.80), channel_id=1, source_target_pairs={{0,3},{1,0},{2,1},{3,2},{4,7},{5,4},{6,5},{7,6},{8,11},{9,8},{10,9... | collective-permute-start | bytes 1277960 | tf_op jit(solution)/shard_map/ppermute | solution.py:293
  99.8 7.3 %collective-permute-start.18 = (bf16[80,1024]{1,0:T(8,128)(2,1)S(1)}, bf16[80,1024]{1,0:T(8,128)(2,1)S(1)}, u32[]{:S(2)}, u32[]{:S(2)}) collective-permute-start(bf16[80,1024]{1,0:T(8,128)(2,1)S(1)} %get-tuple-element.89), channel_id=1, source_target_pairs={{0,16},{16,0},{1,17},{17,1},{2,18},{18,2},{3,19},{19,3},{4,20},{20... | collective-permute-start | bytes 491528 | tf_op jit(solution)/shard_map/ppermute | solution.py:289
  107.2 4.5 %collective-permute-start.19 = (bf16[40,1024]{1,0:T(8,128)(2,1)S(1)}, bf16[40,1024]{1,0:T(8,128)(2,1)S(1)}, u32[]{:S(2)}, u32[]{:S(2)}) collective-permute-start(bf16[40,1024]{1,0:T(8,128)(2,1)S(1)} %get-tuple-element.91), channel_id=1, source_target_pairs={{0,32},{32,0},{64,96},{96,64},{128,160},{160,128},{192,224},{224,1... | collective-permute-start | bytes 245768 | tf_op jit(solution)/shard_map/ppermute | solution.py:289
  111.7 5.4 %collective-permute-start.20 = (bf16[20,1024]{1,0:T(8,128)(2,1)S(1)}, bf16[20,1024]{1,0:T(8,128)(2,1)S(1)}, u32[]{:S(2)}, u32[]{:S(2)}) collective-permute-start(bf16[20,1024]{1,0:T(8,128)(2,1)S(1)} %get-tuple-element.93), channel_id=1, source_target_pairs={{0,64},{32,96},{64,0},{96,32},{128,192},{160,224},{192,128},{224,1... | collective-permute-start | bytes 122888 | tf_op jit(solution)/shard_map/ppermute | solution.py:289
  117.2 8.8 %collective-permute-start.21 = (bf16[10,1024]{1,0:T(8,128)(2,1)S(1)}, bf16[10,1024]{1,0:T(8,128)(2,1)S(1)}, u32[]{:S(2)}, u32[]{:S(2)}) collective-permute-start(bf16[10,1024]{1,0:T(8,128)(2,1)S(1)} %get-tuple-element.95), channel_id=1, source_target_pairs={{0,128},{32,160},{64,192},{96,224},{128,0},{160,32},{192,64},{224,... | collective-permute-start | bytes 61448 | tf_op jit(solution)/shard_map/ppermute | solution.py:289
  (3 other events, 54.8 us)

commit v7 on v6

--- a/solution.py
+++ b/solution.py
@@ -84,8 +84,7 @@
 
 
 def tile_row(z, low, y):
-    row = (low % 2) * 320 + y * 160 + (low // 2) * 80
-    return row + (z % 2) * 40 + (z // 2 % 2) * 20 + (z // 4) * 10
+    return (low % 2) * 320 + (low // 2) * 160 + y * 80 + (z // 2) * 20 + (z % 2) * 10
 
 
 def turn_kernel(in_ref, *refs):
@@ -104,10 +103,7 @@
         outs[s][...] = tile[lax.rem(lax.axis_index("x") + s, 4)].astype(jnp.bfloat16)
 
 
-def attention_kernel(docs_ref, order_ref, *refs):
-    in_ref, dq_ref, dq_far_ref, keep_ref, send_ref = refs[:5]
-    q_s, d_s, k_s, v_s, kt_s, dq_s, dkv_s, place, begin = refs[5:]
-
+def place_blocks(docs_ref, order_ref, place):
     first = lax.fori_loop(
         0, 17, lambda i, a: jnp.where(docs_ref[i] == docs_ref[i + 15], i, a), jnp.int32(0)
     )
@@ -119,6 +115,17 @@
         return carry
 
     lax.fori_loop(0, 32, place_block, 0)
+    return first
+
+
+def tile_begin(i):
+    return 64 * i * (i + 1)
+
+
+def attention_kernel(docs_ref, order_ref, *refs):
+    in_ref, grad_ref, kt_ref, keep_ref, send_ref = refs[:5]
+    q_s, d_s, k_s, v_s, dkv_s, place, begin = refs[5:]
+    first = place_blocks(docs_ref, order_ref, place)
 
     def begin_block(t, carry):
         last_doc, last_begin = carry
@@ -138,7 +145,7 @@
         k_s[rows, :] = in_ref[src, block, 2 * Q_COLS : 2 * Q_COLS + HEAD_WIDTH]
         v_s[rows, :] = in_ref[src, block, 2 * Q_COLS + HEAD_WIDTH :]
     for j in range(SLAB // 128):
-        kt_s[:, j * 128 : (j + 1) * 128] = k_s[j * 128 : (j + 1) * 128, :].T
+        kt_ref[:, j * 128 : (j + 1) * 128] = k_s[j * 128 : (j + 1) * 128, :].T
     dkv_s[...] = jnp.zeros_like(dkv_s)
 
     def half(hf, carry):
@@ -172,9 +179,7 @@
                 probs_low = probs.astype(jnp.bfloat16)
                 dkv_s[keys, 0:128] += dot(score_grad, qs, NN)
                 dkv_s[keys, 128:256] += dot(probs_low, ds, NN)
-                dqt = dot(kt_s[:, keys], score_grad, NN) * SCALE
-                for e in range(2):
-                    dq_s[rows, cols[e]] = dqt[:, e * 128 : (e + 1) * 128].T.astype(jnp.bfloat16)
+                grad_ref[hf, g, tile_begin(i) : tile_begin(i) + n, :] = score_grad
         return carry
 
     lax.fori_loop(0, 2, half, 0)
@@ -186,8 +191,23 @@
             rows = pl.ds(pl.multiple_of(place[half_y * 16 + t] * BLK, BLK), BLK)
             ref[block, 0:128] = (dkv_s[rows, 0:128] * SCALE).astype(ref.dtype)
             ref[block, 128:256] = dkv_s[rows, 128:256].astype(ref.dtype)
+
+def query_kernel(docs_ref, order_ref, grad_ref, kt_ref, near_ref, far_ref, dq_s, place):
+    place_blocks(docs_ref, order_ref, place)
+    for hf in range(2):
+        for i in range(HALF // 128):
+            n = (i + 1) * 128
+            rows = slice(hf * HALF + i * 128, hf * HALF + (i + 1) * 128)
+            for g in range(2):
+                part = grad_ref[hf, g, tile_begin(i) : tile_begin(i) + n, :]
+                dqt = dot(kt_ref[:, hf * HALF : hf * HALF + n], part, NN) * SCALE
+                for e in range(2):
+                    at = (2 * g + e) * 128
+                    block = dqt[:, e * 128 : (e + 1) * 128].T
+                    dq_s[rows, at : at + 128] = block.astype(jnp.bfloat16)
+    y = lax.axis_index("y")
     for t in range(16):
-        for half_y, ref in ((y, dq_ref), (1 - y, dq_far_ref)):
+        for half_y, ref in ((y, near_ref), (1 - y, far_ref)):
             rows = pl.ds(pl.multiple_of(place[half_y * 16 + t] * BLK, BLK), BLK)
             for g in range(4):
                 at = g * 128 + (t % 4) * BLK
@@ -217,13 +237,19 @@
     kv_rows_ref[...] = kv_ref[pl.ds(pl.multiple_of(x * ROWS, ROWS), ROWS), :]
 
 
-def halve_kernel(axis, mask, keep_ref, got_ref, send_ref, kept_ref):
-    part = kept_ref.shape[0]
-    total = keep_ref[...] + got_ref[...].astype(jnp.float32)
-    low, high = total[:part, :], total[part:, :]
-    upper = (lax.axis_index(axis) & mask) != 0
-    send_ref[...] = jnp.where(upper, low, high).astype(send_ref.dtype)
-    kept_ref[...] = jnp.where(upper, high, low)
+def split_kernel(number, count, *refs):
+    count_in = len(refs) - count - 1
+    ins, sends, keep_ref, parts = refs[:count_in], refs[count_in:-2], refs[-2], refs[-1]
+    total = ins[0][...]
+    for ref in ins[1:]:
+        total = total + ref[...].astype(jnp.float32)
+    rows = keep_ref.shape[0]
+    for k in range(count):
+        parts[k] = total[k * rows : (k + 1) * rows, :]
+    own = number()
+    keep_ref[...] = parts[own]
+    for k in range(1, count):
+        sends[k - 1][...] = parts[own ^ k].astype(jnp.bfloat16)
 
 
 def add_kernel(keep_ref, got_ref, out_ref):
@@ -353,14 +379,15 @@
         cost_estimate=cost(0, 1_300_000),
     )(inputs[0])
     got_x = [to_shift(turned[s], s) for s in range(4)]
-
-    dq_near, dq_far, keep, send = pl.pallas_call(
+    tile_got = swap(tile, 1)
+
+    score_grad, keys_turned, keep, send = pl.pallas_call(
         attention_kernel,
         in_specs=[SMEM] * 2 + [VMEM],
         out_specs=[VMEM] * 4,
         out_shape=[
-            shape((4, Q_COLS, ROWS)),
-            shape((4, Q_COLS, ROWS)),
+            shape((2, 2, tile_begin(4), 256)),
+            shape((HEAD_WIDTH, SLAB)),
             shape((SLAB // 2, 2 * HEAD_WIDTH), jnp.float32),
             shape((SLAB // 2, 2 * HEAD_WIDTH)),
         ],
@@ -369,8 +396,6 @@
             pltpu.VMEM((SLAB, Q_COLS), jnp.bfloat16),
             pltpu.VMEM((SLAB, HEAD_WIDTH), jnp.bfloat16),
             pltpu.VMEM((SLAB, HEAD_WIDTH), jnp.bfloat16),
-            pltpu.VMEM((HEAD_WIDTH, SLAB), jnp.bfloat16),
-            pltpu.VMEM((SLAB, Q_COLS), jnp.bfloat16),
             pltpu.VMEM((SLAB, 2 * HEAD_WIDTH), jnp.float32),
             pltpu.SMEM((32,), jnp.int32),
             pltpu.SMEM((32,), jnp.int32),
@@ -379,11 +404,21 @@
         cost_estimate=cost(10_000_000_000, 5_000_000),
     )(doc_ids[0], block_order, got)
 
-    send, got_x = lax.optimization_barrier((send, got_x))
+    send, got_x, tile_got = lax.optimization_barrier((send, got_x, tile_got))
     taken = lax.ppermute(send, "y", [(0, 1), (1, 0)])
-    taken, tile, dq_far = lax.optimization_barrier((taken, tile, dq_far))
-    dq_got = lax.ppermute(dq_far, "y", [(0, 1), (1, 0)])
-    tile_got = swap(tile, 1)
+    dq_near, dq_far = pl.pallas_call(
+        query_kernel,
+        in_specs=[SMEM] * 2 + [VMEM] * 2,
+        out_specs=[VMEM] * 2,
+        out_shape=[shape((4, Q_COLS, ROWS))] * 2,
+        scratch_shapes=[
+            pltpu.VMEM((SLAB, Q_COLS), jnp.bfloat16),
+            pltpu.SMEM((32,), jnp.int32),
+        ],
+        compiler_params=params(12),
+        cost_estimate=cost(2_000_000_000, 4_000_000),
+    )(doc_ids[0], block_order, score_grad, keys_turned)
+    taken, dq_near, dq_far = lax.optimization_barrier((taken, dq_near, dq_far))
     own_cols = pl.pallas_call(
         pair_kernel,
         in_specs=[VMEM] * 2,
@@ -393,7 +428,11 @@
         cost_estimate=cost(0, 2_000_000),
     )(keep, taken)
     pieces = [to_shift(own_cols, s) for s in range(4)]
-    pieces, dq_got, tile_got = lax.optimization_barrier((pieces, dq_got, tile_got))
+    _, dq_far, tile, tile_got = lax.optimization_barrier((own_cols, dq_far, tile, tile_got))
+    dq_got = lax.ppermute(dq_far, "y", [(0, 1), (1, 0)])
+    tile = widen(tile, tile_got)
+    far_tile = swap(tile, 0)
+    pieces, dq_got, far_tile = lax.optimization_barrier((pieces, dq_got, far_tile))
 
     kv_half, kv_rows, wg_send, wg_keep = pl.pallas_call(
         weight_kernel,
@@ -411,8 +450,6 @@
     )(*pieces, *got_x)
 
     wg_got = swap(wg_send, 0)
-    tile = widen(tile, tile_got)
-    far_tile = swap(tile, 0)
     parts = pl.pallas_call(
         input_kernel,
         in_specs=[VMEM] * 5,
@@ -425,24 +462,36 @@
         compiler_params=params(12),
         cost_estimate=cost(700_000_000, 6_000_000),
     )(kv_half, tile, far_tile, dq_near, dq_got)
+    wg_got, parts = lax.optimization_barrier((wg_got, parts))
     parts_got = [to_shift(parts[s], s) for s in range(4)]
 
-    def halve(axis, mask, keep, got):
-        rows = keep.shape[0] // 2
-        return pl.pallas_call(
-            functools.partial(halve_kernel, axis, mask),
-            in_specs=[VMEM] * 2,
-            out_specs=[VMEM] * 2,
-            out_shape=[shape((rows, 1024)), shape((rows, 1024), jnp.float32)],
-            compiler_params=params(6),
-            cost_estimate=cost(0, rows * 1024 * 16),
-        )(keep, got)
-
-    wg_send, wg_keep = halve("y", 1, wg_keep, wg_got)
-    wg_got = lax.ppermute(wg_send, "y", [(0, 1), (1, 0)])
-    for bit in (1, 2, 3, 4):
-        wg_send, wg_keep = halve(*BIT_AXES[bit], wg_keep, wg_got)
-        wg_got = swap(wg_send, bit)
+    def split(number, count, keep, *arrived):
+        rows = keep.shape[0] // count
+        results = pl.pallas_call(
+            functools.partial(split_kernel, number, count),
+            in_specs=[VMEM] * (1 + len(arrived)),
+            out_specs=[VMEM] * count,
+            out_shape=[shape((rows, 1024))] * (count - 1) + [shape((rows, 1024), jnp.float32)],
+            scratch_shapes=[pltpu.VMEM((count, rows, 1024), jnp.float32)],
+            compiler_params=params(8),
+            cost_estimate=cost(0, count * rows * 1024 * 16),
+        )(keep, *arrived)
+        return results[:-1], results[-1]
+
+    sends, wg_keep = split(
+        lambda: lax.axis_index("yh") * 2 + lax.axis_index("y"), 4, wg_keep, wg_got
+    )
+    arrived = [
+        lax.ppermute(part, ("yh", "y"), [(i, i ^ (k + 1)) for i in range(4)])
+        for k, part in enumerate(sends)
+    ]
+    sends, wg_keep = split(lambda: lax.axis_index("z") // 2, 4, wg_keep, *arrived)
+    arrived = [
+        lax.ppermute(part, "z", [(i, i ^ (2 * (k + 1))) for i in range(8)])
+        for k, part in enumerate(sends)
+    ]
+    sends, wg_keep = split(lambda: lax.rem(lax.axis_index("z"), 2), 2, wg_keep, *arrived)
+    wg_got = swap(sends[0], 2)
     weight_grad = pl.pallas_call(
         add_kernel,
         in_specs=[VMEM] * 2,

time: 129 us -> 128 us (level); the launches traced: 127 us -> 127 us
  Pallas kernels: 17.6 us -> 19.7 us
    ppermute x8 -> x5, waiting for transfers between devices: 21.1 us -> 8.17 us  [swap(): lax.ppermute(value, axis, [(i, i ^ mask) for i in range(8 if axis == 'z'...]
    ppermute x1 -> x6, starting transfers between devices: 2.16 us -> 15 us  [the longest x3 11.4 us: body(): lax.ppermute(part, 'z', [(i, i ^ 2 * (k + 1)) for i in range(8)])]
    ppermute x8 -> x5, starting transfers between devices: 20.6 us -> 7.8 us  [swap(): lax.ppermute(value, axis, [(i, i ^ mask) for i in range(8 if axis == 'z'...]
    ppermute x1 -> x6, waiting for transfers between devices: 1.95 us -> 11 us  [the longest x3 7.3 us: body(): lax.ppermute(part, ('yh', 'y'), [(i, i ^ k + 1) for i in range(4)])]
    ppermute x9, waiting for transfers between devices: 6.46 us -> 12 us  [to_shift(): lax.ppermute(value, 'x', [(i, (i + s) % 4) for i in range(4)])]
    ppermute x1, waiting for transfers between devices: 6.27 us -> 3.43 us  [body(): taken = lax.ppermute(send, 'y', [(0, 1), (1, 0)])]
    pallas_call x5 -> x4, Pallas kernels: 0.37 us -> 2.15 us  [the longest x1 1.76 us: body(): pl.pallas_call(query_kernel, in_specs=[SMEM] * 2 + [VMEM] * 2, out_specs=...]
    ppermute x9, starting transfers between devices: 19.2 us -> 17.7 us  [to_shift(): lax.ppermute(value, 'x', [(i, (i + s) % 4) for i in range(4)])]
  transfers between devices with their start and end apart: 23 -> 25, of which waited for: 14 -> 13; matrix products, arithmetic and copies ran while one was open for 0% -> 0% of each run, Pallas kernels for 10% -> 10%
where the time goes in v7:
time: 128 us; the launch traced here: 127 us
  starting transfers between devices  59.2 us (46%)
  waiting for transfers between devices  46.5 us (36%)
  Pallas kernels  19.7 us (15%)
    ppermute x9, starting transfers between devices, to_shift(): lax.ppermute(value, 'x', [(i, (i + s) % 4) for i in range(4)])  17.7 us
    ppermute x9, waiting for transfers between devices, to_shift(): lax.ppermute(value, 'x', [(i, (i + s) % 4) for i in range(4)])  12 us
    ppermute x3, starting transfers between devices, body(): lax.ppermute(part, 'z', [(i, i ^ 2 * (k + 1)) for i in range(8)])  11.4 us
    ppermute x2, starting transfers between devices, body(): lax.ppermute(tile, ('z', 'x'), pairs)  10.4 us
    pallas_call x1, Pallas kernels, body(): pl.pallas_call(attention_kernel, in_specs=[SMEM] * 2 + [VMEM], out_specs=...  9.17 us
    ppermute x5, waiting for transfers between devices, swap(): lax.ppermute(value, axis, [(i, i ^ mask) for i in range(8 if axis == 'z'...  8.17 us
    ppermute x5, starting transfers between devices, swap(): lax.ppermute(value, axis, [(i, i ^ mask) for i in range(8 if axis == 'z'...  7.8 us
    ppermute x3, waiting for transfers between devices, body(): lax.ppermute(part, ('yh', 'y'), [(i, i ^ k + 1) for i in range(4)])  7.3 us
  transfers between devices with their start and end apart: 25, of which 13 were waited for; matrix products, arithmetic and copies ran while one was open for 0% of the time, Pallas kernels for 10%

profile of v7, /device:TPU:8, one launch (start us, length us, event | category | flops | bytes accessed | tf_op | source)
XLA Modules:
  0.0 127.3 jit_solution(14622843627805825282)
XLA Ops:
  0.6 2.9 %shard_map.111 = bf16[8,128,1280]{2,1,0:T(8,128)(2,1)} custom-call(bf16[128,4096]{1,0:T(8,128)(2,1)} %bitcast.15, bf16[128,4096]{1,0:T(8,128)(2,1)} %bitcast.16, bf16[128,512]{1,0:T(8,128)(2,1)} %bitcast.17, bf16[128,512]{1,0:T(8,128)(2,1)} %bitcast.18), custom_call_target="tpu_custom_call" | custom-call | bytes 5000000 | tf_op jit(solution)/shard_map/pallas_call | solution.py:327
  3.6 5.9 %all-to-all-start = ((bf16[8,128,1280]{2,1,0:T(8,128)(2,1)}), bf16[8,128,1280]{2,1,0:T(8,128)(2,1)S(1)}, u32[]{:S(2)}, u32[]{:S(2)}) async-start(bf16[8,128,1280]{2,1,0:T(8,128)(2,1)} %shard_map.111), calls=%async_computation | async-start | bytes 5242880 | tf_op jit(solution)/shard_map/all_to_all | solution.py:323
  9.5 9.1 %collective-permute-start = (bf16[80,1024]{1,0:T(8,128)(2,1)S(1)}, bf16[80,1024]{1,0:T(8,128)(2,1)S(1)}, u32[]{:S(2)}, u32[]{:S(2)}) collective-permute-start(bf16[80,1024]{1,0:T(8,128)(2,1)S(1)} %copy-done.1), channel_id=1, source_target_pairs={{0,128},{32,160},{65,193},{97,225},{130,2},{162,34},{195,67},{227,... | collective-permute-start | bytes 491528 | tf_op jit(solution)/shard_map/ppermute | solution.py:353
  18.6 2.9 %collective-permute-done.got_ref = bf16[80,1024]{1,0:T(8,128)(2,1)S(1)} collective-permute-done((bf16[80,1024]{1,0:T(8,128)(2,1)S(1)}, bf16[80,1024]{1,0:T(8,128)(2,1)S(1)}, u32[]{:S(2)}, u32[]{:S(2)}) %collective-permute-start) | collective-permute-done | bytes 163872 | tf_op jit(solution)/shard_map/ppermute | solution.py:353
  22.8 2.9 %collective-permute-done.1.got_ref = bf16[80,1024]{1,0:T(8,128)(2,1)S(1)} collective-permute-done((bf16[80,1024]{1,0:T(8,128)(2,1)S(1)}, bf16[80,1024]{1,0:T(8,128)(2,1)S(1)}, u32[]{:S(2)}, u32[]{:S(2)}) %collective-permute-start.1) | collective-permute-done | bytes 163872 | tf_op jit(solution)/shard_map/ppermute | solution.py:353
  25.7 4.4 %collective-permute-start.2 = (bf16[1,80,1024]{2,1,0:T(8,128)(2,1)S(1)}, bf16[1,80,1024]{2,1,0:T(8,128)(2,1)S(1)}, u32[]{:S(2)}, u32[]{:S(2)}) collective-permute-start(bf16[1,80,1024]{2,1,0:T(8,128)(2,1)S(1)} %bitcast.11), channel_id=1, source_target_pairs={{0,32},{32,0},{64,96},{96,64},{128,160},{160,128},{192,224},{224,1... | collective-permute-start | bytes 491528 | tf_op jit(solution)/shard_map/ppermute | solution.py:315
  30.1 4.3 %collective-permute-done.2.far_ref = bf16[1,80,1024]{2,1,0:T(8,128)(2,1)S(1)} collective-permute-done((bf16[1,80,1024]{2,1,0:T(8,128)(2,1)S(1)}, bf16[1,80,1024]{2,1,0:T(8,128)(2,1)S(1)}, u32[]{:S(2)}, u32[]{:S(2)}) %collective-permute-start.2) | collective-permute-done | bytes 163872 | tf_op jit(solution)/shard_map/ppermute | solution.py:315
  34.4 6.2 %all-to-all-done.refs_0_ = bf16[8,128,1280]{2,1,0:T(8,128)(2,1)S(1)} async-done(((bf16[8,128,1280]{2,1,0:T(8,128)(2,1)}), bf16[8,128,1280]{2,1,0:T(8,128)(2,1)S(1)}, u32[]{:S(2)}, u32[]{:S(2)}) %all-to-all-start) | async-done | bytes 2621472 | tf_op jit(solution)/shard_map/all_to_all | solution.py:323
  42.3 4.7 %collective-permute-start.3 = (bf16[640,128]{1,0:T(8,128)(2,1)S(1)}, bf16[640,128]{1,0:T(8,128)(2,1)S(1)}, u32[]{:S(2)}, u32[]{:S(2)}) collective-permute-start(bf16[640,128]{1,0:T(8,128)(2,1)S(1)} %get-tuple-element.67), channel_id=1, source_target_pairs={{0,1},{1,2},{2,3},{3,0},{4,5},{5,6},{6,7},{7,4},{8,9},{9,10},{10,1... | collective-permute-start | bytes 491528 | tf_op jit(solution)/shard_map/ppermute | solution.py:319
  46.9 4.5 %collective-permute-start.4 = (bf16[640,128]{1,0:T(8,128)(2,1)S(1)}, bf16[640,128]{1,0:T(8,128)(2,1)S(1)}, u32[]{:S(2)}, u32[]{:S(2)}) collective-permute-start(bf16[640,128]{1,0:T(8,128)(2,1)S(1)} %get-tuple-element.68), channel_id=1, source_target_pairs={{0,2},{1,3},{2,0},{3,1},{4,6},{5,7},{6,4},{7,5},{8,10},{9,11},{10,... | collective-permute-start | bytes 491528 | tf_op jit(solution)/shard_map/ppermute | solution.py:319
  51.5 2.3 %collective-permute-start.6 = (bf16[2,80,1024]{2,1,0:T(8,128)(2,1)S(1)}, bf16[2,80,1024]{2,1,0:T(8,128)(2,1)S(1)}, u32[]{:S(2)}, u32[]{:S(2)}) collective-permute-start(bf16[2,80,1024]{2,1,0:T(8,128)(2,1)S(1)} %shard_map.114.near_ref), channel_id=1, source_target_pairs={{0,16},{16,0},{1,17},{17,1},{2,18},{18,2},{3,19},{19,3},{4,20},{20... | collective-permute-start | bytes 983048 | tf_op jit(solution)/shard_map/ppermute | solution.py:315
  53.8 9.2 %shard_map.115 = (bf16[2,2,1280,256]{3,2,1,0:T(8,128)(2,1)S(1)}, bf16[128,1024]{1,0:T(8,128)(2,1)S(1)}, f32[512,256]{1,0:T(8,128)S(1)}, bf16[512,256]{1,0:T(8,128)(2,1)S(1)}) custom-call(s32[32]{0:T(128)S(1)} %bitcast.13, s32[32]{0:T(128)S(1)} %copy-done.3, bf16[8,128,1280]{2,1,0:T(8,128)(2,1)S(1)} %all-to-all-done.refs_0_), custom_call_target="tpu_custom_call" | custom-call | flops 10000000000 | bytes 5000000 | tf_op jit(solution)/shard_map/pallas_call | solution.py:384
  66.0 3.4 %collective-permute-done.7.taken_ref = bf16[512,256]{1,0:T(8,128)(2,1)S(1)} collective-permute-done((bf16[512,256]{1,0:T(8,128)(2,1)S(1)}, bf16[512,256]{1,0:T(8,128)(2,1)S(1)}, u32[]{:S(2)}, u32[]{:S(2)}) %collective-permute-start.7) | collective-permute-done | bytes 262176 | tf_op jit(solution)/shard_map/ppermute | solution.py:408
  72.9 2.1 %collective-permute-start.9 = (bf16[512,256]{1,0:T(8,128)(2,1)S(1)}, bf16[512,256]{1,0:T(8,128)(2,1)S(1)}, u32[]{:S(2)}, u32[]{:S(2)}) collective-permute-start(bf16[512,256]{1,0:T(8,128)(2,1)S(1)} %shard_map.118.refs_0_), channel_id=1, source_target_pairs={{0,2},{1,3},{2,0},{3,1},{4,6},{5,7},{6,4},{7,5},{8,10},{9,11},{10,... | collective-permute-start | bytes 786440 | tf_op jit(solution)/shard_map/ppermute | solution.py:319
  75.0 5.0 %collective-permute-done.10.refs_3_ = bf16[512,256]{1,0:T(8,128)(2,1)S(1)} collective-permute-done((bf16[512,256]{1,0:T(8,128)(2,1)S(1)}, bf16[512,256]{1,0:T(8,128)(2,1)S(1)}, u32[]{:S(2)}, u32[]{:S(2)}) %collective-permute-start.10) | collective-permute-done | bytes 262176 | tf_op jit(solution)/shard_map/ppermute | solution.py:319
  81.0 6.0 %collective-permute-done.9.refs_2_ = bf16[512,256]{1,0:T(8,128)(2,1)S(1)} collective-permute-done((bf16[512,256]{1,0:T(8,128)(2,1)S(1)}, bf16[512,256]{1,0:T(8,128)(2,1)S(1)}, u32[]{:S(2)}, u32[]{:S(2)}) %collective-permute-start.9) | collective-permute-done | bytes 262176 | tf_op jit(solution)/shard_map/ppermute | solution.py:319
  91.6 2.3 %collective-permute-start.15 = (bf16[1664,128]{1,0:T(8,128)(2,1)S(1)}, bf16[1664,128]{1,0:T(8,128)(2,1)S(1)}, u32[]{:S(2)}, u32[]{:S(2)}) collective-permute-start(bf16[1664,128]{1,0:T(8,128)(2,1)S(1)} %get-tuple-element.101), channel_id=1, source_target_pairs={{0,2},{1,3},{2,0},{3,1},{4,6},{5,7},{6,4},{7,5},{8,10},{9,11},{10,... | collective-permute-start | bytes 1277960 | tf_op jit(solution)/shard_map/ppermute | solution.py:319
  98.6 4.2 %collective-permute-done.18.refs_2_ = bf16[80,1024]{1,0:T(8,128)(2,1)S(1)} collective-permute-done((bf16[80,1024]{1,0:T(8,128)(2,1)S(1)}, bf16[80,1024]{1,0:T(8,128)(2,1)S(1)}, u32[]{:S(2)}, u32[]{:S(2)}) %collective-permute-start.18) | collective-permute-done | bytes 163872 | tf_op jit(solution)/shard_map/ppermute | solution.py:485
  102.8 3.0 %collective-permute-done.19.refs_3_ = bf16[80,1024]{1,0:T(8,128)(2,1)S(1)} collective-permute-done((bf16[80,1024]{1,0:T(8,128)(2,1)S(1)}, bf16[80,1024]{1,0:T(8,128)(2,1)S(1)}, u32[]{:S(2)}, u32[]{:S(2)}) %collective-permute-start.19) | collective-permute-done | bytes 163872 | tf_op jit(solution)/shard_map/ppermute | solution.py:485
  106.0 3.4 %collective-permute-start.20 = (bf16[20,1024]{1,0:T(8,128)(2,1)S(1)}, bf16[20,1024]{1,0:T(8,128)(2,1)S(1)}, u32[]{:S(2)}, u32[]{:S(2)}) collective-permute-start(bf16[20,1024]{1,0:T(8,128)(2,1)S(1)} %get-tuple-element.113), channel_id=1, source_target_pairs={{0,64},{32,96},{64,0},{96,32},{128,192},{160,224},{192,128},{224,1... | collective-permute-start | bytes 122888 | tf_op jit(solution)/shard_map/ppermute | solution.py:490
  109.3 5.4 %collective-permute-start.21 = (bf16[20,1024]{1,0:T(8,128)(2,1)S(1)}, bf16[20,1024]{1,0:T(8,128)(2,1)S(1)}, u32[]{:S(2)}, u32[]{:S(2)}) collective-permute-start(bf16[20,1024]{1,0:T(8,128)(2,1)S(1)} %get-tuple-element.114), channel_id=1, source_target_pairs={{0,128},{32,160},{64,192},{96,224},{128,0},{160,32},{192,64},{224,... | collective-permute-start | bytes 122888 | tf_op jit(solution)/shard_map/ppermute | solution.py:490
  114.7 2.6 %collective-permute-start.22 = (bf16[20,1024]{1,0:T(8,128)(2,1)S(1)}, bf16[20,1024]{1,0:T(8,128)(2,1)S(1)}, u32[]{:S(2)}, u32[]{:S(2)}) collective-permute-start(bf16[20,1024]{1,0:T(8,128)(2,1)S(1)} %get-tuple-element.115), channel_id=1, source_target_pairs={{0,192},{32,224},{64,128},{96,160},{128,64},{160,96},{192,0},{224,... | collective-permute-start | bytes 122888 | tf_op jit(solution)/shard_map/ppermute | solution.py:490
  117.4 3.7 %collective-permute-done.22.refs_3_ = bf16[20,1024]{1,0:T(8,128)(2,1)S(1)} collective-permute-done((bf16[20,1024]{1,0:T(8,128)(2,1)S(1)}, bf16[20,1024]{1,0:T(8,128)(2,1)S(1)}, u32[]{:S(2)}, u32[]{:S(2)}) %collective-permute-start.22) | collective-permute-done | bytes 40992 | tf_op jit(solution)/shard_map/ppermute | solution.py:490
  122.1 3.0 %collective-permute-done.23.got_ref = bf16[10,1024]{1,0:T(8,128)(2,1)S(1)} collective-permute-done((bf16[10,1024]{1,0:T(8,128)(2,1)S(1)}, bf16[10,1024]{1,0:T(8,128)(2,1)S(1)}, u32[]{:S(2)}, u32[]{:S(2)}) %collective-permute-start.23) | collective-permute-done | bytes 20512 | tf_op jit(solution)/shard_map/ppermute | solution.py:315
  (50 shorter events, 23.2 us)
Async XLA Ops:
  3.6 37.0 %all-to-all-start = ((bf16[8,128,1280]{2,1,0:T(8,128)(2,1)}), bf16[8,128,1280]{2,1,0:T(8,128)(2,1)S(1)}, u32[]{:S(2)}, u32[]{:S(2)}) async-start(bf16[8,128,1280]{2,1,0:T(8,128)(2,1)} %shard_map.111), calls=%async_computation | async-start | bytes 5242880 | tf_op jit(solution)/shard_map/all_to_all | solution.py:323
  9.5 12.0 %collective-permute-start = (bf16[80,1024]{1,0:T(8,128)(2,1)S(1)}, bf16[80,1024]{1,0:T(8,128)(2,1)S(1)}, u32[]{:S(2)}, u32[]{:S(2)}) collective-permute-start(bf16[80,1024]{1,0:T(8,128)(2,1)S(1)} %copy-done.1), channel_id=1, source_target_pairs={{0,128},{32,160},{65,193},{97,225},{130,2},{162,34},{195,67},{227,... | collective-permute-start | bytes 491528 | tf_op jit(solution)/shard_map/ppermute | solution.py:353
  21.5 4.2 %collective-permute-start.1 = (bf16[80,1024]{1,0:T(8,128)(2,1)S(1)}, bf16[80,1024]{1,0:T(8,128)(2,1)S(1)}, u32[]{:S(2)}, u32[]{:S(2)}) collective-permute-start(bf16[80,1024]{1,0:T(8,128)(2,1)S(1)} %shard_map.112.own_ref), channel_id=1, source_target_pairs={{0,64},{2,66},{32,96},{34,98},{65,1},{67,3},{97,33},{99,35},{128,1... | collective-permute-start | bytes 491528 | tf_op jit(solution)/shard_map/ppermute | solution.py:353
  25.7 8.7 %collective-permute-start.2 = (bf16[1,80,1024]{2,1,0:T(8,128)(2,1)S(1)}, bf16[1,80,1024]{2,1,0:T(8,128)(2,1)S(1)}, u32[]{:S(2)}, u32[]{:S(2)}) collective-permute-start(bf16[1,80,1024]{2,1,0:T(8,128)(2,1)S(1)} %bitcast.11), channel_id=1, source_target_pairs={{0,32},{32,0},{64,96},{96,64},{128,160},{160,128},{192,224},{224,1... | collective-permute-start | bytes 491528 | tf_op jit(solution)/shard_map/ppermute | solution.py:315
  42.3 20.7 %collective-permute-start.3 = (bf16[640,128]{1,0:T(8,128)(2,1)S(1)}, bf16[640,128]{1,0:T(8,128)(2,1)S(1)}, u32[]{:S(2)}, u32[]{:S(2)}) collective-permute-start(bf16[640,128]{1,0:T(8,128)(2,1)S(1)} %get-tuple-element.67), channel_id=1, source_target_pairs={{0,1},{1,2},{2,3},{3,0},{4,5},{5,6},{6,7},{7,4},{8,9},{9,10},{10,1... | collective-permute-start | bytes 491528 | tf_op jit(solution)/shard_map/ppermute | solution.py:319
  46.9 16.0 %collective-permute-start.4 = (bf16[640,128]{1,0:T(8,128)(2,1)S(1)}, bf16[640,128]{1,0:T(8,128)(2,1)S(1)}, u32[]{:S(2)}, u32[]{:S(2)}) collective-permute-start(bf16[640,128]{1,0:T(8,128)(2,1)S(1)} %get-tuple-element.68), channel_id=1, source_target_pairs={{0,2},{1,3},{2,0},{3,1},{4,6},{5,7},{6,4},{7,5},{8,10},{9,11},{10,... | collective-permute-start | bytes 491528 | tf_op jit(solution)/shard_map/ppermute | solution.py:319
  51.5 11.5 %collective-permute-start.5 = (bf16[640,128]{1,0:T(8,128)(2,1)S(1)}, bf16[640,128]{1,0:T(8,128)(2,1)S(1)}, u32[]{:S(2)}, u32[]{:S(2)}) collective-permute-start(bf16[640,128]{1,0:T(8,128)(2,1)S(1)} %get-tuple-element.69), channel_id=1, source_target_pairs={{0,3},{1,0},{2,1},{3,2},{4,7},{5,4},{6,5},{7,6},{8,11},{9,8},{10,9... | collective-permute-start | bytes 491528 | tf_op jit(solution)/shard_map/ppermute | solution.py:319
  51.5 11.5 %collective-permute-start.6 = (bf16[2,80,1024]{2,1,0:T(8,128)(2,1)S(1)}, bf16[2,80,1024]{2,1,0:T(8,128)(2,1)S(1)}, u32[]{:S(2)}, u32[]{:S(2)}) collective-permute-start(bf16[2,80,1024]{2,1,0:T(8,128)(2,1)S(1)} %shard_map.114.near_ref), channel_id=1, source_target_pairs={{0,16},{16,0},{1,17},{17,1},{2,18},{18,2},{3,19},{19,3},{4,20},{20... | collective-permute-start | bytes 983048 | tf_op jit(solution)/shard_map/ppermute | solution.py:315
  63.0 6.5 %collective-permute-start.7 = (bf16[512,256]{1,0:T(8,128)(2,1)S(1)}, bf16[512,256]{1,0:T(8,128)(2,1)S(1)}, u32[]{:S(2)}, u32[]{:S(2)}) collective-permute-start(bf16[512,256]{1,0:T(8,128)(2,1)S(1)} %get-tuple-element.71), channel_id=1, source_target_pairs={{0,4},{4,0},{1,5},{5,1},{2,6},{6,2},{3,7},{7,3},{8,12},{12,8},{9,1... | collective-permute-start | bytes 786440 | tf_op jit(solution)/shard_map/ppermute | solution.py:408
  69.5 17.4 %collective-permute-start.12 = (bf16[4,80,1024]{2,1,0:T(8,128)(2,1)S(1)}, bf16[4,80,1024]{2,1,0:T(8,128)(2,1)S(1)}, u32[]{:S(2)}, u32[]{:S(2)}) collective-permute-start(bf16[4,80,1024]{2,1,0:T(8,128)(2,1)S(1)} %shard_map.119.w_ref), channel_id=1, source_target_pairs={{0,8},{8,0},{1,9},{9,1},{2,10},{10,2},{3,11},{11,3},{4,12},{12,4},... | collective-permute-start | bytes 1966088 | tf_op jit(solution)/shard_map/ppermute | solution.py:315
  69.6 17.3 %collective-permute-start.11 = (bf16[4,512,128]{2,1,0:T(8,128)(2,1)S(1)}, bf16[4,512,128]{2,1,0:T(8,128)(2,1)S(1)}, u32[]{:S(2)}, u32[]{:S(2)}) collective-permute-start(bf16[4,512,128]{2,1,0:T(8,128)(2,1)S(1)} %get-tuple-element.79), channel_id=1, source_target_pairs={{0,4},{4,0},{1,5},{5,1},{2,6},{6,2},{3,7},{7,3},{8,12},{12,8},{9,1... | collective-permute-start | bytes 1572872 | tf_op jit(solution)/shard_map/ppermute | solution.py:432
  70.9 9.1 %collective-permute-start.10 = (bf16[512,256]{1,0:T(8,128)(2,1)S(1)}, bf16[512,256]{1,0:T(8,128)(2,1)S(1)}, u32[]{:S(2)}, u32[]{:S(2)}) collective-permute-start(bf16[512,256]{1,0:T(8,128)(2,1)S(1)} %shard_map.118.refs_0_), channel_id=1, source_target_pairs={{0,3},{1,0},{2,1},{3,2},{4,7},{5,4},{6,5},{7,6},{8,11},{9,8},{10,9... | collective-permute-start | bytes 786440 | tf_op jit(solution)/shard_map/ppermute | solution.py:319
  71.5 9.5 %collective-permute-start.8 = (bf16[512,256]{1,0:T(8,128)(2,1)S(1)}, bf16[512,256]{1,0:T(8,128)(2,1)S(1)}, u32[]{:S(2)}, u32[]{:S(2)}) collective-permute-start(bf16[512,256]{1,0:T(8,128)(2,1)S(1)} %shard_map.118.refs_0_), channel_id=1, source_target_pairs={{0,1},{1,2},{2,3},{3,0},{4,5},{5,6},{6,7},{7,4},{8,9},{9,10},{10,1... | collective-permute-start | bytes 786440 | tf_op jit(solution)/shard_map/ppermute | solution.py:319
  72.9 14.0 %collective-permute-start.9 = (bf16[512,256]{1,0:T(8,128)(2,1)S(1)}, bf16[512,256]{1,0:T(8,128)(2,1)S(1)}, u32[]{:S(2)}, u32[]{:S(2)}) collective-permute-start(bf16[512,256]{1,0:T(8,128)(2,1)S(1)} %shard_map.118.refs_0_), channel_id=1, source_target_pairs={{0,2},{1,3},{2,0},{3,1},{4,6},{5,7},{6,4},{7,5},{8,10},{9,11},{10,... | collective-permute-start | bytes 786440 | tf_op jit(solution)/shard_map/ppermute | solution.py:319
  90.6 6.6 %collective-permute-start.17 = (bf16[80,1024]{1,0:T(8,128)(2,1)S(1)}, bf16[80,1024]{1,0:T(8,128)(2,1)S(1)}, u32[]{:S(2)}, u32[]{:S(2)}) collective-permute-start(bf16[80,1024]{1,0:T(8,128)(2,1)S(1)} %get-tuple-element.109), channel_id=1, source_target_pairs={{0,4},{4,0},{16,20},{20,16},{1,5},{5,1},{17,21},{21,17},{2,6},{6,2... | collective-permute-start | bytes 491528 | tf_op jit(solution)/shard_map/ppermute | solution.py:485
  91.5 34.2 %collective-permute-start.14 = (bf16[1664,128]{1,0:T(8,128)(2,1)S(1)}, bf16[1664,128]{1,0:T(8,128)(2,1)S(1)}, u32[]{:S(2)}, u32[]{:S(2)}) collective-permute-start(bf16[1664,128]{1,0:T(8,128)(2,1)S(1)} %get-tuple-element.100), channel_id=1, source_target_pairs={{0,1},{1,2},{2,3},{3,0},{4,5},{5,6},{6,7},{7,4},{8,9},{9,10},{10,1... | collective-permute-start | bytes 1277960 | tf_op jit(solution)/shard_map/ppermute | solution.py:319
  91.6 34.2 %collective-permute-start.15 = (bf16[1664,128]{1,0:T(8,128)(2,1)S(1)}, bf16[1664,128]{1,0:T(8,128)(2,1)S(1)}, u32[]{:S(2)}, u32[]{:S(2)}) collective-permute-start(bf16[1664,128]{1,0:T(8,128)(2,1)S(1)} %get-tuple-element.101), channel_id=1, source_target_pairs={{0,2},{1,3},{2,0},{3,1},{4,6},{5,7},{6,4},{7,5},{8,10},{9,11},{10,... | collective-permute-start | bytes 1277960 | tf_op jit(solution)/shard_map/ppermute | solution.py:319
  93.9 31.8 %collective-permute-start.16 = (bf16[1664,128]{1,0:T(8,128)(2,1)S(1)}, bf16[1664,128]{1,0:T(8,128)(2,1)S(1)}, u32[]{:S(2)}, u32[]{:S(2)}) collective-permute-start(bf16[1664,128]{1,0:T(8,128)(2,1)S(1)} %get-tuple-element.102), channel_id=1, source_target_pairs={{0,3},{1,0},{2,1},{3,2},{4,7},{5,4},{6,5},{7,6},{8,11},{9,8},{10,9... | collective-permute-start | bytes 1277960 | tf_op jit(solution)/shard_map/ppermute | solution.py:319
  95.9 6.9 %collective-permute-start.18 = (bf16[80,1024]{1,0:T(8,128)(2,1)S(1)}, bf16[80,1024]{1,0:T(8,128)(2,1)S(1)}, u32[]{:S(2)}, u32[]{:S(2)}) collective-permute-start(bf16[80,1024]{1,0:T(8,128)(2,1)S(1)} %get-tuple-element.110), channel_id=1, source_target_pairs={{0,16},{4,20},{16,0},{20,4},{1,17},{5,21},{17,1},{21,5},{2,18},{6,... | collective-permute-start | bytes 491528 | tf_op jit(solution)/shard_map/ppermute | solution.py:485
  97.2 8.7 %collective-permute-start.19 = (bf16[80,1024]{1,0:T(8,128)(2,1)S(1)}, bf16[80,1024]{1,0:T(8,128)(2,1)S(1)}, u32[]{:S(2)}, u32[]{:S(2)}) collective-permute-start(bf16[80,1024]{1,0:T(8,128)(2,1)S(1)} %get-tuple-element.111), channel_id=1, source_target_pairs={{0,20},{4,16},{16,4},{20,0},{1,21},{5,17},{17,5},{21,1},{2,22},{6,... | collective-permute-start | bytes 491528 | tf_op jit(solution)/shard_map/ppermute | solution.py:485
  106.0 8.8 %collective-permute-start.20 = (bf16[20,1024]{1,0:T(8,128)(2,1)S(1)}, bf16[20,1024]{1,0:T(8,128)(2,1)S(1)}, u32[]{:S(2)}, u32[]{:S(2)}) collective-permute-start(bf16[20,1024]{1,0:T(8,128)(2,1)S(1)} %get-tuple-element.113), channel_id=1, source_target_pairs={{0,64},{32,96},{64,0},{96,32},{128,192},{160,224},{192,128},{224,1... | collective-permute-start | bytes 122888 | tf_op jit(solution)/shard_map/ppermute | solution.py:490
  109.3 8.0 %collective-permute-start.21 = (bf16[20,1024]{1,0:T(8,128)(2,1)S(1)}, bf16[20,1024]{1,0:T(8,128)(2,1)S(1)}, u32[]{:S(2)}, u32[]{:S(2)}) collective-permute-start(bf16[20,1024]{1,0:T(8,128)(2,1)S(1)} %get-tuple-element.114), channel_id=1, source_target_pairs={{0,128},{32,160},{64,192},{96,224},{128,0},{160,32},{192,64},{224,... | collective-permute-start | bytes 122888 | tf_op jit(solution)/shard_map/ppermute | solution.py:490
  114.7 6.3 %collective-permute-start.22 = (bf16[20,1024]{1,0:T(8,128)(2,1)S(1)}, bf16[20,1024]{1,0:T(8,128)(2,1)S(1)}, u32[]{:S(2)}, u32[]{:S(2)}) collective-permute-start(bf16[20,1024]{1,0:T(8,128)(2,1)S(1)} %get-tuple-element.115), channel_id=1, source_target_pairs={{0,192},{32,224},{64,128},{96,160},{128,64},{160,96},{192,0},{224,... | collective-permute-start | bytes 122888 | tf_op jit(solution)/shard_map/ppermute | solution.py:490
  121.1 4.0 %collective-permute-start.23 = (bf16[10,1024]{1,0:T(8,128)(2,1)S(1)}, bf16[10,1024]{1,0:T(8,128)(2,1)S(1)}, u32[]{:S(2)}, u32[]{:S(2)}) collective-permute-start(bf16[10,1024]{1,0:T(8,128)(2,1)S(1)} %get-tuple-element.117), channel_id=1, source_target_pairs={{0,32},{32,0},{64,96},{96,64},{128,160},{160,128},{192,224},{224,1... | collective-permute-start | bytes 61448 | tf_op jit(solution)/shard_map/ppermute | solution.py:315
  (5 other events, 109.5 us)

commit v8 on v7

--- a/solution.py
+++ b/solution.py
@@ -84,7 +84,8 @@
 
 
 def tile_row(z, low, y):
-    return (low % 2) * 320 + (low // 2) * 160 + y * 80 + (z // 2) * 20 + (z % 2) * 10
+    row = (low % 2) * 320 + y * 160 + (low // 2) * 80
+    return row + (z % 2) * 40 + (z // 2 % 2) * 20 + (z // 4) * 10
 
 
 def turn_kernel(in_ref, *refs):
@@ -164,22 +165,28 @@
             seen = (row >= low) & (row <= lane + i * 128)
             bias = jnp.where(seen, 0.0, LOWEST)
             bias = jnp.concatenate([bias, bias], axis=1)
+            q_rows = [q_s[rows, e * 128 : (e + 1) * 128] for e in range(4)]
+            d_rows = [d_s[rows, e * 128 : (e + 1) * 128] for e in range(4)]
+            grads, lows = [], []
             for g in range(2):
-                cols = [slice((2 * g + e) * 128, (2 * g + e + 1) * 128) for e in range(2)]
-                qs = jnp.concatenate([q_s[rows, e] for e in cols], axis=0)
-                ds = jnp.concatenate([d_s[rows, e] for e in cols], axis=0)
+                qs = jnp.concatenate(q_rows[2 * g : 2 * g + 2], axis=0)
+                ds = jnp.concatenate(d_rows[2 * g : 2 * g + 2], axis=0)
                 scores = dot(key_n, qs, NT) * (SCALE * LOG2E) + bias
                 top = jnp.max(scores, axis=0, keepdims=True)
-                probs = jnp.exp2(scores - top)
-                total = jnp.sum(probs, axis=0, keepdims=True)
-                probs = probs * (1.0 / total)
+                weights = jnp.exp2(scores - top)
+                share = 1.0 / jnp.sum(weights, axis=0, keepdims=True)
                 products = dot(value_n, ds, NT)
-                delta = jnp.sum(probs * products, axis=0, keepdims=True)
-                score_grad = (probs * (products - delta)).astype(jnp.bfloat16)
-                probs_low = probs.astype(jnp.bfloat16)
-                dkv_s[keys, 0:128] += dot(score_grad, qs, NN)
-                dkv_s[keys, 128:256] += dot(probs_low, ds, NN)
-                grad_ref[hf, g, tile_begin(i) : tile_begin(i) + n, :] = score_grad
+                delta = jnp.sum(weights * products, axis=0, keepdims=True) * share
+                probs = weights * share
+                grads.append((probs * (products - delta)).astype(jnp.bfloat16))
+                lows.append(probs.astype(jnp.bfloat16))
+                grad_ref[hf, g, tile_begin(i) : tile_begin(i) + n, :] = grads[g]
+            dkv_s[keys, 0:128] += dot(
+                jnp.concatenate(grads, axis=1), jnp.concatenate(q_rows, axis=0), NN
+            )
+            dkv_s[keys, 128:256] += dot(
+                jnp.concatenate(lows, axis=1), jnp.concatenate(d_rows, axis=0), NN
+            )
         return carry
 
     lax.fori_loop(0, 2, half, 0)
@@ -418,7 +425,10 @@
         compiler_params=params(12),
         cost_estimate=cost(2_000_000_000, 4_000_000),
     )(doc_ids[0], block_order, score_grad, keys_turned)
-    taken, dq_near, dq_far = lax.optimization_barrier((taken, dq_near, dq_far))
+    dq_far, tile, tile_got = lax.optimization_barrier((dq_far, tile, tile_got))
+    tile = widen(tile, tile_got)
+    far_tile = swap(tile, 0)
+    taken, dq_near, dq_far, tile = lax.optimization_barrier((taken, dq_near, dq_far, tile))
     own_cols = pl.pallas_call(
         pair_kernel,
         in_specs=[VMEM] * 2,
@@ -428,10 +438,8 @@
         cost_estimate=cost(0, 2_000_000),
     )(keep, taken)
     pieces = [to_shift(own_cols, s) for s in range(4)]
-    _, dq_far, tile, tile_got = lax.optimization_barrier((own_cols, dq_far, tile, tile_got))
+    _, dq_far = lax.optimization_barrier((own_cols, dq_far))
     dq_got = lax.ppermute(dq_far, "y", [(0, 1), (1, 0)])
-    tile = widen(tile, tile_got)
-    far_tile = swap(tile, 0)
     pieces, dq_got, far_tile = lax.optimization_barrier((pieces, dq_got, far_tile))
 
     kv_half, kv_rows, wg_send, wg_keep = pl.pallas_call(
@@ -478,20 +486,13 @@
         )(keep, *arrived)
         return results[:-1], results[-1]
 
-    sends, wg_keep = split(
-        lambda: lax.axis_index("yh") * 2 + lax.axis_index("y"), 4, wg_keep, wg_got
-    )
-    arrived = [
-        lax.ppermute(part, ("yh", "y"), [(i, i ^ (k + 1)) for i in range(4)])
-        for k, part in enumerate(sends)
-    ]
-    sends, wg_keep = split(lambda: lax.axis_index("z") // 2, 4, wg_keep, *arrived)
-    arrived = [
-        lax.ppermute(part, "z", [(i, i ^ (2 * (k + 1))) for i in range(8)])
-        for k, part in enumerate(sends)
-    ]
-    sends, wg_keep = split(lambda: lax.rem(lax.axis_index("z"), 2), 2, wg_keep, *arrived)
-    wg_got = swap(sends[0], 2)
+    def bit_of(axis, mask):
+        return lambda: (lax.axis_index(axis) & mask) // mask
+
+    for axis, mask in (("y", 1), ("yh", 1), ("z", 1), ("z", 2), ("z", 4)):
+        sends, wg_keep = split(bit_of(axis, mask), 2, wg_keep, wg_got)
+        size = 8 if axis == "z" else 2
+        wg_got = lax.ppermute(sends[0], axis, [(i, i ^ mask) for i in range(size)])
     weight_grad = pl.pallas_call(
         add_kernel,
         in_specs=[VMEM] * 2,

time: 128 us -> 122 us (0.953)
  waiting for transfers between devices: 46.5 us -> 43 us
  Pallas kernels: 19.7 us -> 17.3 us
    ppermute x9, waiting for transfers between devices: 12 us -> 8.16 us  [to_shift(): lax.ppermute(value, 'x', [(i, (i + s) % 4) for i in range(4)])]
    ppermute x6 -> x5, waiting for transfers between devices: 11 us -> 14.3 us  [body(): wg_got = lax.ppermute(sends[0], axis, [(i, i ^ mask) for i in range(size)])]
    ppermute x5 -> x4, waiting for transfers between devices: 8.17 us -> 5.29 us  [swap(): lax.ppermute(value, axis, [(i, i ^ mask) for i in range(8 if axis == 'z'...]
    pallas_call x1, Pallas kernels: 9.17 us -> 6.71 us  [body(): pl.pallas_call(attention_kernel, in_specs=[SMEM] * 2 + [VMEM], out_specs=...]
    ppermute x5 -> x4, starting transfers between devices: 7.8 us -> 6.77 us  [swap(): lax.ppermute(value, axis, [(i, i ^ mask) for i in range(8 if axis == 'z'...]
    ppermute x6 -> x5, starting transfers between devices: 15 us -> 15.6 us  [body(): wg_got = lax.ppermute(sends[0], axis, [(i, i ^ mask) for i in range(size)])]
  transfers between devices with their start and end apart: 25 -> 23, of which waited for: 13 -> 15; matrix products, arithmetic and copies ran while one was open for 0% -> 0% of each run, Pallas kernels for 10% -> 10%
where the time goes in v8:
time: 122 us; the launch traced here: 121 us
  starting transfers between devices  59.1 us (48%)
  waiting for transfers between devices  43 us (35%)
  Pallas kernels  17.3 us (14%)
    ppermute x9, starting transfers between devices, to_shift(): lax.ppermute(value, 'x', [(i, (i + s) % 4) for i in range(4)])  17.7 us
    ppermute x5, starting transfers between devices, body(): wg_got = lax.ppermute(sends[0], axis, [(i, i ^ mask) for i in range(size)])  15.6 us
    ppermute x5, waiting for transfers between devices, body(): wg_got = lax.ppermute(sends[0], axis, [(i, i ^ mask) for i in range(size)])  14.3 us
    ppermute x2, starting transfers between devices, body(): lax.ppermute(tile, ('z', 'x'), pairs)  10.4 us
    ppermute x9, waiting for transfers between devices, to_shift(): lax.ppermute(value, 'x', [(i, (i + s) % 4) for i in range(4)])  8.16 us
    ppermute x4, starting transfers between devices, swap(): lax.ppermute(value, axis, [(i, i ^ mask) for i in range(8 if axis == 'z'...  6.77 us
    pallas_call x1, Pallas kernels, body(): pl.pallas_call(attention_kernel, in_specs=[SMEM] * 2 + [VMEM], out_specs=...  6.71 us
    all_to_all x1, waiting for transfers between devices, exchange(): return lax.all_to_all(value, axis, 0, 0, tiled=True)  6.2 us
  transfers between devices with their start and end apart: 23, of which 15 were waited for; matrix products, arithmetic and copies ran while one was open for 0% of the time, Pallas kernels for 10%

profile of v8, /device:TPU:8, one launch (start us, length us, event | category | flops | bytes accessed | tf_op | source)
XLA Modules:
  0.0 121.3 jit_solution(13442842000570091660)
XLA Ops:
  0.6 2.9 %shard_map.111 = bf16[8,128,1280]{2,1,0:T(8,128)(2,1)} custom-call(bf16[128,4096]{1,0:T(8,128)(2,1)} %bitcast.15, bf16[128,4096]{1,0:T(8,128)(2,1)} %bitcast.16, bf16[128,512]{1,0:T(8,128)(2,1)} %bitcast.17, bf16[128,512]{1,0:T(8,128)(2,1)} %bitcast.18), custom_call_target="tpu_custom_call" | custom-call | bytes 5000000 | tf_op jit(solution)/shard_map/pallas_call | solution.py:334
  3.6 5.9 %all-to-all-start = ((bf16[8,128,1280]{2,1,0:T(8,128)(2,1)}), bf16[8,128,1280]{2,1,0:T(8,128)(2,1)S(1)}, u32[]{:S(2)}, u32[]{:S(2)}) async-start(bf16[8,128,1280]{2,1,0:T(8,128)(2,1)} %shard_map.111), calls=%async_computation | async-start | bytes 5242880 | tf_op jit(solution)/shard_map/all_to_all | solution.py:330
  9.5 9.1 %collective-permute-start = (bf16[80,1024]{1,0:T(8,128)(2,1)S(1)}, bf16[80,1024]{1,0:T(8,128)(2,1)S(1)}, u32[]{:S(2)}, u32[]{:S(2)}) collective-permute-start(bf16[80,1024]{1,0:T(8,128)(2,1)S(1)} %copy-done.1), channel_id=1, source_target_pairs={{0,128},{32,160},{65,193},{97,225},{130,2},{162,34},{195,67},{227,... | collective-permute-start | bytes 491528 | tf_op jit(solution)/shard_map/ppermute | solution.py:360
  18.6 2.9 %collective-permute-done.got_ref = bf16[80,1024]{1,0:T(8,128)(2,1)S(1)} collective-permute-done((bf16[80,1024]{1,0:T(8,128)(2,1)S(1)}, bf16[80,1024]{1,0:T(8,128)(2,1)S(1)}, u32[]{:S(2)}, u32[]{:S(2)}) %collective-permute-start) | collective-permute-done | bytes 163872 | tf_op jit(solution)/shard_map/ppermute | solution.py:360
  22.8 2.9 %collective-permute-done.1.got_ref = bf16[80,1024]{1,0:T(8,128)(2,1)S(1)} collective-permute-done((bf16[80,1024]{1,0:T(8,128)(2,1)S(1)}, bf16[80,1024]{1,0:T(8,128)(2,1)S(1)}, u32[]{:S(2)}, u32[]{:S(2)}) %collective-permute-start.1) | collective-permute-done | bytes 163872 | tf_op jit(solution)/shard_map/ppermute | solution.py:360
  25.7 4.4 %collective-permute-start.2 = (bf16[1,80,1024]{2,1,0:T(8,128)(2,1)S(1)}, bf16[1,80,1024]{2,1,0:T(8,128)(2,1)S(1)}, u32[]{:S(2)}, u32[]{:S(2)}) collective-permute-start(bf16[1,80,1024]{2,1,0:T(8,128)(2,1)S(1)} %bitcast.11), channel_id=1, source_target_pairs={{0,32},{32,0},{64,96},{96,64},{128,160},{160,128},{192,224},{224,1... | collective-permute-start | bytes 491528 | tf_op jit(solution)/shard_map/ppermute | solution.py:322
  30.1 4.3 %collective-permute-done.2.far_ref = bf16[1,80,1024]{2,1,0:T(8,128)(2,1)S(1)} collective-permute-done((bf16[1,80,1024]{2,1,0:T(8,128)(2,1)S(1)}, bf16[1,80,1024]{2,1,0:T(8,128)(2,1)S(1)}, u32[]{:S(2)}, u32[]{:S(2)}) %collective-permute-start.2) | collective-permute-done | bytes 163872 | tf_op jit(solution)/shard_map/ppermute | solution.py:322
  34.4 6.2 %all-to-all-done.refs_0_ = bf16[8,128,1280]{2,1,0:T(8,128)(2,1)S(1)} async-done(((bf16[8,128,1280]{2,1,0:T(8,128)(2,1)}), bf16[8,128,1280]{2,1,0:T(8,128)(2,1)S(1)}, u32[]{:S(2)}, u32[]{:S(2)}) %all-to-all-start) | async-done | bytes 2621472 | tf_op jit(solution)/shard_map/all_to_all | solution.py:330
  42.2 4.7 %collective-permute-start.3 = (bf16[640,128]{1,0:T(8,128)(2,1)S(1)}, bf16[640,128]{1,0:T(8,128)(2,1)S(1)}, u32[]{:S(2)}, u32[]{:S(2)}) collective-permute-start(bf16[640,128]{1,0:T(8,128)(2,1)S(1)} %get-tuple-element.69), channel_id=1, source_target_pairs={{0,1},{1,2},{2,3},{3,0},{4,5},{5,6},{6,7},{7,4},{8,9},{9,10},{10,1... | collective-permute-start | bytes 491528 | tf_op jit(solution)/shard_map/ppermute | solution.py:326
  46.8 4.5 %collective-permute-start.4 = (bf16[640,128]{1,0:T(8,128)(2,1)S(1)}, bf16[640,128]{1,0:T(8,128)(2,1)S(1)}, u32[]{:S(2)}, u32[]{:S(2)}) collective-permute-start(bf16[640,128]{1,0:T(8,128)(2,1)S(1)} %get-tuple-element.70), channel_id=1, source_target_pairs={{0,2},{1,3},{2,0},{3,1},{4,6},{5,7},{6,4},{7,5},{8,10},{9,11},{10,... | collective-permute-start | bytes 491528 | tf_op jit(solution)/shard_map/ppermute | solution.py:326
  51.4 2.3 %collective-permute-start.6 = (bf16[2,80,1024]{2,1,0:T(8,128)(2,1)S(1)}, bf16[2,80,1024]{2,1,0:T(8,128)(2,1)S(1)}, u32[]{:S(2)}, u32[]{:S(2)}) collective-permute-start(bf16[2,80,1024]{2,1,0:T(8,128)(2,1)S(1)} %shard_map.114.near_ref), channel_id=1, source_target_pairs={{0,16},{16,0},{1,17},{17,1},{2,18},{18,2},{3,19},{19,3},{4,20},{20... | collective-permute-start | bytes 983048 | tf_op jit(solution)/shard_map/ppermute | solution.py:322
  53.7 6.7 %shard_map.115 = (bf16[2,2,1280,256]{3,2,1,0:T(8,128)(2,1)S(1)}, bf16[128,1024]{1,0:T(8,128)(2,1)S(1)}, f32[512,256]{1,0:T(8,128)S(1)}, bf16[512,256]{1,0:T(8,128)(2,1)S(1)}) custom-call(s32[32]{0:T(128)S(1)} %bitcast.13, s32[32]{0:T(128)S(1)} %copy-done.3, bf16[8,128,1280]{2,1,0:T(8,128)(2,1)S(1)} %all-to-all-done.refs_0_), custom_call_target="tpu_custom_call" | custom-call | flops 10000000000 | bytes 5000000 | tf_op jit(solution)/shard_map/pallas_call | solution.py:391
  63.6 3.3 %collective-permute-done.7.taken_ref = bf16[512,256]{1,0:T(8,128)(2,1)S(1)} collective-permute-done((bf16[512,256]{1,0:T(8,128)(2,1)S(1)}, bf16[512,256]{1,0:T(8,128)(2,1)S(1)}, u32[]{:S(2)}, u32[]{:S(2)}) %collective-permute-start.7) | collective-permute-done | bytes 262176 | tf_op jit(solution)/shard_map/ppermute | solution.py:415
  70.5 2.1 %collective-permute-start.9 = (bf16[512,256]{1,0:T(8,128)(2,1)S(1)}, bf16[512,256]{1,0:T(8,128)(2,1)S(1)}, u32[]{:S(2)}, u32[]{:S(2)}) collective-permute-start(bf16[512,256]{1,0:T(8,128)(2,1)S(1)} %shard_map.119.refs_0_), channel_id=1, source_target_pairs={{0,2},{1,3},{2,0},{3,1},{4,6},{5,7},{6,4},{7,5},{8,10},{9,11},{10,... | collective-permute-start | bytes 786440 | tf_op jit(solution)/shard_map/ppermute | solution.py:326
  72.6 3.5 %collective-permute-done.10.refs_3_ = bf16[512,256]{1,0:T(8,128)(2,1)S(1)} collective-permute-done((bf16[512,256]{1,0:T(8,128)(2,1)S(1)}, bf16[512,256]{1,0:T(8,128)(2,1)S(1)}, u32[]{:S(2)}, u32[]{:S(2)}) %collective-permute-start.10) | collective-permute-done | bytes 262176 | tf_op jit(solution)/shard_map/ppermute | solution.py:326
  77.9 2.8 %collective-permute-done.9.refs_2_ = bf16[512,256]{1,0:T(8,128)(2,1)S(1)} collective-permute-done((bf16[512,256]{1,0:T(8,128)(2,1)S(1)}, bf16[512,256]{1,0:T(8,128)(2,1)S(1)}, u32[]{:S(2)}, u32[]{:S(2)}) %collective-permute-start.9) | collective-permute-done | bytes 262176 | tf_op jit(solution)/shard_map/ppermute | solution.py:326
  88.0 2.0 %collective-permute-start.16 = (bf16[1664,128]{1,0:T(8,128)(2,1)S(1)}, bf16[1664,128]{1,0:T(8,128)(2,1)S(1)}, u32[]{:S(2)}, u32[]{:S(2)}) collective-permute-start(bf16[1664,128]{1,0:T(8,128)(2,1)S(1)} %get-tuple-element.106), channel_id=1, source_target_pairs={{0,3},{1,0},{2,1},{3,2},{4,7},{5,4},{6,5},{7,6},{8,11},{9,8},{10,9... | collective-permute-start | bytes 1277960 | tf_op jit(solution)/shard_map/ppermute | solution.py:326
  90.1 4.2 %collective-permute-done.17.refs_1_ = bf16[160,1024]{1,0:T(8,128)(2,1)S(1)} collective-permute-done((bf16[160,1024]{1,0:T(8,128)(2,1)S(1)}, bf16[160,1024]{1,0:T(8,128)(2,1)S(1)}, u32[]{:S(2)}, u32[]{:S(2)}) %collective-permute-start.17) | collective-permute-done | bytes 327712 | tf_op jit(solution)/shard_map/ppermute | solution.py:495
  94.4 2.1 %collective-permute-start.18 = (bf16[80,1024]{1,0:T(8,128)(2,1)S(1)}, bf16[80,1024]{1,0:T(8,128)(2,1)S(1)}, u32[]{:S(2)}, u32[]{:S(2)}) collective-permute-start(bf16[80,1024]{1,0:T(8,128)(2,1)S(1)} %get-tuple-element.115), channel_id=1, source_target_pairs={{0,16},{16,0},{1,17},{17,1},{2,18},{18,2},{3,19},{19,3},{4,20},{20... | collective-permute-start | bytes 491528 | tf_op jit(solution)/shard_map/ppermute | solution.py:495
  96.5 4.9 %collective-permute-done.18.refs_1_ = bf16[80,1024]{1,0:T(8,128)(2,1)S(1)} collective-permute-done((bf16[80,1024]{1,0:T(8,128)(2,1)S(1)}, bf16[80,1024]{1,0:T(8,128)(2,1)S(1)}, u32[]{:S(2)}, u32[]{:S(2)}) %collective-permute-start.18) | collective-permute-done | bytes 163872 | tf_op jit(solution)/shard_map/ppermute | solution.py:495
  103.5 2.5 %collective-permute-done.19.refs_1_ = bf16[40,1024]{1,0:T(8,128)(2,1)S(1)} collective-permute-done((bf16[40,1024]{1,0:T(8,128)(2,1)S(1)}, bf16[40,1024]{1,0:T(8,128)(2,1)S(1)}, u32[]{:S(2)}, u32[]{:S(2)}) %collective-permute-start.19) | collective-permute-done | bytes 81952 | tf_op jit(solution)/shard_map/ppermute | solution.py:495
  106.0 3.3 %collective-permute-start.20 = (bf16[20,1024]{1,0:T(8,128)(2,1)S(1)}, bf16[20,1024]{1,0:T(8,128)(2,1)S(1)}, u32[]{:S(2)}, u32[]{:S(2)}) collective-permute-start(bf16[20,1024]{1,0:T(8,128)(2,1)S(1)} %get-tuple-element.119), channel_id=1, source_target_pairs={{0,64},{32,96},{64,0},{96,32},{128,192},{160,224},{192,128},{224,1... | collective-permute-start | bytes 122888 | tf_op jit(solution)/shard_map/ppermute | solution.py:495
  109.4 2.1 %collective-permute-done.20.refs_1_ = bf16[20,1024]{1,0:T(8,128)(2,1)S(1)} collective-permute-done((bf16[20,1024]{1,0:T(8,128)(2,1)S(1)}, bf16[20,1024]{1,0:T(8,128)(2,1)S(1)}, u32[]{:S(2)}, u32[]{:S(2)}) %collective-permute-start.20) | collective-permute-done | bytes 40992 | tf_op jit(solution)/shard_map/ppermute | solution.py:495
  111.5 6.9 %collective-permute-start.21 = (bf16[10,1024]{1,0:T(8,128)(2,1)S(1)}, bf16[10,1024]{1,0:T(8,128)(2,1)S(1)}, u32[]{:S(2)}, u32[]{:S(2)}) collective-permute-start(bf16[10,1024]{1,0:T(8,128)(2,1)S(1)} %get-tuple-element.121), channel_id=1, source_target_pairs={{0,128},{32,160},{64,192},{96,224},{128,0},{160,32},{192,64},{224,... | collective-permute-start | bytes 61448 | tf_op jit(solution)/shard_map/ppermute | solution.py:495
  (48 shorter events, 23.9 us)
Async XLA Ops:
  3.6 50.1 %copy-start.2 = (s32[1,32]{1,0:T(1,128)S(1)}, s32[1,32]{1,0:T(1,128)}, u32[]{:S(2)}) copy-start(s32[1,32]{1,0:T(1,128)} %param.14) | copy-start | bytes 388
  3.6 37.0 %all-to-all-start = ((bf16[8,128,1280]{2,1,0:T(8,128)(2,1)}), bf16[8,128,1280]{2,1,0:T(8,128)(2,1)S(1)}, u32[]{:S(2)}, u32[]{:S(2)}) async-start(bf16[8,128,1280]{2,1,0:T(8,128)(2,1)} %shard_map.111), calls=%async_computation | async-start | bytes 5242880 | tf_op jit(solution)/shard_map/all_to_all | solution.py:330
  9.5 12.0 %collective-permute-start = (bf16[80,1024]{1,0:T(8,128)(2,1)S(1)}, bf16[80,1024]{1,0:T(8,128)(2,1)S(1)}, u32[]{:S(2)}, u32[]{:S(2)}) collective-permute-start(bf16[80,1024]{1,0:T(8,128)(2,1)S(1)} %copy-done.1), channel_id=1, source_target_pairs={{0,128},{32,160},{65,193},{97,225},{130,2},{162,34},{195,67},{227,... | collective-permute-start | bytes 491528 | tf_op jit(solution)/shard_map/ppermute | solution.py:360
  21.5 4.2 %collective-permute-start.1 = (bf16[80,1024]{1,0:T(8,128)(2,1)S(1)}, bf16[80,1024]{1,0:T(8,128)(2,1)S(1)}, u32[]{:S(2)}, u32[]{:S(2)}) collective-permute-start(bf16[80,1024]{1,0:T(8,128)(2,1)S(1)} %shard_map.112.own_ref), channel_id=1, source_target_pairs={{0,64},{2,66},{32,96},{34,98},{65,1},{67,3},{97,33},{99,35},{128,1... | collective-permute-start | bytes 491528 | tf_op jit(solution)/shard_map/ppermute | solution.py:360
  25.7 8.7 %collective-permute-start.2 = (bf16[1,80,1024]{2,1,0:T(8,128)(2,1)S(1)}, bf16[1,80,1024]{2,1,0:T(8,128)(2,1)S(1)}, u32[]{:S(2)}, u32[]{:S(2)}) collective-permute-start(bf16[1,80,1024]{2,1,0:T(8,128)(2,1)S(1)} %bitcast.11), channel_id=1, source_target_pairs={{0,32},{32,0},{64,96},{96,64},{128,160},{160,128},{192,224},{224,1... | collective-permute-start | bytes 491528 | tf_op jit(solution)/shard_map/ppermute | solution.py:322
  42.2 18.2 %collective-permute-start.3 = (bf16[640,128]{1,0:T(8,128)(2,1)S(1)}, bf16[640,128]{1,0:T(8,128)(2,1)S(1)}, u32[]{:S(2)}, u32[]{:S(2)}) collective-permute-start(bf16[640,128]{1,0:T(8,128)(2,1)S(1)} %get-tuple-element.69), channel_id=1, source_target_pairs={{0,1},{1,2},{2,3},{3,0},{4,5},{5,6},{6,7},{7,4},{8,9},{9,10},{10,1... | collective-permute-start | bytes 491528 | tf_op jit(solution)/shard_map/ppermute | solution.py:326
  46.8 13.6 %collective-permute-start.4 = (bf16[640,128]{1,0:T(8,128)(2,1)S(1)}, bf16[640,128]{1,0:T(8,128)(2,1)S(1)}, u32[]{:S(2)}, u32[]{:S(2)}) collective-permute-start(bf16[640,128]{1,0:T(8,128)(2,1)S(1)} %get-tuple-element.70), channel_id=1, source_target_pairs={{0,2},{1,3},{2,0},{3,1},{4,6},{5,7},{6,4},{7,5},{8,10},{9,11},{10,... | collective-permute-start | bytes 491528 | tf_op jit(solution)/shard_map/ppermute | solution.py:326
  51.4 9.0 %collective-permute-start.5 = (bf16[640,128]{1,0:T(8,128)(2,1)S(1)}, bf16[640,128]{1,0:T(8,128)(2,1)S(1)}, u32[]{:S(2)}, u32[]{:S(2)}) collective-permute-start(bf16[640,128]{1,0:T(8,128)(2,1)S(1)} %get-tuple-element.71), channel_id=1, source_target_pairs={{0,3},{1,0},{2,1},{3,2},{4,7},{5,4},{6,5},{7,6},{8,11},{9,8},{10,9... | collective-permute-start | bytes 491528 | tf_op jit(solution)/shard_map/ppermute | solution.py:326
  51.4 9.1 %collective-permute-start.6 = (bf16[2,80,1024]{2,1,0:T(8,128)(2,1)S(1)}, bf16[2,80,1024]{2,1,0:T(8,128)(2,1)S(1)}, u32[]{:S(2)}, u32[]{:S(2)}) collective-permute-start(bf16[2,80,1024]{2,1,0:T(8,128)(2,1)S(1)} %shard_map.114.near_ref), channel_id=1, source_target_pairs={{0,16},{16,0},{1,17},{17,1},{2,18},{18,2},{3,19},{19,3},{4,20},{20... | collective-permute-start | bytes 983048 | tf_op jit(solution)/shard_map/ppermute | solution.py:322
  60.5 6.4 %collective-permute-start.7 = (bf16[512,256]{1,0:T(8,128)(2,1)S(1)}, bf16[512,256]{1,0:T(8,128)(2,1)S(1)}, u32[]{:S(2)}, u32[]{:S(2)}) collective-permute-start(bf16[512,256]{1,0:T(8,128)(2,1)S(1)} %get-tuple-element.73), channel_id=1, source_target_pairs={{0,4},{4,0},{1,5},{5,1},{2,6},{6,2},{3,7},{7,3},{8,12},{12,8},{9,1... | collective-permute-start | bytes 786440 | tf_op jit(solution)/shard_map/ppermute | solution.py:415
  63.5 17.2 %collective-permute-start.12 = (bf16[4,80,1024]{2,1,0:T(8,128)(2,1)S(1)}, bf16[4,80,1024]{2,1,0:T(8,128)(2,1)S(1)}, u32[]{:S(2)}, u32[]{:S(2)}) collective-permute-start(bf16[4,80,1024]{2,1,0:T(8,128)(2,1)S(1)} %shard_map.118.w_ref), channel_id=1, source_target_pairs={{0,8},{8,0},{1,9},{9,1},{2,10},{10,2},{3,11},{11,3},{4,12},{12,4},... | collective-permute-start | bytes 1966088 | tf_op jit(solution)/shard_map/ppermute | solution.py:322
  66.9 13.8 %collective-permute-start.11 = (bf16[4,512,128]{2,1,0:T(8,128)(2,1)S(1)}, bf16[4,512,128]{2,1,0:T(8,128)(2,1)S(1)}, u32[]{:S(2)}, u32[]{:S(2)}) collective-permute-start(bf16[4,512,128]{2,1,0:T(8,128)(2,1)S(1)} %get-tuple-element.84), channel_id=1, source_target_pairs={{0,4},{4,0},{1,5},{5,1},{2,6},{6,2},{3,7},{7,3},{8,12},{12,8},{9,1... | collective-permute-start | bytes 1572872 | tf_op jit(solution)/shard_map/ppermute | solution.py:442
  68.5 7.6 %collective-permute-start.10 = (bf16[512,256]{1,0:T(8,128)(2,1)S(1)}, bf16[512,256]{1,0:T(8,128)(2,1)S(1)}, u32[]{:S(2)}, u32[]{:S(2)}) collective-permute-start(bf16[512,256]{1,0:T(8,128)(2,1)S(1)} %shard_map.119.refs_0_), channel_id=1, source_target_pairs={{0,3},{1,0},{2,1},{3,2},{4,7},{5,4},{6,5},{7,6},{8,11},{9,8},{10,9... | collective-permute-start | bytes 786440 | tf_op jit(solution)/shard_map/ppermute | solution.py:326
  69.1 8.8 %collective-permute-start.8 = (bf16[512,256]{1,0:T(8,128)(2,1)S(1)}, bf16[512,256]{1,0:T(8,128)(2,1)S(1)}, u32[]{:S(2)}, u32[]{:S(2)}) collective-permute-start(bf16[512,256]{1,0:T(8,128)(2,1)S(1)} %shard_map.119.refs_0_), channel_id=1, source_target_pairs={{0,1},{1,2},{2,3},{3,0},{4,5},{5,6},{6,7},{7,4},{8,9},{9,10},{10,1... | collective-permute-start | bytes 786440 | tf_op jit(solution)/shard_map/ppermute | solution.py:326
  70.5 10.2 %collective-permute-start.9 = (bf16[512,256]{1,0:T(8,128)(2,1)S(1)}, bf16[512,256]{1,0:T(8,128)(2,1)S(1)}, u32[]{:S(2)}, u32[]{:S(2)}) collective-permute-start(bf16[512,256]{1,0:T(8,128)(2,1)S(1)} %shard_map.119.refs_0_), channel_id=1, source_target_pairs={{0,2},{1,3},{2,0},{3,1},{4,6},{5,7},{6,4},{7,5},{8,10},{9,11},{10,... | collective-permute-start | bytes 786440 | tf_op jit(solution)/shard_map/ppermute | solution.py:326
  82.1 2.1 %collective-permute-start.13 = (bf16[320,1024]{1,0:T(8,128)(2,1)S(1)}, bf16[320,1024]{1,0:T(8,128)(2,1)S(1)}, u32[]{:S(2)}, u32[]{:S(2)}) collective-permute-start(bf16[320,1024]{1,0:T(8,128)(2,1)S(1)} %get-tuple-element.93), channel_id=1, source_target_pairs={{0,8},{8,0},{1,9},{9,1},{2,10},{10,2},{3,11},{11,3},{4,12},{12,4},... | collective-permute-start | bytes 1966088 | tf_op jit(solution)/shard_map/ppermute | solution.py:322
  84.4 9.8 %collective-permute-start.17 = (bf16[160,1024]{1,0:T(8,128)(2,1)S(1)}, bf16[160,1024]{1,0:T(8,128)(2,1)S(1)}, u32[]{:S(2)}, u32[]{:S(2)}) collective-permute-start(bf16[160,1024]{1,0:T(8,128)(2,1)S(1)} %get-tuple-element.113), channel_id=1, source_target_pairs={{0,4},{4,0},{1,5},{5,1},{2,6},{6,2},{3,7},{7,3},{8,12},{12,8},{9,1... | collective-permute-start | bytes 983048 | tf_op jit(solution)/shard_map/ppermute | solution.py:495
  85.7 32.8 %collective-permute-start.14 = (bf16[1664,128]{1,0:T(8,128)(2,1)S(1)}, bf16[1664,128]{1,0:T(8,128)(2,1)S(1)}, u32[]{:S(2)}, u32[]{:S(2)}) collective-permute-start(bf16[1664,128]{1,0:T(8,128)(2,1)S(1)} %get-tuple-element.104), channel_id=1, source_target_pairs={{0,1},{1,2},{2,3},{3,0},{4,5},{5,6},{6,7},{7,4},{8,9},{9,10},{10,1... | collective-permute-start | bytes 1277960 | tf_op jit(solution)/shard_map/ppermute | solution.py:326
  86.4 32.1 %collective-permute-start.15 = (bf16[1664,128]{1,0:T(8,128)(2,1)S(1)}, bf16[1664,128]{1,0:T(8,128)(2,1)S(1)}, u32[]{:S(2)}, u32[]{:S(2)}) collective-permute-start(bf16[1664,128]{1,0:T(8,128)(2,1)S(1)} %get-tuple-element.105), channel_id=1, source_target_pairs={{0,2},{1,3},{2,0},{3,1},{4,6},{5,7},{6,4},{7,5},{8,10},{9,11},{10,... | collective-permute-start | bytes 1277960 | tf_op jit(solution)/shard_map/ppermute | solution.py:326
  88.0 30.4 %collective-permute-start.16 = (bf16[1664,128]{1,0:T(8,128)(2,1)S(1)}, bf16[1664,128]{1,0:T(8,128)(2,1)S(1)}, u32[]{:S(2)}, u32[]{:S(2)}) collective-permute-start(bf16[1664,128]{1,0:T(8,128)(2,1)S(1)} %get-tuple-element.106), channel_id=1, source_target_pairs={{0,3},{1,0},{2,1},{3,2},{4,7},{5,4},{6,5},{7,6},{8,11},{9,8},{10,9... | collective-permute-start | bytes 1277960 | tf_op jit(solution)/shard_map/ppermute | solution.py:326
  94.4 7.0 %collective-permute-start.18 = (bf16[80,1024]{1,0:T(8,128)(2,1)S(1)}, bf16[80,1024]{1,0:T(8,128)(2,1)S(1)}, u32[]{:S(2)}, u32[]{:S(2)}) collective-permute-start(bf16[80,1024]{1,0:T(8,128)(2,1)S(1)} %get-tuple-element.115), channel_id=1, source_target_pairs={{0,16},{16,0},{1,17},{17,1},{2,18},{18,2},{3,19},{19,3},{4,20},{20... | collective-permute-start | bytes 491528 | tf_op jit(solution)/shard_map/ppermute | solution.py:495
  101.5 4.5 %collective-permute-start.19 = (bf16[40,1024]{1,0:T(8,128)(2,1)S(1)}, bf16[40,1024]{1,0:T(8,128)(2,1)S(1)}, u32[]{:S(2)}, u32[]{:S(2)}) collective-permute-start(bf16[40,1024]{1,0:T(8,128)(2,1)S(1)} %get-tuple-element.117), channel_id=1, source_target_pairs={{0,32},{32,0},{64,96},{96,64},{128,160},{160,128},{192,224},{224,1... | collective-permute-start | bytes 245768 | tf_op jit(solution)/shard_map/ppermute | solution.py:495
  106.0 5.4 %collective-permute-start.20 = (bf16[20,1024]{1,0:T(8,128)(2,1)S(1)}, bf16[20,1024]{1,0:T(8,128)(2,1)S(1)}, u32[]{:S(2)}, u32[]{:S(2)}) collective-permute-start(bf16[20,1024]{1,0:T(8,128)(2,1)S(1)} %get-tuple-element.119), channel_id=1, source_target_pairs={{0,64},{32,96},{64,0},{96,32},{128,192},{160,224},{192,128},{224,1... | collective-permute-start | bytes 122888 | tf_op jit(solution)/shard_map/ppermute | solution.py:495
  111.5 9.2 %collective-permute-start.21 = (bf16[10,1024]{1,0:T(8,128)(2,1)S(1)}, bf16[10,1024]{1,0:T(8,128)(2,1)S(1)}, u32[]{:S(2)}, u32[]{:S(2)}) collective-permute-start(bf16[10,1024]{1,0:T(8,128)(2,1)S(1)} %get-tuple-element.121), channel_id=1, source_target_pairs={{0,128},{32,160},{64,192},{96,224},{128,0},{160,32},{192,64},{224,... | collective-permute-start | bytes 61448 | tf_op jit(solution)/shard_map/ppermute | solution.py:495
  (3 other events, 57.1 us)

commit v9 on v8

--- a/solution.py
+++ b/solution.py
@@ -371,8 +371,6 @@
         )(tile, tile_got)
 
     tile = widen(tile[None], swap(tile[None], 2))
-    got, tile, inputs = lax.optimization_barrier((got, tile, inputs))
-
     turned = pl.pallas_call(
         turn_kernel,
         in_specs=[VMEM],
@@ -408,7 +406,7 @@
             pltpu.SMEM((32,), jnp.int32),
         ],
         compiler_params=params(24),
-        cost_estimate=cost(10_000_000_000, 5_000_000),
+        cost_estimate=cost(0, 5_000),
     )(doc_ids[0], block_order, got)
 
     send, got_x, tile_got = lax.optimization_barrier((send, got_x, tile_got))

time: 122 us -> 119 us (0.975)
  waiting for transfers between devices: 43 us -> 39.4 us
  Pallas kernels: 17.3 us -> 19 us
    all_to_all x1, waiting for transfers between devices: 6.2 us -> 0.01 us  [exchange(): return lax.all_to_all(value, axis, 0, 0, tiled=True)]
    ppermute x9, starting transfers between devices: 17.7 us -> 14.8 us  [to_shift(): lax.ppermute(value, 'x', [(i, (i + s) % 4) for i in range(4)])]
    ppermute x9, waiting for transfers between devices: 8.16 us -> 10.7 us  [to_shift(): lax.ppermute(value, 'x', [(i, (i + s) % 4) for i in range(4)])]
    ppermute x5, starting transfers between devices: 15.6 us -> 17.9 us  [body(): wg_got = lax.ppermute(sends[0], axis, [(i, i ^ mask) for i in range(size)])]
  transfers between devices with their start and end apart: 23 -> 23, of which waited for: 15 -> 13; matrix products, arithmetic and copies ran while one was open for 0% -> 0% of each run, Pallas kernels for 10% -> 11%
where the time goes in v9:
time: 119 us; the launch traced here: 118 us
  starting transfers between devices  57.9 us (49%)
  waiting for transfers between devices  39.4 us (33%)
  Pallas kernels  19 us (16%)
    ppermute x5, starting transfers between devices, body(): wg_got = lax.ppermute(sends[0], axis, [(i, i ^ mask) for i in range(size)])  17.9 us
    ppermute x9, starting transfers between devices, to_shift(): lax.ppermute(value, 'x', [(i, (i + s) % 4) for i in range(4)])  14.8 us
    ppermute x5, waiting for transfers between devices, body(): wg_got = lax.ppermute(sends[0], axis, [(i, i ^ mask) for i in range(size)])  14 us
    ppermute x9, waiting for transfers between devices, to_shift(): lax.ppermute(value, 'x', [(i, (i + s) % 4) for i in range(4)])  10.7 us
    ppermute x2, starting transfers between devices, body(): lax.ppermute(tile, ('z', 'x'), pairs)  10.4 us
    ppermute x4, starting transfers between devices, swap(): lax.ppermute(value, axis, [(i, i ^ mask) for i in range(8 if axis == 'z'...  6.92 us
    pallas_call x1, Pallas kernels, body(): pl.pallas_call(attention_kernel, in_specs=[SMEM] * 2 + [VMEM], out_specs=...  6.72 us
    all_to_all x1, starting transfers between devices, exchange(): return lax.all_to_all(value, axis, 0, 0, tiled=True)  5.9 us
  transfers between devices with their start and end apart: 23, of which 13 were waited for; matrix products, arithmetic and copies ran while one was open for 0% of the time, Pallas kernels for 11%

profile of v9, /device:TPU:8, one launch (start us, length us, event | category | flops | bytes accessed | tf_op | source)
XLA Modules:
  0.0 118.2 jit_solution(5345062488877877976)
XLA Ops:
  0.6 2.9 %shard_map.111 = bf16[8,128,1280]{2,1,0:T(8,128)(2,1)} custom-call(bf16[128,4096]{1,0:T(8,128)(2,1)} %bitcast.15, bf16[128,4096]{1,0:T(8,128)(2,1)} %bitcast.16, bf16[128,512]{1,0:T(8,128)(2,1)} %bitcast.17, bf16[128,512]{1,0:T(8,128)(2,1)} %bitcast.18), custom_call_target="tpu_custom_call" | custom-call | bytes 5000000 | tf_op jit(solution)/shard_map/pallas_call | solution.py:334
  3.6 5.9 %all-to-all-start = ((bf16[8,128,1280]{2,1,0:T(8,128)(2,1)}), bf16[8,128,1280]{2,1,0:T(8,128)(2,1)S(1)}, u32[]{:S(2)}, u32[]{:S(2)}) async-start(bf16[8,128,1280]{2,1,0:T(8,128)(2,1)} %shard_map.111), calls=%async_computation | async-start | bytes 5242880 | tf_op jit(solution)/shard_map/all_to_all | solution.py:330
  9.5 9.1 %collective-permute-start.3 = (bf16[80,1024]{1,0:T(8,128)(2,1)S(1)}, bf16[80,1024]{1,0:T(8,128)(2,1)S(1)}, u32[]{:S(2)}, u32[]{:S(2)}) collective-permute-start(bf16[80,1024]{1,0:T(8,128)(2,1)S(1)} %copy-done.1), channel_id=1, source_target_pairs={{0,128},{32,160},{65,193},{97,225},{130,2},{162,34},{195,67},{227,... | collective-permute-start | bytes 491528 | tf_op jit(solution)/shard_map/ppermute | solution.py:360
  18.6 2.9 %collective-permute-done.3.got_ref = bf16[80,1024]{1,0:T(8,128)(2,1)S(1)} collective-permute-done((bf16[80,1024]{1,0:T(8,128)(2,1)S(1)}, bf16[80,1024]{1,0:T(8,128)(2,1)S(1)}, u32[]{:S(2)}, u32[]{:S(2)}) %collective-permute-start.3) | collective-permute-done | bytes 163872 | tf_op jit(solution)/shard_map/ppermute | solution.py:360
  22.8 2.9 %collective-permute-done.4.got_ref = bf16[80,1024]{1,0:T(8,128)(2,1)S(1)} collective-permute-done((bf16[80,1024]{1,0:T(8,128)(2,1)S(1)}, bf16[80,1024]{1,0:T(8,128)(2,1)S(1)}, u32[]{:S(2)}, u32[]{:S(2)}) %collective-permute-start.4) | collective-permute-done | bytes 163872 | tf_op jit(solution)/shard_map/ppermute | solution.py:360
  25.7 4.4 %collective-permute-start.5 = (bf16[1,80,1024]{2,1,0:T(8,128)(2,1)S(1)}, bf16[1,80,1024]{2,1,0:T(8,128)(2,1)S(1)}, u32[]{:S(2)}, u32[]{:S(2)}) collective-permute-start(bf16[1,80,1024]{2,1,0:T(8,128)(2,1)S(1)} %bitcast.11), channel_id=1, source_target_pairs={{0,32},{32,0},{64,96},{96,64},{128,160},{160,128},{192,224},{224,1... | collective-permute-start | bytes 491528 | tf_op jit(solution)/shard_map/ppermute | solution.py:322
  30.1 4.3 %collective-permute-done.5.far_ref = bf16[1,80,1024]{2,1,0:T(8,128)(2,1)S(1)} collective-permute-done((bf16[1,80,1024]{2,1,0:T(8,128)(2,1)S(1)}, bf16[1,80,1024]{2,1,0:T(8,128)(2,1)S(1)}, u32[]{:S(2)}, u32[]{:S(2)}) %collective-permute-start.5) | collective-permute-done | bytes 163872 | tf_op jit(solution)/shard_map/ppermute | solution.py:322
  34.4 2.4 %collective-permute-start.6 = (bf16[2,80,1024]{2,1,0:T(8,128)(2,1)S(1)}, bf16[2,80,1024]{2,1,0:T(8,128)(2,1)S(1)}, u32[]{:S(2)}, u32[]{:S(2)}) collective-permute-start(bf16[2,80,1024]{2,1,0:T(8,128)(2,1)S(1)} %shard_map.116.near_ref), channel_id=1, source_target_pairs={{0,16},{16,0},{1,17},{17,1},{2,18},{18,2},{3,19},{19,3},{4,20},{20... | collective-permute-start | bytes 983048 | tf_op jit(solution)/shard_map/ppermute | solution.py:322
  39.1 4.1 %collective-permute-start = (bf16[640,128]{1,0:T(8,128)(2,1)}, bf16[640,128]{1,0:T(8,128)(2,1)}, u32[]{:S(2)}, u32[]{:S(2)}) collective-permute-start(bf16[640,128]{1,0:T(8,128)(2,1)} %get-tuple-element.63), channel_id=1, source_target_pairs={{0,1},{1,2},{2,3},{3,0},{4,5},{5,6},{6,7},{7,4},{8,9},{9,10},{10,1... | collective-permute-start | bytes 491528 | tf_op jit(solution)/shard_map/ppermute | solution.py:326
  43.3 2.3 %collective-permute-start.1 = (bf16[640,128]{1,0:T(8,128)(2,1)}, bf16[640,128]{1,0:T(8,128)(2,1)}, u32[]{:S(2)}, u32[]{:S(2)}) collective-permute-start(bf16[640,128]{1,0:T(8,128)(2,1)} %get-tuple-element.64), channel_id=1, source_target_pairs={{0,2},{1,3},{2,0},{3,1},{4,6},{5,7},{6,4},{7,5},{8,10},{9,11},{10,... | collective-permute-start | bytes 491528 | tf_op jit(solution)/shard_map/ppermute | solution.py:326
  45.9 6.7 %shard_map.112 = (bf16[2,2,1280,256]{3,2,1,0:T(8,128)(2,1)S(1)}, bf16[128,1024]{1,0:T(8,128)(2,1)S(1)}, f32[512,256]{1,0:T(8,128)S(1)}, bf16[512,256]{1,0:T(8,128)(2,1)S(1)}) custom-call(s32[32]{0:T(128)S(1)} %bitcast.13, s32[32]{0:T(128)S(1)} %copy-done.3, bf16[8,128,1280]{2,1,0:T(8,128)(2,1)S(1)} %all-to-all-done.refs_0_), custom_call_target="tpu_custom_call" | custom-call | bytes 5000 | tf_op jit(solution)/shard_map/pallas_call | solution.py:389
  55.9 3.8 %collective-permute-done.7.taken_ref = bf16[512,256]{1,0:T(8,128)(2,1)S(1)} collective-permute-done((bf16[512,256]{1,0:T(8,128)(2,1)S(1)}, bf16[512,256]{1,0:T(8,128)(2,1)S(1)}, u32[]{:S(2)}, u32[]{:S(2)}) %collective-permute-start.7) | collective-permute-done | bytes 262176 | tf_op jit(solution)/shard_map/ppermute | solution.py:413
  60.5 3.3 %collective-permute-start.10 = (bf16[512,256]{1,0:T(8,128)(2,1)S(1)}, bf16[512,256]{1,0:T(8,128)(2,1)S(1)}, u32[]{:S(2)}, u32[]{:S(2)}) collective-permute-start(bf16[512,256]{1,0:T(8,128)(2,1)S(1)} %shard_map.119.refs_0_), channel_id=1, source_target_pairs={{0,3},{1,0},{2,1},{3,2},{4,7},{5,4},{6,5},{7,6},{8,11},{9,8},{10,9... | collective-permute-start | bytes 786440 | tf_op jit(solution)/shard_map/ppermute | solution.py:326
  65.3 7.7 %collective-permute-done.10.refs_3_ = bf16[512,256]{1,0:T(8,128)(2,1)S(1)} collective-permute-done((bf16[512,256]{1,0:T(8,128)(2,1)S(1)}, bf16[512,256]{1,0:T(8,128)(2,1)S(1)}, u32[]{:S(2)}, u32[]{:S(2)}) %collective-permute-start.10) | collective-permute-done | bytes 262176 | tf_op jit(solution)/shard_map/ppermute | solution.py:326
  73.0 2.9 %collective-permute-done.8.refs_1_ = bf16[512,256]{1,0:T(8,128)(2,1)S(1)} collective-permute-done((bf16[512,256]{1,0:T(8,128)(2,1)S(1)}, bf16[512,256]{1,0:T(8,128)(2,1)S(1)}, u32[]{:S(2)}, u32[]{:S(2)}) %collective-permute-start.8) | collective-permute-done | bytes 262176 | tf_op jit(solution)/shard_map/ppermute | solution.py:326
  76.0 2.3 %shard_map.120 = (bf16[512,1024]{1,0:T(8,128)(2,1)S(1)}, bf16[128,1024]{1,0:T(8,128)(2,1)}, bf16[320,1024]{1,0:T(8,128)(2,1)S(1)}, f32[320,1024]{1,0:T(8,128)S(1)}) custom-call(bf16[512,256]{1,0:T(8,128)(2,1)S(1)} %shard_map.119.refs_0_, bf16[512,256]{1,0:T(8,128)(2,1)S(1)} %collective-permute-done.8.refs_1_, ...), custom_call_target="tpu_custom_call" | custom-call | flops 700000000 | bytes 6000000 | tf_op jit(solution)/shard_map/pallas_call | solution.py:443
  82.4 2.3 %collective-permute-start.15 = (bf16[1664,128]{1,0:T(8,128)(2,1)S(1)}, bf16[1664,128]{1,0:T(8,128)(2,1)S(1)}, u32[]{:S(2)}, u32[]{:S(2)}) collective-permute-start(bf16[1664,128]{1,0:T(8,128)(2,1)S(1)} %get-tuple-element.99), channel_id=1, source_target_pairs={{0,2},{1,3},{2,0},{3,1},{4,6},{5,7},{6,4},{7,5},{8,10},{9,11},{10,... | collective-permute-start | bytes 1277960 | tf_op jit(solution)/shard_map/ppermute | solution.py:326
  85.7 4.9 %collective-permute-done.17.refs_1_ = bf16[160,1024]{1,0:T(8,128)(2,1)S(1)} collective-permute-done((bf16[160,1024]{1,0:T(8,128)(2,1)S(1)}, bf16[160,1024]{1,0:T(8,128)(2,1)S(1)}, u32[]{:S(2)}, u32[]{:S(2)}) %collective-permute-start.17) | collective-permute-done | bytes 327712 | tf_op jit(solution)/shard_map/ppermute | solution.py:493
  90.7 3.0 %collective-permute-start.18 = (bf16[80,1024]{1,0:T(8,128)(2,1)S(1)}, bf16[80,1024]{1,0:T(8,128)(2,1)S(1)}, u32[]{:S(2)}, u32[]{:S(2)}) collective-permute-start(bf16[80,1024]{1,0:T(8,128)(2,1)S(1)} %get-tuple-element.109), channel_id=1, source_target_pairs={{0,16},{16,0},{1,17},{17,1},{2,18},{18,2},{3,19},{19,3},{4,20},{20... | collective-permute-start | bytes 491528 | tf_op jit(solution)/shard_map/ppermute | solution.py:493
  93.7 4.0 %collective-permute-done.18.refs_1_ = bf16[80,1024]{1,0:T(8,128)(2,1)S(1)} collective-permute-done((bf16[80,1024]{1,0:T(8,128)(2,1)S(1)}, bf16[80,1024]{1,0:T(8,128)(2,1)S(1)}, u32[]{:S(2)}, u32[]{:S(2)}) %collective-permute-start.18) | collective-permute-done | bytes 163872 | tf_op jit(solution)/shard_map/ppermute | solution.py:493
  97.7 2.6 %collective-permute-start.19 = (bf16[40,1024]{1,0:T(8,128)(2,1)S(1)}, bf16[40,1024]{1,0:T(8,128)(2,1)S(1)}, u32[]{:S(2)}, u32[]{:S(2)}) collective-permute-start(bf16[40,1024]{1,0:T(8,128)(2,1)S(1)} %get-tuple-element.111), channel_id=1, source_target_pairs={{0,32},{32,0},{64,96},{96,64},{128,160},{160,128},{192,224},{224,1... | collective-permute-start | bytes 245768 | tf_op jit(solution)/shard_map/ppermute | solution.py:493
  100.4 2.4 %collective-permute-done.19.refs_1_ = bf16[40,1024]{1,0:T(8,128)(2,1)S(1)} collective-permute-done((bf16[40,1024]{1,0:T(8,128)(2,1)S(1)}, bf16[40,1024]{1,0:T(8,128)(2,1)S(1)}, u32[]{:S(2)}, u32[]{:S(2)}) %collective-permute-start.19) | collective-permute-done | bytes 81952 | tf_op jit(solution)/shard_map/ppermute | solution.py:493
  102.8 3.6 %collective-permute-start.20 = (bf16[20,1024]{1,0:T(8,128)(2,1)S(1)}, bf16[20,1024]{1,0:T(8,128)(2,1)S(1)}, u32[]{:S(2)}, u32[]{:S(2)}) collective-permute-start(bf16[20,1024]{1,0:T(8,128)(2,1)S(1)} %get-tuple-element.113), channel_id=1, source_target_pairs={{0,64},{32,96},{64,0},{96,32},{128,192},{160,224},{192,128},{224,1... | collective-permute-start | bytes 122888 | tf_op jit(solution)/shard_map/ppermute | solution.py:493
  108.5 6.9 %collective-permute-start.21 = (bf16[10,1024]{1,0:T(8,128)(2,1)S(1)}, bf16[10,1024]{1,0:T(8,128)(2,1)S(1)}, u32[]{:S(2)}, u32[]{:S(2)}) collective-permute-start(bf16[10,1024]{1,0:T(8,128)(2,1)S(1)} %get-tuple-element.115), channel_id=1, source_target_pairs={{0,128},{32,160},{64,192},{96,224},{128,0},{160,32},{192,64},{224,... | collective-permute-start | bytes 61448 | tf_op jit(solution)/shard_map/ppermute | solution.py:493
  (48 shorter events, 19.9 us)
Async XLA Ops:
  3.6 42.4 %copy-start.2 = (s32[1,32]{1,0:T(1,128)S(1)}, s32[1,32]{1,0:T(1,128)}, u32[]{:S(2)}) copy-start(s32[1,32]{1,0:T(1,128)} %param.14) | copy-start | bytes 388
  3.6 42.3 %all-to-all-start = ((bf16[8,128,1280]{2,1,0:T(8,128)(2,1)}), bf16[8,128,1280]{2,1,0:T(8,128)(2,1)S(1)}, u32[]{:S(2)}, u32[]{:S(2)}) async-start(bf16[8,128,1280]{2,1,0:T(8,128)(2,1)} %shard_map.111), calls=%async_computation | async-start | bytes 5242880 | tf_op jit(solution)/shard_map/all_to_all | solution.py:330
  9.5 12.0 %collective-permute-start.3 = (bf16[80,1024]{1,0:T(8,128)(2,1)S(1)}, bf16[80,1024]{1,0:T(8,128)(2,1)S(1)}, u32[]{:S(2)}, u32[]{:S(2)}) collective-permute-start(bf16[80,1024]{1,0:T(8,128)(2,1)S(1)} %copy-done.1), channel_id=1, source_target_pairs={{0,128},{32,160},{65,193},{97,225},{130,2},{162,34},{195,67},{227,... | collective-permute-start | bytes 491528 | tf_op jit(solution)/shard_map/ppermute | solution.py:360
  21.5 4.2 %collective-permute-start.4 = (bf16[80,1024]{1,0:T(8,128)(2,1)S(1)}, bf16[80,1024]{1,0:T(8,128)(2,1)S(1)}, u32[]{:S(2)}, u32[]{:S(2)}) collective-permute-start(bf16[80,1024]{1,0:T(8,128)(2,1)S(1)} %shard_map.114.own_ref), channel_id=1, source_target_pairs={{0,64},{2,66},{32,96},{34,98},{65,1},{67,3},{97,33},{99,35},{128,1... | collective-permute-start | bytes 491528 | tf_op jit(solution)/shard_map/ppermute | solution.py:360
  25.7 8.7 %collective-permute-start.5 = (bf16[1,80,1024]{2,1,0:T(8,128)(2,1)S(1)}, bf16[1,80,1024]{2,1,0:T(8,128)(2,1)S(1)}, u32[]{:S(2)}, u32[]{:S(2)}) collective-permute-start(bf16[1,80,1024]{2,1,0:T(8,128)(2,1)S(1)} %bitcast.11), channel_id=1, source_target_pairs={{0,32},{32,0},{64,96},{96,64},{128,160},{160,128},{192,224},{224,1... | collective-permute-start | bytes 491528 | tf_op jit(solution)/shard_map/ppermute | solution.py:322
  34.4 18.4 %collective-permute-start.6 = (bf16[2,80,1024]{2,1,0:T(8,128)(2,1)S(1)}, bf16[2,80,1024]{2,1,0:T(8,128)(2,1)S(1)}, u32[]{:S(2)}, u32[]{:S(2)}) collective-permute-start(bf16[2,80,1024]{2,1,0:T(8,128)(2,1)S(1)} %shard_map.116.near_ref), channel_id=1, source_target_pairs={{0,16},{16,0},{1,17},{17,1},{2,18},{18,2},{3,19},{19,3},{4,20},{20... | collective-permute-start | bytes 983048 | tf_op jit(solution)/shard_map/ppermute | solution.py:322
  39.1 13.6 %collective-permute-start = (bf16[640,128]{1,0:T(8,128)(2,1)}, bf16[640,128]{1,0:T(8,128)(2,1)}, u32[]{:S(2)}, u32[]{:S(2)}) collective-permute-start(bf16[640,128]{1,0:T(8,128)(2,1)} %get-tuple-element.63), channel_id=1, source_target_pairs={{0,1},{1,2},{2,3},{3,0},{4,5},{5,6},{6,7},{7,4},{8,9},{9,10},{10,1... | collective-permute-start | bytes 491528 | tf_op jit(solution)/shard_map/ppermute | solution.py:326
  43.3 9.4 %collective-permute-start.1 = (bf16[640,128]{1,0:T(8,128)(2,1)}, bf16[640,128]{1,0:T(8,128)(2,1)}, u32[]{:S(2)}, u32[]{:S(2)}) collective-permute-start(bf16[640,128]{1,0:T(8,128)(2,1)} %get-tuple-element.64), channel_id=1, source_target_pairs={{0,2},{1,3},{2,0},{3,1},{4,6},{5,7},{6,4},{7,5},{8,10},{9,11},{10,... | collective-permute-start | bytes 491528 | tf_op jit(solution)/shard_map/ppermute | solution.py:326
  45.6 7.2 %collective-permute-start.2 = (bf16[640,128]{1,0:T(8,128)(2,1)}, bf16[640,128]{1,0:T(8,128)(2,1)}, u32[]{:S(2)}, u32[]{:S(2)}) collective-permute-start(bf16[640,128]{1,0:T(8,128)(2,1)} %get-tuple-element.65), channel_id=1, source_target_pairs={{0,3},{1,0},{2,1},{3,2},{4,7},{5,4},{6,5},{7,6},{8,11},{9,8},{10,9... | collective-permute-start | bytes 491528 | tf_op jit(solution)/shard_map/ppermute | solution.py:326
  52.8 6.9 %collective-permute-start.7 = (bf16[512,256]{1,0:T(8,128)(2,1)S(1)}, bf16[512,256]{1,0:T(8,128)(2,1)S(1)}, u32[]{:S(2)}, u32[]{:S(2)}) collective-permute-start(bf16[512,256]{1,0:T(8,128)(2,1)S(1)} %get-tuple-element.67), channel_id=1, source_target_pairs={{0,4},{4,0},{1,5},{5,1},{2,6},{6,2},{3,7},{7,3},{8,12},{12,8},{9,1... | collective-permute-start | bytes 786440 | tf_op jit(solution)/shard_map/ppermute | solution.py:413
  55.8 20.2 %collective-permute-start.12 = (bf16[4,80,1024]{2,1,0:T(8,128)(2,1)S(1)}, bf16[4,80,1024]{2,1,0:T(8,128)(2,1)S(1)}, u32[]{:S(2)}, u32[]{:S(2)}) collective-permute-start(bf16[4,80,1024]{2,1,0:T(8,128)(2,1)S(1)} %shard_map.118.w_ref), channel_id=1, source_target_pairs={{0,8},{8,0},{1,9},{9,1},{2,10},{10,2},{3,11},{11,3},{4,12},{12,4},... | collective-permute-start | bytes 1966088 | tf_op jit(solution)/shard_map/ppermute | solution.py:322
  59.7 16.2 %collective-permute-start.11 = (bf16[4,512,128]{2,1,0:T(8,128)(2,1)S(1)}, bf16[4,512,128]{2,1,0:T(8,128)(2,1)S(1)}, u32[]{:S(2)}, u32[]{:S(2)}) collective-permute-start(bf16[4,512,128]{2,1,0:T(8,128)(2,1)S(1)} %get-tuple-element.78), channel_id=1, source_target_pairs={{0,4},{4,0},{1,5},{5,1},{2,6},{6,2},{3,7},{7,3},{8,12},{12,8},{9,1... | collective-permute-start | bytes 1572872 | tf_op jit(solution)/shard_map/ppermute | solution.py:440
  60.5 12.5 %collective-permute-start.10 = (bf16[512,256]{1,0:T(8,128)(2,1)S(1)}, bf16[512,256]{1,0:T(8,128)(2,1)S(1)}, u32[]{:S(2)}, u32[]{:S(2)}) collective-permute-start(bf16[512,256]{1,0:T(8,128)(2,1)S(1)} %shard_map.119.refs_0_), channel_id=1, source_target_pairs={{0,3},{1,0},{2,1},{3,2},{4,7},{5,4},{6,5},{7,6},{8,11},{9,8},{10,9... | collective-permute-start | bytes 786440 | tf_op jit(solution)/shard_map/ppermute | solution.py:326
  63.8 12.1 %collective-permute-start.8 = (bf16[512,256]{1,0:T(8,128)(2,1)S(1)}, bf16[512,256]{1,0:T(8,128)(2,1)S(1)}, u32[]{:S(2)}, u32[]{:S(2)}) collective-permute-start(bf16[512,256]{1,0:T(8,128)(2,1)S(1)} %shard_map.119.refs_0_), channel_id=1, source_target_pairs={{0,1},{1,2},{2,3},{3,0},{4,5},{5,6},{6,7},{7,4},{8,9},{9,10},{10,1... | collective-permute-start | bytes 786440 | tf_op jit(solution)/shard_map/ppermute | solution.py:326
  63.8 12.1 %collective-permute-start.9 = (bf16[512,256]{1,0:T(8,128)(2,1)S(1)}, bf16[512,256]{1,0:T(8,128)(2,1)S(1)}, u32[]{:S(2)}, u32[]{:S(2)}) collective-permute-start(bf16[512,256]{1,0:T(8,128)(2,1)S(1)} %shard_map.119.refs_0_), channel_id=1, source_target_pairs={{0,2},{1,3},{2,0},{3,1},{4,6},{5,7},{6,4},{7,5},{8,10},{9,11},{10,... | collective-permute-start | bytes 786440 | tf_op jit(solution)/shard_map/ppermute | solution.py:326
  78.2 2.2 %collective-permute-start.13 = (bf16[320,1024]{1,0:T(8,128)(2,1)S(1)}, bf16[320,1024]{1,0:T(8,128)(2,1)S(1)}, u32[]{:S(2)}, u32[]{:S(2)}) collective-permute-start(bf16[320,1024]{1,0:T(8,128)(2,1)S(1)} %get-tuple-element.87), channel_id=1, source_target_pairs={{0,8},{8,0},{1,9},{9,1},{2,10},{10,2},{3,11},{11,3},{4,12},{12,4},... | collective-permute-start | bytes 1966088 | tf_op jit(solution)/shard_map/ppermute | solution.py:322
  80.7 9.8 %collective-permute-start.17 = (bf16[160,1024]{1,0:T(8,128)(2,1)S(1)}, bf16[160,1024]{1,0:T(8,128)(2,1)S(1)}, u32[]{:S(2)}, u32[]{:S(2)}) collective-permute-start(bf16[160,1024]{1,0:T(8,128)(2,1)S(1)} %get-tuple-element.107), channel_id=1, source_target_pairs={{0,4},{4,0},{1,5},{5,1},{2,6},{6,2},{3,7},{7,3},{8,12},{12,8},{9,1... | collective-permute-start | bytes 983048 | tf_op jit(solution)/shard_map/ppermute | solution.py:493
  82.4 32.9 %collective-permute-start.14 = (bf16[1664,128]{1,0:T(8,128)(2,1)S(1)}, bf16[1664,128]{1,0:T(8,128)(2,1)S(1)}, u32[]{:S(2)}, u32[]{:S(2)}) collective-permute-start(bf16[1664,128]{1,0:T(8,128)(2,1)S(1)} %get-tuple-element.98), channel_id=1, source_target_pairs={{0,1},{1,2},{2,3},{3,0},{4,5},{5,6},{6,7},{7,4},{8,9},{9,10},{10,1... | collective-permute-start | bytes 1277960 | tf_op jit(solution)/shard_map/ppermute | solution.py:326
  82.4 32.9 %collective-permute-start.15 = (bf16[1664,128]{1,0:T(8,128)(2,1)S(1)}, bf16[1664,128]{1,0:T(8,128)(2,1)S(1)}, u32[]{:S(2)}, u32[]{:S(2)}) collective-permute-start(bf16[1664,128]{1,0:T(8,128)(2,1)S(1)} %get-tuple-element.99), channel_id=1, source_target_pairs={{0,2},{1,3},{2,0},{3,1},{4,6},{5,7},{6,4},{7,5},{8,10},{9,11},{10,... | collective-permute-start | bytes 1277960 | tf_op jit(solution)/shard_map/ppermute | solution.py:326
  84.7 30.7 %collective-permute-start.16 = (bf16[1664,128]{1,0:T(8,128)(2,1)S(1)}, bf16[1664,128]{1,0:T(8,128)(2,1)S(1)}, u32[]{:S(2)}, u32[]{:S(2)}) collective-permute-start(bf16[1664,128]{1,0:T(8,128)(2,1)S(1)} %get-tuple-element.100), channel_id=1, source_target_pairs={{0,3},{1,0},{2,1},{3,2},{4,7},{5,4},{6,5},{7,6},{8,11},{9,8},{10,9... | collective-permute-start | bytes 1277960 | tf_op jit(solution)/shard_map/ppermute | solution.py:326
  90.7 7.0 %collective-permute-start.18 = (bf16[80,1024]{1,0:T(8,128)(2,1)S(1)}, bf16[80,1024]{1,0:T(8,128)(2,1)S(1)}, u32[]{:S(2)}, u32[]{:S(2)}) collective-permute-start(bf16[80,1024]{1,0:T(8,128)(2,1)S(1)} %get-tuple-element.109), channel_id=1, source_target_pairs={{0,16},{16,0},{1,17},{17,1},{2,18},{18,2},{3,19},{19,3},{4,20},{20... | collective-permute-start | bytes 491528 | tf_op jit(solution)/shard_map/ppermute | solution.py:493
  97.7 5.1 %collective-permute-start.19 = (bf16[40,1024]{1,0:T(8,128)(2,1)S(1)}, bf16[40,1024]{1,0:T(8,128)(2,1)S(1)}, u32[]{:S(2)}, u32[]{:S(2)}) collective-permute-start(bf16[40,1024]{1,0:T(8,128)(2,1)S(1)} %get-tuple-element.111), channel_id=1, source_target_pairs={{0,32},{32,0},{64,96},{96,64},{128,160},{160,128},{192,224},{224,1... | collective-permute-start | bytes 245768 | tf_op jit(solution)/shard_map/ppermute | solution.py:493
  102.8 5.6 %collective-permute-start.20 = (bf16[20,1024]{1,0:T(8,128)(2,1)S(1)}, bf16[20,1024]{1,0:T(8,128)(2,1)S(1)}, u32[]{:S(2)}, u32[]{:S(2)}) collective-permute-start(bf16[20,1024]{1,0:T(8,128)(2,1)S(1)} %get-tuple-element.113), channel_id=1, source_target_pairs={{0,64},{32,96},{64,0},{96,32},{128,192},{160,224},{192,128},{224,1... | collective-permute-start | bytes 122888 | tf_op jit(solution)/shard_map/ppermute | solution.py:493
  108.5 9.1 %collective-permute-start.21 = (bf16[10,1024]{1,0:T(8,128)(2,1)S(1)}, bf16[10,1024]{1,0:T(8,128)(2,1)S(1)}, u32[]{:S(2)}, u32[]{:S(2)}) collective-permute-start(bf16[10,1024]{1,0:T(8,128)(2,1)S(1)} %get-tuple-element.115), channel_id=1, source_target_pairs={{0,128},{32,160},{64,192},{96,224},{128,0},{160,32},{192,64},{224,... | collective-permute-start | bytes 61448 | tf_op jit(solution)/shard_map/ppermute | solution.py:493
  (3 other events, 49.4 us)

commit v10 on v9

--- a/solution.py
+++ b/solution.py
@@ -84,8 +84,8 @@
 
 
 def tile_row(z, low, y):
-    row = (low % 2) * 320 + y * 160 + (low // 2) * 80
-    return row + (z % 2) * 40 + (z // 2 % 2) * 20 + (z // 4) * 10
+    row = (low % 2) * 320 + y * 160 + (z % 2) * 80
+    return row + (low // 2) * 40 + (z // 2 % 2) * 20 + (z // 4) * 10
 
 
 def turn_kernel(in_ref, *refs):
@@ -225,15 +225,21 @@
     out_ref[...] = (keep_ref[...] + taken_ref[...].astype(jnp.float32)).astype(jnp.bfloat16)
 
 
+def rows_kernel(*refs):
+    ins, out_ref = refs[:4], refs[4]
+    for s in range(4):
+        at = pl.multiple_of(lax.rem(lax.axis_index("x") + 4 - s, 4) * 128, 128)
+        out_ref[:, pl.ds(at, 128)] = ins[s][...]
+
+
 def weight_kernel(*refs):
-    pieces, ins = refs[:4], refs[4:8]
-    kv_ref, kv_rows_ref, send_ref, keep_ref, x_s = refs[8:]
+    pieces, x_s = refs[:4], refs[4]
+    kv_ref, kv_rows_ref, send_ref, keep_ref = refs[5:]
     core, x = lax.axis_index("core"), lax.axis_index("x")
     for s in range(4):
         at = pl.multiple_of(lax.rem(x + 4 - s, 4) * 128, 128)
         kv_ref[:, pl.ds(at, 128)] = pieces[s][:, 0:128]
         kv_ref[:, pl.ds(pl.multiple_of(512 + at, 128), 128)] = pieces[s][:, 128:256]
-        x_s[:, pl.ds(at, 128)] = ins[s][...]
     part = FEAT_TILE // 2
     other = pl.ds(pl.multiple_of((1 - core) * part, part), part)
     own = pl.ds(pl.multiple_of(core * part, part), part)
@@ -426,7 +432,17 @@
     dq_far, tile, tile_got = lax.optimization_barrier((dq_far, tile, tile_got))
     tile = widen(tile, tile_got)
     far_tile = swap(tile, 0)
-    taken, dq_near, dq_far, tile = lax.optimization_barrier((taken, dq_near, dq_far, tile))
+    rows_x = pl.pallas_call(
+        rows_kernel,
+        in_specs=[VMEM] * 4,
+        out_specs=VMEM,
+        out_shape=shape((FEAT_TILE, SLAB // 2)),
+        compiler_params=params(4),
+        cost_estimate=cost(0, 1_300_000),
+    )(*got_x)
+    taken, dq_near, dq_far, tile, rows_x = lax.optimization_barrier(
+        (taken, dq_near, dq_far, tile, rows_x)
+    )
     own_cols = pl.pallas_call(
         pair_kernel,
         in_specs=[VMEM] * 2,
@@ -442,7 +458,7 @@
 
     kv_half, kv_rows, wg_send, wg_keep = pl.pallas_call(
         weight_kernel,
-        in_specs=[VMEM] * 8,
+        in_specs=[VMEM] * 5,
         out_specs=[VMEM] * 4,
         out_shape=[
             shape((SLAB // 2, 1024)),
@@ -450,10 +466,9 @@
             shape((FEAT_TILE // 2, 1024)),
             shape((FEAT_TILE // 2, 1024), jnp.float32),
         ],
-        scratch_shapes=[pltpu.VMEM((FEAT_TILE, SLAB // 2), jnp.bfloat16)],
         compiler_params=params(12),
         cost_estimate=cost(700_000_000, 6_000_000),
-    )(*pieces, *got_x)
+    )(*pieces, rows_x)
 
     wg_got = swap(wg_send, 0)
     parts = pl.pallas_call(
@@ -487,7 +502,7 @@
     def bit_of(axis, mask):
         return lambda: (lax.axis_index(axis) & mask) // mask
 
-    for axis, mask in (("y", 1), ("yh", 1), ("z", 1), ("z", 2), ("z", 4)):
+    for axis, mask in (("y", 1), ("z", 1), ("yh", 1), ("z", 2), ("z", 4)):
         sends, wg_keep = split(bit_of(axis, mask), 2, wg_keep, wg_got)
         size = 8 if axis == "z" else 2
         wg_got = lax.ppermute(sends[0], axis, [(i, i ^ mask) for i in range(size)])

time: 119 us -> 118 us (level)
  starting transfers between devices: 57.9 us -> 55.3 us
  waiting for transfers between devices: 39.4 us -> 41.2 us
    ppermute x5, starting transfers between devices: 17.9 us -> 15.4 us  [body(): wg_got = lax.ppermute(sends[0], axis, [(i, i ^ mask) for i in range(size)])]
    ppermute x5, waiting for transfers between devices: 14 us -> 15.9 us  [body(): wg_got = lax.ppermute(sends[0], axis, [(i, i ^ mask) for i in range(size)])]
    ppermute x1, waiting for transfers between devices: 3.81 us -> 2.56 us  [body(): taken = lax.ppermute(send, 'y', [(0, 1), (1, 0)])]
    pallas_call x1 -> x2, Pallas kernels: 2.26 us -> 2.46 us  [the longest x1 1.25 us: body(): pl.pallas_call(rows_kernel, in_specs=[VMEM] * 4, out_specs=VMEM, out_shap...]
  transfers between devices with their start and end apart: 23 -> 23, of which waited for: 13 -> 13; matrix products, arithmetic and copies ran while one was open for 0% -> 0% of each run, Pallas kernels for 11% -> 12%
where the time goes in v10:
time: 118 us
  starting transfers between devices  55.3 us (47%)
  waiting for transfers between devices  41.2 us (35%)
  Pallas kernels  19.2 us (16%)
    ppermute x5, waiting for transfers between devices, body(): wg_got = lax.ppermute(sends[0], axis, [(i, i ^ mask) for i in range(size)])  15.9 us
    ppermute x5, starting transfers between devices, body(): wg_got = lax.ppermute(sends[0], axis, [(i, i ^ mask) for i in range(size)])  15.4 us
    ppermute x9, starting transfers between devices, to_shift(): lax.ppermute(value, 'x', [(i, (i + s) % 4) for i in range(4)])  14.8 us
    ppermute x9, waiting for transfers between devices, to_shift(): lax.ppermute(value, 'x', [(i, (i + s) % 4) for i in range(4)])  11.8 us
    ppermute x2, starting transfers between devices, body(): lax.ppermute(tile, ('z', 'x'), pairs)  10.4 us
    ppermute x4, starting transfers between devices, swap(): lax.ppermute(value, axis, [(i, i ^ mask) for i in range(8 if axis == 'z'...  6.85 us
    pallas_call x1, Pallas kernels, body(): pl.pallas_call(attention_kernel, in_specs=[SMEM] * 2 + [VMEM], out_specs=...  6.71 us
    all_to_all x1, starting transfers between devices, exchange(): return lax.all_to_all(value, axis, 0, 0, tiled=True)  5.9 us
  transfers between devices with their start and end apart: 23, of which 13 were waited for; matrix products, arithmetic and copies ran while one was open for 0% of the time, Pallas kernels for 12%

profile of v10, /device:TPU:8, one launch (start us, length us, event | category | flops | bytes accessed | tf_op | source)
XLA Modules:
  0.0 117.6 jit_solution(3769803923823855057)
XLA Ops:
  0.6 2.9 %shard_map.111 = bf16[8,128,1280]{2,1,0:T(8,128)(2,1)} custom-call(bf16[128,4096]{1,0:T(8,128)(2,1)} %bitcast.15, bf16[128,4096]{1,0:T(8,128)(2,1)} %bitcast.16, bf16[128,512]{1,0:T(8,128)(2,1)} %bitcast.17, bf16[128,512]{1,0:T(8,128)(2,1)} %bitcast.18), custom_call_target="tpu_custom_call" | custom-call | bytes 5000000 | tf_op jit(solution)/shard_map/pallas_call | solution.py:340
  3.6 5.9 %all-to-all-start = ((bf16[8,128,1280]{2,1,0:T(8,128)(2,1)}), bf16[8,128,1280]{2,1,0:T(8,128)(2,1)S(1)}, u32[]{:S(2)}, u32[]{:S(2)}) async-start(bf16[8,128,1280]{2,1,0:T(8,128)(2,1)} %shard_map.111), calls=%async_computation | async-start | bytes 5242880 | tf_op jit(solution)/shard_map/all_to_all | solution.py:336
  9.5 9.1 %collective-permute-start.3 = (bf16[80,1024]{1,0:T(8,128)(2,1)S(1)}, bf16[80,1024]{1,0:T(8,128)(2,1)S(1)}, u32[]{:S(2)}, u32[]{:S(2)}) collective-permute-start(bf16[80,1024]{1,0:T(8,128)(2,1)S(1)} %copy-done.1), channel_id=1, source_target_pairs={{0,128},{32,160},{65,193},{97,225},{130,2},{162,34},{195,67},{227,... | collective-permute-start | bytes 491528 | tf_op jit(solution)/shard_map/ppermute | solution.py:366
  18.6 2.9 %collective-permute-done.3.got_ref = bf16[80,1024]{1,0:T(8,128)(2,1)S(1)} collective-permute-done((bf16[80,1024]{1,0:T(8,128)(2,1)S(1)}, bf16[80,1024]{1,0:T(8,128)(2,1)S(1)}, u32[]{:S(2)}, u32[]{:S(2)}) %collective-permute-start.3) | collective-permute-done | bytes 163872 | tf_op jit(solution)/shard_map/ppermute | solution.py:366
  22.8 2.9 %collective-permute-done.4.got_ref = bf16[80,1024]{1,0:T(8,128)(2,1)S(1)} collective-permute-done((bf16[80,1024]{1,0:T(8,128)(2,1)S(1)}, bf16[80,1024]{1,0:T(8,128)(2,1)S(1)}, u32[]{:S(2)}, u32[]{:S(2)}) %collective-permute-start.4) | collective-permute-done | bytes 163872 | tf_op jit(solution)/shard_map/ppermute | solution.py:366
  25.7 4.4 %collective-permute-start.5 = (bf16[1,80,1024]{2,1,0:T(8,128)(2,1)S(1)}, bf16[1,80,1024]{2,1,0:T(8,128)(2,1)S(1)}, u32[]{:S(2)}, u32[]{:S(2)}) collective-permute-start(bf16[1,80,1024]{2,1,0:T(8,128)(2,1)S(1)} %bitcast.11), channel_id=1, source_target_pairs={{0,32},{32,0},{64,96},{96,64},{128,160},{160,128},{192,224},{224,1... | collective-permute-start | bytes 491528 | tf_op jit(solution)/shard_map/ppermute | solution.py:328
  30.1 4.3 %collective-permute-done.5.far_ref = bf16[1,80,1024]{2,1,0:T(8,128)(2,1)S(1)} collective-permute-done((bf16[1,80,1024]{2,1,0:T(8,128)(2,1)S(1)}, bf16[1,80,1024]{2,1,0:T(8,128)(2,1)S(1)}, u32[]{:S(2)}, u32[]{:S(2)}) %collective-permute-start.5) | collective-permute-done | bytes 163872 | tf_op jit(solution)/shard_map/ppermute | solution.py:328
  34.4 2.4 %collective-permute-start.6 = (bf16[2,80,1024]{2,1,0:T(8,128)(2,1)S(1)}, bf16[2,80,1024]{2,1,0:T(8,128)(2,1)S(1)}, u32[]{:S(2)}, u32[]{:S(2)}) collective-permute-start(bf16[2,80,1024]{2,1,0:T(8,128)(2,1)S(1)} %shard_map.116.near_ref), channel_id=1, source_target_pairs={{0,16},{16,0},{1,17},{17,1},{2,18},{18,2},{3,19},{19,3},{4,20},{20... | collective-permute-start | bytes 983048 | tf_op jit(solution)/shard_map/ppermute | solution.py:328
  39.1 4.1 %collective-permute-start = (bf16[640,128]{1,0:T(8,128)(2,1)}, bf16[640,128]{1,0:T(8,128)(2,1)}, u32[]{:S(2)}, u32[]{:S(2)}) collective-permute-start(bf16[640,128]{1,0:T(8,128)(2,1)} %get-tuple-element.64), channel_id=1, source_target_pairs={{0,1},{1,2},{2,3},{3,0},{4,5},{5,6},{6,7},{7,4},{8,9},{9,10},{10,1... | collective-permute-start | bytes 491528 | tf_op jit(solution)/shard_map/ppermute | solution.py:332
  43.2 2.3 %collective-permute-start.1 = (bf16[640,128]{1,0:T(8,128)(2,1)}, bf16[640,128]{1,0:T(8,128)(2,1)}, u32[]{:S(2)}, u32[]{:S(2)}) collective-permute-start(bf16[640,128]{1,0:T(8,128)(2,1)} %get-tuple-element.65), channel_id=1, source_target_pairs={{0,2},{1,3},{2,0},{3,1},{4,6},{5,7},{6,4},{7,5},{8,10},{9,11},{10,... | collective-permute-start | bytes 491528 | tf_op jit(solution)/shard_map/ppermute | solution.py:332
  45.9 6.7 %shard_map.112 = (bf16[2,2,1280,256]{3,2,1,0:T(8,128)(2,1)S(1)}, bf16[128,1024]{1,0:T(8,128)(2,1)S(1)}, f32[512,256]{1,0:T(8,128)S(1)}, bf16[512,256]{1,0:T(8,128)(2,1)S(1)}) custom-call(s32[32]{0:T(128)S(1)} %bitcast.13, s32[32]{0:T(128)S(1)} %copy-done.3, bf16[8,128,1280]{2,1,0:T(8,128)(2,1)S(1)} %all-to-all-done.refs_0_), custom_call_target="tpu_custom_call" | custom-call | bytes 5000 | tf_op jit(solution)/shard_map/pallas_call | solution.py:395
  57.1 2.6 %collective-permute-done.7.taken_ref = bf16[512,256]{1,0:T(8,128)(2,1)S(1)} collective-permute-done((bf16[512,256]{1,0:T(8,128)(2,1)S(1)}, bf16[512,256]{1,0:T(8,128)(2,1)S(1)}, u32[]{:S(2)}, u32[]{:S(2)}) %collective-permute-start.7) | collective-permute-done | bytes 262176 | tf_op jit(solution)/shard_map/ppermute | solution.py:419
  60.5 3.3 %collective-permute-start.10 = (bf16[512,256]{1,0:T(8,128)(2,1)S(1)}, bf16[512,256]{1,0:T(8,128)(2,1)S(1)}, u32[]{:S(2)}, u32[]{:S(2)}) collective-permute-start(bf16[512,256]{1,0:T(8,128)(2,1)S(1)} %shard_map.120.refs_0_), channel_id=1, source_target_pairs={{0,3},{1,0},{2,1},{3,2},{4,7},{5,4},{6,5},{7,6},{8,11},{9,8},{10,9... | collective-permute-start | bytes 786440 | tf_op jit(solution)/shard_map/ppermute | solution.py:332
  65.3 8.3 %collective-permute-done.10.refs_3_ = bf16[512,256]{1,0:T(8,128)(2,1)S(1)} collective-permute-done((bf16[512,256]{1,0:T(8,128)(2,1)S(1)}, bf16[512,256]{1,0:T(8,128)(2,1)S(1)}, u32[]{:S(2)}, u32[]{:S(2)}) %collective-permute-start.10) | collective-permute-done | bytes 262176 | tf_op jit(solution)/shard_map/ppermute | solution.py:332
  73.6 3.4 %collective-permute-done.8.refs_1_ = bf16[512,256]{1,0:T(8,128)(2,1)S(1)} collective-permute-done((bf16[512,256]{1,0:T(8,128)(2,1)S(1)}, bf16[512,256]{1,0:T(8,128)(2,1)S(1)}, u32[]{:S(2)}, u32[]{:S(2)}) %collective-permute-start.8) | collective-permute-done | bytes 262176 | tf_op jit(solution)/shard_map/ppermute | solution.py:332
  81.3 2.3 %collective-permute-start.15 = (bf16[1664,128]{1,0:T(8,128)(2,1)S(1)}, bf16[1664,128]{1,0:T(8,128)(2,1)S(1)}, u32[]{:S(2)}, u32[]{:S(2)}) collective-permute-start(bf16[1664,128]{1,0:T(8,128)(2,1)S(1)} %get-tuple-element.101), channel_id=1, source_target_pairs={{0,2},{1,3},{2,0},{3,1},{4,6},{5,7},{6,4},{7,5},{8,10},{9,11},{10,... | collective-permute-start | bytes 1277960 | tf_op jit(solution)/shard_map/ppermute | solution.py:332
  84.5 5.9 %collective-permute-done.17.refs_1_ = bf16[160,1024]{1,0:T(8,128)(2,1)S(1)} collective-permute-done((bf16[160,1024]{1,0:T(8,128)(2,1)S(1)}, bf16[160,1024]{1,0:T(8,128)(2,1)S(1)}, u32[]{:S(2)}, u32[]{:S(2)}) %collective-permute-start.17) | collective-permute-done | bytes 327712 | tf_op jit(solution)/shard_map/ppermute | solution.py:508
  90.6 2.1 %collective-permute-start.18 = (bf16[80,1024]{1,0:T(8,128)(2,1)S(1)}, bf16[80,1024]{1,0:T(8,128)(2,1)S(1)}, u32[]{:S(2)}, u32[]{:S(2)}) collective-permute-start(bf16[80,1024]{1,0:T(8,128)(2,1)S(1)} %get-tuple-element.111), channel_id=1, source_target_pairs={{0,32},{32,0},{64,96},{96,64},{128,160},{160,128},{192,224},{224,1... | collective-permute-start | bytes 491528 | tf_op jit(solution)/shard_map/ppermute | solution.py:508
  92.6 3.7 %collective-permute-done.18.refs_1_ = bf16[80,1024]{1,0:T(8,128)(2,1)S(1)} collective-permute-done((bf16[80,1024]{1,0:T(8,128)(2,1)S(1)}, bf16[80,1024]{1,0:T(8,128)(2,1)S(1)}, u32[]{:S(2)}, u32[]{:S(2)}) %collective-permute-start.18) | collective-permute-done | bytes 163872 | tf_op jit(solution)/shard_map/ppermute | solution.py:508
  96.4 2.4 %collective-permute-start.19 = (bf16[40,1024]{1,0:T(8,128)(2,1)S(1)}, bf16[40,1024]{1,0:T(8,128)(2,1)S(1)}, u32[]{:S(2)}, u32[]{:S(2)}) collective-permute-start(bf16[40,1024]{1,0:T(8,128)(2,1)S(1)} %get-tuple-element.113), channel_id=1, source_target_pairs={{0,16},{16,0},{1,17},{17,1},{2,18},{18,2},{3,19},{19,3},{4,20},{20... | collective-permute-start | bytes 245768 | tf_op jit(solution)/shard_map/ppermute | solution.py:508
  98.8 3.6 %collective-permute-done.19.refs_1_ = bf16[40,1024]{1,0:T(8,128)(2,1)S(1)} collective-permute-done((bf16[40,1024]{1,0:T(8,128)(2,1)S(1)}, bf16[40,1024]{1,0:T(8,128)(2,1)S(1)}, u32[]{:S(2)}, u32[]{:S(2)}) %collective-permute-start.19) | collective-permute-done | bytes 81952 | tf_op jit(solution)/shard_map/ppermute | solution.py:508
  102.4 3.4 %collective-permute-start.20 = (bf16[20,1024]{1,0:T(8,128)(2,1)S(1)}, bf16[20,1024]{1,0:T(8,128)(2,1)S(1)}, u32[]{:S(2)}, u32[]{:S(2)}) collective-permute-start(bf16[20,1024]{1,0:T(8,128)(2,1)S(1)} %get-tuple-element.115), channel_id=1, source_target_pairs={{0,64},{32,96},{64,0},{96,32},{128,192},{160,224},{192,128},{224,1... | collective-permute-start | bytes 122888 | tf_op jit(solution)/shard_map/ppermute | solution.py:508
  105.8 2.1 %collective-permute-done.20.refs_1_ = bf16[20,1024]{1,0:T(8,128)(2,1)S(1)} collective-permute-done((bf16[20,1024]{1,0:T(8,128)(2,1)S(1)}, bf16[20,1024]{1,0:T(8,128)(2,1)S(1)}, u32[]{:S(2)}, u32[]{:S(2)}) %collective-permute-start.20) | collective-permute-done | bytes 40992 | tf_op jit(solution)/shard_map/ppermute | solution.py:508
  107.9 6.8 %collective-permute-start.21 = (bf16[10,1024]{1,0:T(8,128)(2,1)S(1)}, bf16[10,1024]{1,0:T(8,128)(2,1)S(1)}, u32[]{:S(2)}, u32[]{:S(2)}) collective-permute-start(bf16[10,1024]{1,0:T(8,128)(2,1)S(1)} %get-tuple-element.117), channel_id=1, source_target_pairs={{0,128},{32,160},{64,192},{96,224},{128,0},{160,32},{192,64},{224,... | collective-permute-start | bytes 61448 | tf_op jit(solution)/shard_map/ppermute | solution.py:508
  (49 shorter events, 19.2 us)
Async XLA Ops:
  3.6 42.4 %copy-start.2 = (s32[1,32]{1,0:T(1,128)S(1)}, s32[1,32]{1,0:T(1,128)}, u32[]{:S(2)}) copy-start(s32[1,32]{1,0:T(1,128)} %param.14) | copy-start | bytes 388
  3.6 42.3 %all-to-all-start = ((bf16[8,128,1280]{2,1,0:T(8,128)(2,1)}), bf16[8,128,1280]{2,1,0:T(8,128)(2,1)S(1)}, u32[]{:S(2)}, u32[]{:S(2)}) async-start(bf16[8,128,1280]{2,1,0:T(8,128)(2,1)} %shard_map.111), calls=%async_computation | async-start | bytes 5242880 | tf_op jit(solution)/shard_map/all_to_all | solution.py:336
  9.5 12.0 %collective-permute-start.3 = (bf16[80,1024]{1,0:T(8,128)(2,1)S(1)}, bf16[80,1024]{1,0:T(8,128)(2,1)S(1)}, u32[]{:S(2)}, u32[]{:S(2)}) collective-permute-start(bf16[80,1024]{1,0:T(8,128)(2,1)S(1)} %copy-done.1), channel_id=1, source_target_pairs={{0,128},{32,160},{65,193},{97,225},{130,2},{162,34},{195,67},{227,... | collective-permute-start | bytes 491528 | tf_op jit(solution)/shard_map/ppermute | solution.py:366
  21.5 4.2 %collective-permute-start.4 = (bf16[80,1024]{1,0:T(8,128)(2,1)S(1)}, bf16[80,1024]{1,0:T(8,128)(2,1)S(1)}, u32[]{:S(2)}, u32[]{:S(2)}) collective-permute-start(bf16[80,1024]{1,0:T(8,128)(2,1)S(1)} %shard_map.114.own_ref), channel_id=1, source_target_pairs={{0,64},{2,66},{32,96},{34,98},{65,1},{67,3},{97,33},{99,35},{128,1... | collective-permute-start | bytes 491528 | tf_op jit(solution)/shard_map/ppermute | solution.py:366
  25.7 8.7 %collective-permute-start.5 = (bf16[1,80,1024]{2,1,0:T(8,128)(2,1)S(1)}, bf16[1,80,1024]{2,1,0:T(8,128)(2,1)S(1)}, u32[]{:S(2)}, u32[]{:S(2)}) collective-permute-start(bf16[1,80,1024]{2,1,0:T(8,128)(2,1)S(1)} %bitcast.11), channel_id=1, source_target_pairs={{0,32},{32,0},{64,96},{96,64},{128,160},{160,128},{192,224},{224,1... | collective-permute-start | bytes 491528 | tf_op jit(solution)/shard_map/ppermute | solution.py:328
  34.4 18.4 %collective-permute-start.6 = (bf16[2,80,1024]{2,1,0:T(8,128)(2,1)S(1)}, bf16[2,80,1024]{2,1,0:T(8,128)(2,1)S(1)}, u32[]{:S(2)}, u32[]{:S(2)}) collective-permute-start(bf16[2,80,1024]{2,1,0:T(8,128)(2,1)S(1)} %shard_map.116.near_ref), channel_id=1, source_target_pairs={{0,16},{16,0},{1,17},{17,1},{2,18},{18,2},{3,19},{19,3},{4,20},{20... | collective-permute-start | bytes 983048 | tf_op jit(solution)/shard_map/ppermute | solution.py:328
  39.1 13.5 %collective-permute-start = (bf16[640,128]{1,0:T(8,128)(2,1)}, bf16[640,128]{1,0:T(8,128)(2,1)}, u32[]{:S(2)}, u32[]{:S(2)}) collective-permute-start(bf16[640,128]{1,0:T(8,128)(2,1)} %get-tuple-element.64), channel_id=1, source_target_pairs={{0,1},{1,2},{2,3},{3,0},{4,5},{5,6},{6,7},{7,4},{8,9},{9,10},{10,1... | collective-permute-start | bytes 491528 | tf_op jit(solution)/shard_map/ppermute | solution.py:332
  43.2 9.4 %collective-permute-start.1 = (bf16[640,128]{1,0:T(8,128)(2,1)}, bf16[640,128]{1,0:T(8,128)(2,1)}, u32[]{:S(2)}, u32[]{:S(2)}) collective-permute-start(bf16[640,128]{1,0:T(8,128)(2,1)} %get-tuple-element.65), channel_id=1, source_target_pairs={{0,2},{1,3},{2,0},{3,1},{4,6},{5,7},{6,4},{7,5},{8,10},{9,11},{10,... | collective-permute-start | bytes 491528 | tf_op jit(solution)/shard_map/ppermute | solution.py:332
  45.6 7.2 %collective-permute-start.2 = (bf16[640,128]{1,0:T(8,128)(2,1)}, bf16[640,128]{1,0:T(8,128)(2,1)}, u32[]{:S(2)}, u32[]{:S(2)}) collective-permute-start(bf16[640,128]{1,0:T(8,128)(2,1)} %get-tuple-element.66), channel_id=1, source_target_pairs={{0,3},{1,0},{2,1},{3,2},{4,7},{5,4},{6,5},{7,6},{8,11},{9,8},{10,9... | collective-permute-start | bytes 491528 | tf_op jit(solution)/shard_map/ppermute | solution.py:332
  52.8 6.9 %collective-permute-start.7 = (bf16[512,256]{1,0:T(8,128)(2,1)S(1)}, bf16[512,256]{1,0:T(8,128)(2,1)S(1)}, u32[]{:S(2)}, u32[]{:S(2)}) collective-permute-start(bf16[512,256]{1,0:T(8,128)(2,1)S(1)} %get-tuple-element.68), channel_id=1, source_target_pairs={{0,4},{4,0},{1,5},{5,1},{2,6},{6,2},{3,7},{7,3},{8,12},{12,8},{9,1... | collective-permute-start | bytes 786440 | tf_op jit(solution)/shard_map/ppermute | solution.py:419
  55.8 21.2 %collective-permute-start.12 = (bf16[4,80,1024]{2,1,0:T(8,128)(2,1)S(1)}, bf16[4,80,1024]{2,1,0:T(8,128)(2,1)S(1)}, u32[]{:S(2)}, u32[]{:S(2)}) collective-permute-start(bf16[4,80,1024]{2,1,0:T(8,128)(2,1)S(1)} %shard_map.118.w_ref), channel_id=1, source_target_pairs={{0,8},{8,0},{1,9},{9,1},{2,10},{10,2},{3,11},{11,3},{4,12},{12,4},... | collective-permute-start | bytes 1966088 | tf_op jit(solution)/shard_map/ppermute | solution.py:328
  59.7 17.3 %collective-permute-start.11 = (bf16[4,512,128]{2,1,0:T(8,128)(2,1)S(1)}, bf16[4,512,128]{2,1,0:T(8,128)(2,1)S(1)}, u32[]{:S(2)}, u32[]{:S(2)}) collective-permute-start(bf16[4,512,128]{2,1,0:T(8,128)(2,1)S(1)} %get-tuple-element.83), channel_id=1, source_target_pairs={{0,4},{4,0},{1,5},{5,1},{2,6},{6,2},{3,7},{7,3},{8,12},{12,8},{9,1... | collective-permute-start | bytes 1572872 | tf_op jit(solution)/shard_map/ppermute | solution.py:456
  60.5 13.1 %collective-permute-start.10 = (bf16[512,256]{1,0:T(8,128)(2,1)S(1)}, bf16[512,256]{1,0:T(8,128)(2,1)S(1)}, u32[]{:S(2)}, u32[]{:S(2)}) collective-permute-start(bf16[512,256]{1,0:T(8,128)(2,1)S(1)} %shard_map.120.refs_0_), channel_id=1, source_target_pairs={{0,3},{1,0},{2,1},{3,2},{4,7},{5,4},{6,5},{7,6},{8,11},{9,8},{10,9... | collective-permute-start | bytes 786440 | tf_op jit(solution)/shard_map/ppermute | solution.py:332
  63.8 13.2 %collective-permute-start.8 = (bf16[512,256]{1,0:T(8,128)(2,1)S(1)}, bf16[512,256]{1,0:T(8,128)(2,1)S(1)}, u32[]{:S(2)}, u32[]{:S(2)}) collective-permute-start(bf16[512,256]{1,0:T(8,128)(2,1)S(1)} %shard_map.120.refs_0_), channel_id=1, source_target_pairs={{0,1},{1,2},{2,3},{3,0},{4,5},{5,6},{6,7},{7,4},{8,9},{9,10},{10,1... | collective-permute-start | bytes 786440 | tf_op jit(solution)/shard_map/ppermute | solution.py:332
  63.8 13.2 %collective-permute-start.9 = (bf16[512,256]{1,0:T(8,128)(2,1)S(1)}, bf16[512,256]{1,0:T(8,128)(2,1)S(1)}, u32[]{:S(2)}, u32[]{:S(2)}) collective-permute-start(bf16[512,256]{1,0:T(8,128)(2,1)S(1)} %shard_map.120.refs_0_), channel_id=1, source_target_pairs={{0,2},{1,3},{2,0},{3,1},{4,6},{5,7},{6,4},{7,5},{8,10},{9,11},{10,... | collective-permute-start | bytes 786440 | tf_op jit(solution)/shard_map/ppermute | solution.py:332
  78.2 2.1 %collective-permute-start.13 = (bf16[320,1024]{1,0:T(8,128)(2,1)S(1)}, bf16[320,1024]{1,0:T(8,128)(2,1)S(1)}, u32[]{:S(2)}, u32[]{:S(2)}) collective-permute-start(bf16[320,1024]{1,0:T(8,128)(2,1)S(1)} %get-tuple-element.89), channel_id=1, source_target_pairs={{0,8},{8,0},{1,9},{9,1},{2,10},{10,2},{3,11},{11,3},{4,12},{12,4},... | collective-permute-start | bytes 1966088 | tf_op jit(solution)/shard_map/ppermute | solution.py:328
  80.6 9.8 %collective-permute-start.17 = (bf16[160,1024]{1,0:T(8,128)(2,1)S(1)}, bf16[160,1024]{1,0:T(8,128)(2,1)S(1)}, u32[]{:S(2)}, u32[]{:S(2)}) collective-permute-start(bf16[160,1024]{1,0:T(8,128)(2,1)S(1)} %get-tuple-element.109), channel_id=1, source_target_pairs={{0,4},{4,0},{1,5},{5,1},{2,6},{6,2},{3,7},{7,3},{8,12},{12,8},{9,1... | collective-permute-start | bytes 983048 | tf_op jit(solution)/shard_map/ppermute | solution.py:508
  81.3 33.4 %collective-permute-start.14 = (bf16[1664,128]{1,0:T(8,128)(2,1)S(1)}, bf16[1664,128]{1,0:T(8,128)(2,1)S(1)}, u32[]{:S(2)}, u32[]{:S(2)}) collective-permute-start(bf16[1664,128]{1,0:T(8,128)(2,1)S(1)} %get-tuple-element.100), channel_id=1, source_target_pairs={{0,1},{1,2},{2,3},{3,0},{4,5},{5,6},{6,7},{7,4},{8,9},{9,10},{10,1... | collective-permute-start | bytes 1277960 | tf_op jit(solution)/shard_map/ppermute | solution.py:332
  81.3 33.4 %collective-permute-start.15 = (bf16[1664,128]{1,0:T(8,128)(2,1)S(1)}, bf16[1664,128]{1,0:T(8,128)(2,1)S(1)}, u32[]{:S(2)}, u32[]{:S(2)}) collective-permute-start(bf16[1664,128]{1,0:T(8,128)(2,1)S(1)} %get-tuple-element.101), channel_id=1, source_target_pairs={{0,2},{1,3},{2,0},{3,1},{4,6},{5,7},{6,4},{7,5},{8,10},{9,11},{10,... | collective-permute-start | bytes 1277960 | tf_op jit(solution)/shard_map/ppermute | solution.py:332
  83.6 31.1 %collective-permute-start.16 = (bf16[1664,128]{1,0:T(8,128)(2,1)S(1)}, bf16[1664,128]{1,0:T(8,128)(2,1)S(1)}, u32[]{:S(2)}, u32[]{:S(2)}) collective-permute-start(bf16[1664,128]{1,0:T(8,128)(2,1)S(1)} %get-tuple-element.102), channel_id=1, source_target_pairs={{0,3},{1,0},{2,1},{3,2},{4,7},{5,4},{6,5},{7,6},{8,11},{9,8},{10,9... | collective-permute-start | bytes 1277960 | tf_op jit(solution)/shard_map/ppermute | solution.py:332
  90.6 5.7 %collective-permute-start.18 = (bf16[80,1024]{1,0:T(8,128)(2,1)S(1)}, bf16[80,1024]{1,0:T(8,128)(2,1)S(1)}, u32[]{:S(2)}, u32[]{:S(2)}) collective-permute-start(bf16[80,1024]{1,0:T(8,128)(2,1)S(1)} %get-tuple-element.111), channel_id=1, source_target_pairs={{0,32},{32,0},{64,96},{96,64},{128,160},{160,128},{192,224},{224,1... | collective-permute-start | bytes 491528 | tf_op jit(solution)/shard_map/ppermute | solution.py:508
  96.4 6.0 %collective-permute-start.19 = (bf16[40,1024]{1,0:T(8,128)(2,1)S(1)}, bf16[40,1024]{1,0:T(8,128)(2,1)S(1)}, u32[]{:S(2)}, u32[]{:S(2)}) collective-permute-start(bf16[40,1024]{1,0:T(8,128)(2,1)S(1)} %get-tuple-element.113), channel_id=1, source_target_pairs={{0,16},{16,0},{1,17},{17,1},{2,18},{18,2},{3,19},{19,3},{4,20},{20... | collective-permute-start | bytes 245768 | tf_op jit(solution)/shard_map/ppermute | solution.py:508
  102.4 5.5 %collective-permute-start.20 = (bf16[20,1024]{1,0:T(8,128)(2,1)S(1)}, bf16[20,1024]{1,0:T(8,128)(2,1)S(1)}, u32[]{:S(2)}, u32[]{:S(2)}) collective-permute-start(bf16[20,1024]{1,0:T(8,128)(2,1)S(1)} %get-tuple-element.115), channel_id=1, source_target_pairs={{0,64},{32,96},{64,0},{96,32},{128,192},{160,224},{192,128},{224,1... | collective-permute-start | bytes 122888 | tf_op jit(solution)/shard_map/ppermute | solution.py:508
  107.9 9.0 %collective-permute-start.21 = (bf16[10,1024]{1,0:T(8,128)(2,1)S(1)}, bf16[10,1024]{1,0:T(8,128)(2,1)S(1)}, u32[]{:S(2)}, u32[]{:S(2)}) collective-permute-start(bf16[10,1024]{1,0:T(8,128)(2,1)S(1)} %get-tuple-element.117), channel_id=1, source_target_pairs={{0,128},{32,160},{64,192},{96,224},{128,0},{160,32},{192,64},{224,... | collective-permute-start | bytes 61448 | tf_op jit(solution)/shard_map/ppermute | solution.py:508
  (3 other events, 49.4 us)

commit v11 on v10

--- a/solution.py
+++ b/solution.py
@@ -149,20 +149,23 @@
         kt_ref[:, j * 128 : (j + 1) * 128] = k_s[j * 128 : (j + 1) * 128, :].T
     dkv_s[...] = jnp.zeros_like(dkv_s)
 
-    def half(hf, carry):
-        base = pl.multiple_of(hf * HALF, HALF)
+    for hf in range(2):
+        base = hf * HALF
         for i in range(HALF // 128):
             n = (i + 1) * 128
-            rows = pl.ds(pl.multiple_of(base + i * 128, 128), 128)
+            rows = pl.ds(base + i * 128, 128)
             keys = pl.ds(base, n)
             key_n = k_s[keys, :]
             value_n = v_s[keys, :]
-            lane = lax.broadcasted_iota(jnp.int32, (n, 128), 1)
-            row = lax.broadcasted_iota(jnp.int32, (n, 128), 0)
-            low = jnp.zeros((n, 128), jnp.int32)
-            for kk in range(4):
-                low = jnp.where(lane // BLK == kk, begin[hf * 16 + i * 4 + kk], low)
-            seen = (row >= low) & (row <= lane + i * 128)
+            masked = 128 if hf == 0 else n
+            lane = lax.broadcasted_iota(jnp.int32, (masked, 128), 1)
+            row = lax.broadcasted_iota(jnp.int32, (masked, 128), 0) + (n - masked)
+            seen = row <= lane + i * 128
+            if hf == 1:
+                low = jnp.zeros((masked, 128), jnp.int32)
+                for kk in range(4):
+                    low = jnp.where(lane // BLK == kk, begin[16 + i * 4 + kk], low)
+                seen = seen & (row >= low)
             bias = jnp.where(seen, 0.0, LOWEST)
             bias = jnp.concatenate([bias, bias], axis=1)
             q_rows = [q_s[rows, e * 128 : (e + 1) * 128] for e in range(4)]
@@ -171,7 +174,13 @@
             for g in range(2):
                 qs = jnp.concatenate(q_rows[2 * g : 2 * g + 2], axis=0)
                 ds = jnp.concatenate(d_rows[2 * g : 2 * g + 2], axis=0)
-                scores = dot(key_n, qs, NT) * (SCALE * LOG2E) + bias
+                scores = dot(key_n, qs, NT) * (SCALE * LOG2E)
+                if masked < n:
+                    scores = jnp.concatenate(
+                        [scores[: n - masked], scores[n - masked :] + bias], axis=0
+                    )
+                else:
+                    scores = scores + bias
                 top = jnp.max(scores, axis=0, keepdims=True)
                 weights = jnp.exp2(scores - top)
                 share = 1.0 / jnp.sum(weights, axis=0, keepdims=True)
@@ -187,9 +196,6 @@
             dkv_s[keys, 128:256] += dot(
                 jnp.concatenate(lows, axis=1), jnp.concatenate(d_rows, axis=0), NN
             )
-        return carry
-
-    lax.fori_loop(0, 2, half, 0)
 
     y = lax.axis_index("y")
     for t in range(16):
@@ -232,22 +238,30 @@
         out_ref[:, pl.ds(at, 128)] = ins[s][...]
 
 
+KV_SHIFTS = (0, 1, 3, 2)
+PART_SHIFTS = (0, 2, 1, 3)
+
+
 def weight_kernel(*refs):
-    pieces, x_s = refs[:4], refs[4]
-    kv_ref, kv_rows_ref, send_ref, keep_ref = refs[5:]
-    core, x = lax.axis_index("core"), lax.axis_index("x")
-    for s in range(4):
-        at = pl.multiple_of(lax.rem(x + 4 - s, 4) * 128, 128)
-        kv_ref[:, pl.ds(at, 128)] = pieces[s][:, 0:128]
-        kv_ref[:, pl.ds(pl.multiple_of(512 + at, 128), 128)] = pieces[s][:, 128:256]
+    pieces, x_s, kv_ref, send_ref = refs[:4], refs[4], refs[5], refs[6]
+    for s, piece in zip(KV_SHIFTS, pieces):
+        at = pl.multiple_of(lax.rem(lax.axis_index("x") + 4 - s, 4) * 128, 128)
+        kv_ref[:, pl.ds(at, 128)] = piece[:, 0:128]
+        kv_ref[:, pl.ds(pl.multiple_of(512 + at, 128), 128)] = piece[:, 128:256]
     part = FEAT_TILE // 2
-    other = pl.ds(pl.multiple_of((1 - core) * part, part), part)
-    own = pl.ds(pl.multiple_of(core * part, part), part)
+    other = pl.ds(pl.multiple_of((1 - lax.axis_index("core")) * part, part), part)
     for j in range(4):
         cols = slice(j * 256, (j + 1) * 256)
         send_ref[:, cols] = dot(x_s[other, :], kv_ref[:, cols], NN).astype(jnp.bfloat16)
+
+
+def weight_keep_kernel(x_s, kv_ref, kv_rows_ref, keep_ref):
+    part = FEAT_TILE // 2
+    own = pl.ds(pl.multiple_of(lax.axis_index("core") * part, part), part)
+    for j in range(4):
+        cols = slice(j * 256, (j + 1) * 256)
         keep_ref[:, cols] = dot(x_s[own, :], kv_ref[:, cols], NN)
-    kv_rows_ref[...] = kv_ref[pl.ds(pl.multiple_of(x * ROWS, ROWS), ROWS), :]
+    kv_rows_ref[...] = kv_ref[pl.ds(pl.multiple_of(lax.axis_index("x") * ROWS, ROWS), ROWS), :]
 
 
 def split_kernel(number, count, *refs):
@@ -309,15 +323,15 @@
 def out_kernel(*refs):
     parts, input_ref, query_ref = refs[:4], refs[4], refs[5]
     x = lax.axis_index("x")
-    for s in range(4):
+    for s, part in zip(PART_SHIFTS, parts):
         src = lax.rem(x + 4 - s, 4)
         for j in range(FEAT_TILE // 128):
             cols = pl.ds(pl.multiple_of(src * FEAT_TILE + j * 128, 128), 128)
-            input_ref[:, cols] = parts[s][j * 128 : (j + 1) * 128, :].T
+            input_ref[:, cols] = part[j * 128 : (j + 1) * 128, :].T
         for g in range(8):
             cols = pl.ds(pl.multiple_of(src * 2 * Q_COLS + g * 128, 128), 128)
             at = FEAT_TILE + g * 128
-            query_ref[:, cols] = parts[s][at : at + 128, :]
+            query_ref[:, cols] = part[at : at + 128, :]
 
 
 BIT_AXES = (("core", 1), ("yh", 1), ("z", 1), ("z", 2), ("z", 4))
@@ -451,26 +465,28 @@
         compiler_params=params(6),
         cost_estimate=cost(0, 2_000_000),
     )(keep, taken)
-    pieces = [to_shift(own_cols, s) for s in range(4)]
+    pieces = [to_shift(own_cols, s) for s in KV_SHIFTS]
     _, dq_far = lax.optimization_barrier((own_cols, dq_far))
     dq_got = lax.ppermute(dq_far, "y", [(0, 1), (1, 0)])
     pieces, dq_got, far_tile = lax.optimization_barrier((pieces, dq_got, far_tile))
 
-    kv_half, kv_rows, wg_send, wg_keep = pl.pallas_call(
+    kv_half, wg_send = pl.pallas_call(
         weight_kernel,
         in_specs=[VMEM] * 5,
-        out_specs=[VMEM] * 4,
-        out_shape=[
-            shape((SLAB // 2, 1024)),
-            shape((ROWS, 1024)),
-            shape((FEAT_TILE // 2, 1024)),
-            shape((FEAT_TILE // 2, 1024), jnp.float32),
-        ],
+        out_specs=[VMEM] * 2,
+        out_shape=[shape((SLAB // 2, 1024)), shape((FEAT_TILE // 2, 1024))],
         compiler_params=params(12),
-        cost_estimate=cost(700_000_000, 6_000_000),
+        cost_estimate=cost(350_000_000, 4_000_000),
     )(*pieces, rows_x)
-
     wg_got = swap(wg_send, 0)
+    kv_rows, wg_keep = pl.pallas_call(
+        weight_keep_kernel,
+        in_specs=[VMEM] * 2,
+        out_specs=[VMEM] * 2,
+        out_shape=[shape((ROWS, 1024)), shape((FEAT_TILE // 2, 1024), jnp.float32)],
+        compiler_params=params(12),
+        cost_estimate=cost(350_000_000, 4_000_000),
+    )(rows_x, kv_half)
     parts = pl.pallas_call(
         input_kernel,
         in_specs=[VMEM] * 5,
@@ -484,7 +500,7 @@
         cost_estimate=cost(700_000_000, 6_000_000),
     )(kv_half, tile, far_tile, dq_near, dq_got)
     wg_got, parts = lax.optimization_barrier((wg_got, parts))
-    parts_got = [to_shift(parts[s], s) for s in range(4)]
+    parts_got = [to_shift(parts[s], s) for s in PART_SHIFTS]
 
     def split(number, count, keep, *arrived):
         rows = keep.shape[0] // count

time: 118 us -> 117 us (level)
  waiting for transfers between devices: 41.2 us -> 37.7 us
  starting transfers between devices: 55.3 us -> 56.8 us
    ppermute x9, waiting for transfers between devices: 11.8 us -> 9.97 us  [to_shift(): lax.ppermute(value, 'x', [(i, (i + s) % 4) for i in range(4)])]
    ppermute x5, starting transfers between devices: 15.4 us -> 16.5 us  [body(): wg_got = lax.ppermute(sends[0], axis, [(i, i ^ mask) for i in range(size)])]
  transfers between devices with their start and end apart: 23 -> 23, of which waited for: 13 -> 13; matrix products, arithmetic and copies ran while one was open for 0% -> 0% of each run, Pallas kernels for 12% -> 13%
where the time goes in v11:
time: 117 us; the launch traced here: 116 us
  starting transfers between devices  56.8 us (49%)
  waiting for transfers between devices  37.7 us (32%)
  Pallas kernels  19.4 us (17%)
    ppermute x5, starting transfers between devices, body(): wg_got = lax.ppermute(sends[0], axis, [(i, i ^ mask) for i in range(size)])  16.5 us
    ppermute x9, starting transfers between devices, to_shift(): lax.ppermute(value, 'x', [(i, (i + s) % 4) for i in range(4)])  15.8 us
    ppermute x5, waiting for transfers between devices, body(): wg_got = lax.ppermute(sends[0], axis, [(i, i ^ mask) for i in range(size)])  14.7 us
    ppermute x2, starting transfers between devices, body(): lax.ppermute(tile, ('z', 'x'), pairs)  10.4 us
    ppermute x9, waiting for transfers between devices, to_shift(): lax.ppermute(value, 'x', [(i, (i + s) % 4) for i in range(4)])  9.97 us
    ppermute x4, starting transfers between devices, swap(): lax.ppermute(value, axis, [(i, i ^ mask) for i in range(8 if axis == 'z'...  6.94 us
    pallas_call x1, Pallas kernels, body(): pl.pallas_call(attention_kernel, in_specs=[SMEM] * 2 + [VMEM], out_specs=...  6.33 us
    all_to_all x1, starting transfers between devices, exchange(): return lax.all_to_all(value, axis, 0, 0, tiled=True)  5.9 us
  transfers between devices with their start and end apart: 23, of which 13 were waited for; matrix products, arithmetic and copies ran while one was open for 0% of the time, Pallas kernels for 13%

profile of v11, /device:TPU:8, one launch (start us, length us, event | category | flops | bytes accessed | tf_op | source)
XLA Modules:
  0.0 115.8 jit_solution(8224019129874998482)
XLA Ops:
  0.6 2.9 %shard_map.111 = bf16[8,128,1280]{2,1,0:T(8,128)(2,1)} custom-call(bf16[128,4096]{1,0:T(8,128)(2,1)} %bitcast.15, bf16[128,4096]{1,0:T(8,128)(2,1)} %bitcast.16, bf16[128,512]{1,0:T(8,128)(2,1)} %bitcast.17, bf16[128,512]{1,0:T(8,128)(2,1)} %bitcast.18), custom_call_target="tpu_custom_call" | custom-call | bytes 5000000 | tf_op jit(solution)/shard_map/pallas_call | solution.py:354
  3.6 5.9 %all-to-all-start = ((bf16[8,128,1280]{2,1,0:T(8,128)(2,1)}), bf16[8,128,1280]{2,1,0:T(8,128)(2,1)S(1)}, u32[]{:S(2)}, u32[]{:S(2)}) async-start(bf16[8,128,1280]{2,1,0:T(8,128)(2,1)} %shard_map.111), calls=%async_computation | async-start | bytes 5242880 | tf_op jit(solution)/shard_map/all_to_all | solution.py:350
  9.5 9.1 %collective-permute-start.3 = (bf16[80,1024]{1,0:T(8,128)(2,1)S(1)}, bf16[80,1024]{1,0:T(8,128)(2,1)S(1)}, u32[]{:S(2)}, u32[]{:S(2)}) collective-permute-start(bf16[80,1024]{1,0:T(8,128)(2,1)S(1)} %copy-done.1), channel_id=1, source_target_pairs={{0,128},{32,160},{65,193},{97,225},{130,2},{162,34},{195,67},{227,... | collective-permute-start | bytes 491528 | tf_op jit(solution)/shard_map/ppermute | solution.py:380
  18.6 2.9 %collective-permute-done.3.got_ref = bf16[80,1024]{1,0:T(8,128)(2,1)S(1)} collective-permute-done((bf16[80,1024]{1,0:T(8,128)(2,1)S(1)}, bf16[80,1024]{1,0:T(8,128)(2,1)S(1)}, u32[]{:S(2)}, u32[]{:S(2)}) %collective-permute-start.3) | collective-permute-done | bytes 163872 | tf_op jit(solution)/shard_map/ppermute | solution.py:380
  22.8 2.9 %collective-permute-done.4.got_ref = bf16[80,1024]{1,0:T(8,128)(2,1)S(1)} collective-permute-done((bf16[80,1024]{1,0:T(8,128)(2,1)S(1)}, bf16[80,1024]{1,0:T(8,128)(2,1)S(1)}, u32[]{:S(2)}, u32[]{:S(2)}) %collective-permute-start.4) | collective-permute-done | bytes 163872 | tf_op jit(solution)/shard_map/ppermute | solution.py:380
  25.7 4.4 %collective-permute-start.5 = (bf16[1,80,1024]{2,1,0:T(8,128)(2,1)S(1)}, bf16[1,80,1024]{2,1,0:T(8,128)(2,1)S(1)}, u32[]{:S(2)}, u32[]{:S(2)}) collective-permute-start(bf16[1,80,1024]{2,1,0:T(8,128)(2,1)S(1)} %bitcast.11), channel_id=1, source_target_pairs={{0,32},{32,0},{64,96},{96,64},{128,160},{160,128},{192,224},{224,1... | collective-permute-start | bytes 491528 | tf_op jit(solution)/shard_map/ppermute | solution.py:342
  30.1 4.3 %collective-permute-done.5.far_ref = bf16[1,80,1024]{2,1,0:T(8,128)(2,1)S(1)} collective-permute-done((bf16[1,80,1024]{2,1,0:T(8,128)(2,1)S(1)}, bf16[1,80,1024]{2,1,0:T(8,128)(2,1)S(1)}, u32[]{:S(2)}, u32[]{:S(2)}) %collective-permute-start.5) | collective-permute-done | bytes 163872 | tf_op jit(solution)/shard_map/ppermute | solution.py:342
  34.4 2.4 %collective-permute-start.6 = (bf16[2,80,1024]{2,1,0:T(8,128)(2,1)S(1)}, bf16[2,80,1024]{2,1,0:T(8,128)(2,1)S(1)}, u32[]{:S(2)}, u32[]{:S(2)}) collective-permute-start(bf16[2,80,1024]{2,1,0:T(8,128)(2,1)S(1)} %shard_map.116.near_ref), channel_id=1, source_target_pairs={{0,16},{16,0},{1,17},{17,1},{2,18},{18,2},{3,19},{19,3},{4,20},{20... | collective-permute-start | bytes 983048 | tf_op jit(solution)/shard_map/ppermute | solution.py:342
  39.1 4.1 %collective-permute-start = (bf16[640,128]{1,0:T(8,128)(2,1)}, bf16[640,128]{1,0:T(8,128)(2,1)}, u32[]{:S(2)}, u32[]{:S(2)}) collective-permute-start(bf16[640,128]{1,0:T(8,128)(2,1)} %get-tuple-element.64), channel_id=1, source_target_pairs={{0,1},{1,2},{2,3},{3,0},{4,5},{5,6},{6,7},{7,4},{8,9},{9,10},{10,1... | collective-permute-start | bytes 491528 | tf_op jit(solution)/shard_map/ppermute | solution.py:346
  43.2 2.3 %collective-permute-start.1 = (bf16[640,128]{1,0:T(8,128)(2,1)}, bf16[640,128]{1,0:T(8,128)(2,1)}, u32[]{:S(2)}, u32[]{:S(2)}) collective-permute-start(bf16[640,128]{1,0:T(8,128)(2,1)} %get-tuple-element.65), channel_id=1, source_target_pairs={{0,2},{1,3},{2,0},{3,1},{4,6},{5,7},{6,4},{7,5},{8,10},{9,11},{10,... | collective-permute-start | bytes 491528 | tf_op jit(solution)/shard_map/ppermute | solution.py:346
  45.9 6.3 %shard_map.112 = (bf16[2,2,1280,256]{3,2,1,0:T(8,128)(2,1)S(1)}, bf16[128,1024]{1,0:T(8,128)(2,1)S(1)}, f32[512,256]{1,0:T(8,128)S(1)}, bf16[512,256]{1,0:T(8,128)(2,1)S(1)}) custom-call(s32[32]{0:T(128)S(1)} %bitcast.13, s32[32]{0:T(128)S(1)} %copy-done.3, bf16[8,128,1280]{2,1,0:T(8,128)(2,1)S(1)} %all-to-all-done.refs_0_), custom_call_target="tpu_custom_call" | custom-call | bytes 5000 | tf_op jit(solution)/shard_map/pallas_call | solution.py:409
  56.8 2.9 %collective-permute-done.7.taken_ref = bf16[512,256]{1,0:T(8,128)(2,1)S(1)} collective-permute-done((bf16[512,256]{1,0:T(8,128)(2,1)S(1)}, bf16[512,256]{1,0:T(8,128)(2,1)S(1)}, u32[]{:S(2)}, u32[]{:S(2)}) %collective-permute-start.7) | collective-permute-done | bytes 262176 | tf_op jit(solution)/shard_map/ppermute | solution.py:433
  61.8 2.9 %collective-permute-start.8 = (bf16[512,256]{1,0:T(8,128)(2,1)S(1)}, bf16[512,256]{1,0:T(8,128)(2,1)S(1)}, u32[]{:S(2)}, u32[]{:S(2)}) collective-permute-start(bf16[512,256]{1,0:T(8,128)(2,1)S(1)} %shard_map.120.refs_0_), channel_id=1, source_target_pairs={{0,1},{1,2},{2,3},{3,0},{4,5},{5,6},{6,7},{7,4},{8,9},{9,10},{10,1... | collective-permute-start | bytes 786440 | tf_op jit(solution)/shard_map/ppermute | solution.py:346
  65.0 5.8 %collective-permute-done.10.refs_3_ = bf16[512,256]{1,0:T(8,128)(2,1)S(1)} collective-permute-done((bf16[512,256]{1,0:T(8,128)(2,1)S(1)}, bf16[512,256]{1,0:T(8,128)(2,1)S(1)}, u32[]{:S(2)}, u32[]{:S(2)}) %collective-permute-start.10) | collective-permute-done | bytes 262176 | tf_op jit(solution)/shard_map/ppermute | solution.py:346
  70.9 2.8 %collective-permute-done.8.refs_1_ = bf16[512,256]{1,0:T(8,128)(2,1)S(1)} collective-permute-done((bf16[512,256]{1,0:T(8,128)(2,1)S(1)}, bf16[512,256]{1,0:T(8,128)(2,1)S(1)}, u32[]{:S(2)}, u32[]{:S(2)}) %collective-permute-start.8) | collective-permute-done | bytes 262176 | tf_op jit(solution)/shard_map/ppermute | solution.py:346
  80.3 2.7 %collective-permute-start.15 = (bf16[1664,128]{1,0:T(8,128)(2,1)S(1)}, bf16[1664,128]{1,0:T(8,128)(2,1)S(1)}, u32[]{:S(2)}, u32[]{:S(2)}) collective-permute-start(bf16[1664,128]{1,0:T(8,128)(2,1)S(1)} %get-tuple-element.101), channel_id=1, source_target_pairs={{0,1},{1,2},{2,3},{3,0},{4,5},{5,6},{6,7},{7,4},{8,9},{9,10},{10,1... | collective-permute-start | bytes 1277960 | tf_op jit(solution)/shard_map/ppermute | solution.py:346
  83.6 4.6 %collective-permute-done.17.refs_1_ = bf16[160,1024]{1,0:T(8,128)(2,1)S(1)} collective-permute-done((bf16[160,1024]{1,0:T(8,128)(2,1)S(1)}, bf16[160,1024]{1,0:T(8,128)(2,1)S(1)}, u32[]{:S(2)}, u32[]{:S(2)}) %collective-permute-start.17) | collective-permute-done | bytes 327712 | tf_op jit(solution)/shard_map/ppermute | solution.py:524
  88.3 2.4 %collective-permute-start.18 = (bf16[80,1024]{1,0:T(8,128)(2,1)S(1)}, bf16[80,1024]{1,0:T(8,128)(2,1)S(1)}, u32[]{:S(2)}, u32[]{:S(2)}) collective-permute-start(bf16[80,1024]{1,0:T(8,128)(2,1)S(1)} %get-tuple-element.111), channel_id=1, source_target_pairs={{0,32},{32,0},{64,96},{96,64},{128,160},{160,128},{192,224},{224,1... | collective-permute-start | bytes 491528 | tf_op jit(solution)/shard_map/ppermute | solution.py:524
  90.7 4.1 %collective-permute-done.18.refs_1_ = bf16[80,1024]{1,0:T(8,128)(2,1)S(1)} collective-permute-done((bf16[80,1024]{1,0:T(8,128)(2,1)S(1)}, bf16[80,1024]{1,0:T(8,128)(2,1)S(1)}, u32[]{:S(2)}, u32[]{:S(2)}) %collective-permute-start.18) | collective-permute-done | bytes 163872 | tf_op jit(solution)/shard_map/ppermute | solution.py:524
  94.9 2.5 %collective-permute-start.19 = (bf16[40,1024]{1,0:T(8,128)(2,1)S(1)}, bf16[40,1024]{1,0:T(8,128)(2,1)S(1)}, u32[]{:S(2)}, u32[]{:S(2)}) collective-permute-start(bf16[40,1024]{1,0:T(8,128)(2,1)S(1)} %get-tuple-element.113), channel_id=1, source_target_pairs={{0,16},{16,0},{1,17},{17,1},{2,18},{18,2},{3,19},{19,3},{4,20},{20... | collective-permute-start | bytes 245768 | tf_op jit(solution)/shard_map/ppermute | solution.py:524
  97.3 3.6 %collective-permute-done.19.refs_1_ = bf16[40,1024]{1,0:T(8,128)(2,1)S(1)} collective-permute-done((bf16[40,1024]{1,0:T(8,128)(2,1)S(1)}, bf16[40,1024]{1,0:T(8,128)(2,1)S(1)}, u32[]{:S(2)}, u32[]{:S(2)}) %collective-permute-start.19) | collective-permute-done | bytes 81952 | tf_op jit(solution)/shard_map/ppermute | solution.py:524
  100.9 3.4 %collective-permute-start.20 = (bf16[20,1024]{1,0:T(8,128)(2,1)S(1)}, bf16[20,1024]{1,0:T(8,128)(2,1)S(1)}, u32[]{:S(2)}, u32[]{:S(2)}) collective-permute-start(bf16[20,1024]{1,0:T(8,128)(2,1)S(1)} %get-tuple-element.115), channel_id=1, source_target_pairs={{0,64},{32,96},{64,0},{96,32},{128,192},{160,224},{192,128},{224,1... | collective-permute-start | bytes 122888 | tf_op jit(solution)/shard_map/ppermute | solution.py:524
  104.3 2.1 %collective-permute-done.20.refs_1_ = bf16[20,1024]{1,0:T(8,128)(2,1)S(1)} collective-permute-done((bf16[20,1024]{1,0:T(8,128)(2,1)S(1)}, bf16[20,1024]{1,0:T(8,128)(2,1)S(1)}, u32[]{:S(2)}, u32[]{:S(2)}) %collective-permute-start.20) | collective-permute-done | bytes 40992 | tf_op jit(solution)/shard_map/ppermute | solution.py:524
  106.4 6.8 %collective-permute-start.21 = (bf16[10,1024]{1,0:T(8,128)(2,1)S(1)}, bf16[10,1024]{1,0:T(8,128)(2,1)S(1)}, u32[]{:S(2)}, u32[]{:S(2)}) collective-permute-start(bf16[10,1024]{1,0:T(8,128)(2,1)S(1)} %get-tuple-element.117), channel_id=1, source_target_pairs={{0,128},{32,160},{64,192},{96,224},{128,0},{160,32},{192,64},{224,... | collective-permute-start | bytes 61448 | tf_op jit(solution)/shard_map/ppermute | solution.py:524
  (50 shorter events, 21.1 us)
Async XLA Ops:
  3.6 42.4 %copy-start.2 = (s32[1,32]{1,0:T(1,128)S(1)}, s32[1,32]{1,0:T(1,128)}, u32[]{:S(2)}) copy-start(s32[1,32]{1,0:T(1,128)} %param.14) | copy-start | bytes 388
  3.6 42.3 %all-to-all-start = ((bf16[8,128,1280]{2,1,0:T(8,128)(2,1)}), bf16[8,128,1280]{2,1,0:T(8,128)(2,1)S(1)}, u32[]{:S(2)}, u32[]{:S(2)}) async-start(bf16[8,128,1280]{2,1,0:T(8,128)(2,1)} %shard_map.111), calls=%async_computation | async-start | bytes 5242880 | tf_op jit(solution)/shard_map/all_to_all | solution.py:350
  9.5 12.0 %collective-permute-start.3 = (bf16[80,1024]{1,0:T(8,128)(2,1)S(1)}, bf16[80,1024]{1,0:T(8,128)(2,1)S(1)}, u32[]{:S(2)}, u32[]{:S(2)}) collective-permute-start(bf16[80,1024]{1,0:T(8,128)(2,1)S(1)} %copy-done.1), channel_id=1, source_target_pairs={{0,128},{32,160},{65,193},{97,225},{130,2},{162,34},{195,67},{227,... | collective-permute-start | bytes 491528 | tf_op jit(solution)/shard_map/ppermute | solution.py:380
  21.5 4.2 %collective-permute-start.4 = (bf16[80,1024]{1,0:T(8,128)(2,1)S(1)}, bf16[80,1024]{1,0:T(8,128)(2,1)S(1)}, u32[]{:S(2)}, u32[]{:S(2)}) collective-permute-start(bf16[80,1024]{1,0:T(8,128)(2,1)S(1)} %shard_map.114.own_ref), channel_id=1, source_target_pairs={{0,64},{2,66},{32,96},{34,98},{65,1},{67,3},{97,33},{99,35},{128,1... | collective-permute-start | bytes 491528 | tf_op jit(solution)/shard_map/ppermute | solution.py:380
  25.7 8.7 %collective-permute-start.5 = (bf16[1,80,1024]{2,1,0:T(8,128)(2,1)S(1)}, bf16[1,80,1024]{2,1,0:T(8,128)(2,1)S(1)}, u32[]{:S(2)}, u32[]{:S(2)}) collective-permute-start(bf16[1,80,1024]{2,1,0:T(8,128)(2,1)S(1)} %bitcast.11), channel_id=1, source_target_pairs={{0,32},{32,0},{64,96},{96,64},{128,160},{160,128},{192,224},{224,1... | collective-permute-start | bytes 491528 | tf_op jit(solution)/shard_map/ppermute | solution.py:342
  34.4 18.4 %collective-permute-start.6 = (bf16[2,80,1024]{2,1,0:T(8,128)(2,1)S(1)}, bf16[2,80,1024]{2,1,0:T(8,128)(2,1)S(1)}, u32[]{:S(2)}, u32[]{:S(2)}) collective-permute-start(bf16[2,80,1024]{2,1,0:T(8,128)(2,1)S(1)} %shard_map.116.near_ref), channel_id=1, source_target_pairs={{0,16},{16,0},{1,17},{17,1},{2,18},{18,2},{3,19},{19,3},{4,20},{20... | collective-permute-start | bytes 983048 | tf_op jit(solution)/shard_map/ppermute | solution.py:342
  39.1 13.2 %collective-permute-start = (bf16[640,128]{1,0:T(8,128)(2,1)}, bf16[640,128]{1,0:T(8,128)(2,1)}, u32[]{:S(2)}, u32[]{:S(2)}) collective-permute-start(bf16[640,128]{1,0:T(8,128)(2,1)} %get-tuple-element.64), channel_id=1, source_target_pairs={{0,1},{1,2},{2,3},{3,0},{4,5},{5,6},{6,7},{7,4},{8,9},{9,10},{10,1... | collective-permute-start | bytes 491528 | tf_op jit(solution)/shard_map/ppermute | solution.py:346
  43.2 9.0 %collective-permute-start.1 = (bf16[640,128]{1,0:T(8,128)(2,1)}, bf16[640,128]{1,0:T(8,128)(2,1)}, u32[]{:S(2)}, u32[]{:S(2)}) collective-permute-start(bf16[640,128]{1,0:T(8,128)(2,1)} %get-tuple-element.65), channel_id=1, source_target_pairs={{0,2},{1,3},{2,0},{3,1},{4,6},{5,7},{6,4},{7,5},{8,10},{9,11},{10,... | collective-permute-start | bytes 491528 | tf_op jit(solution)/shard_map/ppermute | solution.py:346
  45.6 7.2 %collective-permute-start.2 = (bf16[640,128]{1,0:T(8,128)(2,1)}, bf16[640,128]{1,0:T(8,128)(2,1)}, u32[]{:S(2)}, u32[]{:S(2)}) collective-permute-start(bf16[640,128]{1,0:T(8,128)(2,1)} %get-tuple-element.66), channel_id=1, source_target_pairs={{0,3},{1,0},{2,1},{3,2},{4,7},{5,4},{6,5},{7,6},{8,11},{9,8},{10,9... | collective-permute-start | bytes 491528 | tf_op jit(solution)/shard_map/ppermute | solution.py:346
  52.8 6.9 %collective-permute-start.7 = (bf16[512,256]{1,0:T(8,128)(2,1)S(1)}, bf16[512,256]{1,0:T(8,128)(2,1)S(1)}, u32[]{:S(2)}, u32[]{:S(2)}) collective-permute-start(bf16[512,256]{1,0:T(8,128)(2,1)S(1)} %get-tuple-element.68), channel_id=1, source_target_pairs={{0,4},{4,0},{1,5},{5,1},{2,6},{6,2},{3,7},{7,3},{8,12},{12,8},{9,1... | collective-permute-start | bytes 786440 | tf_op jit(solution)/shard_map/ppermute | solution.py:433
  55.4 19.2 %collective-permute-start.12 = (bf16[4,80,1024]{2,1,0:T(8,128)(2,1)S(1)}, bf16[4,80,1024]{2,1,0:T(8,128)(2,1)S(1)}, u32[]{:S(2)}, u32[]{:S(2)}) collective-permute-start(bf16[4,80,1024]{2,1,0:T(8,128)(2,1)S(1)} %shard_map.118.w_ref), channel_id=1, source_target_pairs={{0,8},{8,0},{1,9},{9,1},{2,10},{10,2},{3,11},{11,3},{4,12},{12,4},... | collective-permute-start | bytes 1966088 | tf_op jit(solution)/shard_map/ppermute | solution.py:342
  59.7 14.8 %collective-permute-start.11 = (bf16[4,512,128]{2,1,0:T(8,128)(2,1)S(1)}, bf16[4,512,128]{2,1,0:T(8,128)(2,1)S(1)}, u32[]{:S(2)}, u32[]{:S(2)}) collective-permute-start(bf16[4,512,128]{2,1,0:T(8,128)(2,1)S(1)} %get-tuple-element.83), channel_id=1, source_target_pairs={{0,4},{4,0},{1,5},{5,1},{2,6},{6,2},{3,7},{7,3},{8,12},{12,8},{9,1... | collective-permute-start | bytes 1572872 | tf_op jit(solution)/shard_map/ppermute | solution.py:470
  60.1 10.8 %collective-permute-start.10 = (bf16[512,256]{1,0:T(8,128)(2,1)S(1)}, bf16[512,256]{1,0:T(8,128)(2,1)S(1)}, u32[]{:S(2)}, u32[]{:S(2)}) collective-permute-start(bf16[512,256]{1,0:T(8,128)(2,1)S(1)} %shard_map.120.refs_0_), channel_id=1, source_target_pairs={{0,2},{1,3},{2,0},{3,1},{4,6},{5,7},{6,4},{7,5},{8,10},{9,11},{10,... | collective-permute-start | bytes 786440 | tf_op jit(solution)/shard_map/ppermute | solution.py:346
  61.8 11.9 %collective-permute-start.8 = (bf16[512,256]{1,0:T(8,128)(2,1)S(1)}, bf16[512,256]{1,0:T(8,128)(2,1)S(1)}, u32[]{:S(2)}, u32[]{:S(2)}) collective-permute-start(bf16[512,256]{1,0:T(8,128)(2,1)S(1)} %shard_map.120.refs_0_), channel_id=1, source_target_pairs={{0,1},{1,2},{2,3},{3,0},{4,5},{5,6},{6,7},{7,4},{8,9},{9,10},{10,1... | collective-permute-start | bytes 786440 | tf_op jit(solution)/shard_map/ppermute | solution.py:346
  64.7 9.9 %collective-permute-start.9 = (bf16[512,256]{1,0:T(8,128)(2,1)S(1)}, bf16[512,256]{1,0:T(8,128)(2,1)S(1)}, u32[]{:S(2)}, u32[]{:S(2)}) collective-permute-start(bf16[512,256]{1,0:T(8,128)(2,1)S(1)} %shard_map.120.refs_0_), channel_id=1, source_target_pairs={{0,3},{1,0},{2,1},{3,2},{4,7},{5,4},{6,5},{7,6},{8,11},{9,8},{10,9... | collective-permute-start | bytes 786440 | tf_op jit(solution)/shard_map/ppermute | solution.py:346
  75.2 2.4 %collective-permute-start.13 = (bf16[320,1024]{1,0:T(8,128)(2,1)S(1)}, bf16[320,1024]{1,0:T(8,128)(2,1)S(1)}, u32[]{:S(2)}, u32[]{:S(2)}) collective-permute-start(bf16[320,1024]{1,0:T(8,128)(2,1)S(1)} %get-tuple-element.89), channel_id=1, source_target_pairs={{0,8},{8,0},{1,9},{9,1},{2,10},{10,2},{3,11},{11,3},{4,12},{12,4},... | collective-permute-start | bytes 1966088 | tf_op jit(solution)/shard_map/ppermute | solution.py:342
  78.0 10.2 %collective-permute-start.17 = (bf16[160,1024]{1,0:T(8,128)(2,1)S(1)}, bf16[160,1024]{1,0:T(8,128)(2,1)S(1)}, u32[]{:S(2)}, u32[]{:S(2)}) collective-permute-start(bf16[160,1024]{1,0:T(8,128)(2,1)S(1)} %get-tuple-element.109), channel_id=1, source_target_pairs={{0,4},{4,0},{1,5},{5,1},{2,6},{6,2},{3,7},{7,3},{8,12},{12,8},{9,1... | collective-permute-start | bytes 983048 | tf_op jit(solution)/shard_map/ppermute | solution.py:524
  79.4 33.8 %collective-permute-start.14 = (bf16[1664,128]{1,0:T(8,128)(2,1)S(1)}, bf16[1664,128]{1,0:T(8,128)(2,1)S(1)}, u32[]{:S(2)}, u32[]{:S(2)}) collective-permute-start(bf16[1664,128]{1,0:T(8,128)(2,1)S(1)} %get-tuple-element.100), channel_id=1, source_target_pairs={{0,2},{1,3},{2,0},{3,1},{4,6},{5,7},{6,4},{7,5},{8,10},{9,11},{10,... | collective-permute-start | bytes 1277960 | tf_op jit(solution)/shard_map/ppermute | solution.py:346
  80.3 32.9 %collective-permute-start.15 = (bf16[1664,128]{1,0:T(8,128)(2,1)S(1)}, bf16[1664,128]{1,0:T(8,128)(2,1)S(1)}, u32[]{:S(2)}, u32[]{:S(2)}) collective-permute-start(bf16[1664,128]{1,0:T(8,128)(2,1)S(1)} %get-tuple-element.101), channel_id=1, source_target_pairs={{0,1},{1,2},{2,3},{3,0},{4,5},{5,6},{6,7},{7,4},{8,9},{9,10},{10,1... | collective-permute-start | bytes 1277960 | tf_op jit(solution)/shard_map/ppermute | solution.py:346
  83.0 30.2 %collective-permute-start.16 = (bf16[1664,128]{1,0:T(8,128)(2,1)S(1)}, bf16[1664,128]{1,0:T(8,128)(2,1)S(1)}, u32[]{:S(2)}, u32[]{:S(2)}) collective-permute-start(bf16[1664,128]{1,0:T(8,128)(2,1)S(1)} %get-tuple-element.102), channel_id=1, source_target_pairs={{0,3},{1,0},{2,1},{3,2},{4,7},{5,4},{6,5},{7,6},{8,11},{9,8},{10,9... | collective-permute-start | bytes 1277960 | tf_op jit(solution)/shard_map/ppermute | solution.py:346
  88.3 6.5 %collective-permute-start.18 = (bf16[80,1024]{1,0:T(8,128)(2,1)S(1)}, bf16[80,1024]{1,0:T(8,128)(2,1)S(1)}, u32[]{:S(2)}, u32[]{:S(2)}) collective-permute-start(bf16[80,1024]{1,0:T(8,128)(2,1)S(1)} %get-tuple-element.111), channel_id=1, source_target_pairs={{0,32},{32,0},{64,96},{96,64},{128,160},{160,128},{192,224},{224,1... | collective-permute-start | bytes 491528 | tf_op jit(solution)/shard_map/ppermute | solution.py:524
  94.9 6.0 %collective-permute-start.19 = (bf16[40,1024]{1,0:T(8,128)(2,1)S(1)}, bf16[40,1024]{1,0:T(8,128)(2,1)S(1)}, u32[]{:S(2)}, u32[]{:S(2)}) collective-permute-start(bf16[40,1024]{1,0:T(8,128)(2,1)S(1)} %get-tuple-element.113), channel_id=1, source_target_pairs={{0,16},{16,0},{1,17},{17,1},{2,18},{18,2},{3,19},{19,3},{4,20},{20... | collective-permute-start | bytes 245768 | tf_op jit(solution)/shard_map/ppermute | solution.py:524
  100.9 5.5 %collective-permute-start.20 = (bf16[20,1024]{1,0:T(8,128)(2,1)S(1)}, bf16[20,1024]{1,0:T(8,128)(2,1)S(1)}, u32[]{:S(2)}, u32[]{:S(2)}) collective-permute-start(bf16[20,1024]{1,0:T(8,128)(2,1)S(1)} %get-tuple-element.115), channel_id=1, source_target_pairs={{0,64},{32,96},{64,0},{96,32},{128,192},{160,224},{192,128},{224,1... | collective-permute-start | bytes 122888 | tf_op jit(solution)/shard_map/ppermute | solution.py:524
  106.4 8.8 %collective-permute-start.21 = (bf16[10,1024]{1,0:T(8,128)(2,1)S(1)}, bf16[10,1024]{1,0:T(8,128)(2,1)S(1)}, u32[]{:S(2)}, u32[]{:S(2)}) collective-permute-start(bf16[10,1024]{1,0:T(8,128)(2,1)S(1)} %get-tuple-element.117), channel_id=1, source_target_pairs={{0,128},{32,160},{64,192},{96,224},{128,0},{160,32},{192,64},{224,... | collective-permute-start | bytes 61448 | tf_op jit(solution)/shard_map/ppermute | solution.py:524
  (3 other events, 49.4 us)

commit v12 on v11

--- a/solution.py
+++ b/solution.py
@@ -25,7 +25,7 @@
 HALF = 512
 SCALE = 1.0 / math.sqrt(HEAD_WIDTH)
 LOG2E = math.log2(math.e)
-LOWEST = -1e30
+LOWEST = -3e38
 NN = (((1,), (0,)), ((), ()))
 NT = (((1,), (1,)), ((), ()))
 VMEM = pl.BlockSpec(memory_space=pltpu.VMEM)

time: 117 us -> 117 us (level)
  no operation moved by 1% of the time
where the time goes in v12:
time: 117 us; the launch traced here: 116 us
  starting transfers between devices  56.7 us (48%)
  waiting for transfers between devices  37.7 us (32%)
  Pallas kernels  19.4 us (17%)
    ppermute x5, starting transfers between devices, body(): wg_got = lax.ppermute(sends[0], axis, [(i, i ^ mask) for i in range(size)])  16.5 us
    ppermute x9, starting transfers between devices, to_shift(): lax.ppermute(value, 'x', [(i, (i + s) % 4) for i in range(4)])  15.8 us
    ppermute x5, waiting for transfers between devices, body(): wg_got = lax.ppermute(sends[0], axis, [(i, i ^ mask) for i in range(size)])  14.8 us
    ppermute x2, starting transfers between devices, body(): lax.ppermute(tile, ('z', 'x'), pairs)  10.4 us
    ppermute x9, waiting for transfers between devices, to_shift(): lax.ppermute(value, 'x', [(i, (i + s) % 4) for i in range(4)])  9.98 us
    ppermute x4, starting transfers between devices, swap(): lax.ppermute(value, axis, [(i, i ^ mask) for i in range(8 if axis == 'z'...  6.94 us
    pallas_call x1, Pallas kernels, body(): pl.pallas_call(attention_kernel, in_specs=[SMEM] * 2 + [VMEM], out_specs=...  6.34 us
    all_to_all x1, starting transfers between devices, exchange(): return lax.all_to_all(value, axis, 0, 0, tiled=True)  5.9 us
  transfers between devices with their start and end apart: 23, of which 13 were waited for; matrix products, arithmetic and copies ran while one was open for 0% of the time, Pallas kernels for 13%

profile of v12, /device:TPU:8, one launch (start us, length us, event | category | flops | bytes accessed | tf_op | source)
XLA Modules:
  0.0 115.8 jit_solution(5349260708910732487)
XLA Ops:
  0.6 2.9 %shard_map.111 = bf16[8,128,1280]{2,1,0:T(8,128)(2,1)} custom-call(bf16[128,4096]{1,0:T(8,128)(2,1)} %bitcast.15, bf16[128,4096]{1,0:T(8,128)(2,1)} %bitcast.16, bf16[128,512]{1,0:T(8,128)(2,1)} %bitcast.17, bf16[128,512]{1,0:T(8,128)(2,1)} %bitcast.18), custom_call_target="tpu_custom_call" | custom-call | bytes 5000000 | tf_op jit(solution)/shard_map/pallas_call | solution.py:354
  3.6 5.9 %all-to-all-start = ((bf16[8,128,1280]{2,1,0:T(8,128)(2,1)}), bf16[8,128,1280]{2,1,0:T(8,128)(2,1)S(1)}, u32[]{:S(2)}, u32[]{:S(2)}) async-start(bf16[8,128,1280]{2,1,0:T(8,128)(2,1)} %shard_map.111), calls=%async_computation | async-start | bytes 5242880 | tf_op jit(solution)/shard_map/all_to_all | solution.py:350
  9.5 9.1 %collective-permute-start.3 = (bf16[80,1024]{1,0:T(8,128)(2,1)S(1)}, bf16[80,1024]{1,0:T(8,128)(2,1)S(1)}, u32[]{:S(2)}, u32[]{:S(2)}) collective-permute-start(bf16[80,1024]{1,0:T(8,128)(2,1)S(1)} %copy-done.1), channel_id=1, source_target_pairs={{0,128},{32,160},{65,193},{97,225},{130,2},{162,34},{195,67},{227,... | collective-permute-start | bytes 491528 | tf_op jit(solution)/shard_map/ppermute | solution.py:380
  18.6 2.9 %collective-permute-done.3.got_ref = bf16[80,1024]{1,0:T(8,128)(2,1)S(1)} collective-permute-done((bf16[80,1024]{1,0:T(8,128)(2,1)S(1)}, bf16[80,1024]{1,0:T(8,128)(2,1)S(1)}, u32[]{:S(2)}, u32[]{:S(2)}) %collective-permute-start.3) | collective-permute-done | bytes 163872 | tf_op jit(solution)/shard_map/ppermute | solution.py:380
  22.8 2.9 %collective-permute-done.4.got_ref = bf16[80,1024]{1,0:T(8,128)(2,1)S(1)} collective-permute-done((bf16[80,1024]{1,0:T(8,128)(2,1)S(1)}, bf16[80,1024]{1,0:T(8,128)(2,1)S(1)}, u32[]{:S(2)}, u32[]{:S(2)}) %collective-permute-start.4) | collective-permute-done | bytes 163872 | tf_op jit(solution)/shard_map/ppermute | solution.py:380
  25.7 4.4 %collective-permute-start.5 = (bf16[1,80,1024]{2,1,0:T(8,128)(2,1)S(1)}, bf16[1,80,1024]{2,1,0:T(8,128)(2,1)S(1)}, u32[]{:S(2)}, u32[]{:S(2)}) collective-permute-start(bf16[1,80,1024]{2,1,0:T(8,128)(2,1)S(1)} %bitcast.11), channel_id=1, source_target_pairs={{0,32},{32,0},{64,96},{96,64},{128,160},{160,128},{192,224},{224,1... | collective-permute-start | bytes 491528 | tf_op jit(solution)/shard_map/ppermute | solution.py:342
  30.1 4.3 %collective-permute-done.5.far_ref = bf16[1,80,1024]{2,1,0:T(8,128)(2,1)S(1)} collective-permute-done((bf16[1,80,1024]{2,1,0:T(8,128)(2,1)S(1)}, bf16[1,80,1024]{2,1,0:T(8,128)(2,1)S(1)}, u32[]{:S(2)}, u32[]{:S(2)}) %collective-permute-start.5) | collective-permute-done | bytes 163872 | tf_op jit(solution)/shard_map/ppermute | solution.py:342
  34.4 2.4 %collective-permute-start.6 = (bf16[2,80,1024]{2,1,0:T(8,128)(2,1)S(1)}, bf16[2,80,1024]{2,1,0:T(8,128)(2,1)S(1)}, u32[]{:S(2)}, u32[]{:S(2)}) collective-permute-start(bf16[2,80,1024]{2,1,0:T(8,128)(2,1)S(1)} %shard_map.116.near_ref), channel_id=1, source_target_pairs={{0,16},{16,0},{1,17},{17,1},{2,18},{18,2},{3,19},{19,3},{4,20},{20... | collective-permute-start | bytes 983048 | tf_op jit(solution)/shard_map/ppermute | solution.py:342
  39.1 4.1 %collective-permute-start = (bf16[640,128]{1,0:T(8,128)(2,1)}, bf16[640,128]{1,0:T(8,128)(2,1)}, u32[]{:S(2)}, u32[]{:S(2)}) collective-permute-start(bf16[640,128]{1,0:T(8,128)(2,1)} %get-tuple-element.64), channel_id=1, source_target_pairs={{0,1},{1,2},{2,3},{3,0},{4,5},{5,6},{6,7},{7,4},{8,9},{9,10},{10,1... | collective-permute-start | bytes 491528 | tf_op jit(solution)/shard_map/ppermute | solution.py:346
  43.2 2.3 %collective-permute-start.1 = (bf16[640,128]{1,0:T(8,128)(2,1)}, bf16[640,128]{1,0:T(8,128)(2,1)}, u32[]{:S(2)}, u32[]{:S(2)}) collective-permute-start(bf16[640,128]{1,0:T(8,128)(2,1)} %get-tuple-element.65), channel_id=1, source_target_pairs={{0,2},{1,3},{2,0},{3,1},{4,6},{5,7},{6,4},{7,5},{8,10},{9,11},{10,... | collective-permute-start | bytes 491528 | tf_op jit(solution)/shard_map/ppermute | solution.py:346
  45.9 6.3 %shard_map.112 = (bf16[2,2,1280,256]{3,2,1,0:T(8,128)(2,1)S(1)}, bf16[128,1024]{1,0:T(8,128)(2,1)S(1)}, f32[512,256]{1,0:T(8,128)S(1)}, bf16[512,256]{1,0:T(8,128)(2,1)S(1)}) custom-call(s32[32]{0:T(128)S(1)} %bitcast.13, s32[32]{0:T(128)S(1)} %copy-done.3, bf16[8,128,1280]{2,1,0:T(8,128)(2,1)S(1)} %all-to-all-done.refs_0_), custom_call_target="tpu_custom_call" | custom-call | bytes 5000 | tf_op jit(solution)/shard_map/pallas_call | solution.py:409
  56.7 3.0 %collective-permute-done.7.taken_ref = bf16[512,256]{1,0:T(8,128)(2,1)S(1)} collective-permute-done((bf16[512,256]{1,0:T(8,128)(2,1)S(1)}, bf16[512,256]{1,0:T(8,128)(2,1)S(1)}, u32[]{:S(2)}, u32[]{:S(2)}) %collective-permute-start.7) | collective-permute-done | bytes 262176 | tf_op jit(solution)/shard_map/ppermute | solution.py:433
  61.8 2.9 %collective-permute-start.8 = (bf16[512,256]{1,0:T(8,128)(2,1)S(1)}, bf16[512,256]{1,0:T(8,128)(2,1)S(1)}, u32[]{:S(2)}, u32[]{:S(2)}) collective-permute-start(bf16[512,256]{1,0:T(8,128)(2,1)S(1)} %shard_map.120.refs_0_), channel_id=1, source_target_pairs={{0,1},{1,2},{2,3},{3,0},{4,5},{5,6},{6,7},{7,4},{8,9},{9,10},{10,1... | collective-permute-start | bytes 786440 | tf_op jit(solution)/shard_map/ppermute | solution.py:346
  65.0 5.8 %collective-permute-done.10.refs_3_ = bf16[512,256]{1,0:T(8,128)(2,1)S(1)} collective-permute-done((bf16[512,256]{1,0:T(8,128)(2,1)S(1)}, bf16[512,256]{1,0:T(8,128)(2,1)S(1)}, u32[]{:S(2)}, u32[]{:S(2)}) %collective-permute-start.10) | collective-permute-done | bytes 262176 | tf_op jit(solution)/shard_map/ppermute | solution.py:346
  70.9 2.8 %collective-permute-done.8.refs_1_ = bf16[512,256]{1,0:T(8,128)(2,1)S(1)} collective-permute-done((bf16[512,256]{1,0:T(8,128)(2,1)S(1)}, bf16[512,256]{1,0:T(8,128)(2,1)S(1)}, u32[]{:S(2)}, u32[]{:S(2)}) %collective-permute-start.8) | collective-permute-done | bytes 262176 | tf_op jit(solution)/shard_map/ppermute | solution.py:346
  80.3 2.7 %collective-permute-start.15 = (bf16[1664,128]{1,0:T(8,128)(2,1)S(1)}, bf16[1664,128]{1,0:T(8,128)(2,1)S(1)}, u32[]{:S(2)}, u32[]{:S(2)}) collective-permute-start(bf16[1664,128]{1,0:T(8,128)(2,1)S(1)} %get-tuple-element.101), channel_id=1, source_target_pairs={{0,1},{1,2},{2,3},{3,0},{4,5},{5,6},{6,7},{7,4},{8,9},{9,10},{10,1... | collective-permute-start | bytes 1277960 | tf_op jit(solution)/shard_map/ppermute | solution.py:346
  83.5 4.6 %collective-permute-done.17.refs_1_ = bf16[160,1024]{1,0:T(8,128)(2,1)S(1)} collective-permute-done((bf16[160,1024]{1,0:T(8,128)(2,1)S(1)}, bf16[160,1024]{1,0:T(8,128)(2,1)S(1)}, u32[]{:S(2)}, u32[]{:S(2)}) %collective-permute-start.17) | collective-permute-done | bytes 327712 | tf_op jit(solution)/shard_map/ppermute | solution.py:524
  88.3 2.4 %collective-permute-start.18 = (bf16[80,1024]{1,0:T(8,128)(2,1)S(1)}, bf16[80,1024]{1,0:T(8,128)(2,1)S(1)}, u32[]{:S(2)}, u32[]{:S(2)}) collective-permute-start(bf16[80,1024]{1,0:T(8,128)(2,1)S(1)} %get-tuple-element.111), channel_id=1, source_target_pairs={{0,32},{32,0},{64,96},{96,64},{128,160},{160,128},{192,224},{224,1... | collective-permute-start | bytes 491528 | tf_op jit(solution)/shard_map/ppermute | solution.py:524
  90.7 4.1 %collective-permute-done.18.refs_1_ = bf16[80,1024]{1,0:T(8,128)(2,1)S(1)} collective-permute-done((bf16[80,1024]{1,0:T(8,128)(2,1)S(1)}, bf16[80,1024]{1,0:T(8,128)(2,1)S(1)}, u32[]{:S(2)}, u32[]{:S(2)}) %collective-permute-start.18) | collective-permute-done | bytes 163872 | tf_op jit(solution)/shard_map/ppermute | solution.py:524
  94.9 2.4 %collective-permute-start.19 = (bf16[40,1024]{1,0:T(8,128)(2,1)S(1)}, bf16[40,1024]{1,0:T(8,128)(2,1)S(1)}, u32[]{:S(2)}, u32[]{:S(2)}) collective-permute-start(bf16[40,1024]{1,0:T(8,128)(2,1)S(1)} %get-tuple-element.113), channel_id=1, source_target_pairs={{0,16},{16,0},{1,17},{17,1},{2,18},{18,2},{3,19},{19,3},{4,20},{20... | collective-permute-start | bytes 245768 | tf_op jit(solution)/shard_map/ppermute | solution.py:524
  97.3 3.6 %collective-permute-done.19.refs_1_ = bf16[40,1024]{1,0:T(8,128)(2,1)S(1)} collective-permute-done((bf16[40,1024]{1,0:T(8,128)(2,1)S(1)}, bf16[40,1024]{1,0:T(8,128)(2,1)S(1)}, u32[]{:S(2)}, u32[]{:S(2)}) %collective-permute-start.19) | collective-permute-done | bytes 81952 | tf_op jit(solution)/shard_map/ppermute | solution.py:524
  100.9 3.4 %collective-permute-start.20 = (bf16[20,1024]{1,0:T(8,128)(2,1)S(1)}, bf16[20,1024]{1,0:T(8,128)(2,1)S(1)}, u32[]{:S(2)}, u32[]{:S(2)}) collective-permute-start(bf16[20,1024]{1,0:T(8,128)(2,1)S(1)} %get-tuple-element.115), channel_id=1, source_target_pairs={{0,64},{32,96},{64,0},{96,32},{128,192},{160,224},{192,128},{224,1... | collective-permute-start | bytes 122888 | tf_op jit(solution)/shard_map/ppermute | solution.py:524
  104.3 2.1 %collective-permute-done.20.refs_1_ = bf16[20,1024]{1,0:T(8,128)(2,1)S(1)} collective-permute-done((bf16[20,1024]{1,0:T(8,128)(2,1)S(1)}, bf16[20,1024]{1,0:T(8,128)(2,1)S(1)}, u32[]{:S(2)}, u32[]{:S(2)}) %collective-permute-start.20) | collective-permute-done | bytes 40992 | tf_op jit(solution)/shard_map/ppermute | solution.py:524
  106.4 6.8 %collective-permute-start.21 = (bf16[10,1024]{1,0:T(8,128)(2,1)S(1)}, bf16[10,1024]{1,0:T(8,128)(2,1)S(1)}, u32[]{:S(2)}, u32[]{:S(2)}) collective-permute-start(bf16[10,1024]{1,0:T(8,128)(2,1)S(1)} %get-tuple-element.117), channel_id=1, source_target_pairs={{0,128},{32,160},{64,192},{96,224},{128,0},{160,32},{192,64},{224,... | collective-permute-start | bytes 61448 | tf_op jit(solution)/shard_map/ppermute | solution.py:524
  (50 shorter events, 21.0 us)
Async XLA Ops:
  3.6 42.4 %copy-start.2 = (s32[1,32]{1,0:T(1,128)S(1)}, s32[1,32]{1,0:T(1,128)}, u32[]{:S(2)}) copy-start(s32[1,32]{1,0:T(1,128)} %param.14) | copy-start | bytes 388
  3.6 42.3 %all-to-all-start = ((bf16[8,128,1280]{2,1,0:T(8,128)(2,1)}), bf16[8,128,1280]{2,1,0:T(8,128)(2,1)S(1)}, u32[]{:S(2)}, u32[]{:S(2)}) async-start(bf16[8,128,1280]{2,1,0:T(8,128)(2,1)} %shard_map.111), calls=%async_computation | async-start | bytes 5242880 | tf_op jit(solution)/shard_map/all_to_all | solution.py:350
  9.5 12.0 %collective-permute-start.3 = (bf16[80,1024]{1,0:T(8,128)(2,1)S(1)}, bf16[80,1024]{1,0:T(8,128)(2,1)S(1)}, u32[]{:S(2)}, u32[]{:S(2)}) collective-permute-start(bf16[80,1024]{1,0:T(8,128)(2,1)S(1)} %copy-done.1), channel_id=1, source_target_pairs={{0,128},{32,160},{65,193},{97,225},{130,2},{162,34},{195,67},{227,... | collective-permute-start | bytes 491528 | tf_op jit(solution)/shard_map/ppermute | solution.py:380
  21.5 4.2 %collective-permute-start.4 = (bf16[80,1024]{1,0:T(8,128)(2,1)S(1)}, bf16[80,1024]{1,0:T(8,128)(2,1)S(1)}, u32[]{:S(2)}, u32[]{:S(2)}) collective-permute-start(bf16[80,1024]{1,0:T(8,128)(2,1)S(1)} %shard_map.114.own_ref), channel_id=1, source_target_pairs={{0,64},{2,66},{32,96},{34,98},{65,1},{67,3},{97,33},{99,35},{128,1... | collective-permute-start | bytes 491528 | tf_op jit(solution)/shard_map/ppermute | solution.py:380
  25.7 8.7 %collective-permute-start.5 = (bf16[1,80,1024]{2,1,0:T(8,128)(2,1)S(1)}, bf16[1,80,1024]{2,1,0:T(8,128)(2,1)S(1)}, u32[]{:S(2)}, u32[]{:S(2)}) collective-permute-start(bf16[1,80,1024]{2,1,0:T(8,128)(2,1)S(1)} %bitcast.11), channel_id=1, source_target_pairs={{0,32},{32,0},{64,96},{96,64},{128,160},{160,128},{192,224},{224,1... | collective-permute-start | bytes 491528 | tf_op jit(solution)/shard_map/ppermute | solution.py:342
  34.4 18.4 %collective-permute-start.6 = (bf16[2,80,1024]{2,1,0:T(8,128)(2,1)S(1)}, bf16[2,80,1024]{2,1,0:T(8,128)(2,1)S(1)}, u32[]{:S(2)}, u32[]{:S(2)}) collective-permute-start(bf16[2,80,1024]{2,1,0:T(8,128)(2,1)S(1)} %shard_map.116.near_ref), channel_id=1, source_target_pairs={{0,16},{16,0},{1,17},{17,1},{2,18},{18,2},{3,19},{19,3},{4,20},{20... | collective-permute-start | bytes 983048 | tf_op jit(solution)/shard_map/ppermute | solution.py:342
  39.1 13.2 %collective-permute-start = (bf16[640,128]{1,0:T(8,128)(2,1)}, bf16[640,128]{1,0:T(8,128)(2,1)}, u32[]{:S(2)}, u32[]{:S(2)}) collective-permute-start(bf16[640,128]{1,0:T(8,128)(2,1)} %get-tuple-element.64), channel_id=1, source_target_pairs={{0,1},{1,2},{2,3},{3,0},{4,5},{5,6},{6,7},{7,4},{8,9},{9,10},{10,1... | collective-permute-start | bytes 491528 | tf_op jit(solution)/shard_map/ppermute | solution.py:346
  43.2 9.0 %collective-permute-start.1 = (bf16[640,128]{1,0:T(8,128)(2,1)}, bf16[640,128]{1,0:T(8,128)(2,1)}, u32[]{:S(2)}, u32[]{:S(2)}) collective-permute-start(bf16[640,128]{1,0:T(8,128)(2,1)} %get-tuple-element.65), channel_id=1, source_target_pairs={{0,2},{1,3},{2,0},{3,1},{4,6},{5,7},{6,4},{7,5},{8,10},{9,11},{10,... | collective-permute-start | bytes 491528 | tf_op jit(solution)/shard_map/ppermute | solution.py:346
  45.6 7.2 %collective-permute-start.2 = (bf16[640,128]{1,0:T(8,128)(2,1)}, bf16[640,128]{1,0:T(8,128)(2,1)}, u32[]{:S(2)}, u32[]{:S(2)}) collective-permute-start(bf16[640,128]{1,0:T(8,128)(2,1)} %get-tuple-element.66), channel_id=1, source_target_pairs={{0,3},{1,0},{2,1},{3,2},{4,7},{5,4},{6,5},{7,6},{8,11},{9,8},{10,9... | collective-permute-start | bytes 491528 | tf_op jit(solution)/shard_map/ppermute | solution.py:346
  52.8 6.9 %collective-permute-start.7 = (bf16[512,256]{1,0:T(8,128)(2,1)S(1)}, bf16[512,256]{1,0:T(8,128)(2,1)S(1)}, u32[]{:S(2)}, u32[]{:S(2)}) collective-permute-start(bf16[512,256]{1,0:T(8,128)(2,1)S(1)} %get-tuple-element.68), channel_id=1, source_target_pairs={{0,4},{4,0},{1,5},{5,1},{2,6},{6,2},{3,7},{7,3},{8,12},{12,8},{9,1... | collective-permute-start | bytes 786440 | tf_op jit(solution)/shard_map/ppermute | solution.py:433
  55.4 19.2 %collective-permute-start.12 = (bf16[4,80,1024]{2,1,0:T(8,128)(2,1)S(1)}, bf16[4,80,1024]{2,1,0:T(8,128)(2,1)S(1)}, u32[]{:S(2)}, u32[]{:S(2)}) collective-permute-start(bf16[4,80,1024]{2,1,0:T(8,128)(2,1)S(1)} %shard_map.118.w_ref), channel_id=1, source_target_pairs={{0,8},{8,0},{1,9},{9,1},{2,10},{10,2},{3,11},{11,3},{4,12},{12,4},... | collective-permute-start | bytes 1966088 | tf_op jit(solution)/shard_map/ppermute | solution.py:342
  59.7 14.8 %collective-permute-start.11 = (bf16[4,512,128]{2,1,0:T(8,128)(2,1)S(1)}, bf16[4,512,128]{2,1,0:T(8,128)(2,1)S(1)}, u32[]{:S(2)}, u32[]{:S(2)}) collective-permute-start(bf16[4,512,128]{2,1,0:T(8,128)(2,1)S(1)} %get-tuple-element.83), channel_id=1, source_target_pairs={{0,4},{4,0},{1,5},{5,1},{2,6},{6,2},{3,7},{7,3},{8,12},{12,8},{9,1... | collective-permute-start | bytes 1572872 | tf_op jit(solution)/shard_map/ppermute | solution.py:470
  60.1 10.8 %collective-permute-start.10 = (bf16[512,256]{1,0:T(8,128)(2,1)S(1)}, bf16[512,256]{1,0:T(8,128)(2,1)S(1)}, u32[]{:S(2)}, u32[]{:S(2)}) collective-permute-start(bf16[512,256]{1,0:T(8,128)(2,1)S(1)} %shard_map.120.refs_0_), channel_id=1, source_target_pairs={{0,2},{1,3},{2,0},{3,1},{4,6},{5,7},{6,4},{7,5},{8,10},{9,11},{10,... | collective-permute-start | bytes 786440 | tf_op jit(solution)/shard_map/ppermute | solution.py:346
  61.8 11.9 %collective-permute-start.8 = (bf16[512,256]{1,0:T(8,128)(2,1)S(1)}, bf16[512,256]{1,0:T(8,128)(2,1)S(1)}, u32[]{:S(2)}, u32[]{:S(2)}) collective-permute-start(bf16[512,256]{1,0:T(8,128)(2,1)S(1)} %shard_map.120.refs_0_), channel_id=1, source_target_pairs={{0,1},{1,2},{2,3},{3,0},{4,5},{5,6},{6,7},{7,4},{8,9},{9,10},{10,1... | collective-permute-start | bytes 786440 | tf_op jit(solution)/shard_map/ppermute | solution.py:346
  64.7 9.9 %collective-permute-start.9 = (bf16[512,256]{1,0:T(8,128)(2,1)S(1)}, bf16[512,256]{1,0:T(8,128)(2,1)S(1)}, u32[]{:S(2)}, u32[]{:S(2)}) collective-permute-start(bf16[512,256]{1,0:T(8,128)(2,1)S(1)} %shard_map.120.refs_0_), channel_id=1, source_target_pairs={{0,3},{1,0},{2,1},{3,2},{4,7},{5,4},{6,5},{7,6},{8,11},{9,8},{10,9... | collective-permute-start | bytes 786440 | tf_op jit(solution)/shard_map/ppermute | solution.py:346
  75.3 2.4 %collective-permute-start.13 = (bf16[320,1024]{1,0:T(8,128)(2,1)S(1)}, bf16[320,1024]{1,0:T(8,128)(2,1)S(1)}, u32[]{:S(2)}, u32[]{:S(2)}) collective-permute-start(bf16[320,1024]{1,0:T(8,128)(2,1)S(1)} %get-tuple-element.89), channel_id=1, source_target_pairs={{0,8},{8,0},{1,9},{9,1},{2,10},{10,2},{3,11},{11,3},{4,12},{12,4},... | collective-permute-start | bytes 1966088 | tf_op jit(solution)/shard_map/ppermute | solution.py:342
  78.0 10.2 %collective-permute-start.17 = (bf16[160,1024]{1,0:T(8,128)(2,1)S(1)}, bf16[160,1024]{1,0:T(8,128)(2,1)S(1)}, u32[]{:S(2)}, u32[]{:S(2)}) collective-permute-start(bf16[160,1024]{1,0:T(8,128)(2,1)S(1)} %get-tuple-element.109), channel_id=1, source_target_pairs={{0,4},{4,0},{1,5},{5,1},{2,6},{6,2},{3,7},{7,3},{8,12},{12,8},{9,1... | collective-permute-start | bytes 983048 | tf_op jit(solution)/shard_map/ppermute | solution.py:524
  79.4 33.8 %collective-permute-start.14 = (bf16[1664,128]{1,0:T(8,128)(2,1)S(1)}, bf16[1664,128]{1,0:T(8,128)(2,1)S(1)}, u32[]{:S(2)}, u32[]{:S(2)}) collective-permute-start(bf16[1664,128]{1,0:T(8,128)(2,1)S(1)} %get-tuple-element.100), channel_id=1, source_target_pairs={{0,2},{1,3},{2,0},{3,1},{4,6},{5,7},{6,4},{7,5},{8,10},{9,11},{10,... | collective-permute-start | bytes 1277960 | tf_op jit(solution)/shard_map/ppermute | solution.py:346
  80.3 32.9 %collective-permute-start.15 = (bf16[1664,128]{1,0:T(8,128)(2,1)S(1)}, bf16[1664,128]{1,0:T(8,128)(2,1)S(1)}, u32[]{:S(2)}, u32[]{:S(2)}) collective-permute-start(bf16[1664,128]{1,0:T(8,128)(2,1)S(1)} %get-tuple-element.101), channel_id=1, source_target_pairs={{0,1},{1,2},{2,3},{3,0},{4,5},{5,6},{6,7},{7,4},{8,9},{9,10},{10,1... | collective-permute-start | bytes 1277960 | tf_op jit(solution)/shard_map/ppermute | solution.py:346
  83.0 30.3 %collective-permute-start.16 = (bf16[1664,128]{1,0:T(8,128)(2,1)S(1)}, bf16[1664,128]{1,0:T(8,128)(2,1)S(1)}, u32[]{:S(2)}, u32[]{:S(2)}) collective-permute-start(bf16[1664,128]{1,0:T(8,128)(2,1)S(1)} %get-tuple-element.102), channel_id=1, source_target_pairs={{0,3},{1,0},{2,1},{3,2},{4,7},{5,4},{6,5},{7,6},{8,11},{9,8},{10,9... | collective-permute-start | bytes 1277960 | tf_op jit(solution)/shard_map/ppermute | solution.py:346
  88.3 6.5 %collective-permute-start.18 = (bf16[80,1024]{1,0:T(8,128)(2,1)S(1)}, bf16[80,1024]{1,0:T(8,128)(2,1)S(1)}, u32[]{:S(2)}, u32[]{:S(2)}) collective-permute-start(bf16[80,1024]{1,0:T(8,128)(2,1)S(1)} %get-tuple-element.111), channel_id=1, source_target_pairs={{0,32},{32,0},{64,96},{96,64},{128,160},{160,128},{192,224},{224,1... | collective-permute-start | bytes 491528 | tf_op jit(solution)/shard_map/ppermute | solution.py:524
  94.9 6.0 %collective-permute-start.19 = (bf16[40,1024]{1,0:T(8,128)(2,1)S(1)}, bf16[40,1024]{1,0:T(8,128)(2,1)S(1)}, u32[]{:S(2)}, u32[]{:S(2)}) collective-permute-start(bf16[40,1024]{1,0:T(8,128)(2,1)S(1)} %get-tuple-element.113), channel_id=1, source_target_pairs={{0,16},{16,0},{1,17},{17,1},{2,18},{18,2},{3,19},{19,3},{4,20},{20... | collective-permute-start | bytes 245768 | tf_op jit(solution)/shard_map/ppermute | solution.py:524
  100.9 5.4 %collective-permute-start.20 = (bf16[20,1024]{1,0:T(8,128)(2,1)S(1)}, bf16[20,1024]{1,0:T(8,128)(2,1)S(1)}, u32[]{:S(2)}, u32[]{:S(2)}) collective-permute-start(bf16[20,1024]{1,0:T(8,128)(2,1)S(1)} %get-tuple-element.115), channel_id=1, source_target_pairs={{0,64},{32,96},{64,0},{96,32},{128,192},{160,224},{192,128},{224,1... | collective-permute-start | bytes 122888 | tf_op jit(solution)/shard_map/ppermute | solution.py:524
  106.4 8.8 %collective-permute-start.21 = (bf16[10,1024]{1,0:T(8,128)(2,1)S(1)}, bf16[10,1024]{1,0:T(8,128)(2,1)S(1)}, u32[]{:S(2)}, u32[]{:S(2)}) collective-permute-start(bf16[10,1024]{1,0:T(8,128)(2,1)S(1)} %get-tuple-element.117), channel_id=1, source_target_pairs={{0,128},{32,160},{64,192},{96,224},{128,0},{160,32},{192,64},{224,... | collective-permute-start | bytes 61448 | tf_op jit(solution)/shard_map/ppermute | solution.py:524
  (3 other events, 49.4 us)
